TPU v7x, 32 devices: a whole 2x2x4 slice. The times are simulated.
32 devices in a mesh: fsdp: 4 (over x, core), ctx: 4 (over z), tp: 2 (over y).
Axes of the slice: x: 2, y: 2, z: 4, core: 2. Of those that a mesh axis runs over, the one named last changes fastest.
Arguments:
- tokens: bfloat16 [4096, 2048], P(('fsdp', 'ctx')), may hold values from -7 to 7
- cotangent: bfloat16 [4096, 2048], P(('fsdp', 'ctx')), may hold values from -6 to 6
- attn_routes: int32 [4096, 2], P(('fsdp', 'ctx')), may hold values from 0 to 3, as said below
- ffn_routes: int32 [4096, 2], P(('fsdp', 'ctx')), may hold values from 0 to 3, as said below
- norm_gain1: float32 [2048], replicated, may hold values from 0.1 to 1.9
- norm_gain2: float32 [2048], replicated, may hold values from 0.1 to 1.9
- attn_router: bfloat16 [2048, 4], replicated, may hold values from -1 to 1
- ffn_router: bfloat16 [2048, 4], replicated, may hold values from -1 to 1
- key_proj: bfloat16 [2048, 2048], P(('fsdp', 'ctx'), 'tp'), may hold values from -0.125 to 0.125
- value_proj: bfloat16 [2048, 2048], P(('fsdp', 'ctx'), 'tp'), may hold values from -0.125 to 0.125
- query_proj: bfloat16 [4, 2048, 2048], P('ctx', 'fsdp', 'tp'), may hold values from -0.125 to 0.125
- out_proj: bfloat16 [4, 2048, 2048], P('ctx', 'tp', 'fsdp'), may hold values from -0.5 to 0.5
- gate_proj: bfloat16 [4, 2048, 5632], P('ctx', 'fsdp', 'tp'), may hold values from -0.125 to 0.125
- up_proj: bfloat16 [4, 2048, 5632], P('ctx', 'fsdp', 'tp'), may hold values from -0.125 to 0.125
- down_proj: bfloat16 [4, 5632, 2048], P('ctx', 'tp', 'fsdp'), may hold values from -0.078125 to 0.078125
Outputs:
- output: bfloat16 [4096, 2048], P(('fsdp', 'ctx'))
- input_grad: float32 [4096, 2048], P(('fsdp', 'ctx'))
- attn_loss: float32 [], replicated
- ffn_loss: float32 [], replicated
- gain1_grad: float32 [2048], replicated
- gain2_grad: float32 [2048], replicated
- attn_router_grad: float32 [2048, 4], replicated
- ffn_router_grad: float32 [2048, 4], replicated
- key_grad: float32 [2048, 2048], P(('fsdp', 'ctx'), 'tp')
- value_grad: float32 [2048, 2048], P(('fsdp', 'ctx'), 'tp')
- query_grad: float32 [4, 2048, 2048], P('ctx', 'fsdp', 'tp')
- out_proj_grad: float32 [4, 2048, 2048], P('ctx', 'tp', 'fsdp')
- gate_grad: float32 [4, 2048, 5632], P('ctx', 'fsdp', 'tp')
- up_grad: float32 [4, 2048, 5632], P('ctx', 'fsdp', 'tp')
- down_grad: float32 [4, 5632, 2048], P('ctx', 'tp', 'fsdp')
Inputs may be any that keep to these rules, and one draw needn't show every extreme that they name: `attn_routes`: each row names 2 different attention experts; in each aligned block of 256 rows (the rows of one device) no expert is named more than 160 times, and some expert exactly 160 times; every expert is named by some row. `ffn_routes`: each row names 2 different feed-forward experts; in each aligned block of 256 rows (the rows of one device) no expert is named more than 160 times, and some expert exactly 160 times; every expert is named by some row.
All inputs are finite; a program needn't handle non-finite values.
Results may differ from a plain program's by a relative error of at most 0.023.
Values may be sent and summed in bfloat16 or wider, within the bound.
A program may use at most 256 MiB of HBM per device.

v0:
```python
import math

import jax
import jax.numpy as jnp
from jax import lax
from jax.sharding import PartitionSpec as P

HEAD = 128
BLOCK = 256


EPSILON = 1e-06
ROPE_BASE = 10000.0
AUX_WEIGHT = 0.1
MASKED = -1e30
PRECISE = lax.Precision.HIGHEST


def matmul(lhs_mat, rhs_mat):
    return jnp.dot(lhs_mat, rhs_mat, preferred_element_type=jnp.float32)


def matmul_tn(lhs_mat, rhs_mat):
    return lax.dot_general(
        lhs_mat, rhs_mat, (((0,), (0,)), ((), ())), preferred_element_type=jnp.float32
    )


def matmul_nt(lhs_mat, rhs_mat):
    return lax.dot_general(
        lhs_mat, rhs_mat, (((1,), (1,)), ((), ())), preferred_element_type=jnp.float32
    )


def precise_tn(lhs_mat, rhs_mat):
    return lax.dot_general(lhs_mat, rhs_mat, (((0,), (0,)), ((), ())), precision=PRECISE)


def precise_nt(lhs_mat, rhs_mat):
    return lax.dot_general(lhs_mat, rhs_mat, (((1,), (1,)), ((), ())), precision=PRECISE)


def norm_apply(values, gain_vec):
    norm_scale = lax.rsqrt(jnp.mean(values * values, axis=-1, keepdims=True) + EPSILON)
    return (values * norm_scale * gain_vec, norm_scale)


def norm_back(values, norm_scale, gain_vec, upstream):
    weighted = upstream * gain_vec
    inner_mean = jnp.mean(weighted * values, axis=-1, keepdims=True)
    d_values = norm_scale * weighted - values * norm_scale**3 * inner_mean
    d_gain = jnp.sum(upstream * values * norm_scale, axis=0)
    return (d_values, d_gain)


def rope_tables(places):
    half_head = HEAD // 2
    frequency = ROPE_BASE ** (-jnp.arange(half_head, dtype=jnp.float32) * 2.0 / HEAD)
    angles = places.astype(jnp.float32)[:, None] * frequency[None, :]
    return (jnp.cos(angles)[:, None, :], jnp.sin(angles)[:, None, :])


def rotate(values, cos_table, sin_table, direction):
    half_head = HEAD // 2
    pieces = values.reshape(values.shape[0], -1, HEAD)
    first_half = pieces[..., :half_head]
    second = pieces[..., half_head:]
    turned = jnp.concatenate(
        [
            first_half * cos_table - direction * second * sin_table,
            second * cos_table + direction * first_half * sin_table,
        ],
        axis=-1,
    )
    return turned.reshape(values.shape)


def route_table(routes, expert_count, capacity):
    rows_here, pick_count = routes.shape
    flat_routes = routes.reshape(-1)
    onehot = (flat_routes[:, None] == jnp.arange(expert_count, dtype=jnp.int32)[None, :]).astype(
        jnp.int32
    )
    within = jnp.sum(onehot * (jnp.cumsum(onehot, axis=0) - 1), axis=1)
    slot_of = flat_routes * capacity + within
    slot_match = slot_of[None, :] == jnp.arange(expert_count * capacity, dtype=jnp.int32)[:, None]
    owners = jnp.arange(rows_here * pick_count, dtype=jnp.int32) // pick_count
    slot_token = jnp.sum(jnp.where(slot_match, owners[None, :], 0), axis=1)
    filled = jnp.any(slot_match, axis=1)
    return (slot_of.reshape(rows_here, pick_count), slot_token, filled, slot_match)


def slot_gates(slot_match, gate_mix):
    return jnp.sum(jnp.where(slot_match, gate_mix.reshape(-1)[None, :], 0.0), axis=1)


def collect(returned, slot_of):
    features = returned.shape[-1]
    flat_back = returned.reshape(-1, features)
    picked = jnp.take(flat_back, slot_of.reshape(-1), axis=0)
    return picked.reshape(slot_of.shape[0], slot_of.shape[1], features).astype(jnp.float32)


def router_back(gate_mix, gate_grad, probs_all, routes, expert_count, share, all_tokens):
    d_chosen = gate_mix * (gate_grad - jnp.sum(gate_mix * gate_grad, axis=1, keepdims=True))
    onehot = (
        routes[:, :, None] == jnp.arange(expert_count, dtype=jnp.int32)[None, None, :]
    ).astype(jnp.float32)
    d_logits = jnp.sum(onehot * d_chosen[:, :, None], axis=1)
    d_probs = AUX_WEIGHT * expert_count / all_tokens * share
    return d_logits + probs_all * (
        d_probs[None, :] - jnp.sum(probs_all * d_probs[None, :], axis=1, keepdims=True)
    )


def head_total(partial_sum):
    return lax.psum(partial_sum.astype(jnp.bfloat16), "tp").astype(jnp.float32)


def to_experts(slot_rows):
    return lax.all_to_all(slot_rows, "ctx", split_axis=0, concat_axis=0, tiled=True)


def from_experts(slot_rows):
    return lax.all_to_all(slot_rows, "ctx", split_axis=0, concat_axis=0, tiled=True)


def heads_forward(query_low, seq_keys, seq_values, allowed, head_scale):
    head_count = query_low.shape[1] // HEAD
    slot_rows = query_low.shape[0]

    def head_step(head_index, state_pair):
        outputs, log_sums = state_pair
        offset = head_index * HEAD
        query_head = lax.dynamic_slice_in_dim(query_low, offset, HEAD, 1)
        key_head = lax.dynamic_slice_in_dim(seq_keys, offset, HEAD, 1)
        value_head = lax.dynamic_slice_in_dim(seq_values, offset, HEAD, 1)
        scores = jnp.where(allowed, matmul_nt(query_head, key_head) * head_scale, MASKED)
        top_score = jnp.max(scores, axis=1, keepdims=True)
        exponents = jnp.exp(scores - top_score)
        totals = jnp.sum(exponents, axis=1, keepdims=True)
        weights = (exponents / totals).astype(jnp.bfloat16)
        outputs = lax.dynamic_update_slice_in_dim(outputs, matmul(weights, value_head), offset, 1)
        log_row = (top_score + jnp.log(totals)).reshape(1, slot_rows)
        log_sums = lax.dynamic_update_slice_in_dim(log_sums, log_row, head_index, 0)
        return (outputs, log_sums)

    initial = (
        jnp.zeros((slot_rows, head_count * HEAD), jnp.float32),
        jnp.zeros((head_count, slot_rows), jnp.float32),
    )
    return lax.fori_loop(0, head_count, head_step, initial)


def heads_backward(query_low, seq_keys, seq_values, allowed, log_sums, grad_heads, head_scale):
    head_count = query_low.shape[1] // HEAD

    def head_step(head_index, state_all):
        d_query, d_keys, d_values = state_all
        offset = head_index * HEAD
        query_head = lax.dynamic_slice_in_dim(query_low, offset, HEAD, 1)
        key_head = lax.dynamic_slice_in_dim(seq_keys, offset, HEAD, 1)
        value_head = lax.dynamic_slice_in_dim(seq_values, offset, HEAD, 1)
        grad_head = lax.dynamic_slice_in_dim(grad_heads, offset, HEAD, 1)
        scores = jnp.where(allowed, matmul_nt(query_head, key_head) * head_scale, MASKED)
        log_row = lax.dynamic_slice_in_dim(log_sums, head_index, 1, 0).reshape(-1, 1)
        weights = jnp.exp(scores - log_row)
        d_weights = matmul_nt(grad_head, value_head)
        delta_row = jnp.sum(weights * d_weights, axis=1, keepdims=True)
        d_scores = (weights * (d_weights - delta_row)).astype(jnp.bfloat16)
        d_query = lax.dynamic_update_slice_in_dim(
            d_query, matmul(d_scores, key_head) * head_scale, offset, 1
        )
        d_keys = lax.dynamic_update_slice_in_dim(
            d_keys, matmul_tn(d_scores, query_head) * head_scale, offset, 1
        )
        d_values = lax.dynamic_update_slice_in_dim(
            d_values, matmul_tn(weights.astype(jnp.bfloat16), grad_head), offset, 1
        )
        return (d_query, d_keys, d_values)

    initial = (
        jnp.zeros(query_low.shape, jnp.float32),
        jnp.zeros(seq_keys.shape, jnp.float32),
        jnp.zeros(seq_values.shape, jnp.float32),
    )
    return lax.fori_loop(0, head_count, head_step, initial)


def on_device(
    tokens,
    cotangent,
    attn_routes,
    ffn_routes,
    norm_gain1,
    norm_gain2,
    attn_router,
    ffn_router,
    key_proj,
    value_proj,
    query_proj,
    out_proj,
    gate_proj,
    up_proj,
    down_proj,
):
    rows_here, features = tokens.shape
    pick_count = attn_routes.shape[1]
    expert_count = attn_router.shape[1]
    capacity = rows_here * pick_count // expert_count * 5 // 4
    all_tokens = rows_here * lax.axis_size("fsdp") * lax.axis_size("ctx")
    head_scale = 1.0 / math.sqrt(HEAD)
    places = lax.axis_index("ctx") * rows_here + jnp.arange(rows_here, dtype=jnp.int32)
    cos_keys, sin_keys = rope_tables(places)
    expert_full = (
        lax.all_gather(query_proj, "fsdp", axis=1, tiled=True),
        lax.all_gather(out_proj, "fsdp", axis=2, tiled=True),
        lax.all_gather(gate_proj, "fsdp", axis=1, tiled=True),
        lax.all_gather(up_proj, "fsdp", axis=1, tiled=True),
        lax.all_gather(down_proj, "fsdp", axis=2, tiled=True),
    )
    query_full, out_full, gate_full, up_full, down_full = [piece[0] for piece in expert_full]
    key_full, value_full = (
        lax.all_gather(key_proj, ("fsdp", "ctx"), axis=0, tiled=True),
        lax.all_gather(value_proj, ("fsdp", "ctx"), axis=0, tiled=True),
    )
    inputs = tokens.astype(jnp.float32)
    normed1, scale_one = norm_apply(inputs, norm_gain1)
    a_low = normed1.astype(jnp.bfloat16)
    attn_logits = matmul(a_low, attn_router)
    attn_probs = jax.nn.softmax(attn_logits, axis=1)
    attn_gates = jax.nn.softmax(jnp.take_along_axis(attn_logits, attn_routes, axis=1), axis=1)
    key_low = rotate(matmul(a_low, key_full), cos_keys, sin_keys, 1.0).astype(jnp.bfloat16)
    value_low = matmul(a_low, value_full).astype(jnp.bfloat16)
    seq_keys, seq_values = (
        lax.all_gather(key_low, "ctx", axis=0, tiled=True),
        lax.all_gather(value_low, "ctx", axis=0, tiled=True),
    )
    attn_slot, attn_token, attn_filled, attn_match = route_table(
        attn_routes, expert_count, capacity
    )
    query_rows = jnp.where(
        attn_filled[:, None], jnp.take(a_low, attn_token, axis=0), jnp.zeros((), jnp.bfloat16)
    )
    query_places = jnp.where(attn_filled, jnp.take(places, attn_token), 0)
    recv_rows, recv_places = (
        lax.all_to_all(
            query_rows.reshape(expert_count, capacity, features),
            "ctx",
            split_axis=0,
            concat_axis=0,
            tiled=True,
        ),
        lax.all_to_all(
            query_places.reshape(expert_count, capacity),
            "ctx",
            split_axis=0,
            concat_axis=0,
            tiled=True,
        ),
    )
    rows_in = recv_rows.reshape(-1, features)
    slot_places = recv_places.reshape(-1)
    cos_query, sin_query = rope_tables(slot_places)
    query_low = rotate(matmul(rows_in, query_full), cos_query, sin_query, 1.0).astype(jnp.bfloat16)
    key_blocks = jnp.arange(seq_keys.shape[0], dtype=jnp.int32) // BLOCK
    allowed = key_blocks[None, :] <= (slot_places // BLOCK)[:, None]
    heads_out, log_sums = heads_forward(query_low, seq_keys, seq_values, allowed, head_scale)
    heads_low = heads_out.astype(jnp.bfloat16)
    attn_expert = head_total(matmul(heads_low, out_full)).astype(jnp.bfloat16)
    attn_back = from_experts(attn_expert.reshape(expert_count, capacity, features))
    attn_picked = collect(attn_back, attn_slot)
    attended = inputs + jnp.sum(attn_gates[:, :, None] * attn_picked, axis=1)
    normed2, scale_two = norm_apply(attended, norm_gain2)
    b_low = normed2.astype(jnp.bfloat16)
    ffn_logits = matmul(b_low, ffn_router)
    ffn_probs = jax.nn.softmax(ffn_logits, axis=1)
    ffn_gates = jax.nn.softmax(jnp.take_along_axis(ffn_logits, ffn_routes, axis=1), axis=1)
    ffn_slot, ffn_token, ffn_filled, ffn_match = route_table(ffn_routes, expert_count, capacity)
    ffn_rows = jnp.where(
        ffn_filled[:, None], jnp.take(b_low, ffn_token, axis=0), jnp.zeros((), jnp.bfloat16)
    )
    rows_ffn = to_experts(ffn_rows.reshape(expert_count, capacity, features)).reshape(-1, features)
    gate_lin = matmul(rows_ffn, gate_full)
    up_lin = matmul(rows_ffn, up_full)
    hidden_low = (jax.nn.silu(gate_lin) * up_lin).astype(jnp.bfloat16)
    ffn_expert = head_total(matmul(hidden_low, down_full)).astype(jnp.bfloat16)
    ffn_back = from_experts(ffn_expert.reshape(expert_count, capacity, features))
    ffn_picked = collect(ffn_back, ffn_slot)
    result = attended + jnp.sum(ffn_gates[:, :, None] * ffn_picked, axis=1)
    output = result.astype(jnp.bfloat16)
    expert_ids = jnp.arange(expert_count, dtype=jnp.int32)[None, None, :]
    attn_hits = jnp.sum((attn_routes[:, :, None] == expert_ids).astype(jnp.float32), axis=(0, 1))
    ffn_hits = jnp.sum((ffn_routes[:, :, None] == expert_ids).astype(jnp.float32), axis=(0, 1))
    stat_totals = lax.psum(
        (attn_hits, ffn_hits, jnp.sum(attn_probs, axis=0), jnp.sum(ffn_probs, axis=0)),
        ("fsdp", "ctx"),
    )
    attn_share = stat_totals[0] / (all_tokens * pick_count)
    ffn_share = stat_totals[1] / (all_tokens * pick_count)
    attn_loss = expert_count * jnp.sum(attn_share * stat_totals[2] / all_tokens)
    ffn_loss = expert_count * jnp.sum(ffn_share * stat_totals[3] / all_tokens)
    back_full = (
        lax.all_gather(query_proj, "fsdp", axis=1, tiled=True),
        lax.all_gather(out_proj, "fsdp", axis=2, tiled=True),
        lax.all_gather(gate_proj, "fsdp", axis=1, tiled=True),
        lax.all_gather(up_proj, "fsdp", axis=1, tiled=True),
        lax.all_gather(down_proj, "fsdp", axis=2, tiled=True),
    )
    query_full, out_full, gate_full, up_full, down_full = [piece[0] for piece in back_full]
    grad_out = cotangent.astype(jnp.float32)
    ffn_gate_grad = jnp.sum(grad_out[:, None, :] * ffn_picked, axis=2)
    ffn_slot_gate = slot_gates(ffn_match, ffn_gates)
    dz_rows = (jnp.take(grad_out, ffn_token, axis=0) * ffn_slot_gate[:, None]).astype(jnp.bfloat16)
    grad_z = to_experts(dz_rows.reshape(expert_count, capacity, features)).reshape(-1, features)
    d_hidden = matmul_nt(grad_z, down_full)
    sigmoid_gate = jax.nn.sigmoid(gate_lin)
    d_gate_low = (
        d_hidden * up_lin * sigmoid_gate * (1.0 + gate_lin * (1.0 - sigmoid_gate))
    ).astype(jnp.bfloat16)
    d_up_low = (d_hidden * gate_lin * sigmoid_gate).astype(jnp.bfloat16)
    down_expert_grad = matmul_tn(hidden_low, grad_z)
    gate_expert_grad = matmul_tn(rows_ffn, d_gate_low)
    up_expert_grad = matmul_tn(rows_ffn, d_up_low)
    db_slots = head_total(matmul_nt(d_gate_low, gate_full) + matmul_nt(d_up_low, up_full)).astype(
        jnp.bfloat16
    )
    db_back = collect(from_experts(db_slots.reshape(expert_count, capacity, features)), ffn_slot)
    ffn_d_logits = router_back(
        ffn_gates, ffn_gate_grad, ffn_probs, ffn_routes, expert_count, ffn_share, all_tokens
    )
    d_normed2 = jnp.sum(db_back, axis=1) + precise_nt(ffn_d_logits, ffn_router.astype(jnp.float32))
    d_extra_two, gain2_grad = norm_back(attended, scale_two, norm_gain2, d_normed2)
    d_attended = grad_out + d_extra_two
    attn_gate_grad = jnp.sum(d_attended[:, None, :] * attn_picked, axis=2)
    attn_slot_gate = slot_gates(attn_match, attn_gates)
    dy_rows = (jnp.take(d_attended, attn_token, axis=0) * attn_slot_gate[:, None]).astype(
        jnp.bfloat16
    )
    grad_y = to_experts(dy_rows.reshape(expert_count, capacity, features)).reshape(-1, features)
    d_heads_low = matmul_nt(grad_y, out_full).astype(jnp.bfloat16)
    out_expert_grad = matmul_tn(heads_low, grad_y)
    d_query, d_keys, d_values = heads_backward(
        query_low, seq_keys, seq_values, allowed, log_sums, d_heads_low, head_scale
    )
    dq_low = rotate(d_query, cos_query, sin_query, -1.0).astype(jnp.bfloat16)
    query_expert_grad = matmul_tn(rows_in, dq_low)
    da_slots = head_total(matmul_nt(dq_low, query_full)).astype(jnp.bfloat16)
    da_back = collect(from_experts(da_slots.reshape(expert_count, capacity, features)), attn_slot)
    key_mine, value_mine = (
        lax.psum_scatter(
            d_keys.astype(jnp.bfloat16), "ctx", scatter_dimension=0, tiled=True
        ).astype(jnp.float32),
        lax.psum_scatter(
            d_values.astype(jnp.bfloat16), "ctx", scatter_dimension=0, tiled=True
        ).astype(jnp.float32),
    )
    dk_low = rotate(key_mine, cos_keys, sin_keys, -1.0).astype(jnp.bfloat16)
    dv_low = value_mine.astype(jnp.bfloat16)
    key_weight_grad = matmul_tn(a_low, dk_low)
    value_weight_grad = matmul_tn(a_low, dv_low)
    da_keypath = lax.psum(
        (matmul_nt(dk_low, key_full) + matmul_nt(dv_low, value_full)).astype(jnp.bfloat16), "tp"
    ).astype(jnp.float32)
    attn_d_logits = router_back(
        attn_gates, attn_gate_grad, attn_probs, attn_routes, expert_count, attn_share, all_tokens
    )
    d_normed1 = (
        jnp.sum(da_back, axis=1)
        + da_keypath
        + precise_nt(attn_d_logits, attn_router.astype(jnp.float32))
    )
    d_extra_one, gain1_grad = norm_back(inputs, scale_one, norm_gain1, d_normed1)
    input_grad = d_attended + d_extra_one
    attn_router_grad = precise_tn(a_low.astype(jnp.float32), attn_d_logits)
    ffn_router_grad = precise_tn(b_low.astype(jnp.float32), ffn_d_logits)
    expert_sums = (
        lax.psum_scatter(
            query_expert_grad[None].astype(jnp.bfloat16), "fsdp", scatter_dimension=1, tiled=True
        ).astype(jnp.float32),
        lax.psum_scatter(
            out_expert_grad[None].astype(jnp.bfloat16), "fsdp", scatter_dimension=2, tiled=True
        ).astype(jnp.float32),
        lax.psum_scatter(
            gate_expert_grad[None].astype(jnp.bfloat16), "fsdp", scatter_dimension=1, tiled=True
        ).astype(jnp.float32),
        lax.psum_scatter(
            up_expert_grad[None].astype(jnp.bfloat16), "fsdp", scatter_dimension=1, tiled=True
        ).astype(jnp.float32),
        lax.psum_scatter(
            down_expert_grad[None].astype(jnp.bfloat16), "fsdp", scatter_dimension=2, tiled=True
        ).astype(jnp.float32),
    )
    key_grad, value_grad = (
        lax.psum_scatter(key_weight_grad, ("fsdp", "ctx"), scatter_dimension=0, tiled=True),
        lax.psum_scatter(value_weight_grad, ("fsdp", "ctx"), scatter_dimension=0, tiled=True),
    )
    gain1_sum, gain2_sum, attn_router_sum, ffn_router_sum = lax.psum(
        (gain1_grad, gain2_grad, attn_router_grad, ffn_router_grad), ("fsdp", "ctx")
    )
    return (
        output,
        input_grad,
        attn_loss,
        ffn_loss,
        gain1_sum,
        gain2_sum,
        attn_router_sum,
        ffn_router_sum,
        key_grad,
        value_grad,
        expert_sums[0],
        expert_sums[1],
        expert_sums[2],
        expert_sums[3],
        expert_sums[4],
    )


def solution(mesh):
    placed = (
        P(("fsdp", "ctx"), None),
        P(("fsdp", "ctx"), None),
        P(("fsdp", "ctx"), None),
        P(("fsdp", "ctx"), None),
        P(),
        P(),
        P(),
        P(),
        P(("fsdp", "ctx"), "tp"),
        P(("fsdp", "ctx"), "tp"),
        P("ctx", "fsdp", "tp"),
        P("ctx", "tp", "fsdp"),
        P("ctx", "fsdp", "tp"),
        P("ctx", "fsdp", "tp"),
        P("ctx", "tp", "fsdp"),
    )
    return jax.shard_map(
        on_device,
        mesh=mesh,
        in_specs=placed,
        out_specs=(
            P(("fsdp", "ctx"), None),
            P(("fsdp", "ctx"), None),
            P(),
            P(),
            P(),
            P(),
            P(),
            P(),
            P(("fsdp", "ctx"), "tp"),
            P(("fsdp", "ctx"), "tp"),
            P("ctx", "fsdp", "tp"),
            P("ctx", "tp", "fsdp"),
            P("ctx", "fsdp", "tp"),
            P("ctx", "fsdp", "tp"),
            P("ctx", "tp", "fsdp"),
        ),
        check_vma=False,
    )
```

profile of v0, /device:TPU:0, one launch (start us, length us, event | category | flops | bytes accessed | tf_op | source)
XLA Modules:
  0.0 2160.1 jit_solution(7737263158448942738)
XLA Ops:
  17.0 46.7 %all-gather.12.cloned.1.call-done = bf16[2048,1024]{1,0:T(8,128)(2,1)} async-done(((bf16[128,1024]{1,0:T(8,128)(2,1)}), bf16[2048,1024]{1,0:T(8,128)(2,1)}) %all-gather.12.cloned.1.call-update) | async-done | bytes 4194320 | tf_op jit(solution)/shard_map/all_gather | solution.py:224
  92.1 42.4 %all-gather.16.cloned.1.call-done = bf16[2048,1024]{1,0:T(8,128)(2,1)} async-done(((bf16[128,1024]{1,0:T(8,128)(2,1)}), bf16[2048,1024]{1,0:T(8,128)(2,1)}) %all-gather.16.cloned.1.call-update) | async-done | bytes 4194320 | tf_op jit(solution)/shard_map/all_gather | solution.py:225
  186.7 31.3 %all-gather.14.cloned.1.call-done = bf16[1024,1024]{1,0:T(8,128)(2,1)} async-done(((bf16[256,1024]{1,0:T(8,128)(2,1)}), bf16[1024,1024]{1,0:T(8,128)(2,1)}) %all-gather.14.cloned.1.call-update) | async-done | bytes 2097168 | tf_op jit(solution)/shard_map/all_gather | solution.py:236
  218.1 46.7 %all-gather.18.cloned.1.call-done = bf16[1024,1024]{1,0:T(8,128)(2,1)} async-done(((bf16[256,1024]{1,0:T(8,128)(2,1)}), bf16[1024,1024]{1,0:T(8,128)(2,1)}) %all-gather.18.cloned.1.call-update) | async-done | bytes 2097168 | tf_op jit(solution)/shard_map/all_gather | solution.py:237
  266.0 78.9 %while.34 = (s32[]{:T(128)}, bf16[640,1024]{1,0:T(8,128)(2,1)}, f32[8,640]{1,0:T(8,128)}, bf16[640,1024]{1,0:T(8,128)(2,1)}, bf16[1024,1024]{1,0:T(8,128)(2,1)},...) while((s32[]{:T(128)}, bf16[640,1024]{1,0:T(8,128)(2,1)}, ...), condition=%wide.region_11.14_spmd.clone, body=%wide.region_8.13_spmd.clone.sunk | while | flops 341441920 | bytes 8919719 | solution.py:152
  354.0 70.8 %all-reduce.8.cloned.1.call-done = bf16[4,160,2048]{2,1,0:T(8,128)(2,1)} async-done(((bf16[4,160,2048]{2,1,0:T(8,128)(2,1)}), bf16[4,160,2048]{2,1,0:T(8,128)(2,1)}) %all-reduce.8.cloned.1.call-update) | async-done | bytes 2621456 | tf_op jit(solution)/shard_map/psum | solution.py:117
  436.3 52.9 %all-to-all-done.2 = bf16[4,160,2048]{2,1,0:T(8,128)(2,1)} async-done(((bf16[4,160,2048]{2,1,0:T(8,128)(2,1)}), bf16[4,160,2048]{2,1,0:T(8,128)(2,1)}, u32[]{:S(2)}, u32[]{:S(2)}) %all-to-all-start.2) | async-done | bytes 2621472 | tf_op jit(solution)/shard_map/all_to_all | solution.py:125
  545.0 41.5 %all-to-all-done.3 = bf16[4,160,2048]{2,1,0:T(8,128)(2,1)} async-done(((bf16[4,160,2048]{2,1,0:T(8,128)(2,1)}), bf16[4,160,2048]{2,1,0:T(8,128)(2,1)}, u32[]{:S(2)}, u32[]{:S(2)}) %all-to-all-start.3) | async-done | bytes 2621472 | tf_op jit(solution)/shard_map/all_to_all | solution.py:121
  606.8 43.4 %all-to-all-done.5 = bf16[4,160,2048]{2,1,0:T(8,128)(2,1)} async-done(((bf16[4,160,2048]{2,1,0:T(8,128)(2,1)}), bf16[4,160,2048]{2,1,0:T(8,128)(2,1)}, u32[]{:S(2)}, u32[]{:S(2)}) %all-to-all-start.5) | async-done | bytes 2621472 | tf_op jit(solution)/shard_map/all_to_all | solution.py:121
  720.3 129.6 %all-reduce.14.cloned.1.call-done = (bf16[4,160,2048]{2,1,0:T(8,128)(2,1)}, bf16[4,160,2048]{2,1,0:T(8,128)(2,1)}) async-done(((bf16[4,160,2048]{2,1,0:T(8,128)(2,1)}, bf16[4,160,2048]{2,1,0:T(8,128)(2,1)}), (bf16[4,160,2048]{2,1,0:T(8,128)(2,1)}, bf16[4,160,2048]{2,1,0:T(8,128)(2,1)})) %all-reduce.14.cloned.1.call-update) | async-done | bytes 5242896 | tf_op jit(solution)/shard_map/psum | solution.py:117
  849.9 64.2 %all_to_all.46 = bf16[4,160,2048]{2,1,0:T(8,128)(2,1)} all-to-all(bf16[4,160,2048]{2,1,0:T(8,128)(2,1)} %get-tuple-element.521), channel_id=1, replica_groups=mesh['fsdp'=4,'ctx'=4,'tp'=2] {'ctx'}, dimensions={0} | all-to-all | bytes 5242880 | tf_op jit(solution)/shard_map/all_to_all | solution.py:125
  940.8 60.7 %psum.94 = f32[4]{0:T(128)S(1)} all-reduce(f32[4]{0:T(128)S(1)} %get-tuple-element.471), channel_id=1, replica_groups=mesh['fsdp'=4,'ctx'=4,'tp'=2] {'fsdp','ctx'}, use_global_device_ids=true, to_apply=%region_33.38 | all-reduce | flops 4 | bytes 32 | tf_op jit(solution)/shard_map/psum | solution.py:295
  1065.9 56.7 %all-to-all-done.7 = bf16[4,160,2048]{2,1,0:T(8,128)(2,1)} async-done(((bf16[4,160,2048]{2,1,0:T(8,128)(2,1)}), bf16[4,160,2048]{2,1,0:T(8,128)(2,1)}, u32[]{:S(2)}, u32[]{:S(2)}) %all-to-all-start.7) | async-done | bytes 2621472 | tf_op jit(solution)/shard_map/all_to_all | solution.py:121
  1133.6 130.2 %while.35 = (s32[]{:T(128)}, f32[640,1024]{0,1:T(8,128)}, bf16[1024,1024]{1,0:T(8,128)(2,1)}, bf16[1024,1024]{1,0:T(8,128)(2,1)}, bf16[640,1024]{1,0:T(8,128)(2,...) while((s32[]{:T(128)}, f32[640,1024]{0,1:T(8,128)}, ...), condition=%wide.region_39.44_spmd.clone, body=%wide.region_37.43_spmd.clone.sunk | while | flops 845626752 | bytes 55270712 | solution.py:187
  1272.0 34.0 %reduce-scatter.10.cloned.1.call-done = bf16[256,1024]{1,0:T(8,128)(2,1)} async-done(((bf16[1024,1024]{1,0:T(8,128)(2,1)}), bf16[256,1024]{1,0:T(8,128)(2,1)}) %reduce-scatter.10.cloned.1.call-update) | async-done | bytes 524304 | tf_op jit(solution)/shard_map/reduce_scatter | solution.py:351
  1312.3 39.8 %reduce-scatter.12.cloned.1.call-done = bf16[256,1024]{1,0:T(8,128)(2,1)} async-done(((bf16[1024,1024]{1,0:T(8,128)(2,1)}), bf16[256,1024]{1,0:T(8,128)(2,1)}) %reduce-scatter.12.cloned.1.call-update) | async-done | bytes 524304 | tf_op jit(solution)/shard_map/reduce_scatter | solution.py:354
  1416.0 38.3 %all-reduce.12.cloned.1.call-done = (bf16[4,160,2048]{2,1,0:T(8,128)(2,1)}, bf16[256,2048]{1,0:T(8,128)(2,1)}) async-done(((bf16[4,160,2048]{2,1,0:T(8,128)(2,1)}, bf16[256,2048]{1,0:T(8,128)(2,1)}), (bf16[4,160,2048]{2,1,0:T(8,128)(2,1)}, bf16[256,2048]{1,0:T(8,128)(2,1)})) %all-reduce.12.cloned.1.call-update) | async-done | bytes 3670032 | tf_op jit(solution)/shard_map/psum | solution.py:117
  1473.9 69.0 %psum.97 = f32[4]{0:T(128)S(1)} all-reduce(f32[4]{0:T(128)S(1)} %get-tuple-element.469), channel_id=1, replica_groups=mesh['fsdp'=4,'ctx'=4,'tp'=2] {'fsdp','ctx'}, use_global_device_ids=true, to_apply=%region_51.56 | all-reduce | flops 4 | bytes 32 | tf_op jit(solution)/shard_map/psum | solution.py:295
  1597.5 46.5 %reduce-scatter.22.cloned.1.call-done = bf16[1,512,2816]{2,1,0:T(8,128)(2,1)} async-done(((bf16[1,2048,2816]{2,1,0:T(8,128)(2,1)}), bf16[1,512,2816]{2,1,0:T(8,128)(2,1)}) %reduce-scatter.22.cloned.1.call-update) | async-done | bytes 2883600 | tf_op jit(solution)/shard_map/reduce_scatter | solution.py:384
  1648.7 90.1 %reduce-scatter.24.cloned.1.call-done = bf16[1,512,2816]{2,1,0:T(8,128)(2,1)} async-done(((bf16[1,2048,2816]{2,1,0:T(8,128)(2,1)}), bf16[1,512,2816]{2,1,0:T(8,128)(2,1)}) %reduce-scatter.24.cloned.1.call-update) | async-done | bytes 2883600 | tf_op jit(solution)/shard_map/reduce_scatter | solution.py:387
  1743.6 90.2 %reduce-scatter.26.cloned.1.call-done = bf16[1,2816,512]{2,1,0:T(8,128)(2,1)} async-done(((bf16[1,2816,2048]{2,1,0:T(8,128)(2,1)}), bf16[1,2816,512]{2,1,0:T(8,128)(2,1)}) %reduce-scatter.26.cloned.1.call-update) | async-done | bytes 2883600 | tf_op jit(solution)/shard_map/reduce_scatter | solution.py:390
  1841.0 84.9 %all-reduce.10.cloned.1.call-done = (f32[4]{0:T(128)}, f32[4]{0:T(128)}, f32[2048]{0:T(1024)}, f32[2048]{0:T(1024)}, f32[2048,4]{0,1:T(4,128)}, /*index=5*/f32[2048,4]{0,1:T(4,128)}) async-done(((f32[4]{0:T(128)}, f32[4]{0:T(128)}, f32[2048]{0:T(1024)}, f32[2048]{0:T(1024)}, f32[2048,4]{0,1:T(4,128)}, /*index=5*/f32[2048,4]{0,1:T(4,128)}), (f32[4]{0:T(128)}, f32[4]{0:T(128)}, f32[2048]{0:T(1024)}, ...) | async-done | bytes 81968 | tf_op jit(solution)/shard_map/psum | solution.py:295
  1929.7 106.5 %reduce-scatter.14.cloned.1.call-done = f32[128,1024]{1,0:T(8,128)} async-done(((f32[2048,1024]{1,0:T(8,128)}), f32[128,1024]{1,0:T(8,128)}) %reduce-scatter.14.cloned.1.call-update) | async-done | bytes 524304 | tf_op jit(solution)/shard_map/reduce_scatter | solution.py:395
  2036.2 109.0 %reduce-scatter.16.cloned.1.call-done = f32[128,1024]{1,0:T(8,128)} async-done(((f32[2048,1024]{1,0:T(8,128)}), f32[128,1024]{1,0:T(8,128)}) %reduce-scatter.16.cloned.1.call-update) | async-done | bytes 524304 | tf_op jit(solution)/shard_map/reduce_scatter | solution.py:396
  (592 shorter events, 745.1 us)
Async XLA Ops:
  8.0 126.5 %all-gather.16.cloned.1.call-start = ((), (), s32[]{:S(2)}) async-start(), calls=%async_computation.21 | async-start | bytes 4456448 | tf_op jit(solution)/shard_map/all_gather | solution.py:225
  8.7 161.4 %all-gather.10.cloned.1.call-start = ((), (), s32[]{:S(2)}) async-start(), calls=%async_computation.18 | async-start | bytes 5242880 | tf_op jit(solution)/shard_map/all_gather | solution.py:216
  9.4 208.6 %all-gather.14.cloned.1.call-start = ((), (), s32[]{:S(2)}) async-start(), calls=%async_computation.20 | async-start | bytes 2621440 | tf_op jit(solution)/shard_map/all_gather | solution.py:236
  87.1 89.5 %all-to-all-start = ((bf16[4,160,2048]{2,1,0:T(8,128)(2,1)}), bf16[4,160,2048]{2,1,0:T(8,128)(2,1)}, u32[]{:S(2)}, u32[]{:S(2)}) async-start(bf16[4,160,2048]{2,1,0:T(8,128)(2,1)} %bitcast.169), calls=%async_computation | async-start | bytes 5242880 | tf_op jit(solution)/shard_map/all_to_all | solution.py:247
  92.1 172.6 %all-gather.18.cloned.1.call-start = ((), (), s32[]{:S(2)}) async-start(), calls=%async_computation.22 | async-start | bytes 2621440 | tf_op jit(solution)/shard_map/all_gather | solution.py:237
  138.7 206.1 %all-gather.20.cloned.1.call-start = ((), (), s32[]{:S(2)}) async-start(), calls=%async_computation.23 | async-start | bytes 5242880 | tf_op jit(solution)/shard_map/all_gather | solution.py:217
  139.3 285.5 %all-reduce.8.cloned.1.call-start = ((), (), s32[]{:S(2)}) async-start(), calls=%async_computation.24 | async-start | bytes 5242880 | tf_op jit(solution)/shard_map/psum | solution.py:117
  351.9 239.4 %all-gather.24.cloned.1.call-start = ((), (), s32[]{:S(2)}) async-start(), calls=%async_computation.26 | async-start | bytes 14417920 | tf_op jit(solution)/shard_map/all_gather | solution.py:219
  352.6 254.2 %all-gather.26.cloned.1.call-start = ((), (), s32[]{:S(2)}) async-start(), calls=%async_computation.27 | async-start | bytes 14417920 | tf_op jit(solution)/shard_map/all_gather | solution.py:220
  353.4 310.6 %all-gather.22.cloned.1.call-start = ((), (), s32[]{:S(2)}) async-start(), calls=%async_computation.25 | async-start | bytes 14417920 | tf_op jit(solution)/shard_map/all_gather | solution.py:218
  591.2 258.7 %all-reduce.14.cloned.1.call-start = ((), (), s32[]{:S(2)}) async-start(), calls=%async_computation.39 | async-start | bytes 10485760 | tf_op jit(solution)/shard_map/psum | solution.py:117
  914.1 87.4 %all-to-all-start.6 = ((bf16[4,160,2048]{2,1,0:T(8,128)(2,1)}), bf16[4,160,2048]{2,1,0:T(8,128)(2,1)}, u32[]{:S(2)}, u32[]{:S(2)}) async-start(bf16[4,160,2048]{2,1,0:T(8,128)(2,1)} %get-tuple-element.522), calls=%async_computation.6 | async-start | bytes 5242880 | tf_op jit(solution)/shard_map/all_to_all | solution.py:125
  1065.7 240.2 %reduce-scatter.10.cloned.1.call-start = ((), (), s32[]{:S(2)}) async-start(), calls=%async_computation.28 | async-start | bytes 2621440 | tf_op jit(solution)/shard_map/reduce_scatter | solution.py:351
  1263.8 88.4 %reduce-scatter.12.cloned.1.call-start = ((), (), s32[]{:S(2)}) async-start(), calls=%async_computation.29 | async-start | bytes 2621440 | tf_op jit(solution)/shard_map/reduce_scatter | solution.py:354
  1264.5 189.8 %all-reduce.12.cloned.1.call-start = ((), (), s32[]{:S(2)}) async-start(), calls=%async_computation.38 | async-start | bytes 7340032 | tf_op jit(solution)/shard_map/psum | solution.py:117
  1357.4 234.4 %reduce-scatter.20.cloned.1.call-start = ((), (), s32[]{:S(2)}) async-start(), calls=%async_computation.33 | async-start | bytes 5242880 | tf_op jit(solution)/shard_map/reduce_scatter | solution.py:381
  1365.6 229.1 %reduce-scatter.18.cloned.1.call-start = ((), (), s32[]{:S(2)}) async-start(), calls=%async_computation.32 | async-start | bytes 5242880 | tf_op jit(solution)/shard_map/reduce_scatter | solution.py:378
  1372.5 271.5 %reduce-scatter.22.cloned.1.call-start = ((), (), s32[]{:S(2)}) async-start(), calls=%async_computation.34 | async-start | bytes 14417920 | tf_op jit(solution)/shard_map/reduce_scatter | solution.py:384
  1387.0 351.8 %reduce-scatter.24.cloned.1.call-start = ((), (), s32[]{:S(2)}) async-start(), calls=%async_computation.35 | async-start | bytes 14417920 | tf_op jit(solution)/shard_map/reduce_scatter | solution.py:387
  1401.6 432.2 %reduce-scatter.26.cloned.1.call-start = ((), (), s32[]{:S(2)}) async-start(), calls=%async_computation.36 | async-start | bytes 14417920 | tf_op jit(solution)/shard_map/reduce_scatter | solution.py:390
  1454.3 92.8 %all-to-all-start.8 = ((bf16[4,160,2048]{2,1,0:T(8,128)(2,1)}), bf16[4,160,2048]{2,1,0:T(8,128)(2,1)}, u32[]{:S(2)}, u32[]{:S(2)}) async-start(bf16[4,160,2048]{2,1,0:T(8,128)(2,1)} %get-tuple-element.519), calls=%async_computation.8 | async-start | bytes 5242880 | tf_op jit(solution)/shard_map/all_to_all | solution.py:125
  1459.1 466.9 %all-reduce.10.cloned.1.call-start = ((), (), s32[]{:S(2)}) async-start(), calls=%async_computation.37 | async-start | bytes 165888 | tf_op jit(solution)/shard_map/psum | solution.py:295
  1580.2 456.0 %reduce-scatter.14.cloned.1.call-start = ((), (), s32[]{:S(2)}) async-start(), calls=%async_computation.30 | async-start | bytes 8912896 | tf_op jit(solution)/shard_map/reduce_scatter | solution.py:395
  1586.1 559.1 %reduce-scatter.16.cloned.1.call-start = ((), (), s32[]{:S(2)}) async-start(), calls=%async_computation.31 | async-start | bytes 8912896 | tf_op jit(solution)/shard_map/reduce_scatter | solution.py:396
  (118 other events, 3980.7 us)
Sparse Core Ops, SparseCore 0:
  10.3 53.3 all-gather.11
  65.9 68.5 all-gather.15
  136.1 33.9 all-gather.9
  172.1 45.9 all-gather.13
  220.1 44.6 all-gather.17
  266.2 33.1 all-gather.19
  352.0 72.7 all-reduce.7
  426.4 76.1 all-gather.23
  504.3 76.1 all-gather.25
  581.9 76.1 all-gather.21
  720.4 129.4 all-reduce.13
  1263.9 41.9 reduce-scatter.9
  1308.9 43.1 reduce-scatter.11
  1357.6 96.7 all-reduce.11
  1456.9 44.5 reduce-scatter.19
  1504.4 44.7 reduce-scatter.17
  1551.7 92.1 reduce-scatter.21
  1646.6 92.1 reduce-scatter.23
  1741.6 92.1 reduce-scatter.25
  1839.0 86.8 all-reduce.9
  1930.6 105.6 reduce-scatter.13
  2040.9 104.3 reduce-scatter.15
where the time goes:
time: 2170 us; the launch traced here: 2160 us
  waiting for transfers between devices  1240 us (57%)
  matrix products  340 us (16%)
  blocking collectives  194 us (9%)
  local copies, waits for them, and re-layouts  191 us (9%)
  other arithmetic  141 us (6%)
  starting transfers between devices  38.2 us (2%)
    psum x3, waiting for transfers between devices, head_total(): return lax.psum(partial_sum.astype(jnp.bfloat16), 'tp').astype(jnp.float32)  239 us
    all_to_all x3, waiting for transfers between devices, to_experts(): lax.all_to_all(slot_rows, 'ctx', split_axis=0, concat_axis=0, tiled=True)  142 us
    psum x2, blocking collectives, on_device(): lax.psum((attn_hits, ffn_hits, jnp.sum(attn_probs, axis=0), jnp.sum(ffn_p...  130 us
    dot_general x31, matrix products, matmul_nt(): lax.dot_general(lhs_mat, rhs_mat, (((1,), (1,)), ((), ())), preferred_ele...  112 us
    dot_general x25, matrix products, matmul(): return jnp.dot(lhs_mat, rhs_mat, preferred_element_type=jnp.float32)  111 us
    reduce_scatter x1, waiting for transfers between devices, on_device(): lax.psum_scatter(value_weight_grad, ('fsdp', 'ctx'), scatter_dimension=0,...  109 us
    reduce_scatter x1, waiting for transfers between devices, on_device(): lax.psum_scatter(key_weight_grad, ('fsdp', 'ctx'), scatter_dimension=0, t...  107 us
    dot_general x23, matrix products, matmul_tn(): lax.dot_general(lhs_mat, rhs_mat, (((0,), (0,)), ((), ())), preferred_ele...  104 us
  transfers between devices with their start and end apart: 30, of which 20 were waited for; matrix products, arithmetic and copies ran while one was open for 18% of the time, Pallas kernels for 0%

commit v1 on v0

v1 whole, which is shorter than its diff:
```python
import functools
import math

import jax
import jax.numpy as jnp
from jax import lax
from jax.experimental import pallas as pl
from jax.experimental.pallas import tpu as pltpu
from jax.sharding import PartitionSpec as P

HEAD = 128
EPSILON = 1e-06
ROPE_BASE = 10000.0
AUX_WEIGHT = 0.1
PRECISE = lax.Precision.HIGHEST
LOW = jnp.bfloat16
FULL = jnp.float32
VMEM_BYTES = 56 * 1024 * 1024


def matmul(lhs, rhs):
    return jnp.dot(lhs, rhs, preferred_element_type=FULL)


def matmul_tn(lhs, rhs):
    return lax.dot_general(lhs, rhs, (((0,), (0,)), ((), ())), preferred_element_type=FULL)


def matmul_nt(lhs, rhs):
    return lax.dot_general(lhs, rhs, (((1,), (1,)), ((), ())), preferred_element_type=FULL)


def precise_tn(lhs, rhs):
    return lax.dot_general(lhs, rhs, (((0,), (0,)), ((), ())), precision=PRECISE)


def swap(value, axis, distance):
    size = lax.axis_size(axis)
    return lax.ppermute(value, axis, [(i, i ^ distance) for i in range(size)])


def after(value, *earlier):
    return lax.optimization_barrier((value,) + earlier)[0]


def bits_down(size):
    bit = size // 2
    while bit >= 1:
        yield bit
        bit //= 2


def spread_order(size):
    order = [0]
    for bit in bits_down(size):
        order = order + [place | bit for place in order]
    return order


def gather_pieces(piece):
    pieces = [piece]
    for bit in bits_down(lax.axis_size("fsdp")):
        pieces = pieces + [swap(item, "fsdp", bit) for item in pieces]
    return pieces


def flip_blocks(value, axis, index, count):
    shape = value.shape
    width = shape[axis] // count
    for bit in bits_down(count):
        outer = shape[axis] // (2 * bit * width)
        split = value.reshape(shape[:axis] + (outer, 2, bit * width) + shape[axis + 1 :])
        turned = jnp.flip(split, axis + 1).reshape(shape)
        value = jnp.where((index // bit) % 2 == 1, turned, value)
    return value


def to_spread(value, axis):
    size = lax.axis_size("fsdp")
    value = flip_blocks(value, axis, lax.axis_index("fsdp"), size)
    parts = jnp.split(value, size, axis)
    return jnp.concatenate([parts[place] for place in spread_order(size)], axis)


def from_spread(value, axis):
    size = lax.axis_size("fsdp")
    parts = jnp.split(value, size, axis)
    order = spread_order(size)
    value = jnp.concatenate([parts[order.index(place)] for place in range(size)], axis)
    return flip_blocks(value, axis, lax.axis_index("fsdp"), size)


def my_half(value):
    width = value.shape[-1] // 2
    return jnp.where(lax.axis_index("tp") == 0, value[..., :width], value[..., width:])


def other_half(value):
    width = value.shape[-1] // 2
    return jnp.where(lax.axis_index("tp") == 0, value[..., width:], value[..., :width])


def join_halves(mine, other):
    first = lax.axis_index("tp") == 0
    return jnp.concatenate([jnp.where(first, mine, other), jnp.where(first, other, mine)], -1)


def tp_sum(value):
    return value + swap(value, "tp", 1)


def all_sum(value, axes):
    for axis in axes:
        for bit in bits_down(lax.axis_size(axis)):
            value = value + swap(value, axis, bit)
    return value


def far_first(size):
    return list(range(size // 2, size)) + list(range(size // 2 - 1, -1, -1))


def place_blocks(blocks):
    index = lax.axis_index("ctx")
    rows = blocks[0].shape[0]
    total = jnp.zeros((rows * len(blocks),) + blocks[0].shape[1:], blocks[0].dtype)
    for distance, block in enumerate(blocks):
        total = lax.dynamic_update_slice_in_dim(total, block, (index ^ distance) * rows, 0)
    return total


def block_for(value, distance):
    size = lax.axis_size("ctx")
    rows = value.shape[0] // size
    return lax.dynamic_slice_in_dim(value, (lax.axis_index("ctx") ^ distance) * rows, rows, 0)


def send_out(half_rows):
    size = lax.axis_size("ctx")
    blocks = [None] * size
    for distance in far_first(size):
        block = block_for(half_rows, distance)
        if distance:
            block = swap(block, "ctx", distance)
        blocks[distance] = join_halves(block, swap(block, "tp", 1))
    return place_blocks(blocks)


def send_home(partial_rows):
    size = lax.axis_size("ctx")
    blocks = [None] * size
    for distance in far_first(size):
        block = block_for(partial_rows, distance)
        arrived = swap(other_half(block).astype(LOW), "tp", 1)
        block = (my_half(block).astype(FULL) + arrived.astype(FULL)).astype(LOW)
        if distance:
            block = swap(block, "ctx", distance)
        blocks[distance] = block
    return blocks


def scatter_sum(keep, send, first_dim):
    size = lax.axis_size("fsdp")
    bit = 1
    while True:
        total = keep + swap(send, "fsdp", bit).astype(FULL)
        bit *= 2
        if bit >= size:
            return total
        width = total.shape[first_dim] // 2
        keep = lax.slice_in_dim(total, 0, width, axis=first_dim)
        send = lax.slice_in_dim(total, width, 2 * width, axis=first_dim).astype(LOW)


def turn_tables(places):
    half_head = HEAD // 2
    frequency = ROPE_BASE ** (-jnp.arange(half_head, dtype=FULL) * 2.0 / HEAD)
    angles = places.astype(FULL)[:, None] * frequency[None, :]
    cosine, sine = jnp.cos(angles), jnp.sin(angles)
    return jnp.concatenate([cosine, cosine, -sine, sine], axis=1)


def turn(value, table):
    return value * table[:, :HEAD] + pltpu.roll(value, HEAD // 2, 1) * table[:, HEAD:]


def turn_back(value, table):
    return value * table[:, :HEAD] - pltpu.roll(value, HEAD // 2, 1) * table[:, HEAD:]


def attend_kernel(
    groups, scale, q_lin, k_lin, v_lin, q_table, k_table, q_low, k_low, v_low, heads, log_sum
):
    q_low[...] = turn(q_lin[...], q_table[...]).astype(LOW)
    k_low[...] = turn(k_lin[...], k_table[...]).astype(LOW)
    v_low[...] = v_lin[...].astype(LOW)
    rows = q_low.shape[0] // groups
    block = k_low.shape[0] // groups
    for group in range(groups):
        span = slice(group * rows, (group + 1) * rows)
        seen = slice(0, (group + 1) * block)
        scores = matmul_nt(q_low[span, :], k_low[seen, :]) * scale
        top = jnp.max(scores, axis=1, keepdims=True)
        weights = jnp.exp(scores - top)
        total = jnp.sum(weights, axis=1, keepdims=True)
        weights = (weights * (1.0 / total)).astype(LOW)
        heads[span, :] = matmul(weights, v_low[seen, :]).astype(LOW)
        log_sum[span, :] = jnp.broadcast_to(top + jnp.log(total), (rows, HEAD))


def attend(query_lin, kv_lin, query_table, key_table, groups):
    slots, width = query_lin.shape
    length = kv_lin.shape[0]
    count = width // HEAD
    by_head = lambda rows: pl.BlockSpec((rows, HEAD), lambda h: (0, h))
    whole = lambda rows: pl.BlockSpec((rows, 2 * HEAD), lambda h: (0, 0))
    return pl.pallas_call(
        functools.partial(attend_kernel, groups, 1.0 / math.sqrt(HEAD)),
        grid=(count,),
        in_specs=[
            by_head(slots),
            by_head(length),
            pl.BlockSpec((length, HEAD), lambda h: (0, h + count)),
            whole(slots),
            whole(length),
        ],
        out_specs=[by_head(slots), by_head(length), by_head(length), by_head(slots), by_head(slots)],
        out_shape=[
            jax.ShapeDtypeStruct((slots, width), LOW),
            jax.ShapeDtypeStruct((length, width), LOW),
            jax.ShapeDtypeStruct((length, width), LOW),
            jax.ShapeDtypeStruct((slots, width), LOW),
            jax.ShapeDtypeStruct((slots, width), FULL),
        ],
        compiler_params=pltpu.CompilerParams(vmem_limit_bytes=VMEM_BYTES),
        cost_estimate=pl.CostEstimate(
            flops=3 * slots * length * width,
            bytes_accessed=20 * length * width,
            transcendentals=slots * length * count,
        ),
    )(query_lin, kv_lin, kv_lin, query_table, key_table)


def attend_back_kernel(
    groups, scale, q_low, k_low, v_low, d_heads, log_sum, q_table, k_table, dq, dk, dv, dk_sum, dv_sum
):
    dk_sum[...] = jnp.zeros_like(dk_sum)
    dv_sum[...] = jnp.zeros_like(dv_sum)
    rows = q_low.shape[0] // groups
    block = k_low.shape[0] // groups
    for group in range(groups):
        span = slice(group * rows, (group + 1) * rows)
        seen = slice(0, (group + 1) * block)
        query, keys = q_low[span, :], k_low[seen, :]
        grads = d_heads[span, :]
        scores = matmul_nt(query, keys) * scale
        weights = jnp.exp(scores - log_sum[span, :1])
        d_weights = matmul_nt(grads, v_low[seen, :])
        delta = jnp.sum(weights * d_weights, axis=1, keepdims=True)
        d_scores = (weights * (d_weights - delta)).astype(LOW)
        dq[span, :] = turn_back(matmul(d_scores, keys) * scale, q_table[span, :]).astype(LOW)
        dk_sum[seen, :] += matmul_tn(d_scores, query) * scale
        dv_sum[seen, :] += matmul_tn(weights.astype(LOW), grads)
    dk[...] = turn_back(dk_sum[...], k_table[...]).astype(LOW)
    dv[...] = dv_sum[...].astype(LOW)


def attend_back(q_low, k_low, v_low, d_heads, log_sum, query_table, key_table, groups):
    slots, width = q_low.shape
    length = k_low.shape[0]
    count = width // HEAD
    by_head = lambda rows: pl.BlockSpec((rows, HEAD), lambda h: (0, h))
    whole = lambda rows: pl.BlockSpec((rows, 2 * HEAD), lambda h: (0, 0))
    return pl.pallas_call(
        functools.partial(attend_back_kernel, groups, 1.0 / math.sqrt(HEAD)),
        grid=(count,),
        in_specs=[
            by_head(slots),
            by_head(length),
            by_head(length),
            by_head(slots),
            by_head(slots),
            whole(slots),
            whole(length),
        ],
        out_specs=[by_head(slots), by_head(length), by_head(length)],
        out_shape=[
            jax.ShapeDtypeStruct((slots, width), LOW),
            jax.ShapeDtypeStruct((length, width), LOW),
            jax.ShapeDtypeStruct((length, width), LOW),
        ],
        scratch_shapes=[pltpu.VMEM((length, HEAD), FULL), pltpu.VMEM((length, HEAD), FULL)],
        compiler_params=pltpu.CompilerParams(vmem_limit_bytes=VMEM_BYTES),
        cost_estimate=pl.CostEstimate(
            flops=7 * slots * length * width,
            bytes_accessed=14 * length * width,
            transcendentals=slots * length * count,
        ),
    )(q_low, k_low, v_low, d_heads, log_sum, query_table, key_table)


def chosen_picks(routes, expert_count, capacity):
    experts = jnp.arange(expert_count, dtype=jnp.int32)
    onehot = (routes[:, :, None] == experts[None, None, :]).astype(jnp.int32)
    order = jnp.cumsum(jnp.sum(onehot, axis=1), axis=0) - 1
    slot = routes * capacity + jnp.sum(onehot * order[:, None, :], axis=2)
    slots = jnp.arange(expert_count * capacity, dtype=jnp.int32)
    picks = [(slot[:, k : k + 1] == slots[None, :]).astype(LOW) for k in range(routes.shape[1])]
    return picks, onehot.astype(FULL)


def expert_picks(routes_seq, expert, capacity):
    named = jnp.any(routes_seq == expert, axis=1)
    order = jnp.cumsum(named.astype(jnp.int32), axis=1) - 1
    slot = jnp.where(named, order, -1)
    return (slot[:, None, :] == jnp.arange(capacity, dtype=jnp.int32)[None, :, None]).astype(LOW)


def mix_of(logits, onehot):
    chosen = jnp.sum(onehot * logits[:, None, :], axis=2)
    return jax.nn.softmax(chosen, axis=1)


def logits_back(mix, mix_grad, probs, onehot, share_grad):
    d_chosen = mix * (mix_grad - jnp.sum(mix * mix_grad, axis=1, keepdims=True))
    d_logits = jnp.sum(onehot * d_chosen[:, :, None], axis=1)
    inner = jnp.sum(probs * share_grad[None, :], axis=1, keepdims=True)
    return d_logits + probs * (share_grad[None, :] - inner)


def through_router(d_logits, router_half):
    total = d_logits[:, 0:1] * router_half[:, 0][None, :]
    for expert in range(1, d_logits.shape[1]):
        total = total + d_logits[:, expert : expert + 1] * router_half[:, expert][None, :]
    return total


def on_device(
    tokens,
    cotangent,
    attn_routes,
    ffn_routes,
    norm_gain1,
    norm_gain2,
    attn_router,
    ffn_router,
    key_proj,
    value_proj,
    query_proj,
    out_proj,
    gate_proj,
    up_proj,
    down_proj,
):
    rows_here, features = tokens.shape
    half_width = features // 2
    picks_each = attn_routes.shape[1]
    expert_count = attn_router.shape[1]
    groups = lax.axis_size("ctx")
    mine = lax.axis_index("ctx")
    capacity = rows_here * picks_each // expert_count * 5 // 4
    slots = groups * capacity
    all_tokens = rows_here * lax.axis_size("fsdp") * groups
    distances = far_first(groups)

    query_pieces = gather_pieces(query_proj[0])
    out_pieces = gather_pieces(out_proj[0])

    tokens_spread = to_spread(tokens, 1)
    token_half = my_half(tokens_spread)
    routes_mine = jnp.concatenate([attn_routes, ffn_routes], axis=1).T[None]
    kv_mine = jnp.concatenate([key_proj, value_proj], axis=1)
    token_blocks, route_blocks, kv_blocks = [None] * groups, [None] * groups, [None] * groups
    for distance in distances:
        if distance == 0:
            token_blocks[0], route_blocks[0], kv_blocks[0] = tokens_spread, routes_mine, kv_mine
            continue
        route_blocks[distance] = swap(routes_mine, "ctx", distance)
        token_blocks[distance] = swap(token_half, "ctx", distance)
        kv_blocks[distance] = swap(kv_mine, "ctx", distance)
    for distance in distances:
        if distance:
            token_blocks[distance] = join_halves(
                token_blocks[distance], swap(token_blocks[distance], "tp", 1)
            )
    seq_tokens = place_blocks(token_blocks).astype(FULL)
    seq_routes = place_blocks(route_blocks)
    kv_group = place_blocks(kv_blocks)
    kv_pieces = gather_pieces(kv_group)
    kv_full = jnp.concatenate(kv_pieces, axis=0)
    query_full = jnp.concatenate(query_pieces, axis=0)
    out_full = jnp.concatenate(out_pieces, axis=1)

    gate_pieces = gather_pieces(after(gate_proj[0], kv_group))
    up_pieces = gather_pieces(after(up_proj[0], kv_group, gate_pieces[0]))
    down_pieces = gather_pieces(after(down_proj[0], kv_group, up_pieces[0]))

    gain1 = to_spread(norm_gain1, 0)
    gain2_half = my_half(to_spread(norm_gain2, 0))
    router1 = to_spread(attn_router, 0)
    router2 = to_spread(ffn_router, 0)
    router1_half = my_half(router1.T).T.astype(FULL)
    router2_half = my_half(router2.T).T

    scale_seq = lax.rsqrt(jnp.mean(seq_tokens * seq_tokens, axis=1, keepdims=True) + EPSILON)
    a_seq = (seq_tokens * scale_seq * gain1).astype(LOW)
    a_mine = lax.dynamic_slice_in_dim(a_seq, mine * rows_here, rows_here, 0)
    scale_one = lax.dynamic_slice_in_dim(scale_seq, mine * rows_here, rows_here, 0)
    attn_logits = matmul(a_mine, router1)
    attn_probs = jax.nn.softmax(attn_logits, axis=1)
    attn_picks, attn_onehot = chosen_picks(attn_routes, expert_count, capacity)
    ffn_picks, ffn_onehot = chosen_picks(ffn_routes, expert_count, capacity)
    attn_mix = mix_of(attn_logits, attn_onehot)

    expert_onehot = expert_picks(seq_routes[:, :picks_each], mine, capacity)
    key_table = turn_tables(jnp.arange(groups * rows_here, dtype=jnp.int32))
    query_table = jnp.einsum(
        "bsr,brh->bsh",
        expert_onehot.astype(FULL),
        key_table.reshape(groups, rows_here, -1),
        precision=PRECISE,
    ).reshape(slots, -1)
    rows_in = (
        jnp.einsum(
            "bsr,brd->bsd",
            expert_onehot,
            a_seq.reshape(groups, rows_here, features),
            preferred_element_type=FULL,
        )
        .astype(LOW)
        .reshape(slots, features)
    )
    query_lin = matmul(rows_in, query_full)
    kv_lin = matmul(a_seq, kv_full)
    q_low, k_low, v_low, heads_low, log_sum = attend(
        query_lin, kv_lin, query_table, key_table, groups
    )
    attn_blocks = send_home(matmul(heads_low, out_full))
    attn_back = place_blocks(attn_blocks)

    cot_half = my_half(to_spread(cotangent, 1))
    ffn_pick = ffn_picks[0]
    for pick in ffn_picks[1:]:
        ffn_pick = ffn_pick + pick
    cot_rows = send_out(after(matmul_tn(ffn_pick, cot_half).astype(LOW), kv_group))

    input_half = my_half(tokens_spread).astype(FULL)
    attn_picked = [matmul(pick, attn_back) for pick in attn_picks]
    attended = input_half
    for k in range(picks_each):
        attended = attended + attn_mix[:, k : k + 1] * attn_picked[k]
    square_sum = tp_sum(jnp.sum(attended * attended, axis=1, keepdims=True))
    scale_two = lax.rsqrt(square_sum / features + EPSILON)
    b_half = (attended * scale_two * gain2_half).astype(LOW)
    ffn_rows = send_out(matmul_tn(ffn_pick, b_half).astype(LOW))
    ffn_logits = tp_sum(matmul(b_half, router2_half))
    ffn_probs = jax.nn.softmax(ffn_logits, axis=1)
    ffn_mix = mix_of(ffn_logits, ffn_onehot)
    mix_slots = jnp.zeros((slots,), FULL)
    for k in range(picks_each):
        mix_slots = mix_slots + jnp.sum(ffn_picks[k].astype(FULL) * ffn_mix[:, k : k + 1], axis=0)
    mix_slots = mix_slots.reshape(groups, 1, capacity)
    mix_rows = place_blocks(
        [
            swap(block_for(mix_slots, distance), "ctx", distance) if distance else block_for(mix_slots, 0)
            for distance in range(groups)
        ]
    ).reshape(slots, 1)

    gate_full = jnp.concatenate(gate_pieces, axis=0)
    up_full = jnp.concatenate(up_pieces, axis=0)
    down_full = jnp.concatenate(down_pieces, axis=1)
    gate_lin = matmul(ffn_rows, gate_full)
    up_lin = matmul(ffn_rows, up_full)
    sigmoid_gate = jax.nn.sigmoid(gate_lin)
    hidden = gate_lin * sigmoid_gate * up_lin
    hidden_low = hidden.astype(LOW)
    d_hidden = matmul_nt(cot_rows, down_full)
    mix_grad_rows = jnp.sum(hidden * d_hidden, axis=1)
    d_gated = d_hidden * mix_rows
    d_gate_low = (d_gated * up_lin * sigmoid_gate * (1.0 + gate_lin * (1.0 - sigmoid_gate))).astype(LOW)
    d_up_low = (d_gated * gate_lin * sigmoid_gate).astype(LOW)
    db_blocks = send_home(matmul_nt(d_gate_low, gate_full) + matmul_nt(d_up_low, up_full))
    mix_grad_blocks = mix_grad_rows.reshape(groups, 1, capacity)
    mix_grad_back = place_blocks(
        [
            tp_sum(
                swap(block_for(mix_grad_blocks, distance), "ctx", distance)
                if distance
                else block_for(mix_grad_blocks, 0)
            )
            for distance in range(groups)
        ]
    ).reshape(1, slots)
    dz_rows = (cot_rows.astype(FULL) * mix_rows).astype(LOW)
    near, far = slice(0, half_width), slice(half_width, features)
    down_grad = scatter_sum(
        matmul_tn(hidden_low, dz_rows[:, near]), matmul_tn(hidden_low, dz_rows[:, far]).astype(LOW), 1
    )
    gate_grad = scatter_sum(
        matmul_tn(ffn_rows[:, near], d_gate_low), matmul_tn(ffn_rows[:, far], d_gate_low).astype(LOW), 0
    )
    up_grad = scatter_sum(
        matmul_tn(ffn_rows[:, near], d_up_low), matmul_tn(ffn_rows[:, far], d_up_low).astype(LOW), 0
    )

    hits = all_sum(
        jnp.stack([jnp.sum(attn_onehot, axis=(0, 1)), jnp.sum(ffn_onehot, axis=(0, 1))]),
        ("fsdp", "ctx"),
    )
    share = hits / (all_tokens * picks_each)
    share_grad = AUX_WEIGHT * expert_count / all_tokens * share
    grad_half = cot_half.astype(FULL)
    db_back = place_blocks(db_blocks)
    d_normed2 = jnp.zeros((rows_here, half_width), FULL)
    ffn_mix_grad = []
    for pick in ffn_picks:
        d_normed2 = d_normed2 + matmul(pick, db_back)
        ffn_mix_grad.append(jnp.sum(pick.astype(FULL) * mix_grad_back, axis=1, keepdims=True))
    ffn_mix_grad = jnp.concatenate(ffn_mix_grad, axis=1)
    ffn_d_logits = logits_back(ffn_mix, ffn_mix_grad, ffn_probs, ffn_onehot, share_grad[1])
    d_normed2 = d_normed2 + through_router(ffn_d_logits, router2_half.astype(FULL))
    weighted2 = d_normed2 * gain2_half
    inner2 = tp_sum(jnp.sum(weighted2 * attended, axis=1, keepdims=True)) / features
    d_attended = grad_half + scale_two * weighted2 - attended * scale_two**3 * inner2
    gain2_part = jnp.sum(d_normed2 * attended * scale_two, axis=0)
    ffn_router_part = precise_tn(b_half.astype(FULL), ffn_d_logits)

    dy_slots = jnp.zeros((slots, half_width), FULL)
    for k in range(picks_each):
        dy_slots = dy_slots + matmul_tn(attn_picks[k], (attn_mix[:, k : k + 1] * d_attended).astype(LOW))
    dy_rows = send_out(dy_slots.astype(LOW))
    d_heads = matmul_nt(dy_rows, out_full).astype(LOW)
    dq_low, dk_low, dv_low = attend_back(
        q_low, k_low, v_low, d_heads, log_sum, query_table, key_table, groups
    )
    out_grad = scatter_sum(
        matmul_tn(heads_low, dy_rows[:, near]), matmul_tn(heads_low, dy_rows[:, far]).astype(LOW), 1
    )
    query_grad = scatter_sum(
        matmul_tn(rows_in[:, near], dq_low), matmul_tn(rows_in[:, far], dq_low).astype(LOW), 0
    )
    dkv_low = jnp.concatenate([dk_low, dv_low], axis=1)
    da_rows = matmul_nt(dq_low, query_full).astype(LOW).reshape(groups, capacity, features)
    da_seq = jnp.einsum("bsr,bsd->brd", expert_onehot, da_rows, preferred_element_type=FULL)
    da_seq = da_seq.reshape(groups * rows_here, features) + matmul_nt(dkv_low, kv_full)
    da_blocks = send_home(da_seq)
    kv_part = scatter_sum(
        matmul_tn(a_seq[:, near], dkv_low), matmul_tn(a_seq[:, far], dkv_low).astype(LOW), 0
    )
    kv_grad = block_for(kv_part, 0)
    kv_part_low = kv_part.astype(LOW)
    for distance in distances:
        if distance:
            kv_grad = kv_grad + swap(block_for(kv_part_low, distance), "ctx", distance).astype(FULL)
    key_width = key_proj.shape[1]

    ffn_back = place_blocks(send_home(matmul(hidden_low, down_full)))
    result = attended
    for k in range(picks_each):
        result = result + ffn_mix[:, k : k + 1] * matmul(ffn_picks[k], ffn_back)
    result_low = result.astype(LOW)
    output = from_spread(join_halves(result_low, swap(result_low, "tp", 1)), 1)

    attn_mix_grad = tp_sum(
        jnp.concatenate(
            [jnp.sum(d_attended * picked, axis=1, keepdims=True) for picked in attn_picked], axis=1
        )
    )
    attn_d_logits = logits_back(attn_mix, attn_mix_grad, attn_probs, attn_onehot, share_grad[0])
    a_half = my_half(a_mine)
    attn_router_part = precise_tn(a_half.astype(FULL), attn_d_logits)

    d_normed1 = through_router(attn_d_logits, router1_half)
    for block in da_blocks:
        d_normed1 = d_normed1 + block.astype(FULL)
    gain1_half = my_half(gain1)
    weighted1 = d_normed1 * gain1_half
    inner1 = tp_sum(jnp.sum(weighted1 * input_half, axis=1, keepdims=True)) / features
    input_grad = d_attended + scale_one * weighted1 - input_half * scale_one**3 * inner1
    input_grad_low = input_grad.astype(LOW)
    input_grad = from_spread(join_halves(input_grad_low, swap(input_grad_low, "tp", 1)), 1).astype(FULL)
    gain1_part = jnp.sum(d_normed1 * input_half * scale_one, axis=0)

    early = jnp.concatenate([gain2_part[None], ffn_router_part.T, attn_router_part.T], axis=0)
    early = from_spread(join_halves(early, swap(early, "tp", 1)), 1)
    early = all_sum(early, ("ctx", "fsdp"))
    late = gain1_part[None]
    late = from_spread(join_halves(late, swap(late, "tp", 1)), 1)
    late = all_sum(late, ("ctx", "fsdp"))
    prob_sums = all_sum(
        jnp.stack([jnp.sum(attn_probs, axis=0), jnp.sum(ffn_probs, axis=0)]), ("fsdp", "ctx")
    )
    losses = expert_count * jnp.sum(share * prob_sums / all_tokens, axis=1)
    return (
        output,
        input_grad,
        losses[0],
        losses[1],
        late[0],
        early[0],
        early[1 + expert_count :].T,
        early[1 : 1 + expert_count].T,
        kv_grad[:, :key_width],
        kv_grad[:, key_width:],
        query_grad[None],
        out_grad[None],
        gate_grad[None],
        up_grad[None],
        down_grad[None],
    )


def solution(mesh):
    by_token = P(("fsdp", "ctx"), None)
    by_row = P(("fsdp", "ctx"), "tp")
    inward = P("ctx", "fsdp", "tp")
    outward = P("ctx", "tp", "fsdp")
    weights = (by_row, by_row, inward, outward, inward, inward, outward)
    return jax.shard_map(
        on_device,
        mesh=mesh,
        in_specs=(by_token,) * 4 + (P(),) * 4 + weights,
        out_specs=(by_token,) * 2 + (P(),) * 6 + weights,
        check_vma=False,
    )
```

time: 2170 us -> 1290 us (0.59)
  waiting for transfers between devices: 1240 us -> 541 us
  blocking collectives: 194 us -> 0 us
  starting transfers between devices: 38.2 us -> 152 us
  matrix products: 340 us -> 244 us
  Pallas kernels: 0 us -> 42.6 us
  other arithmetic: 141 us -> 111 us
    ppermute x0 -> x129, waiting for transfers between devices: none -> 541 us  [swap(): return lax.ppermute(value, axis, [(i, i ^ distance) for i in range(size)])]
    reduce_scatter x9 -> x0, waiting for transfers between devices: 516 us -> none  [the longest x1 109 us: on_device(): lax.psum_scatter(value_weight_grad, ('fsdp', 'ctx'), scatter_dimension=0,...]
    psum x4 -> x0, waiting for transfers between devices: 324 us -> none  [the longest x3 239 us: head_total(): return lax.psum(partial_sum.astype(jnp.bfloat16), 'tp').astype(jnp.float32)]
    all_gather x9 -> x0, waiting for transfers between devices: 196 us -> none  [the longest x1 46.7 us: on_device(): lax.all_gather(key_proj, ('fsdp', 'ctx'), axis=0, tiled=True)]
    all_to_all x8 -> x0, waiting for transfers between devices: 194 us -> none  [the longest x3 142 us: to_experts(): lax.all_to_all(slot_rows, 'ctx', split_axis=0, concat_axis=0, tiled=True)]
    ppermute x0 -> x129, starting transfers between devices: none -> 152 us  [swap(): return lax.ppermute(value, axis, [(i, i ^ distance) for i in range(size)])]
    psum x2 -> x0, blocking collectives: 130 us -> none  [on_device(): lax.psum((attn_hits, ffn_hits, jnp.sum(attn_probs, axis=0), jnp.sum(ffn_p...]
    dot_general x83 -> x41, matrix products: 340 us -> 244 us  [the longest x16 86.3 us: matmul_tn(): lax.dot_general(lhs, rhs, (((0,), (0,)), ((), ())), preferred_element_typ...]
  transfers between devices with their start and end apart: 30 -> 129, of which waited for: 20 -> 62; matrix products, arithmetic and copies ran while one was open for 18% -> 36% of each run, Pallas kernels for 0% -> 3%
where the time goes in v1:
time: 1290 us; the launch traced here: 1280 us
  waiting for transfers between devices  541 us (42%)
  matrix products  244 us (19%)
  local copies, waits for them, and re-layouts  185 us (14%)
  starting transfers between devices  152 us (12%)
  other arithmetic  111 us (9%)
  Pallas kernels  42.6 us (3%)
    ppermute x129, waiting for transfers between devices, swap(): return lax.ppermute(value, axis, [(i, i ^ distance) for i in range(size)])  541 us
    ppermute x129, starting transfers between devices, swap(): return lax.ppermute(value, axis, [(i, i ^ distance) for i in range(size)])  152 us
    dot_general x16, matrix products, matmul_tn(): lax.dot_general(lhs, rhs, (((0,), (0,)), ((), ())), preferred_element_typ...  86.3 us
    dot_general x6, matrix products, matmul_nt(): lax.dot_general(lhs, rhs, (((1,), (1,)), ((), ())), preferred_element_typ...  81 us
    rev x20, local copies, waits for them, and re-layouts, flip_blocks(): turned = jnp.flip(split, axis + 1).reshape(shape)  65.9 us
    dot_general x14, matrix products, matmul(): return jnp.dot(lhs, rhs, preferred_element_type=FULL)  65.7 us
    unnamed x298, local copies, waits for them, and re-layouts  42.5 us
  transfers between devices with their start and end apart: 129, of which 62 were waited for; matrix products, arithmetic and copies ran while one was open for 36% of the time, Pallas kernels for 3%

profile of v1, /device:TPU:0, one launch (start us, length us, event | category | flops | bytes accessed | tf_op | source)
XLA Modules:
  0.0 1280.0 jit_solution(6530319481338317717)
XLA Ops:
  115.2 11.7 collective-permute-done.2
  192.7 39.3 %collective-permute-done.43 = bf16[2816,512]{1,0:T(8,128)(2,1)} collective-permute-done((bf16[2816,512]{1,0:T(8,128)(2,1)S(1)}, bf16[2816,512]{1,0:T(8,128)(2,1)}, u32[]{:S(2)}, u32[]{:S(2)}) %collective-permute-start.43) | collective-permute-done | bytes 2883616 | tf_op jit(solution)/shard_map/ppermute | solution.py:39
  238.7 15.3 %collective-permute-done.18 = bf16[1024,512]{1,0:T(8,128)(2,1)} collective-permute-done((bf16[1024,512]{1,0:T(8,128)(2,1)S(1)}, bf16[1024,512]{1,0:T(8,128)(2,1)}, u32[]{:S(2)}, u32[]{:S(2)}) %collective-permute-start.18) | collective-permute-done | bytes 1048608 | tf_op jit(solution)/shard_map/ppermute | solution.py:39
  254.8 13.4 %fusion.13.k_lin.v_lin = f32[1024,2048]{1,0:T(8,128)} fusion(bf16[1024,2048]{1,0:T(8,128)(2,1)S(1)} %copy-done.1, bf16[512,2048]{1,0:T(8,128)(2,1)} %collective-permute-done.17, bf16[512,2048]{1,0:T(8,128)(2,1)} %collective-permute-done.16, bf16[512,2048]{1,0:T(8,128)(2,1)} %collective-permute-done.15, ...), kind=kOutput, calls=%fused_computation.60 | convolution fusion | flops 8623489024 | bytes 20971520 | tf_op jit(solution)/shard_map/dot_general | solution.py:22
  268.2 19.1 %shard_map.262 = (bf16[640,1024]{1,0:T(8,128)(2,1)}, bf16[1024,1024]{1,0:T(8,128)(2,1)}, bf16[1024,1024]{1,0:T(8,128)(2,1)}, bf16[640,1024]{1,0:T(8,128)(2,1)}, f32[640,1024]{1,0:T(8,128)}) custom-call(f32[640,1024]{1,0:T(8,128)} %fusion.61.q_lin, f32[1024,2048]{1,0:T(8,128)} %fusion.13.k_lin.v_lin, f32[1024,2048]{1,0:T(8,128)} %fusion.13.k_lin.v_lin, ...), custom_call_target="tpu_custom_call" | custom-call | flops 2013265920 | bytes 20971520 | tf_op jit(solution)/shard_map/pallas_call | solution.py:217
  295.2 20.6 %collective-permute-done.40 = bf16[512,2816]{1,0:T(8,128)(2,1)} collective-permute-done((bf16[512,2816]{1,0:T(8,128)(2,1)S(1)}, bf16[512,2816]{1,0:T(8,128)(2,1)}, u32[]{:S(2)}, u32[]{:S(2)}) %collective-permute-start.40) | collective-permute-done | bytes 2883616 | tf_op jit(solution)/shard_map/ppermute | solution.py:39
  336.4 33.7 %collective-permute-done.37 = bf16[512,2816]{1,0:T(8,128)(2,1)} collective-permute-done((bf16[512,2816]{1,0:T(8,128)(2,1)}, bf16[512,2816]{1,0:T(8,128)(2,1)}, u32[]{:S(2)}, u32[]{:S(2)}) %collective-permute-start.37) | collective-permute-done | bytes 2883616 | tf_op jit(solution)/shard_map/ppermute | solution.py:39
  406.9 15.8 %collective-permute-done.33 = bf16[160,1024]{1,0:T(8,128)(2,1)S(1)} collective-permute-done((bf16[160,1024]{1,0:T(8,128)(2,1)}, bf16[160,1024]{1,0:T(8,128)(2,1)S(1)}, u32[]{:S(2)}, u32[]{:S(2)}) %collective-permute-start.33) | collective-permute-done | bytes 327712 | tf_op jit(solution)/shard_map/ppermute | solution.py:39
  460.1 26.6 %multiply_reduce_fusion = (f32[640]{0:T(1024)S(1)}, bf16[640,2816]{1,0:T(8,128)(2,1)}, f32[640,2816]{1,0:T(8,128)}) fusion(f32[640,2816]{1,0:T(8,128)} %fusion.171, f32[640,2816]{1,0:T(8,128)} %fusion.170, bf16[640,2048]{1,0:T(8,128)(2,1)S(1)} %maximum_dynamic-update-slice_fusion.11, bf16[2816,2048]{1,0:T(8,128)(2,1)} %constant_dynamic-update-slice_fusion.10), kind=kOutput, calls=%fused_computation.11 | convolution fusion | flops 7396392448 | bytes 39389696 | tf_op jit(solution)/shard_map/dot_general | solution.py:30
  486.7 13.0 %fusion.129 = f32[640,2048]{1,0:T(8,128)} fusion(bf16[2816,2048]{1,0:T(8,128)(2,1)} %constant_dynamic-update-slice_fusion.10, bf16[640,2816]{1,0:T(8,128)(2,1)} %get-tuple-element.70), kind=kOutput, calls=%fused_computation.428 | convolution fusion | flops 7381975040 | bytes 20381696 | tf_op jit(solution)/shard_map/dot_general | solution.py:22
  554.7 14.6 %fusion.172 = f32[640,2048]{1,0:T(8,128)} fusion(bf16[640,2816]{1,0:T(8,128)(2,1)S(1)} %get-tuple-element.74, bf16[2048,2816]{1,0:T(8,128)(2,1)} %constant_dynamic-update-slice_fusion.6), kind=kOutput, calls=%fused_computation.468 | convolution fusion | flops 7381975040 | bytes 20381696 | tf_op jit(solution)/shard_map/dot_general | solution.py:30
  576.0 11.4 convolution_add_fusion
  648.8 12.7 collective-permute-done.50
  663.3 21.8 %collective-permute-done.68 = bf16[160,1024]{1,0:T(8,128)(2,1)S(1)} collective-permute-done((bf16[160,1024]{1,0:T(8,128)(2,1)S(1)}, bf16[160,1024]{1,0:T(8,128)(2,1)S(1)}, u32[]{:S(2)}, u32[]{:S(2)}) %collective-permute-start.68) | collective-permute-done | bytes 327712 | tf_op jit(solution)/shard_map/ppermute | solution.py:39
  751.2 12.6 collective-permute-done.86
  784.5 23.5 %shard_map.263 = (bf16[640,1024]{1,0:T(8,128)(2,1)}, bf16[1024,1024]{1,0:T(8,128)(2,1)}, bf16[1024,1024]{1,0:T(8,128)(2,1)}) custom-call(bf16[640,1024]{1,0:T(8,128)(2,1)} %get-tuple-element.32.q_low, bf16[1024,1024]{1,0:T(8,128)(2,1)} %get-tuple-element.33.k_low, bf16[1024,1024]{1,0:T(8,128)(2,1)} %get-tuple-element.34.v_low, ...), custom_call_target="tpu_custom_call" | custom-call | flops 4697620480 | bytes 14680064 | tf_op jit(solution)/shard_map/pallas_call | solution.py:274
  821.3 16.7 %bitcast_add_fusion = f32[1024,2048]{1,0:T(8,128)} fusion(f32[4,256,2048]{2,1,0:T(8,128)} %fusion.70, bf16[1024,2048]{1,0:T(8,128)(2,1)} %constant_dynamic-update-slice_fusion.14, bf16[512,2048]{1,0:T(8,128)(2,1)} %collective-permute-done.17, bf16[512,2048]{1,0:T(8,128)(2,1)} %collective-permute-done.16, bf16[512,2048]{1,0:T(8,128)(2,1)} %collective-permute-done.15, ...), kind=kOutput, calls=%fused_computation.9 | convolution fusion | flops 8625586176 | bytes 29360128 | tf_op jit(solution)/shard_map/dot_general | solution.py:30
  857.9 11.2 collective-permute-done.96
  869.2 11.2 collective-permute-done.94
  1065.0 25.7 %collective-permute-done.115 = bf16[512,2048]{1,0:T(8,128)(2,1)} collective-permute-done((bf16[512,2048]{1,0:T(8,128)(2,1)}, bf16[512,2048]{1,0:T(8,128)(2,1)}, u32[]{:S(2)}, u32[]{:S(2)}) %collective-permute-start.115) | collective-permute-done | bytes 2097184 | tf_op jit(solution)/shard_map/ppermute | solution.py:39
  1098.1 13.1 %convert_add_fusion = f32[2816,1024]{1,0:T(8,128)} fusion(bf16[2816,1024]{1,0:T(8,128)(2,1)} %collective-permute-done.127, bf16[640,2048]{1,0:T(8,128)(2,1)} %copy-done.35, bf16[640,2816]{1,0:T(8,128)(2,1)} %get-tuple-element.70), kind=kOutput, calls=%fused_computation | convolution fusion | flops 3696754688 | bytes 22216704 | tf_op jit(solution)/shard_map/dot_general | solution.py:26
  1121.2 17.9 %collective-permute-done.116 = bf16[128,2048]{1,0:T(8,128)(2,1)} collective-permute-done((bf16[128,2048]{1,0:T(8,128)(2,1)S(1)}, bf16[128,2048]{1,0:T(8,128)(2,1)}, u32[]{:S(2)}, u32[]{:S(2)}) %collective-permute-start.116) | collective-permute-done | bytes 524320 | tf_op jit(solution)/shard_map/ppermute | solution.py:39
  1157.3 56.9 %collective-permute-done.126 = bf16[512,2816]{1,0:T(8,128)(2,1)} collective-permute-done((bf16[512,2816]{1,0:T(8,128)(2,1)}, bf16[512,2816]{1,0:T(8,128)(2,1)}, u32[]{:S(2)}, u32[]{:S(2)}) %collective-permute-start.126) | collective-permute-done | bytes 2883616 | tf_op jit(solution)/shard_map/ppermute | solution.py:39
  1219.1 54.6 %collective-permute-done.128 = bf16[2816,512]{1,0:T(8,128)(2,1)S(1)} collective-permute-done((bf16[2816,512]{1,0:T(8,128)(2,1)}, bf16[2816,512]{1,0:T(8,128)(2,1)S(1)}, u32[]{:S(2)}, u32[]{:S(2)}) %collective-permute-start.128) | collective-permute-done | bytes 2883616 | tf_op jit(solution)/shard_map/ppermute | solution.py:39
  (894 shorter events, 763.6 us)
Async XLA Ops:
  4.0 88.5 %collective-permute-start.12 = (bf16[128,2048]{1,0:T(8,128)(2,1)}, bf16[128,2048]{1,0:T(8,128)(2,1)}, u32[]{:S(2)}, u32[]{:S(2)}) collective-permute-start(bf16[128,2048]{1,0:T(8,128)(2,1)} %constant_dynamic-update-slice_fusion), channel_id=1, source_target_pairs={{0,2},{2,0},{4,6},{6,4},{1,3},{3,1},{5,7},{7,5},{8,10},{10,8},{12,... | collective-permute-start | bytes 1572872 | tf_op jit(solution)/shard_map/ppermute | solution.py:39
  7.0 87.7 %collective-permute-start.13 = (bf16[128,2048]{1,0:T(8,128)(2,1)}, bf16[128,2048]{1,0:T(8,128)(2,1)}, u32[]{:S(2)}, u32[]{:S(2)}) collective-permute-start(bf16[128,2048]{1,0:T(8,128)(2,1)} %constant_dynamic-update-slice_fusion), channel_id=1, source_target_pairs={{0,4},{2,6},{4,0},{6,2},{1,5},{3,7},{5,1},{7,3},{8,12},{10,14},{12... | collective-permute-start | bytes 1572872 | tf_op jit(solution)/shard_map/ppermute | solution.py:39
  9.6 87.8 %collective-permute-start.14 = (bf16[128,2048]{1,0:T(8,128)(2,1)}, bf16[128,2048]{1,0:T(8,128)(2,1)}, u32[]{:S(2)}, u32[]{:S(2)}) collective-permute-start(bf16[128,2048]{1,0:T(8,128)(2,1)} %constant_dynamic-update-slice_fusion), channel_id=1, source_target_pairs={{0,6},{2,4},{4,2},{6,0},{1,7},{3,5},{5,3},{7,1},{8,14},{10,12},{12... | collective-permute-start | bytes 1572872 | tf_op jit(solution)/shard_map/ppermute | solution.py:39
  10.9 71.8 %collective-permute-start.6 = (s32[1,4,256]{2,1,0:T(4,128)}, s32[1,4,256]{2,1,0:T(4,128)}, u32[]{:S(2)}, u32[]{:S(2)}) collective-permute-start(s32[1,4,256]{2,1,0:T(4,128)} %add_bitcast_fusion), channel_id=1, source_target_pairs={{0,2},{2,0},{4,6},{6,4},{1,3},{3,1},{5,7},{7,5},{8,10},{10,8},{12,... | collective-permute-start | bytes 12296 | tf_op jit(solution)/shard_map/ppermute | solution.py:39
  11.8 71.7 %collective-permute-start.7 = (s32[1,4,256]{2,1,0:T(4,128)}, s32[1,4,256]{2,1,0:T(4,128)}, u32[]{:S(2)}, u32[]{:S(2)}) collective-permute-start(s32[1,4,256]{2,1,0:T(4,128)} %add_bitcast_fusion), channel_id=1, source_target_pairs={{0,4},{2,6},{4,0},{6,2},{1,5},{3,7},{5,1},{7,3},{8,12},{10,14},{12... | collective-permute-start | bytes 12296 | tf_op jit(solution)/shard_map/ppermute | solution.py:39
  94.7 75.4 %collective-permute-start.9 = (bf16[512,1024]{1,0:T(8,128)(2,1)}, bf16[512,1024]{1,0:T(8,128)(2,1)}, u32[]{:S(2)}, u32[]{:S(2)}) collective-permute-start(bf16[512,1024]{1,0:T(8,128)(2,1)} %bitcast.11), channel_id=1, source_target_pairs={{0,16},{8,24},{16,0},{24,8},{1,17},{9,25},{17,1},{25,9},{2,18},{10... | collective-permute-start | bytes 3145736 | tf_op jit(solution)/shard_map/ppermute | solution.py:39
  113.5 71.4 %collective-permute-start.15 = (bf16[512,2048]{1,0:T(8,128)(2,1)}, bf16[512,2048]{1,0:T(8,128)(2,1)}, u32[]{:S(2)}, u32[]{:S(2)}) collective-permute-start(bf16[512,2048]{1,0:T(8,128)(2,1)} %constant_dynamic-update-slice_fusion.33), channel_id=1, source_target_pairs={{0,16},{8,24},{16,0},{24,8},{1,17},{9,25},{17,1},{25,9},{2,18},{10... | collective-permute-start | bytes 6291464 | tf_op jit(solution)/shard_map/ppermute | solution.py:39
  184.3 69.7 %collective-permute-start.16 = (bf16[512,2048]{1,0:T(8,128)(2,1)}, bf16[512,2048]{1,0:T(8,128)(2,1)}, u32[]{:S(2)}, u32[]{:S(2)}) collective-permute-start(bf16[512,2048]{1,0:T(8,128)(2,1)} %constant_dynamic-update-slice_fusion.33), channel_id=1, source_target_pairs={{0,8},{8,0},{16,24},{24,16},{1,9},{9,1},{17,25},{25,17},{2,10},{10... | collective-permute-start | bytes 6291464 | tf_op jit(solution)/shard_map/ppermute | solution.py:39
  184.9 69.7 %collective-permute-start.17 = (bf16[512,2048]{1,0:T(8,128)(2,1)}, bf16[512,2048]{1,0:T(8,128)(2,1)}, u32[]{:S(2)}, u32[]{:S(2)}) collective-permute-start(bf16[512,2048]{1,0:T(8,128)(2,1)} %collective-permute-done.15), channel_id=1, source_target_pairs={{0,8},{8,0},{16,24},{24,16},{1,9},{9,1},{17,25},{25,17},{2,10},{10... | collective-permute-start | bytes 6291464 | tf_op jit(solution)/shard_map/ppermute | solution.py:39
  185.4 68.6 %collective-permute-start.18 = (bf16[1024,512]{1,0:T(8,128)(2,1)S(1)}, bf16[1024,512]{1,0:T(8,128)(2,1)}, u32[]{:S(2)}, u32[]{:S(2)}) collective-permute-start(bf16[1024,512]{1,0:T(8,128)(2,1)S(1)} %bitcast.348), channel_id=1, source_target_pairs={{0,16},{8,24},{16,0},{24,8},{1,17},{9,25},{17,1},{25,9},{2,18},{10... | collective-permute-start | bytes 3145736 | tf_op jit(solution)/shard_map/ppermute | solution.py:39
  235.7 80.0 %collective-permute-start.40 = (bf16[512,2816]{1,0:T(8,128)(2,1)S(1)}, bf16[512,2816]{1,0:T(8,128)(2,1)}, u32[]{:S(2)}, u32[]{:S(2)}) collective-permute-start(bf16[512,2816]{1,0:T(8,128)(2,1)S(1)} %bitcast.240), channel_id=1, source_target_pairs={{0,16},{8,24},{16,0},{24,8},{1,17},{9,25},{17,1},{25,9},{2,18},{10... | collective-permute-start | bytes 8650760 | tf_op jit(solution)/shard_map/ppermute | solution.py:39
  254.0 116.1 %collective-permute-start.37 = (bf16[512,2816]{1,0:T(8,128)(2,1)}, bf16[512,2816]{1,0:T(8,128)(2,1)}, u32[]{:S(2)}, u32[]{:S(2)}) collective-permute-start(bf16[512,2816]{1,0:T(8,128)(2,1)} %bitcast.25), channel_id=1, source_target_pairs={{0,16},{8,24},{16,0},{24,8},{1,17},{9,25},{17,1},{25,9},{2,18},{10... | collective-permute-start | bytes 8650760 | tf_op jit(solution)/shard_map/ppermute | solution.py:39
  287.3 95.7 %collective-permute-start.38 = (bf16[512,2816]{1,0:T(8,128)(2,1)}, bf16[512,2816]{1,0:T(8,128)(2,1)S(1)}, u32[]{:S(2)}, u32[]{:S(2)}) collective-permute-start(bf16[512,2816]{1,0:T(8,128)(2,1)} %bitcast.25), channel_id=1, source_target_pairs={{0,8},{8,0},{16,24},{24,16},{1,9},{9,1},{17,25},{25,17},{2,10},{10... | collective-permute-start | bytes 8650760 | tf_op jit(solution)/shard_map/ppermute | solution.py:39
  327.2 97.5 %collective-permute-start.45 = (bf16[2816,512]{1,0:T(8,128)(2,1)}, bf16[2816,512]{1,0:T(8,128)(2,1)}, u32[]{:S(2)}, u32[]{:S(2)}) collective-permute-start(bf16[2816,512]{1,0:T(8,128)(2,1)} %collective-permute-done.43), channel_id=1, source_target_pairs={{0,8},{8,0},{16,24},{24,16},{1,9},{9,1},{17,25},{25,17},{2,10},{10... | collective-permute-start | bytes 8650760 | tf_op jit(solution)/shard_map/ppermute | solution.py:39
  507.7 89.3 %collective-permute-start.46 = (bf16[160,1024]{1,0:T(8,128)(2,1)S(1)}, bf16[160,1024]{1,0:T(8,128)(2,1)S(1)}, u32[]{:S(2)}, u32[]{:S(2)}) collective-permute-start(bf16[160,1024]{1,0:T(8,128)(2,1)S(1)} %select_convert_fusion.12), channel_id=1, source_target_pairs={{0,1},{1,0},{2,3},{3,2},{4,5},{5,4},{6,7},{7,6},{8,9},{9,8},{10,11... | collective-permute-start | bytes 983048 | tf_op jit(solution)/shard_map/ppermute | solution.py:39
  601.3 443.5 %collective-permute-start.123 = (bf16[1024,2816]{1,0:T(8,128)(2,1)}, bf16[1024,2816]{1,0:T(8,128)(2,1)}, u32[]{:S(2)}, u32[]{:S(2)}) collective-permute-start(bf16[1024,2816]{1,0:T(8,128)(2,1)} %convolution_convert_fusion.2), channel_id=1, source_target_pairs={{0,8},{8,0},{16,24},{24,16},{1,9},{9,1},{17,25},{25,17},{2,10},{10... | collective-permute-start | bytes 17301512 | tf_op jit(solution)/shard_map/ppermute | solution.py:39
  741.8 105.0 %collective-permute-start.53 = (bf16[256,1024]{1,0:T(8,128)(2,1)}, bf16[256,1024]{1,0:T(8,128)(2,1)S(1)}, u32[]{:S(2)}, u32[]{:S(2)}) collective-permute-start(bf16[256,1024]{1,0:T(8,128)(2,1)} %fusion.32), channel_id=1, source_target_pairs={{0,1},{1,0},{2,3},{3,2},{4,5},{5,4},{6,7},{7,6},{8,9},{9,8},{10,11... | collective-permute-start | bytes 1572872 | tf_op jit(solution)/shard_map/ppermute | solution.py:39
  848.0 68.3 %collective-permute-start.91 = (bf16[256,1024]{1,0:T(8,128)(2,1)}, bf16[256,1024]{1,0:T(8,128)(2,1)}, u32[]{:S(2)}, u32[]{:S(2)}) collective-permute-start(bf16[256,1024]{1,0:T(8,128)(2,1)} %get-tuple-element.75), channel_id=1, source_target_pairs={{0,1},{1,0},{2,3},{3,2},{4,5},{5,4},{6,7},{7,6},{8,9},{9,8},{10,11... | collective-permute-start | bytes 1572872 | tf_op jit(solution)/shard_map/ppermute | solution.py:39
  952.1 80.0 %collective-permute-start.114 = (bf16[1024,2048]{1,0:T(8,128)(2,1)}, bf16[1024,2048]{1,0:T(8,128)(2,1)}, u32[]{:S(2)}, u32[]{:S(2)}) collective-permute-start(bf16[1024,2048]{1,0:T(8,128)(2,1)} %convolution_convert_fusion.3), channel_id=1, source_target_pairs={{0,8},{8,0},{16,24},{24,16},{1,9},{9,1},{17,25},{25,17},{2,10},{10... | collective-permute-start | bytes 12582920 | tf_op jit(solution)/shard_map/ppermute | solution.py:39
  973.3 81.5 %collective-permute-start.125 = (bf16[1024,2816]{1,0:T(8,128)(2,1)}, bf16[1024,2816]{1,0:T(8,128)(2,1)}, u32[]{:S(2)}, u32[]{:S(2)}) collective-permute-start(bf16[1024,2816]{1,0:T(8,128)(2,1)} %convolution_convert_fusion.1), channel_id=1, source_target_pairs={{0,8},{8,0},{16,24},{24,16},{1,9},{9,1},{17,25},{25,17},{2,10},{10... | collective-permute-start | bytes 17301512 | tf_op jit(solution)/shard_map/ppermute | solution.py:39
  988.6 108.3 %collective-permute-start.127 = (bf16[2816,1024]{1,0:T(8,128)(2,1)}, bf16[2816,1024]{1,0:T(8,128)(2,1)}, u32[]{:S(2)}, u32[]{:S(2)}) collective-permute-start(bf16[2816,1024]{1,0:T(8,128)(2,1)} %convolution_convert_fusion), channel_id=1, source_target_pairs={{0,8},{8,0},{16,24},{24,16},{1,9},{9,1},{17,25},{25,17},{2,10},{10... | collective-permute-start | bytes 17301512 | tf_op jit(solution)/shard_map/ppermute | solution.py:39
  1053.5 98.9 %collective-permute-start.124 = (bf16[512,2816]{1,0:T(8,128)(2,1)}, bf16[512,2816]{1,0:T(8,128)(2,1)}, u32[]{:S(2)}, u32[]{:S(2)}) collective-permute-start(bf16[512,2816]{1,0:T(8,128)(2,1)} %slice.598), channel_id=1, source_target_pairs={{0,16},{8,24},{16,0},{24,8},{1,17},{9,25},{17,1},{25,9},{2,18},{10... | collective-permute-start | bytes 8650760 | tf_op jit(solution)/shard_map/ppermute | solution.py:39
  1063.8 150.5 %collective-permute-start.126 = (bf16[512,2816]{1,0:T(8,128)(2,1)}, bf16[512,2816]{1,0:T(8,128)(2,1)}, u32[]{:S(2)}, u32[]{:S(2)}) collective-permute-start(bf16[512,2816]{1,0:T(8,128)(2,1)} %slice.597), channel_id=1, source_target_pairs={{0,16},{8,24},{16,0},{24,8},{1,17},{9,25},{17,1},{25,9},{2,18},{10... | collective-permute-start | bytes 8650760 | tf_op jit(solution)/shard_map/ppermute | solution.py:39
  1115.8 157.9 %collective-permute-start.128 = (bf16[2816,512]{1,0:T(8,128)(2,1)}, bf16[2816,512]{1,0:T(8,128)(2,1)S(1)}, u32[]{:S(2)}, u32[]{:S(2)}) collective-permute-start(bf16[2816,512]{1,0:T(8,128)(2,1)} %slice.596), channel_id=1, source_target_pairs={{0,16},{8,24},{16,0},{24,8},{1,17},{9,25},{17,1},{25,9},{2,18},{10... | collective-permute-start | bytes 8650760 | tf_op jit(solution)/shard_map/ppermute | solution.py:39
  (242 other events, 6203.0 us)

commit v2 on v1

--- a/solution.py
+++ b/solution.py
@@ -65,14 +65,11 @@
 
 
 def flip_blocks(value, axis, index, count):
-    shape = value.shape
-    width = shape[axis] // count
+    parts = jnp.split(value, count, axis)
     for bit in bits_down(count):
-        outer = shape[axis] // (2 * bit * width)
-        split = value.reshape(shape[:axis] + (outer, 2, bit * width) + shape[axis + 1 :])
-        turned = jnp.flip(split, axis + 1).reshape(shape)
-        value = jnp.where((index // bit) % 2 == 1, turned, value)
-    return value
+        turned = (index // bit) % 2 == 1
+        parts = [jnp.where(turned, parts[n ^ bit], parts[n]) for n in range(count)]
+    return jnp.concatenate(parts, axis)
 
 
 def to_spread(value, axis):
@@ -135,7 +132,7 @@
     return lax.dynamic_slice_in_dim(value, (lax.axis_index("ctx") ^ distance) * rows, rows, 0)
 
 
-def send_out(half_rows):
+def spread_out(half_rows):
     size = lax.axis_size("ctx")
     blocks = [None] * size
     for distance in far_first(size):
@@ -146,17 +143,417 @@
     return place_blocks(blocks)
 
 
-def send_home(partial_rows):
+def xor_index(index, distance):
+    result = index
+    bit = 1
+    while bit <= distance:
+        if distance & bit:
+            result = result + bit - 2 * bit * ((index // bit) % 2)
+        bit *= 2
+    return result
+
+
+def span(start, size):
+    return pl.ds(pl.multiple_of(start * size, 16), size)
+
+
+def meet(peers):
+    barrier = pltpu.get_barrier_semaphore()
+    for device in peers:
+        pl.semaphore_signal(barrier, inc=1, device_id=device, device_id_type=pl.DeviceIdType.MESH)
+    pl.semaphore_wait(barrier, len(peers))
+
+
+def remote(source, target, sems, index, device):
+    return pltpu.make_async_remote_copy(
+        src_ref=source,
+        dst_ref=target,
+        send_sem=sems[0].at[index],
+        recv_sem=sems[1].at[index],
+        device_id=device,
+        device_id_type=pl.DeviceIdType.MESH,
+    )
+
+
+def send_out_kernel(size, rows_ref, out_ref, z_land, y_land, z_send, z_recv, y_send, y_recv):
+    mine, first = lax.axis_index("ctx"), lax.axis_index("tp") == 0
+    other_tp = {"tp": 1 - lax.axis_index("tp")}
+    rows, width = z_land.shape[1], z_land.shape[2]
+    at = [xor_index(mine, distance) for distance in range(size)]
+    meet([{"ctx": at[distance]} for distance in range(1, size)] + [other_tp])
+    order = [distance for distance in far_first(size) if distance]
+    across, beside = {}, {}
+    for distance in order:
+        across[distance] = remote(
+            rows_ref.at[span(at[distance], rows)],
+            z_land.at[distance],
+            (z_send, z_recv),
+            distance,
+            {"ctx": at[distance]},
+        )
+        across[distance].start()
+    beside[0] = remote(rows_ref.at[span(mine, rows)], y_land.at[0], (y_send, y_recv), 0, other_tp)
+    beside[0].start()
+    for distance in order:
+        across[distance].wait_recv()
+        beside[distance] = remote(
+            z_land.at[distance], y_land.at[distance], (y_send, y_recv), distance, other_tp
+        )
+        beside[distance].start()
+    for distance in [0] + order:
+        beside[distance].wait_recv()
+        own = z_land[distance] if distance else rows_ref[span(mine, rows), :]
+        theirs = y_land[distance]
+        out_ref[span(at[distance], rows), :width] = jnp.where(first, own, theirs)
+        out_ref[span(at[distance], rows), width:] = jnp.where(first, theirs, own)
+    for distance in order:
+        across[distance].wait_send()
+    for distance in [0] + order:
+        beside[distance].wait_send()
+
+
+def send_out(half_rows, number):
     size = lax.axis_size("ctx")
-    blocks = [None] * size
-    for distance in far_first(size):
-        block = block_for(partial_rows, distance)
-        arrived = swap(other_half(block).astype(LOW), "tp", 1)
-        block = (my_half(block).astype(FULL) + arrived.astype(FULL)).astype(LOW)
+    total, width = half_rows.shape
+    land = pltpu.VMEM((size, total // size, width), half_rows.dtype)
+    return pl.pallas_call(
+        functools.partial(send_out_kernel, size),
+        in_specs=[pl.BlockSpec(memory_space=pltpu.VMEM)],
+        out_specs=pl.BlockSpec(memory_space=pltpu.VMEM),
+        out_shape=jax.ShapeDtypeStruct((total, 2 * width), half_rows.dtype),
+        scratch_shapes=[land, land] + [pltpu.SemaphoreType.DMA((size,))] * 4,
+        compiler_params=pltpu.CompilerParams(
+            collective_id=number, has_side_effects=True, vmem_limit_bytes=VMEM_BYTES
+        ),
+        cost_estimate=pl.CostEstimate(flops=0, bytes_accessed=12 * total * width, transcendentals=0),
+    )(half_rows)
+
+
+def send_home_kernel(size, add_up, has_extra, *refs):
+    part_ref, refs = refs[0], refs[1:]
+    extra_ref, refs = (refs[0], refs[1:]) if has_extra else (None, refs)
+    out_ref, refs = refs[0], refs[1:]
+    extra_out, refs = (refs[0], refs[1:]) if has_extra else (None, refs)
+    y_land, ready, z_land, y_send, y_recv, z_send, z_recv = refs[:7]
+    mine, first = lax.axis_index("ctx"), lax.axis_index("tp") == 0
+    place = lax.axis_index("tp")
+    other_tp = {"tp": 1 - place}
+    rows, width = z_land.shape[1], z_land.shape[2]
+    at = [xor_index(mine, distance) for distance in range(size)]
+    columns = pl.ds(pl.multiple_of((1 - place) * width, 128), width)
+    meet([{"ctx": at[distance]} for distance in range(1, size)] + [other_tp])
+    order = far_first(size)
+    beside, across, extras = {}, {}, {}
+    if has_extra:
+        ey_land, e_ready, ez_land, ey_send, ey_recv, ez_send, ez_recv = refs[7:]
+        extra_beside = remote(extra_ref, ey_land, (ey_send, ey_recv), 0, other_tp)
+        extra_beside.start()
+    for distance in order:
+        beside[distance] = remote(
+            part_ref.at[span(at[distance], rows), columns],
+            y_land.at[distance],
+            (y_send, y_recv),
+            distance,
+            other_tp,
+        )
+        beside[distance].start()
+    if has_extra:
+        extra_beside.wait_recv()
+        e_ready[...] = extra_ref[...] + ey_land[...]
+        for distance in order:
+            if distance:
+                extras[distance] = remote(
+                    e_ready.at[at[distance]],
+                    ez_land.at[distance],
+                    (ez_send, ez_recv),
+                    distance,
+                    {"ctx": at[distance]},
+                )
+                extras[distance].start()
+    for distance in order:
+        beside[distance].wait_recv()
+        whole = part_ref[span(at[distance], rows), :]
+        own = jnp.where(first, whole[:, :width], whole[:, width:])
+        total = (own.astype(FULL) + y_land[distance].astype(FULL)).astype(LOW)
         if distance:
-            block = swap(block, "ctx", distance)
-        blocks[distance] = block
-    return blocks
+            ready[distance] = total
+            across[distance] = remote(
+                ready.at[distance],
+                z_land.at[distance],
+                (z_send, z_recv),
+                distance,
+                {"ctx": at[distance]},
+            )
+            across[distance].start()
+        elif add_up:
+            out_ref[...] = total.astype(FULL)
+        else:
+            out_ref[span(mine, rows), :] = total
+    for distance in order:
+        if distance:
+            across[distance].wait_recv()
+            if add_up:
+                out_ref[...] += z_land[distance].astype(FULL)
+            else:
+                out_ref[span(at[distance], rows), :] = z_land[distance]
+    if has_extra:
+        extra_out[mine] = e_ready[mine]
+        for distance in order:
+            if distance:
+                extras[distance].wait_recv()
+                extra_out[at[distance]] = ez_land[distance]
+                extras[distance].wait_send()
+        extra_beside.wait_send()
+    for distance in order:
+        beside[distance].wait_send()
+        if distance:
+            across[distance].wait_send()
+
+
+def send_home(partial_rows, number, extra=None, add_up=False):
+    size = lax.axis_size("ctx")
+    total, width = partial_rows.shape[0], partial_rows.shape[1] // 2
+    rows = total // size
+    land = pltpu.VMEM((size, rows, width), LOW)
+    sems = [pltpu.SemaphoreType.DMA((size,))] * 4
+    shapes = [jax.ShapeDtypeStruct((rows, width), FULL) if add_up else jax.ShapeDtypeStruct((total, width), LOW)]
+    operands, scratch = [partial_rows], [land, land, land] + sems
+    if extra is not None:
+        operands.append(extra)
+        shapes.append(jax.ShapeDtypeStruct(extra.shape, FULL))
+        scratch += [pltpu.VMEM(extra.shape, FULL)] * 3 + sems
+    results = pl.pallas_call(
+        functools.partial(send_home_kernel, size, add_up, extra is not None),
+        in_specs=[pl.BlockSpec(memory_space=pltpu.VMEM)] * len(operands),
+        out_specs=[pl.BlockSpec(memory_space=pltpu.VMEM)] * len(shapes),
+        out_shape=shapes,
+        scratch_shapes=scratch,
+        compiler_params=pltpu.CompilerParams(
+            collective_id=number, has_side_effects=True, vmem_limit_bytes=VMEM_BYTES
+        ),
+        cost_estimate=pl.CostEstimate(flops=0, bytes_accessed=12 * total * width, transcendentals=0),
+    )(*operands)
+    return results if extra is not None else results[0]
+
+
+def prologue_kernel(sizes, *refs):
+    groups, world = sizes
+    half_in, own_in, routes_in, kv_in, query_in, out_in = refs[:6]
+    seq_ref, routes_ref, kv_ref, query_ref, out_ref = refs[6:11]
+    local_sem, zt, yt, zr, zk, xk, fr, fk, fq, fo = refs[11], *[
+        (refs[12 + 2 * n], refs[13 + 2 * n]) for n in range(9)
+    ]
+    mine, place, spot = lax.axis_index("ctx"), lax.axis_index("tp"), lax.axis_index("fsdp")
+    other_tp = {"tp": 1 - place}
+    rows, width = half_in.shape
+    sub = kv_in.shape[0]
+    piece = sub * groups
+    q_rows, o_columns = query_in.shape[0], out_in.shape[1]
+    at = [xor_index(mine, distance) for distance in range(groups)]
+    ctx_peer = [{"ctx": at[distance]} for distance in range(groups)]
+    steps = list(bits_down(world))
+    beside = {bit: {"fsdp": xor_index(spot, bit)} for bit in steps}
+    meet(ctx_peer[1:] + [other_tp] + [beside[bit] for bit in steps])
+    own_columns = pl.ds(pl.multiple_of(place * width, 128), width)
+    order = [distance for distance in far_first(groups) if distance]
+    locals_ = [
+        pltpu.make_async_copy(own_in, seq_ref.at[span(mine, rows)], local_sem.at[0]),
+        pltpu.make_async_copy(routes_in, routes_ref.at[0, mine], local_sem.at[1]),
+        pltpu.make_async_copy(kv_in, kv_ref.at[span(mine, sub)], local_sem.at[2]),
+        pltpu.make_async_copy(query_in, query_ref.at[pl.ds(0, q_rows)], local_sem.at[3]),
+        pltpu.make_async_copy(out_in, out_ref.at[:, pl.ds(0, o_columns)], local_sem.at[4]),
+    ]
+    for copy in locals_:
+        copy.start()
+    started, landed = [], set()
+
+    def go(copy):
+        copy.start()
+        started.append(copy)
+        return copy
+
+    def arrived(copy):
+        if id(copy) not in landed:
+            copy.wait_recv()
+            landed.add(id(copy))
+
+    first = steps[0]
+
+    query_view = lambda n: query_ref.at[pl.ds(n * q_rows, q_rows)]
+    out_view = lambda n: out_ref.at[:, pl.ds(n * o_columns, o_columns)]
+    query_copies = {1: go(remote(query_in, query_view(1), fq, 1, beside[first]))}
+    route_copies, kv_copies, token_copies = {}, {}, {}
+    for distance in order:
+        route_copies[distance] = go(
+            remote(routes_in, routes_ref.at[0, mine], zr, distance, ctx_peer[distance])
+        )
+    for distance in order:
+        kv_copies[distance] = go(
+            remote(kv_in, kv_ref.at[span(mine, sub)], zk, distance, ctx_peer[distance])
+        )
+    for distance in order:
+        token_copies[distance] = go(
+            remote(
+                half_in, seq_ref.at[span(mine, rows), own_columns], zt, distance, ctx_peer[distance]
+            )
+        )
+    out_copies = {1: go(remote(out_in, out_view(1), fo, 1, beside[first]))}
+
+    def kv_step(distance):
+        if distance:
+            arrived(kv_copies[distance])
+            source = kv_ref.at[span(at[distance], sub)]
+        else:
+            source = kv_in
+        target = kv_ref.at[pl.ds(pl.multiple_of(piece + at[distance] * sub, 16), sub)]
+        return go(remote(source, target, xk, distance, beside[first]))
+
+    kv_first = {0: kv_step(0)}
+    half_copies = {}
+    for distance in order:
+        kv_first[distance] = kv_step(distance)
+    for distance in order:
+        arrived(token_copies[distance])
+        view = seq_ref.at[span(at[distance], rows), own_columns]
+        half_copies[distance] = go(remote(view, view, yt, distance, other_tp))
+    for distance in order:
+        arrived(route_copies[distance])
+    for copy in locals_:
+        copy.wait()
+    kv_view = lambda n: kv_ref.at[pl.ds(n * piece, piece)]
+    route_wait = {}
+    kv_wait = {}
+    count = 1
+    for bit in steps:
+        for n in range(count):
+            peer = beside[bit]
+            if n in route_wait:
+                arrived(route_wait[n])
+            route_wait[count + n] = go(
+                remote(routes_ref.at[n], routes_ref.at[count + n], fr, count + n, peer)
+            )
+            if bit != first:
+                if n:
+                    arrived(query_copies[n])
+                    arrived(out_copies[n])
+                query_copies[count + n] = go(
+                    remote(query_view(n), query_view(count + n), fq, count + n, peer)
+                )
+                out_copies[count + n] = go(remote(out_view(n), out_view(count + n), fo, count + n, peer))
+                if n == 1:
+                    for distance in range(groups):
+                        arrived(kv_first[distance])
+                if n > 1:
+                    arrived(kv_wait[n])
+                kv_wait[count + n] = go(remote(kv_view(n), kv_view(count + n), fk, count + n, peer))
+        count *= 2
+    for copy in started:
+        arrived(copy)
+    for copy in started:
+        copy.wait_send()
+
+
+def prologue(token_half, token_rows, routes, kv_rows, query_piece, out_piece, number):
+    groups, world = lax.axis_size("ctx"), lax.axis_size("fsdp")
+    any_space = pl.BlockSpec(memory_space=pl.ANY)
+    rows, features = token_rows.shape
+    pair = lambda count: [pltpu.SemaphoreType.DMA((count,))] * 2
+    return pl.pallas_call(
+        functools.partial(prologue_kernel, (groups, world)),
+        in_specs=[any_space] * 6,
+        out_specs=[any_space] * 5,
+        out_shape=[
+            jax.ShapeDtypeStruct((groups * rows, features), LOW),
+            jax.ShapeDtypeStruct((world, groups) + routes.shape, jnp.int32),
+            jax.ShapeDtypeStruct((world * groups * kv_rows.shape[0], kv_rows.shape[1]), LOW),
+            jax.ShapeDtypeStruct((world * query_piece.shape[0], query_piece.shape[1]), LOW),
+            jax.ShapeDtypeStruct((out_piece.shape[0], world * out_piece.shape[1]), LOW),
+        ],
+        scratch_shapes=[pltpu.SemaphoreType.DMA((5,))] + pair(groups) * 5 + pair(world) * 4,
+        compiler_params=pltpu.CompilerParams(collective_id=number, has_side_effects=True),
+        cost_estimate=pl.CostEstimate(flops=0, bytes_accessed=100000000, transcendentals=0),
+    )(token_half, token_rows, routes, kv_rows, query_piece, out_piece)
+
+
+def expert_kernel(world, *refs):
+    rows_ref, cot_ref, mix_ref = refs[:3]
+    gates, ups, downs = (refs[3 + n * world : 3 + (n + 1) * world] for n in range(3))
+    hidden_ref, d_gate_ref, d_up_ref, db_ref, out_ref, mix_grad_ref = refs[3 + 3 * world : 9 + 3 * world]
+    db_sum, out_sum = refs[9 + 3 * world :]
+    step = pl.program_id(0)
+    width = rows_ref.shape[1] // world
+
+    @pl.when(step == 0)
+    def _():
+        db_sum[...] = jnp.zeros_like(db_sum)
+        out_sum[...] = jnp.zeros_like(out_sum)
+        mix_grad_ref[...] = jnp.zeros_like(mix_grad_ref)
+
+    gate_lin, up_lin, d_hidden = None, None, None
+    for n in range(world):
+        columns = slice(n * width, (n + 1) * width)
+        terms = (
+            matmul(rows_ref[:, columns], gates[n][...]),
+            matmul(rows_ref[:, columns], ups[n][...]),
+            matmul_nt(cot_ref[:, columns], downs[n][...]),
+        )
+        if n:
+            terms = (gate_lin + terms[0], up_lin + terms[1], d_hidden + terms[2])
+        gate_lin, up_lin, d_hidden = terms
+    sigmoid_gate = 1.0 / (1.0 + jnp.exp(-gate_lin))
+    swish = gate_lin * sigmoid_gate
+    hidden = swish * up_lin
+    mix_grad_ref[...] += jnp.broadcast_to(
+        jnp.sum(hidden * d_hidden, axis=1, keepdims=True), mix_grad_ref.shape
+    )
+    d_gated = d_hidden * mix_ref[:, :1]
+    hidden_low = hidden.astype(LOW)
+    d_gate = (d_gated * up_lin * sigmoid_gate * (1.0 + gate_lin * (1.0 - sigmoid_gate))).astype(LOW)
+    d_up = (d_gated * swish).astype(LOW)
+    hidden_ref[...] = hidden_low
+    d_gate_ref[...] = d_gate
+    d_up_ref[...] = d_up
+    for n in range(world):
+        columns = slice(n * width, (n + 1) * width)
+        out_sum[:, columns] += matmul(hidden_low, downs[n][...])
+        db_sum[:, columns] += matmul_nt(d_gate, gates[n][...]) + matmul_nt(d_up, ups[n][...])
+
+    @pl.when(step == pl.num_programs(0) - 1)
+    def _():
+        db_ref[...] = db_sum[...].astype(LOW)
+        out_ref[...] = out_sum[...].astype(LOW)
+
+
+def expert_both_ways(rows, cot_rows, mix_rows, gate_pieces, up_pieces, down_pieces):
+    world = len(gate_pieces)
+    slots, features = rows.shape
+    depth, hidden_width = gate_pieces[0].shape
+    tile = 256
+    once = pl.Buffered(1)
+    whole = lambda width: pl.BlockSpec((slots, width), lambda i: (0, 0), pipeline_mode=once)
+    kept = lambda width: pl.BlockSpec((slots, width), lambda i: (0, 0))
+    tall = pl.BlockSpec((depth, tile), lambda i: (0, i))
+    flat = pl.BlockSpec((tile, depth), lambda i: (i, 0))
+    strip = pl.BlockSpec((slots, tile), lambda i: (0, i))
+    low = lambda width: jax.ShapeDtypeStruct((slots, width), LOW)
+    return pl.pallas_call(
+        functools.partial(expert_kernel, world),
+        grid=(hidden_width // tile,),
+        in_specs=[whole(features), whole(features), whole(HEAD)]
+        + [tall] * (2 * world)
+        + [flat] * world,
+        out_specs=[strip] * 3 + [kept(features)] * 2 + [kept(HEAD)],
+        out_shape=[low(hidden_width)] * 3
+        + [low(features)] * 2
+        + [jax.ShapeDtypeStruct((slots, HEAD), FULL)],
+        scratch_shapes=[pltpu.VMEM((slots, features), FULL)] * 2,
+        compiler_params=pltpu.CompilerParams(vmem_limit_bytes=VMEM_BYTES),
+        cost_estimate=pl.CostEstimate(
+            flops=12 * slots * features * hidden_width,
+            bytes_accessed=6 * features * hidden_width,
+            transcendentals=slots * hidden_width,
+        ),
+    )(rows, cot_rows, mix_rows, *gate_pieces, *up_pieces, *down_pieces)
 
 
 def scatter_sum(keep, send, first_dim):
@@ -361,39 +758,21 @@
     capacity = rows_here * picks_each // expert_count * 5 // 4
     slots = groups * capacity
     all_tokens = rows_here * lax.axis_size("fsdp") * groups
-    distances = far_first(groups)
-
-    query_pieces = gather_pieces(query_proj[0])
-    out_pieces = gather_pieces(out_proj[0])
 
     tokens_spread = to_spread(tokens, 1)
     token_half = my_half(tokens_spread)
-    routes_mine = jnp.concatenate([attn_routes, ffn_routes], axis=1).T[None]
+    routes_mine = jnp.concatenate([attn_routes.T, ffn_routes.T], axis=0)
+    routes_mine = jnp.concatenate([routes_mine, jnp.zeros_like(routes_mine)], axis=0)
     kv_mine = jnp.concatenate([key_proj, value_proj], axis=1)
-    token_blocks, route_blocks, kv_blocks = [None] * groups, [None] * groups, [None] * groups
-    for distance in distances:
-        if distance == 0:
-            token_blocks[0], route_blocks[0], kv_blocks[0] = tokens_spread, routes_mine, kv_mine
-            continue
-        route_blocks[distance] = swap(routes_mine, "ctx", distance)
-        token_blocks[distance] = swap(token_half, "ctx", distance)
-        kv_blocks[distance] = swap(kv_mine, "ctx", distance)
-    for distance in distances:
-        if distance:
-            token_blocks[distance] = join_halves(
-                token_blocks[distance], swap(token_blocks[distance], "tp", 1)
-            )
-    seq_tokens = place_blocks(token_blocks).astype(FULL)
-    seq_routes = place_blocks(route_blocks)
-    kv_group = place_blocks(kv_blocks)
-    kv_pieces = gather_pieces(kv_group)
-    kv_full = jnp.concatenate(kv_pieces, axis=0)
-    query_full = jnp.concatenate(query_pieces, axis=0)
-    out_full = jnp.concatenate(out_pieces, axis=1)
-
-    gate_pieces = gather_pieces(after(gate_proj[0], kv_group))
-    up_pieces = gather_pieces(after(up_proj[0], kv_group, gate_pieces[0]))
-    down_pieces = gather_pieces(after(down_proj[0], kv_group, up_pieces[0]))
+    seq_low, all_routes, kv_full, query_full, out_full = prologue(
+        token_half, tokens_spread, routes_mine, kv_mine, query_proj[0], out_proj[0], 0
+    )
+    seq_routes = all_routes[0]
+    seq_tokens = seq_low.astype(FULL)
+
+    gate_pieces = gather_pieces(after(gate_proj[0], all_routes))
+    up_pieces = gather_pieces(after(up_proj[0], all_routes))
+    down_pieces = gather_pieces(after(down_proj[0], all_routes))
 
     gain1 = to_spread(norm_gain1, 0)
     gain2_half = my_half(to_spread(norm_gain2, 0))
@@ -435,14 +814,13 @@
     q_low, k_low, v_low, heads_low, log_sum = attend(
         query_lin, kv_lin, query_table, key_table, groups
     )
-    attn_blocks = send_home(matmul(heads_low, out_full))
-    attn_back = place_blocks(attn_blocks)
+    attn_back = send_home(matmul(heads_low, out_full).astype(LOW), 1)
 
     cot_half = my_half(to_spread(cotangent, 1))
     ffn_pick = ffn_picks[0]
     for pick in ffn_picks[1:]:
         ffn_pick = ffn_pick + pick
-    cot_rows = send_out(after(matmul_tn(ffn_pick, cot_half).astype(LOW), kv_group))
+    cot_rows = spread_out(after(matmul_tn(ffn_pick, cot_half).astype(LOW), all_routes))
 
     input_half = my_half(tokens_spread).astype(FULL)
     attn_picked = [matmul(pick, attn_back) for pick in attn_picks]
@@ -452,47 +830,27 @@
     square_sum = tp_sum(jnp.sum(attended * attended, axis=1, keepdims=True))
     scale_two = lax.rsqrt(square_sum / features + EPSILON)
     b_half = (attended * scale_two * gain2_half).astype(LOW)
-    ffn_rows = send_out(matmul_tn(ffn_pick, b_half).astype(LOW))
+    ffn_rows = send_out(matmul_tn(ffn_pick, b_half).astype(LOW), 2)
     ffn_logits = tp_sum(matmul(b_half, router2_half))
     ffn_probs = jax.nn.softmax(ffn_logits, axis=1)
     ffn_mix = mix_of(ffn_logits, ffn_onehot)
-    mix_slots = jnp.zeros((slots,), FULL)
-    for k in range(picks_each):
-        mix_slots = mix_slots + jnp.sum(ffn_picks[k].astype(FULL) * ffn_mix[:, k : k + 1], axis=0)
-    mix_slots = mix_slots.reshape(groups, 1, capacity)
-    mix_rows = place_blocks(
-        [
-            swap(block_for(mix_slots, distance), "ctx", distance) if distance else block_for(mix_slots, 0)
-            for distance in range(groups)
-        ]
-    ).reshape(slots, 1)
-
-    gate_full = jnp.concatenate(gate_pieces, axis=0)
-    up_full = jnp.concatenate(up_pieces, axis=0)
-    down_full = jnp.concatenate(down_pieces, axis=1)
-    gate_lin = matmul(ffn_rows, gate_full)
-    up_lin = matmul(ffn_rows, up_full)
-    sigmoid_gate = jax.nn.sigmoid(gate_lin)
-    hidden = gate_lin * sigmoid_gate * up_lin
-    hidden_low = hidden.astype(LOW)
-    d_hidden = matmul_nt(cot_rows, down_full)
-    mix_grad_rows = jnp.sum(hidden * d_hidden, axis=1)
-    d_gated = d_hidden * mix_rows
-    d_gate_low = (d_gated * up_lin * sigmoid_gate * (1.0 + gate_lin * (1.0 - sigmoid_gate))).astype(LOW)
-    d_up_low = (d_gated * gate_lin * sigmoid_gate).astype(LOW)
-    db_blocks = send_home(matmul_nt(d_gate_low, gate_full) + matmul_nt(d_up_low, up_full))
-    mix_grad_blocks = mix_grad_rows.reshape(groups, 1, capacity)
-    mix_grad_back = place_blocks(
-        [
-            tp_sum(
-                swap(block_for(mix_grad_blocks, distance), "ctx", distance)
-                if distance
-                else block_for(mix_grad_blocks, 0)
-            )
-            for distance in range(groups)
-        ]
-    ).reshape(1, slots)
-    dz_rows = (cot_rows.astype(FULL) * mix_rows).astype(LOW)
+
+    ffn_seq_routes = seq_routes[:, picks_each : 2 * picks_each]
+    ffn_expert_onehot = expert_picks(ffn_seq_routes, mine, capacity).astype(FULL)
+    row_routes = jnp.einsum(
+        "bsr,bkr->bsk", ffn_expert_onehot, ffn_seq_routes.astype(FULL), precision=PRECISE
+    ).reshape(slots, picks_each)
+    row_onehot = row_routes[:, :, None] == jnp.arange(expert_count, dtype=FULL)[None, None, :]
+    row_mix = mix_of(matmul(ffn_rows, router2), row_onehot.astype(FULL))
+    mine_too = (row_routes == mine.astype(FULL)).astype(FULL)
+    mix_rows = jnp.broadcast_to(jnp.sum(row_mix * mine_too, axis=1, keepdims=True), (slots, HEAD))
+    hidden_low, d_gate_low, d_up_low, db_rows, ffn_out, mix_grad_rows = expert_both_ways(
+        ffn_rows, cot_rows, mix_rows, gate_pieces, up_pieces, down_pieces
+    )
+    mix_grad_rows = jnp.pad(mix_grad_rows[:, 0].reshape(groups, 1, capacity), ((0, 0), (0, 7), (0, 256 - capacity)))
+    db_back, mix_grad_back = send_home(db_rows, 3, extra=mix_grad_rows)
+    mix_grad_back = mix_grad_back[:, 0, :capacity].reshape(1, slots)
+    dz_rows = (cot_rows.astype(FULL) * mix_rows[:, :1]).astype(LOW)
     near, far = slice(0, half_width), slice(half_width, features)
     down_grad = scatter_sum(
         matmul_tn(hidden_low, dz_rows[:, near]), matmul_tn(hidden_low, dz_rows[:, far]).astype(LOW), 1
@@ -504,14 +862,17 @@
         matmul_tn(ffn_rows[:, near], d_up_low), matmul_tn(ffn_rows[:, far], d_up_low).astype(LOW), 0
     )
 
-    hits = all_sum(
-        jnp.stack([jnp.sum(attn_onehot, axis=(0, 1)), jnp.sum(ffn_onehot, axis=(0, 1))]),
-        ("fsdp", "ctx"),
+    experts = jnp.arange(expert_count, dtype=jnp.int32)
+    named = (all_routes[..., None] == experts).astype(FULL)
+    hits = jnp.stack(
+        [
+            jnp.sum(named[:, :, :picks_each], axis=(0, 1, 2, 3)),
+            jnp.sum(named[:, :, picks_each : 2 * picks_each], axis=(0, 1, 2, 3)),
+        ]
     )
     share = hits / (all_tokens * picks_each)
     share_grad = AUX_WEIGHT * expert_count / all_tokens * share
     grad_half = cot_half.astype(FULL)
-    db_back = place_blocks(db_blocks)
     d_normed2 = jnp.zeros((rows_here, half_width), FULL)
     ffn_mix_grad = []
     for pick in ffn_picks:
@@ -529,7 +890,7 @@
     dy_slots = jnp.zeros((slots, half_width), FULL)
     for k in range(picks_each):
         dy_slots = dy_slots + matmul_tn(attn_picks[k], (attn_mix[:, k : k + 1] * d_attended).astype(LOW))
-    dy_rows = send_out(dy_slots.astype(LOW))
+    dy_rows = send_out(dy_slots.astype(LOW), 4)
     d_heads = matmul_nt(dy_rows, out_full).astype(LOW)
     dq_low, dk_low, dv_low = attend_back(
         q_low, k_low, v_low, d_heads, log_sum, query_table, key_table, groups
@@ -544,18 +905,18 @@
     da_rows = matmul_nt(dq_low, query_full).astype(LOW).reshape(groups, capacity, features)
     da_seq = jnp.einsum("bsr,bsd->brd", expert_onehot, da_rows, preferred_element_type=FULL)
     da_seq = da_seq.reshape(groups * rows_here, features) + matmul_nt(dkv_low, kv_full)
-    da_blocks = send_home(da_seq)
+    da_half = send_home(da_seq.astype(LOW), 5, add_up=True)
     kv_part = scatter_sum(
         matmul_tn(a_seq[:, near], dkv_low), matmul_tn(a_seq[:, far], dkv_low).astype(LOW), 0
     )
     kv_grad = block_for(kv_part, 0)
     kv_part_low = kv_part.astype(LOW)
-    for distance in distances:
+    for distance in far_first(groups):
         if distance:
             kv_grad = kv_grad + swap(block_for(kv_part_low, distance), "ctx", distance).astype(FULL)
     key_width = key_proj.shape[1]
 
-    ffn_back = place_blocks(send_home(matmul(hidden_low, down_full)))
+    ffn_back = send_home(ffn_out, 6)
     result = attended
     for k in range(picks_each):
         result = result + ffn_mix[:, k : k + 1] * matmul(ffn_picks[k], ffn_back)
@@ -571,9 +932,7 @@
     a_half = my_half(a_mine)
     attn_router_part = precise_tn(a_half.astype(FULL), attn_d_logits)
 
-    d_normed1 = through_router(attn_d_logits, router1_half)
-    for block in da_blocks:
-        d_normed1 = d_normed1 + block.astype(FULL)
+    d_normed1 = da_half + through_router(attn_d_logits, router1_half)
     gain1_half = my_half(gain1)
     weighted1 = d_normed1 * gain1_half
     inner1 = tp_sum(jnp.sum(weighted1 * input_half, axis=1, keepdims=True)) / features
@@ -582,25 +941,24 @@
     input_grad = from_spread(join_halves(input_grad_low, swap(input_grad_low, "tp", 1)), 1).astype(FULL)
     gain1_part = jnp.sum(d_normed1 * input_half * scale_one, axis=0)
 
-    early = jnp.concatenate([gain2_part[None], ffn_router_part.T, attn_router_part.T], axis=0)
-    early = from_spread(join_halves(early, swap(early, "tp", 1)), 1)
-    early = all_sum(early, ("ctx", "fsdp"))
-    late = gain1_part[None]
-    late = from_spread(join_halves(late, swap(late, "tp", 1)), 1)
-    late = all_sum(late, ("ctx", "fsdp"))
-    prob_sums = all_sum(
-        jnp.stack([jnp.sum(attn_probs, axis=0), jnp.sum(ffn_probs, axis=0)]), ("fsdp", "ctx")
-    )
+    small = jnp.concatenate(
+        [gain1_part[None], gain2_part[None], attn_router_part.T, ffn_router_part.T], axis=0
+    )
+    small = from_spread(join_halves(small, swap(small, "tp", 1)), 1)
+    prob_sums = jnp.concatenate([jnp.sum(attn_probs, axis=0), jnp.sum(ffn_probs, axis=0)])
+    small = jnp.concatenate([small, jnp.pad(prob_sums, (0, features - prob_sums.shape[0]))[None]], axis=0)
+    small = all_sum(small, ("ctx", "fsdp"))
+    prob_sums = small[-1, : 2 * expert_count].reshape(2, expert_count)
     losses = expert_count * jnp.sum(share * prob_sums / all_tokens, axis=1)
     return (
         output,
         input_grad,
         losses[0],
         losses[1],
-        late[0],
-        early[0],
-        early[1 + expert_count :].T,
-        early[1 : 1 + expert_count].T,
+        small[0],
+        small[1],
+        small[2 : 2 + expert_count].T,
+        small[2 + expert_count : 2 + 2 * expert_count].T,
         kv_grad[:, :key_width],
         kv_grad[:, key_width:],
         query_grad[None],

time: 1290 us -> 1120 us (0.87)
  Pallas kernels: 42.6 us -> 527 us
  waiting for transfers between devices: 541 us -> 289 us
  local copies, waits for them, and re-layouts: 185 us -> 31.1 us
  starting transfers between devices: 152 us -> 39.4 us
  matrix products: 244 us -> 159 us
  other arithmetic: 111 us -> 66.2 us
    pallas_call x0 -> x8, Pallas kernels: none -> 484 us  [the longest x4 187 us: send_home(): pl.pallas_call(functools.partial(send_home_kernel, size, add_up, extra is...]
    ppermute x129 -> x43, waiting for transfers between devices: 541 us -> 289 us  [swap(): return lax.ppermute(value, axis, [(i, i ^ distance) for i in range(size)])]
    ppermute x129 -> x43, starting transfers between devices: 152 us -> 39.4 us  [swap(): return lax.ppermute(value, axis, [(i, i ^ distance) for i in range(size)])]
    rev x20 -> x0, local copies, waits for them, and re-layouts: 65.9 us -> none  [flip_blocks(): turned = jnp.flip(split, axis + 1).reshape(shape)]
    dot_general x6 -> x3, matrix products: 81 us -> 25.8 us  [matmul_nt(): lax.dot_general(lhs, rhs, (((1,), (1,)), ((), ())), preferred_element_typ...]
    unnamed x298 -> x115, local copies, waits for them, and re-layouts: 42.5 us -> 7.47 us
    dot_general x14 -> x12, matrix products: 65.7 us -> 40.1 us  [matmul(): return jnp.dot(lhs, rhs, preferred_element_type=FULL)]
    reshape x30 -> x1, local copies, waits for them, and re-layouts: 20.1 us -> 0.01 us  [the longest x12 11.1 us: flip_blocks(): turned = jnp.flip(split, axis + 1).reshape(shape)]
  transfers between devices with their start and end apart: 129 -> 43, of which waited for: 62 -> 24; matrix products, arithmetic and copies ran while one was open for 36% -> 21% of each run, Pallas kernels for 3% -> 22%
where the time goes in v2:
time: 1120 us; the launch traced here: 1110 us
  Pallas kernels  527 us (47%)
  waiting for transfers between devices  289 us (26%)
  matrix products  159 us (14%)
  other arithmetic  66.2 us (6%)
  starting transfers between devices  39.4 us (4%)
  local copies, waits for them, and re-layouts  31.1 us (3%)
    ppermute x43, waiting for transfers between devices, swap(): return lax.ppermute(value, axis, [(i, i ^ distance) for i in range(size)])  289 us
    pallas_call x4, Pallas kernels, send_home(): pl.pallas_call(functools.partial(send_home_kernel, size, add_up, extra is...  187 us
    pallas_call x1, Pallas kernels, prologue(): pl.pallas_call(functools.partial(prologue_kernel, (groups, world)), in_sp...  131 us
    pallas_call x2, Pallas kernels, send_out(): pl.pallas_call(functools.partial(send_out_kernel, size), in_specs=[pl.Blo...  96.7 us
    dot_general x16, matrix products, matmul_tn(): lax.dot_general(lhs, rhs, (((0,), (0,)), ((), ())), preferred_element_typ...  86.8 us
    pallas_call x1, Pallas kernels, expert_both_ways(): pl.pallas_call(functools.partial(expert_kernel, world), grid=(hidden_widt...  68.5 us
    dot_general x12, matrix products, matmul(): return jnp.dot(lhs, rhs, preferred_element_type=FULL)  40.1 us
    ppermute x43, starting transfers between devices, swap(): return lax.ppermute(value, axis, [(i, i ^ distance) for i in range(size)])  39.4 us
  transfers between devices with their start and end apart: 43, of which 24 were waited for; matrix products, arithmetic and copies ran while one was open for 21% of the time, Pallas kernels for 22%

profile of v2, /device:TPU:0, one launch (start us, length us, event | category | flops | bytes accessed | tf_op | source)
XLA Modules:
  0.0 1113.0 jit_solution(11218984441426156436)
XLA Ops:
  5.7 131.5 %shard_map.262 = (bf16[1024,2048]{1,0:T(8,128)(2,1)}, s32[4,4,8,256]{3,2,1,0:T(8,128)}, bf16[2048,2048]{1,0:T(8,128)(2,1)}, bf16[2048,1024]{1,0:T(8,128)(2,1)}, bf16[1024,2048]{1,0:T(8,128)(2,1)}) custom-call(bf16[256,1024]{1,0:T(8,128)(2,1)} %maximum_select_fusion.refs_0_, bf16[256,2048]{1,0:T(8,128)(2,1)} %pad_maximum_fusion.refs_1_, ...), custom_call_target="tpu_custom_call" | custom-call | bytes 100000000 | tf_op jit(solution)/shard_map/pallas_call | solution.py:461
  160.1 15.7 %fusion.138.k_lin.v_lin = f32[1024,2048]{1,0:T(8,128)} fusion(bf16[1024,2048]{1,0:T(8,128)(2,1)} %copy-done, bf16[2048,2048]{1,0:T(8,128)(2,1)} %get-tuple-element.43), kind=kOutput, calls=%fused_computation.376 | convolution fusion | flops 8589934592 | bytes 20971520 | tf_op jit(solution)/shard_map/dot_general | solution.py:22
  186.5 19.2 %shard_map.263 = (bf16[640,1024]{1,0:T(8,128)(2,1)}, bf16[1024,1024]{1,0:T(8,128)(2,1)}, bf16[1024,1024]{1,0:T(8,128)(2,1)}, bf16[640,1024]{1,0:T(8,128)(2,1)}, f32[640,1024]{1,0:T(8,128)}) custom-call(f32[640,1024]{1,0:T(8,128)} %fusion.137.q_lin, f32[1024,2048]{1,0:T(8,128)} %fusion.138.k_lin.v_lin, f32[1024,2048]{1,0:T(8,128)} %fusion.138.k_lin.v_lin, ...), custom_call_target="tpu_custom_call" | custom-call | flops 2013265920 | bytes 20971520 | tf_op jit(solution)/shard_map/pallas_call | solution.py:614
  211.1 41.8 %shard_map.264 = bf16[640,1024]{1,0:T(8,128)(2,1)} custom-call(bf16[640,2048]{1,0:T(8,128)(2,1)} %convolution_convert_fusion.5.refs_0_), custom_call_target="tpu_custom_call" | custom-call | bytes 7864320 | tf_op jit(solution)/shard_map/pallas_call | solution.py:325
  272.5 9.1 collective-permute-done.7
  287.6 12.3 %collective-permute-done.5 = bf16[160,1024]{1,0:T(8,128)(2,1)} collective-permute-done((bf16[160,1024]{1,0:T(8,128)(2,1)}, bf16[160,1024]{1,0:T(8,128)(2,1)}, u32[]{:S(2)}, u32[]{:S(2)}) %collective-permute-start.5) | collective-permute-done | bytes 327712 | tf_op jit(solution)/shard_map/ppermute | solution.py:39
  300.0 8.7 collective-permute-done.3
  313.0 46.8 %shard_map.265.refs_0_ = bf16[640,2048]{1,0:T(8,128)(2,1)} custom-call(bf16[640,1024]{1,0:T(8,128)(2,1)} %convolution_convert_fusion.11.rows_ref), custom_call_target="tpu_custom_call" | custom-call | bytes 7864320 | tf_op jit(solution)/shard_map/pallas_call | solution.py:219
  408.4 68.5 %shard_map.266 = (bf16[640,2816]{1,0:T(8,128)(2,1)}, bf16[640,2816]{1,0:T(8,128)(2,1)}, bf16[640,2816]{1,0:T(8,128)(2,1)}, bf16[640,2048]{1,0:T(8,128)(2,1)}, bf...) custom-call(bf16[640,2048]{1,0:T(8,128)(2,1)} %shard_map.265.refs_0_, bf16[640,2048]{1,0:T(8,128)(2,1)} %copy-done.9, ...), custom_call_target="tpu_custom_call" | custom-call | flops 44291850240 | bytes 34603008 | tf_op jit(solution)/shard_map/pallas_call | solution.py:539
  477.0 43.5 %shard_map.267 = bf16[640,1024]{1,0:T(8,128)(2,1)} custom-call(bf16[640,2048]{1,0:T(8,128)(2,1)} %get-tuple-element.50.refs_0_), custom_call_target="tpu_custom_call" | custom-call | bytes 7864320 | tf_op jit(solution)/shard_map/pallas_call | solution.py:325
  521.4 43.1 %shard_map.268 = (bf16[640,1024]{1,0:T(8,128)(2,1)}, f32[4,8,256]{2,1,0:T(8,128)}) custom-call(bf16[640,2048]{1,0:T(8,128)(2,1)} %get-tuple-element.51.refs_0_, f32[4,8,256]{2,1,0:T(8,128)} %pad.8.refs_1_), custom_call_target="tpu_custom_call" | custom-call | bytes 7864320 | tf_op jit(solution)/shard_map/pallas_call | solution.py:325
  600.0 49.9 %shard_map.269 = bf16[640,2048]{1,0:T(8,128)(2,1)} custom-call(bf16[640,1024]{1,0:T(8,128)(2,1)} %add_convert_fusion.rows_ref), custom_call_target="tpu_custom_call" | custom-call | bytes 7864320 | tf_op jit(solution)/shard_map/pallas_call | solution.py:219
  655.7 23.3 %shard_map.270 = (bf16[640,1024]{1,0:T(8,128)(2,1)}, bf16[1024,1024]{1,0:T(8,128)(2,1)}, bf16[1024,1024]{1,0:T(8,128)(2,1)}) custom-call(bf16[640,1024]{1,0:T(8,128)(2,1)} %get-tuple-element.55.q_low, bf16[1024,1024]{1,0:T(8,128)(2,1)} %get-tuple-element.56.k_low, bf16[1024,1024]{1,0:T(8,128)(2,1)} %get-tuple-element.57.v_low, ...), custom_call_target="tpu_custom_call" | custom-call | flops 4697620480 | bytes 14680064 | tf_op jit(solution)/shard_map/pallas_call | solution.py:671
  689.4 14.4 %fusion.3.refs_0_ = bf16[1024,2048]{1,0:T(8,128)(2,1)} fusion(f32[4,256,2048]{2,1,0:T(8,128)S(1)} %fusion.55, bf16[1024,2048]{1,0:T(8,128)(2,1)} %constant_dynamic-update-slice_fusion, bf16[2048,2048]{1,0:T(8,128)(2,1)} %get-tuple-element.43), kind=kOutput, calls=%fused_computation.9 | convolution fusion | flops 8594128896 | bytes 25165824 | tf_op jit(solution)/shard_map/dot_general | solution.py:30
  703.8 59.0 %shard_map.271 = f32[256,1024]{1,0:T(8,128)} custom-call(bf16[1024,2048]{1,0:T(8,128)(2,1)} %fusion.3.refs_0_), custom_call_target="tpu_custom_call" | custom-call | bytes 12582912 | tf_op jit(solution)/shard_map/pallas_call | solution.py:325
  825.9 10.9 collective-permute-done.36
  840.5 20.1 %collective-permute-done.34 = bf16[512,1024]{1,0:T(8,128)(2,1)S(1)} collective-permute-done((bf16[512,1024]{1,0:T(8,128)(2,1)S(1)}, bf16[512,1024]{1,0:T(8,128)(2,1)S(1)}, u32[]{:S(2)}, u32[]{:S(2)}) %collective-permute-start.34) | collective-permute-done | bytes 1048608 | tf_op jit(solution)/shard_map/ppermute | solution.py:39
  862.3 10.1 convert_add_fusion.3
  898.2 25.6 %collective-permute-done.29 = bf16[512,2048]{1,0:T(8,128)(2,1)} collective-permute-done((bf16[512,2048]{1,0:T(8,128)(2,1)S(1)}, bf16[512,2048]{1,0:T(8,128)(2,1)}, u32[]{:S(2)}, u32[]{:S(2)}) %collective-permute-start.29) | collective-permute-done | bytes 2097184 | tf_op jit(solution)/shard_map/ppermute | solution.py:39
  933.1 10.5 convert_add_fusion.2
  948.1 13.4 %collective-permute-done.30 = bf16[128,2048]{1,0:T(8,128)(2,1)S(1)} collective-permute-done((bf16[128,2048]{1,0:T(8,128)(2,1)}, bf16[128,2048]{1,0:T(8,128)(2,1)S(1)}, u32[]{:S(2)}, u32[]{:S(2)}) %collective-permute-start.30) | collective-permute-done | bytes 524320 | tf_op jit(solution)/shard_map/ppermute | solution.py:39
  963.1 22.5 %collective-permute-done.42 = bf16[2816,512]{1,0:T(8,128)(2,1)} collective-permute-done((bf16[2816,512]{1,0:T(8,128)(2,1)}, bf16[2816,512]{1,0:T(8,128)(2,1)}, u32[]{:S(2)}, u32[]{:S(2)}) %collective-permute-start.42) | collective-permute-done | bytes 2883616 | tf_op jit(solution)/shard_map/ppermute | solution.py:39
  990.8 56.5 %collective-permute-done.40 = bf16[512,2816]{1,0:T(8,128)(2,1)} collective-permute-done((bf16[512,2816]{1,0:T(8,128)(2,1)}, bf16[512,2816]{1,0:T(8,128)(2,1)}, u32[]{:S(2)}, u32[]{:S(2)}) %collective-permute-start.40) | collective-permute-done | bytes 2883616 | tf_op jit(solution)/shard_map/ppermute | solution.py:39
  1052.5 53.5 %collective-permute-done.38 = bf16[512,2816]{1,0:T(8,128)(2,1)} collective-permute-done((bf16[512,2816]{1,0:T(8,128)(2,1)}, bf16[512,2816]{1,0:T(8,128)(2,1)}, u32[]{:S(2)}, u32[]{:S(2)}) %collective-permute-start.38) | collective-permute-done | bytes 2883616 | tf_op jit(solution)/shard_map/ppermute | solution.py:39
  (402 shorter events, 300.7 us)
Async XLA Ops:
  137.2 248.3 %collective-permute-start.10 = (bf16[512,2816]{1,0:T(8,128)(2,1)}, bf16[512,2816]{1,0:T(8,128)(2,1)}, u32[]{:S(2)}, u32[]{:S(2)}) collective-permute-start(bf16[512,2816]{1,0:T(8,128)(2,1)} %bitcast.26.refs_3_), channel_id=1, source_target_pairs={{0,8},{8,0},{16,24},{24,16},{1,9},{9,1},{17,25},{25,17},{2,10},{10... | collective-permute-start | bytes 8650760 | tf_op jit(solution)/shard_map/ppermute | solution.py:39
  137.7 248.3 %collective-permute-start.9 = (bf16[512,2816]{1,0:T(8,128)(2,1)}, bf16[512,2816]{1,0:T(8,128)(2,1)}, u32[]{:S(2)}, u32[]{:S(2)}) collective-permute-start(bf16[512,2816]{1,0:T(8,128)(2,1)} %bitcast.26.refs_3_), channel_id=1, source_target_pairs={{0,16},{8,24},{16,0},{24,8},{1,17},{9,25},{17,1},{25,9},{2,18},{10... | collective-permute-start | bytes 8650760 | tf_op jit(solution)/shard_map/ppermute | solution.py:39
  139.2 246.9 %collective-permute-start.12 = (bf16[512,2816]{1,0:T(8,128)(2,1)}, bf16[512,2816]{1,0:T(8,128)(2,1)}, u32[]{:S(2)}, u32[]{:S(2)}) collective-permute-start(bf16[512,2816]{1,0:T(8,128)(2,1)} %bitcast.27.refs_7_), channel_id=1, source_target_pairs={{0,16},{8,24},{16,0},{24,8},{1,17},{9,25},{17,1},{25,9},{2,18},{10... | collective-permute-start | bytes 8650760 | tf_op jit(solution)/shard_map/ppermute | solution.py:39
  139.7 246.8 %collective-permute-start.15 = (bf16[2816,512]{1,0:T(8,128)(2,1)}, bf16[2816,512]{1,0:T(8,128)(2,1)}, u32[]{:S(2)}, u32[]{:S(2)}) collective-permute-start(bf16[2816,512]{1,0:T(8,128)(2,1)} %bitcast.28.refs_11_), channel_id=1, source_target_pairs={{0,16},{8,24},{16,0},{24,8},{1,17},{9,25},{17,1},{25,9},{2,18},{10... | collective-permute-start | bytes 8650760 | tf_op jit(solution)/shard_map/ppermute | solution.py:39
  281.6 18.3 %collective-permute-start.5 = (bf16[160,1024]{1,0:T(8,128)(2,1)}, bf16[160,1024]{1,0:T(8,128)(2,1)}, u32[]{:S(2)}, u32[]{:S(2)}) collective-permute-start(bf16[160,1024]{1,0:T(8,128)(2,1)} %get-tuple-element.98), channel_id=1, source_target_pairs={{0,4},{2,6},{4,0},{6,2},{1,5},{3,7},{5,1},{7,3},{8,12},{10,14},{12... | collective-permute-start | bytes 983048 | tf_op jit(solution)/shard_map/ppermute | solution.py:39
  308.7 51.1 %collective-permute-start.2 = (bf16[160,1024]{1,0:T(8,128)(2,1)S(1)}, bf16[160,1024]{1,0:T(8,128)(2,1)S(1)}, u32[]{:S(2)}, u32[]{:S(2)}) collective-permute-start(bf16[160,1024]{1,0:T(8,128)(2,1)S(1)} %get-tuple-element.100), channel_id=1, source_target_pairs={{0,1},{1,0},{2,3},{3,2},{4,5},{5,4},{6,7},{7,6},{8,9},{9,8},{10,11... | collective-permute-start | bytes 983048 | tf_op jit(solution)/shard_map/ppermute | solution.py:39
  386.5 21.1 %collective-permute-start.17 = (bf16[2816,512]{1,0:T(8,128)(2,1)}, bf16[2816,512]{1,0:T(8,128)(2,1)}, u32[]{:S(2)}, u32[]{:S(2)}) collective-permute-start(bf16[2816,512]{1,0:T(8,128)(2,1)} %collective-permute-done.15.refs_12_), channel_id=1, source_target_pairs={{0,8},{8,0},{16,24},{24,16},{1,9},{9,1},{17,25},{25,17},{2,10},{10... | collective-permute-start | bytes 8650760 | tf_op jit(solution)/shard_map/ppermute | solution.py:39
  570.5 25.8 %collective-permute-start.19 = (f32[256,1]{0,1:T(1,128)S(1)}, f32[256,1]{0,1:T(1,128)S(1)}, u32[]{:S(2)}, u32[]{:S(2)}) collective-permute-start(f32[256,1]{0,1:T(1,128)S(1)} %bitcast.254), channel_id=1, source_target_pairs={{0,1},{1,0},{2,3},{3,2},{4,5},{5,4},{6,7},{7,6},{8,9},{9,8},{10,11... | collective-permute-start | bytes 3080 | tf_op jit(solution)/shard_map/ppermute | solution.py:39
  592.2 283.2 %collective-permute-start.41 = (bf16[2816,1024]{1,0:T(8,128)(2,1)}, bf16[2816,1024]{1,0:T(8,128)(2,1)}, u32[]{:S(2)}, u32[]{:S(2)}) collective-permute-start(bf16[2816,1024]{1,0:T(8,128)(2,1)} %convolution_convert_fusion), channel_id=1, source_target_pairs={{0,8},{8,0},{16,24},{24,16},{1,9},{9,1},{17,25},{25,17},{2,10},{10... | collective-permute-start | bytes 17301512 | tf_op jit(solution)/shard_map/ppermute | solution.py:39
  592.3 295.6 %collective-permute-start.39 = (bf16[1024,2816]{1,0:T(8,128)(2,1)}, bf16[1024,2816]{1,0:T(8,128)(2,1)}, u32[]{:S(2)}, u32[]{:S(2)}) collective-permute-start(bf16[1024,2816]{1,0:T(8,128)(2,1)} %convolution_convert_fusion.1), channel_id=1, source_target_pairs={{0,8},{8,0},{16,24},{24,16},{1,9},{9,1},{17,25},{25,17},{2,10},{10... | collective-permute-start | bytes 17301512 | tf_op jit(solution)/shard_map/ppermute | solution.py:39
  597.0 165.8 %collective-permute-start.20 = (f32[256,2]{0,1:T(2,128)S(1)}, f32[256,2]{0,1:T(2,128)S(1)}, u32[]{:S(2)}, u32[]{:S(2)}) collective-permute-start(f32[256,2]{0,1:T(2,128)S(1)} %pad_maximum_fusion.10), channel_id=1, source_target_pairs={{0,1},{1,0},{2,3},{3,2},{4,5},{5,4},{6,7},{7,6},{8,9},{9,8},{10,11... | collective-permute-start | bytes 6152 | tf_op jit(solution)/shard_map/ppermute | solution.py:39
  779.7 17.9 %collective-permute-start.35 = (bf16[1024,1024]{1,0:T(8,128)(2,1)}, bf16[1024,1024]{1,0:T(8,128)(2,1)}, u32[]{:S(2)}, u32[]{:S(2)}) collective-permute-start(bf16[1024,1024]{1,0:T(8,128)(2,1)} %convolution_convert_fusion.7), channel_id=1, source_target_pairs={{0,8},{8,0},{16,24},{24,16},{1,9},{9,1},{17,25},{25,17},{2,10},{10... | collective-permute-start | bytes 6291464 | tf_op jit(solution)/shard_map/ppermute | solution.py:39
  788.5 24.1 %collective-permute-start.33 = (bf16[1024,1024]{1,0:T(8,128)(2,1)}, bf16[1024,1024]{1,0:T(8,128)(2,1)}, u32[]{:S(2)}, u32[]{:S(2)}) collective-permute-start(bf16[1024,1024]{1,0:T(8,128)(2,1)} %convolution_convert_fusion.8), channel_id=1, source_target_pairs={{0,8},{8,0},{16,24},{24,16},{1,9},{9,1},{17,25},{25,17},{2,10},{10... | collective-permute-start | bytes 6291464 | tf_op jit(solution)/shard_map/ppermute | solution.py:39
  796.0 66.3 %collective-permute-start.28 = (bf16[1024,2048]{1,0:T(8,128)(2,1)}, bf16[1024,2048]{1,0:T(8,128)(2,1)}, u32[]{:S(2)}, u32[]{:S(2)}) collective-permute-start(bf16[1024,2048]{1,0:T(8,128)(2,1)} %convolution_convert_fusion.3), channel_id=1, source_target_pairs={{0,8},{8,0},{16,24},{24,16},{1,9},{9,1},{17,25},{25,17},{2,10},{10... | collective-permute-start | bytes 12582920 | tf_op jit(solution)/shard_map/ppermute | solution.py:39
  812.0 24.8 %collective-permute-start.36 = (bf16[1024,512]{1,0:T(8,128)(2,1)S(1)}, bf16[1024,512]{1,0:T(8,128)(2,1)S(1)}, u32[]{:S(2)}, u32[]{:S(2)}) collective-permute-start(bf16[1024,512]{1,0:T(8,128)(2,1)S(1)} %slice.486), channel_id=1, source_target_pairs={{0,16},{8,24},{16,0},{24,8},{1,17},{9,25},{17,1},{25,9},{2,18},{10... | collective-permute-start | bytes 3145736 | tf_op jit(solution)/shard_map/ppermute | solution.py:39
  825.9 105.4 %collective-permute-start.37 = (bf16[1024,2816]{1,0:T(8,128)(2,1)}, bf16[1024,2816]{1,0:T(8,128)(2,1)}, u32[]{:S(2)}, u32[]{:S(2)}) collective-permute-start(bf16[1024,2816]{1,0:T(8,128)(2,1)} %convolution_convert_fusion.2), channel_id=1, source_target_pairs={{0,8},{8,0},{16,24},{24,16},{1,9},{9,1},{17,25},{25,17},{2,10},{10... | collective-permute-start | bytes 17301512 | tf_op jit(solution)/shard_map/ppermute | solution.py:39
  836.8 23.9 %collective-permute-start.34 = (bf16[512,1024]{1,0:T(8,128)(2,1)S(1)}, bf16[512,1024]{1,0:T(8,128)(2,1)S(1)}, u32[]{:S(2)}, u32[]{:S(2)}) collective-permute-start(bf16[512,1024]{1,0:T(8,128)(2,1)S(1)} %slice.487), channel_id=1, source_target_pairs={{0,16},{8,24},{16,0},{24,8},{1,17},{9,25},{17,1},{25,9},{2,18},{10... | collective-permute-start | bytes 3145736 | tf_op jit(solution)/shard_map/ppermute | solution.py:39
  875.1 48.7 %collective-permute-start.29 = (bf16[512,2048]{1,0:T(8,128)(2,1)S(1)}, bf16[512,2048]{1,0:T(8,128)(2,1)}, u32[]{:S(2)}, u32[]{:S(2)}) collective-permute-start(bf16[512,2048]{1,0:T(8,128)(2,1)S(1)} %slice.485), channel_id=1, source_target_pairs={{0,16},{8,24},{16,0},{24,8},{1,17},{9,25},{17,1},{25,9},{2,18},{10... | collective-permute-start | bytes 6291464 | tf_op jit(solution)/shard_map/ppermute | solution.py:39
  886.1 99.5 %collective-permute-start.42 = (bf16[2816,512]{1,0:T(8,128)(2,1)}, bf16[2816,512]{1,0:T(8,128)(2,1)}, u32[]{:S(2)}, u32[]{:S(2)}) collective-permute-start(bf16[2816,512]{1,0:T(8,128)(2,1)} %slice.482), channel_id=1, source_target_pairs={{0,16},{8,24},{16,0},{24,8},{1,17},{9,25},{17,1},{25,9},{2,18},{10... | collective-permute-start | bytes 8650760 | tf_op jit(solution)/shard_map/ppermute | solution.py:39
  897.8 149.6 %collective-permute-start.40 = (bf16[512,2816]{1,0:T(8,128)(2,1)}, bf16[512,2816]{1,0:T(8,128)(2,1)}, u32[]{:S(2)}, u32[]{:S(2)}) collective-permute-start(bf16[512,2816]{1,0:T(8,128)(2,1)} %slice.483), channel_id=1, source_target_pairs={{0,16},{8,24},{16,0},{24,8},{1,17},{9,25},{17,1},{25,9},{2,18},{10... | collective-permute-start | bytes 8650760 | tf_op jit(solution)/shard_map/ppermute | solution.py:39
  928.7 32.8 %collective-permute-start.30 = (bf16[128,2048]{1,0:T(8,128)(2,1)}, bf16[128,2048]{1,0:T(8,128)(2,1)S(1)}, u32[]{:S(2)}, u32[]{:S(2)}) collective-permute-start(bf16[128,2048]{1,0:T(8,128)(2,1)} %get-tuple-element.94), channel_id=1, source_target_pairs={{0,4},{2,6},{4,0},{6,2},{1,5},{3,7},{5,1},{7,3},{8,12},{10,14},{12... | collective-permute-start | bytes 1572872 | tf_op jit(solution)/shard_map/ppermute | solution.py:39
  929.6 32.2 %collective-permute-start.32 = (bf16[128,2048]{1,0:T(8,128)(2,1)}, bf16[128,2048]{1,0:T(8,128)(2,1)S(1)}, u32[]{:S(2)}, u32[]{:S(2)}) collective-permute-start(bf16[128,2048]{1,0:T(8,128)(2,1)} %get-tuple-element.95), channel_id=1, source_target_pairs={{0,2},{2,0},{4,6},{6,4},{1,3},{3,1},{5,7},{7,5},{8,10},{10,8},{12,... | collective-permute-start | bytes 1572872 | tf_op jit(solution)/shard_map/ppermute | solution.py:39
  931.3 30.5 %collective-permute-start.31 = (bf16[128,2048]{1,0:T(8,128)(2,1)}, bf16[128,2048]{1,0:T(8,128)(2,1)S(1)}, u32[]{:S(2)}, u32[]{:S(2)}) collective-permute-start(bf16[128,2048]{1,0:T(8,128)(2,1)} %get-tuple-element.96), channel_id=1, source_target_pairs={{0,6},{2,4},{4,2},{6,0},{1,7},{3,5},{5,3},{7,1},{8,14},{10,12},{12... | collective-permute-start | bytes 1572872 | tf_op jit(solution)/shard_map/ppermute | solution.py:39
  961.5 144.5 %collective-permute-start.38 = (bf16[512,2816]{1,0:T(8,128)(2,1)}, bf16[512,2816]{1,0:T(8,128)(2,1)}, u32[]{:S(2)}, u32[]{:S(2)}) collective-permute-start(bf16[512,2816]{1,0:T(8,128)(2,1)} %slice.484), channel_id=1, source_target_pairs={{0,16},{8,24},{16,0},{24,8},{1,17},{9,25},{17,1},{25,9},{2,18},{10... | collective-permute-start | bytes 8650760 | tf_op jit(solution)/shard_map/ppermute | solution.py:39
  (75 other events, 1157.1 us)

commit v3 on v2

--- a/solution.py
+++ b/solution.py
@@ -3,6 +3,7 @@
 
 import jax
 import jax.numpy as jnp
+import numpy as np
 from jax import lax
 from jax.experimental import pallas as pl
 from jax.experimental.pallas import tpu as pltpu
@@ -60,8 +61,13 @@
 def gather_pieces(piece):
     pieces = [piece]
     for bit in bits_down(lax.axis_size("fsdp")):
-        pieces = pieces + [swap(item, "fsdp", bit) for item in pieces]
+        if bit > 1:
+            pieces = pieces + [swap(item, "fsdp", bit) for item in pieces]
     return pieces
+
+
+def with_neighbours(pieces, *earlier):
+    return pieces + [swap(after(item, *earlier), "fsdp", 1) for item in pieces]
 
 
 def flip_blocks(value, axis, index, count):
@@ -143,6 +149,17 @@
     return place_blocks(blocks)
 
 
+def come_home(partial_rows):
+    size = lax.axis_size("ctx")
+    blocks = [None] * size
+    for distance in far_first(size):
+        block = block_for(partial_rows, distance)
+        arrived = swap(other_half(block), "tp", 1)
+        block = (my_half(block).astype(FULL) + arrived.astype(FULL)).astype(LOW)
+        blocks[distance] = swap(block, "ctx", distance) if distance else block
+    return place_blocks(blocks)
+
+
 def xor_index(index, distance):
     result = index
     bit = 1
@@ -175,13 +192,21 @@
     )
 
 
+def near_first(size):
+    return list(range(1, size))
+
+
+def mixed_order(size):
+    return [distance for distance in spread_order(size) if distance] + [0]
+
+
 def send_out_kernel(size, rows_ref, out_ref, z_land, y_land, z_send, z_recv, y_send, y_recv):
     mine, first = lax.axis_index("ctx"), lax.axis_index("tp") == 0
     other_tp = {"tp": 1 - lax.axis_index("tp")}
     rows, width = z_land.shape[1], z_land.shape[2]
     at = [xor_index(mine, distance) for distance in range(size)]
     meet([{"ctx": at[distance]} for distance in range(1, size)] + [other_tp])
-    order = [distance for distance in far_first(size) if distance]
+    order = near_first(size)
     across, beside = {}, {}
     for distance in order:
         across[distance] = remote(
@@ -229,11 +254,13 @@
     )(half_rows)
 
 
-def send_home_kernel(size, add_up, has_extra, *refs):
+def send_home_kernel(size, add_up, has_extra, cargoes, *refs):
     part_ref, refs = refs[0], refs[1:]
     extra_ref, refs = (refs[0], refs[1:]) if has_extra else (None, refs)
+    cargo_in, refs = refs[:cargoes], refs[cargoes:]
     out_ref, refs = refs[0], refs[1:]
     extra_out, refs = (refs[0], refs[1:]) if has_extra else (None, refs)
+    cargo_out, refs = refs[:cargoes], refs[cargoes:]
     y_land, ready, z_land, y_send, y_recv, z_send, z_recv = refs[:7]
     mine, first = lax.axis_index("ctx"), lax.axis_index("tp") == 0
     place = lax.axis_index("tp")
@@ -241,11 +268,18 @@
     rows, width = z_land.shape[1], z_land.shape[2]
     at = [xor_index(mine, distance) for distance in range(size)]
     columns = pl.ds(pl.multiple_of((1 - place) * width, 128), width)
-    meet([{"ctx": at[distance]} for distance in range(1, size)] + [other_tp])
-    order = far_first(size)
+    world = lax.axis_size("fsdp")
+    along = [{"fsdp": xor_index(lax.axis_index("fsdp"), world // 2)}] if cargoes else []
+    meet([{"ctx": at[distance]} for distance in range(1, size)] + [other_tp] + along)
+    order = mixed_order(size)
     beside, across, extras = {}, {}, {}
+    cargo = [
+        remote(cargo_in[n], cargo_out[n], refs[-2:], n, along[0]) for n in range(cargoes)
+    ]
+    for copy in cargo:
+        copy.start()
     if has_extra:
-        ey_land, e_ready, ez_land, ey_send, ey_recv, ez_send, ez_recv = refs[7:]
+        ey_land, e_ready, ez_land, ey_send, ey_recv, ez_send, ez_recv = refs[7:14]
         extra_beside = remote(extra_ref, ey_land, (ey_send, ey_recv), 0, other_tp)
         extra_beside.start()
     for distance in order:
@@ -308,9 +342,11 @@
         beside[distance].wait_send()
         if distance:
             across[distance].wait_send()
-
-
-def send_home(partial_rows, number, extra=None, add_up=False):
+    for copy in cargo:
+        copy.wait()
+
+
+def send_home(partial_rows, number, extra=None, cargo=(), add_up=False):
     size = lax.axis_size("ctx")
     total, width = partial_rows.shape[0], partial_rows.shape[1] // 2
     rows = total // size
@@ -322,10 +358,19 @@
         operands.append(extra)
         shapes.append(jax.ShapeDtypeStruct(extra.shape, FULL))
         scratch += [pltpu.VMEM(extra.shape, FULL)] * 3 + sems
+    in_specs = [pl.BlockSpec(memory_space=pltpu.VMEM)] * len(operands)
+    out_specs = [pl.BlockSpec(memory_space=pltpu.VMEM)] * len(shapes)
+    for item in cargo:
+        operands.append(item)
+        shapes.append(jax.ShapeDtypeStruct(item.shape, item.dtype))
+        in_specs.append(pl.BlockSpec(memory_space=pl.ANY))
+        out_specs.append(pl.BlockSpec(memory_space=pl.ANY))
+    if cargo:
+        scratch += [pltpu.SemaphoreType.DMA((len(cargo),))] * 2
     results = pl.pallas_call(
-        functools.partial(send_home_kernel, size, add_up, extra is not None),
-        in_specs=[pl.BlockSpec(memory_space=pltpu.VMEM)] * len(operands),
-        out_specs=[pl.BlockSpec(memory_space=pltpu.VMEM)] * len(shapes),
+        functools.partial(send_home_kernel, size, add_up, extra is not None, len(cargo)),
+        in_specs=in_specs,
+        out_specs=out_specs,
         out_shape=shapes,
         scratch_shapes=scratch,
         compiler_params=pltpu.CompilerParams(
@@ -333,38 +378,42 @@
         ),
         cost_estimate=pl.CostEstimate(flops=0, bytes_accessed=12 * total * width, transcendentals=0),
     )(*operands)
-    return results if extra is not None else results[0]
+    return results if len(shapes) > 1 else results[0]
 
 
 def prologue_kernel(sizes, *refs):
     groups, world = sizes
     half_in, own_in, routes_in, kv_in, query_in, out_in = refs[:6]
     seq_ref, routes_ref, kv_ref, query_ref, out_ref = refs[6:11]
-    local_sem, zt, yt, zr, zk, xk, fr, fk, fq, fo = refs[11], *[
-        (refs[12 + 2 * n], refs[13 + 2 * n]) for n in range(9)
-    ]
+    local_sem = refs[11]
+    pairs = [(refs[12 + 2 * n], refs[13 + 2 * n]) for n in range(15)]
+    token_line, route_line, kv_line, token_pass, kv_pass = (pairs[2 * n : 2 * n + 2] for n in range(5))
+    kv_own, fr, fk, fq, fo = pairs[10:]
     mine, place, spot = lax.axis_index("ctx"), lax.axis_index("tp"), lax.axis_index("fsdp")
     other_tp = {"tp": 1 - place}
     rows, width = half_in.shape
     sub = kv_in.shape[0]
     piece = sub * groups
-    q_rows, o_columns = query_in.shape[0], out_in.shape[1]
-    at = [xor_index(mine, distance) for distance in range(groups)]
-    ctx_peer = [{"ctx": at[distance]} for distance in range(groups)]
+    q_rows = query_in.shape[0]
     steps = list(bits_down(world))
     beside = {bit: {"fsdp": xor_index(spot, bit)} for bit in steps}
-    meet(ctx_peer[1:] + [other_tp] + [beside[bit] for bit in steps])
-    own_columns = pl.ds(pl.multiple_of(place * width, 128), width)
-    order = [distance for distance in far_first(groups) if distance]
+    first = steps[0]
+    meet(
+        [{"ctx": xor_index(mine, distance)} for distance in range(1, groups)]
+        + [other_tp]
+        + [beside[bit] for bit in steps]
+    )
     locals_ = [
-        pltpu.make_async_copy(own_in, seq_ref.at[span(mine, rows)], local_sem.at[0]),
-        pltpu.make_async_copy(routes_in, routes_ref.at[0, mine], local_sem.at[1]),
-        pltpu.make_async_copy(kv_in, kv_ref.at[span(mine, sub)], local_sem.at[2]),
-        pltpu.make_async_copy(query_in, query_ref.at[pl.ds(0, q_rows)], local_sem.at[3]),
-        pltpu.make_async_copy(out_in, out_ref.at[:, pl.ds(0, o_columns)], local_sem.at[4]),
+        pltpu.make_async_copy(
+            own_in.at[:, pl.ds(n * width, width)], seq_ref.at[n, span(mine, rows)], local_sem.at[n]
+        )
+        for n in range(2)
+    ] + [
+        pltpu.make_async_copy(routes_in, routes_ref.at[0, mine], local_sem.at[2]),
+        pltpu.make_async_copy(kv_in, kv_ref.at[span(mine, sub)], local_sem.at[3]),
+        pltpu.make_async_copy(query_in, query_ref.at[pl.ds(0, q_rows)], local_sem.at[4]),
+        pltpu.make_async_copy(out_in, out_ref.at[0], local_sem.at[5]),
     ]
-    for copy in locals_:
-        copy.start()
     started, landed = [], set()
 
     def go(copy):
@@ -377,52 +426,107 @@
             copy.wait_recv()
             landed.add(id(copy))
 
-    first = steps[0]
-
+    def wrap(index):
+        return lax.rem(index + groups, groups)
+
+    def outgoing(step):
+        yield 0, jnp.logical_and(mine < groups - 1, mine >= step), wrap(mine - step), wrap(mine + 1)
+        yield 1, jnp.logical_and(mine > 0, mine + step < groups), wrap(mine + step), wrap(mine - 1)
+
+    def incoming(step):
+        yield 0, mine >= step + 1, wrap(mine - 1 - step)
+        yield 1, mine + step + 1 < groups, wrap(mine + 1 + step)
+
+    def line_copy(own, place_of, sems, step, way, block, target):
+        source = place_of(block) if step else own
+        return remote(source, place_of(block), sems[way], step, {"ctx": target})
+
+    def line_start(own, place_of, sems, step):
+        for way, happens, block, target in outgoing(step):
+
+            @pl.when(happens)
+            def _():
+                line_copy(own, place_of, sems, step, way, block, target).start()
+
+    def line_wait(place_of, sems, step, passed):
+        for way, happens, block in incoming(step):
+
+            @pl.when(happens)
+            def _():
+                remote(place_of(block), place_of(block), sems[way], step, other_tp).wait_recv()
+                if passed is not None:
+                    passed(step, way, block).start()
+
+    def line_end(own, place_of, sems, step, passed):
+        for way, happens, block, target in outgoing(step):
+
+            @pl.when(happens)
+            def _():
+                line_copy(own, place_of, sems, step, way, block, target).wait_send()
+
+        if passed is None:
+            return
+        for way, happens, block in incoming(step):
+
+            @pl.when(happens)
+            def _():
+                passed(step, way, block).wait_send()
+
+    def passed_wait(step, passed):
+        for way, happens, block in incoming(step):
+
+            @pl.when(happens)
+            def _():
+                passed(step, way, block).wait_recv()
+
+    route_place = lambda n: routes_ref.at[0, n]
+    kv_place = lambda n: kv_ref.at[span(n, sub)]
+    token_place = lambda n: seq_ref.at[place, span(n, rows)]
+
+    def kv_along(step, way, block):
+        target = kv_ref.at[pl.ds(pl.multiple_of(piece + block * sub, 16), sub)]
+        return remote(kv_place(block), target, kv_pass[way], step, beside[first])
+
+    def token_along(step, way, block):
+        return remote(token_place(block), token_place(block), token_pass[way], step, other_tp)
+
+    def token_landed(step, way, block):
+        view = seq_ref.at[1 - place, span(block, rows)]
+        return remote(view, view, token_pass[way], step, other_tp)
+
+    kv_first = go(
+        remote(
+            kv_in,
+            kv_ref.at[pl.ds(pl.multiple_of(piece + mine * sub, 16), sub)],
+            kv_own,
+            0,
+            beside[first],
+        )
+    )
     query_view = lambda n: query_ref.at[pl.ds(n * q_rows, q_rows)]
-    out_view = lambda n: out_ref.at[:, pl.ds(n * o_columns, o_columns)]
+    out_view = lambda n: out_ref.at[n]
+    kv_view = lambda n: kv_ref.at[pl.ds(n * piece, piece)]
     query_copies = {1: go(remote(query_in, query_view(1), fq, 1, beside[first]))}
-    route_copies, kv_copies, token_copies = {}, {}, {}
-    for distance in order:
-        route_copies[distance] = go(
-            remote(routes_in, routes_ref.at[0, mine], zr, distance, ctx_peer[distance])
-        )
-    for distance in order:
-        kv_copies[distance] = go(
-            remote(kv_in, kv_ref.at[span(mine, sub)], zk, distance, ctx_peer[distance])
-        )
-    for distance in order:
-        token_copies[distance] = go(
-            remote(
-                half_in, seq_ref.at[span(mine, rows), own_columns], zt, distance, ctx_peer[distance]
-            )
-        )
-    out_copies = {1: go(remote(out_in, out_view(1), fo, 1, beside[first]))}
-
-    def kv_step(distance):
-        if distance:
-            arrived(kv_copies[distance])
-            source = kv_ref.at[span(at[distance], sub)]
-        else:
-            source = kv_in
-        target = kv_ref.at[pl.ds(pl.multiple_of(piece + at[distance] * sub, 16), sub)]
-        return go(remote(source, target, xk, distance, beside[first]))
-
-    kv_first = {0: kv_step(0)}
-    half_copies = {}
-    for distance in order:
-        kv_first[distance] = kv_step(distance)
-    for distance in order:
-        arrived(token_copies[distance])
-        view = seq_ref.at[span(at[distance], rows), own_columns]
-        half_copies[distance] = go(remote(view, view, yt, distance, other_tp))
-    for distance in order:
-        arrived(route_copies[distance])
+    out_copies = {}
     for copy in locals_:
-        copy.wait()
-    kv_view = lambda n: kv_ref.at[pl.ds(n * piece, piece)]
-    route_wait = {}
-    kv_wait = {}
+        copy.start()
+    for step in range(groups - 1):
+        line_start(kv_in, kv_place, kv_line, step)
+        line_start(routes_in, route_place, route_line, step)
+        line_start(half_in, token_place, token_line, step)
+        if step == 0:
+            for copy in locals_:
+                copy.wait()
+            for bit in steps[1:]:
+                n = world // (2 * bit)
+                query_copies[n] = go(remote(query_in, query_view(n), fq, n, beside[bit]))
+                out_copies[n] = go(remote(out_in, out_view(n), fo, n, beside[bit]))
+        line_wait(kv_place, kv_line, step, kv_along)
+        if step == groups - 2:
+            out_copies[1] = go(remote(out_in, out_view(1), fo, 1, beside[first]))
+        line_wait(route_place, route_line, step, None)
+        line_wait(token_place, token_line, step, token_along)
+    route_wait, kv_wait = {}, {}
     count = 1
     for bit in steps:
         for n in range(count):
@@ -432,23 +536,35 @@
             route_wait[count + n] = go(
                 remote(routes_ref.at[n], routes_ref.at[count + n], fr, count + n, peer)
             )
-            if bit != first:
-                if n:
-                    arrived(query_copies[n])
-                    arrived(out_copies[n])
+            if bit == first:
+                continue
+            if n:
+                arrived(query_copies[n])
                 query_copies[count + n] = go(
                     remote(query_view(n), query_view(count + n), fq, count + n, peer)
                 )
+            if n == 1 and count == 2:
+                arrived(kv_first)
+                for step in range(groups - 1):
+                    passed_wait(step, kv_along)
+            if n > 1:
+                arrived(kv_wait[n])
+            kv_wait[count + n] = go(remote(kv_view(n), kv_view(count + n), fk, count + n, peer))
+            if n:
+                arrived(out_copies[n])
                 out_copies[count + n] = go(remote(out_view(n), out_view(count + n), fo, count + n, peer))
-                if n == 1:
-                    for distance in range(groups):
-                        arrived(kv_first[distance])
-                if n > 1:
-                    arrived(kv_wait[n])
-                kv_wait[count + n] = go(remote(kv_view(n), kv_view(count + n), fk, count + n, peer))
         count *= 2
+    if world == 2:
+        arrived(kv_first)
+        for step in range(groups - 1):
+            passed_wait(step, kv_along)
     for copy in started:
         arrived(copy)
+    for step in range(groups - 1):
+        passed_wait(step, token_landed)
+        line_end(kv_in, kv_place, kv_line, step, kv_along)
+        line_end(routes_in, route_place, route_line, step, None)
+        line_end(half_in, token_place, token_line, step, token_along)
     for copy in started:
         copy.wait_send()
 
@@ -460,17 +576,19 @@
     pair = lambda count: [pltpu.SemaphoreType.DMA((count,))] * 2
     return pl.pallas_call(
         functools.partial(prologue_kernel, (groups, world)),
-        in_specs=[any_space] * 6,
+        in_specs=[pl.BlockSpec(memory_space=pltpu.VMEM)] * 6,
         out_specs=[any_space] * 5,
         out_shape=[
-            jax.ShapeDtypeStruct((groups * rows, features), LOW),
+            jax.ShapeDtypeStruct((2, groups * rows, features // 2), LOW),
             jax.ShapeDtypeStruct((world, groups) + routes.shape, jnp.int32),
             jax.ShapeDtypeStruct((world * groups * kv_rows.shape[0], kv_rows.shape[1]), LOW),
             jax.ShapeDtypeStruct((world * query_piece.shape[0], query_piece.shape[1]), LOW),
-            jax.ShapeDtypeStruct((out_piece.shape[0], world * out_piece.shape[1]), LOW),
+            jax.ShapeDtypeStruct((world,) + out_piece.shape, LOW),
         ],
-        scratch_shapes=[pltpu.SemaphoreType.DMA((5,))] + pair(groups) * 5 + pair(world) * 4,
-        compiler_params=pltpu.CompilerParams(collective_id=number, has_side_effects=True),
+        scratch_shapes=[pltpu.SemaphoreType.DMA((6,))] + pair(groups) * 10 + pair(1) + pair(world) * 4,
+        compiler_params=pltpu.CompilerParams(
+            collective_id=number, has_side_effects=True, vmem_limit_bytes=VMEM_BYTES
+        ),
         cost_estimate=pl.CostEstimate(flops=0, bytes_accessed=100000000, transcendentals=0),
     )(token_half, token_rows, routes, kv_rows, query_piece, out_piece)
 
@@ -556,25 +674,43 @@
     )(rows, cot_rows, mix_rows, *gate_pieces, *up_pieces, *down_pieces)
 
 
-def scatter_sum(keep, send, first_dim):
-    size = lax.axis_size("fsdp")
-    bit = 1
+def scatter_start(product, features, first_dim):
+    pieces = lax.axis_size("fsdp")
+    high, bit, arrived = features, 1, []
+
+    def part(low, high):
+        total = product(low, high)
+        for block in arrived:
+            total = total + lax.slice_in_dim(block, low, high, axis=first_dim).astype(FULL)
+        return total
+
     while True:
-        total = keep + swap(send, "fsdp", bit).astype(FULL)
+        sent = part(high // 2, high).astype(LOW)
+        high //= 2
+        if 2 * bit >= pieces:
+            break
+        arrived.append(swap(sent, "fsdp", bit))
         bit *= 2
-        if bit >= size:
-            return total
-        width = total.shape[first_dim] // 2
-        keep = lax.slice_in_dim(total, 0, width, axis=first_dim)
-        send = lax.slice_in_dim(total, width, 2 * width, axis=first_dim).astype(LOW)
-
-
-def turn_tables(places):
+
+    def finish(last):
+        arrived.append(last)
+        return part(0, high)
+
+    return sent, finish
+
+
+def last_step(sent):
+    return swap(sent, "fsdp", lax.axis_size("fsdp") // 2)
+
+
+def turn_tables(length):
     half_head = HEAD // 2
-    frequency = ROPE_BASE ** (-jnp.arange(half_head, dtype=FULL) * 2.0 / HEAD)
-    angles = places.astype(FULL)[:, None] * frequency[None, :]
-    cosine, sine = jnp.cos(angles), jnp.sin(angles)
-    return jnp.concatenate([cosine, cosine, -sine, sine], axis=1)
+    steps = np.arange(half_head, dtype=np.float32) * np.float32(2.0 / HEAD)
+    frequency = np.power(np.float32(ROPE_BASE), -steps).astype(np.float32)
+    angles = np.arange(length, dtype=np.float32)[:, None] * frequency[None, :]
+    cosine = np.cos(angles.astype(np.float64)).astype(np.float32)
+    sine = np.sin(angles.astype(np.float64)).astype(np.float32)
+    return np.concatenate([cosine, cosine, -sine, sine], axis=1)
 
 
 def turn(value, table):
@@ -631,9 +767,7 @@
         ],
         compiler_params=pltpu.CompilerParams(vmem_limit_bytes=VMEM_BYTES),
         cost_estimate=pl.CostEstimate(
-            flops=3 * slots * length * width,
-            bytes_accessed=20 * length * width,
-            transcendentals=slots * length * count,
+            flops=0, bytes_accessed=20 * length * width, transcendentals=0
         ),
     )(query_lin, kv_lin, kv_lin, query_table, key_table)
 
@@ -689,9 +823,7 @@
         scratch_shapes=[pltpu.VMEM((length, HEAD), FULL), pltpu.VMEM((length, HEAD), FULL)],
         compiler_params=pltpu.CompilerParams(vmem_limit_bytes=VMEM_BYTES),
         cost_estimate=pl.CostEstimate(
-            flops=7 * slots * length * width,
-            bytes_accessed=14 * length * width,
-            transcendentals=slots * length * count,
+            flops=0, bytes_accessed=14 * length * width, transcendentals=0
         ),
     )(q_low, k_low, v_low, d_heads, log_sum, query_table, key_table)
 
@@ -699,7 +831,9 @@
 def chosen_picks(routes, expert_count, capacity):
     experts = jnp.arange(expert_count, dtype=jnp.int32)
     onehot = (routes[:, :, None] == experts[None, None, :]).astype(jnp.int32)
-    order = jnp.cumsum(jnp.sum(onehot, axis=1), axis=0) - 1
+    rows = routes.shape[0]
+    below = (jnp.arange(rows)[:, None] > jnp.arange(rows)[None, :]).astype(LOW)
+    order = matmul(below, jnp.sum(onehot, axis=1).astype(LOW)).astype(jnp.int32)
     slot = routes * capacity + jnp.sum(onehot * order[:, None, :], axis=2)
     slots = jnp.arange(expert_count * capacity, dtype=jnp.int32)
     picks = [(slot[:, k : k + 1] == slots[None, :]).astype(LOW) for k in range(routes.shape[1])]
@@ -708,7 +842,9 @@
 
 def expert_picks(routes_seq, expert, capacity):
     named = jnp.any(routes_seq == expert, axis=1)
-    order = jnp.cumsum(named.astype(jnp.int32), axis=1) - 1
+    rows = named.shape[1]
+    above = (jnp.arange(rows)[:, None] < jnp.arange(rows)[None, :]).astype(LOW)
+    order = matmul(named.astype(LOW), above).astype(jnp.int32)
     slot = jnp.where(named, order, -1)
     return (slot[:, None, :] == jnp.arange(capacity, dtype=jnp.int32)[None, :, None]).astype(LOW)
 
@@ -764,11 +900,12 @@
     routes_mine = jnp.concatenate([attn_routes.T, ffn_routes.T], axis=0)
     routes_mine = jnp.concatenate([routes_mine, jnp.zeros_like(routes_mine)], axis=0)
     kv_mine = jnp.concatenate([key_proj, value_proj], axis=1)
-    seq_low, all_routes, kv_full, query_full, out_full = prologue(
+    seq_low, all_routes, kv_full, query_full, out_pieces = prologue(
         token_half, tokens_spread, routes_mine, kv_mine, query_proj[0], out_proj[0], 0
     )
     seq_routes = all_routes[0]
-    seq_tokens = seq_low.astype(FULL)
+    seq_tokens = jnp.concatenate([seq_low[0], seq_low[1]], axis=1).astype(FULL)
+    out_full = jnp.concatenate([out_pieces[n] for n in range(lax.axis_size("fsdp"))], axis=1)
 
     gate_pieces = gather_pieces(after(gate_proj[0], all_routes))
     up_pieces = gather_pieces(after(up_proj[0], all_routes))
@@ -791,8 +928,14 @@
     ffn_picks, ffn_onehot = chosen_picks(ffn_routes, expert_count, capacity)
     attn_mix = mix_of(attn_logits, attn_onehot)
 
+    cot_half = my_half(to_spread(cotangent, 1))
+    ffn_pick = ffn_picks[0]
+    for pick in ffn_picks[1:]:
+        ffn_pick = ffn_pick + pick
+    cot_rows = spread_out(after(matmul_tn(ffn_pick, cot_half).astype(LOW), all_routes))
+
     expert_onehot = expert_picks(seq_routes[:, :picks_each], mine, capacity)
-    key_table = turn_tables(jnp.arange(groups * rows_here, dtype=jnp.int32))
+    key_table = jnp.asarray(turn_tables(groups * rows_here))
     query_table = jnp.einsum(
         "bsr,brh->bsh",
         expert_onehot.astype(FULL),
@@ -814,13 +957,7 @@
     q_low, k_low, v_low, heads_low, log_sum = attend(
         query_lin, kv_lin, query_table, key_table, groups
     )
-    attn_back = send_home(matmul(heads_low, out_full).astype(LOW), 1)
-
-    cot_half = my_half(to_spread(cotangent, 1))
-    ffn_pick = ffn_picks[0]
-    for pick in ffn_picks[1:]:
-        ffn_pick = ffn_pick + pick
-    cot_rows = spread_out(after(matmul_tn(ffn_pick, cot_half).astype(LOW), all_routes))
+    attn_back = send_home(after(matmul(heads_low, out_full).astype(LOW), cot_rows), 1)
 
     input_half = my_half(tokens_spread).astype(FULL)
     attn_picked = [matmul(pick, attn_back) for pick in attn_picks]
@@ -830,7 +967,10 @@
     square_sum = tp_sum(jnp.sum(attended * attended, axis=1, keepdims=True))
     scale_two = lax.rsqrt(square_sum / features + EPSILON)
     b_half = (attended * scale_two * gain2_half).astype(LOW)
-    ffn_rows = send_out(matmul_tn(ffn_pick, b_half).astype(LOW), 2)
+    gate_all = with_neighbours(gate_pieces, heads_low)
+    up_all = with_neighbours(up_pieces, attn_back)
+    b_slots = matmul_tn(ffn_pick, b_half).astype(LOW)
+    ffn_rows = send_out(after(b_slots, *gate_all[1:], *up_all[1:]), 2)
     ffn_logits = tp_sum(matmul(b_half, router2_half))
     ffn_probs = jax.nn.softmax(ffn_logits, axis=1)
     ffn_mix = mix_of(ffn_logits, ffn_onehot)
@@ -845,22 +985,29 @@
     mine_too = (row_routes == mine.astype(FULL)).astype(FULL)
     mix_rows = jnp.broadcast_to(jnp.sum(row_mix * mine_too, axis=1, keepdims=True), (slots, HEAD))
     hidden_low, d_gate_low, d_up_low, db_rows, ffn_out, mix_grad_rows = expert_both_ways(
-        ffn_rows, cot_rows, mix_rows, gate_pieces, up_pieces, down_pieces
-    )
-    mix_grad_rows = jnp.pad(mix_grad_rows[:, 0].reshape(groups, 1, capacity), ((0, 0), (0, 7), (0, 256 - capacity)))
-    db_back, mix_grad_back = send_home(db_rows, 3, extra=mix_grad_rows)
+        ffn_rows,
+        cot_rows,
+        mix_rows,
+        gate_all,
+        up_all,
+        with_neighbours(down_pieces, ffn_rows),
+    )
+    mix_grad_rows = jnp.pad(
+        mix_grad_rows[:, 0].reshape(groups, 1, capacity), ((0, 0), (0, 7), (0, 256 - capacity))
+    )
+    dz_rows = (cot_rows.astype(FULL) * mix_rows[:, :1]).astype(LOW)
+    down_sent, down_finish = scatter_start(
+        lambda low, high: matmul_tn(hidden_low, dz_rows[:, low:high]), features, 1
+    )
+    down_back = last_step(down_sent)
+    d_both = jnp.concatenate([d_gate_low, d_up_low], axis=1)
+    both_sent, both_finish = scatter_start(
+        lambda low, high: matmul_tn(ffn_rows[:, low:high], d_both), features, 0
+    )
+    both_back = last_step(both_sent)
+    db_back, mix_grad_back = send_home(after(db_rows, down_sent), 3, extra=mix_grad_rows)
+    db_back = after(db_back, down_back)
     mix_grad_back = mix_grad_back[:, 0, :capacity].reshape(1, slots)
-    dz_rows = (cot_rows.astype(FULL) * mix_rows[:, :1]).astype(LOW)
-    near, far = slice(0, half_width), slice(half_width, features)
-    down_grad = scatter_sum(
-        matmul_tn(hidden_low, dz_rows[:, near]), matmul_tn(hidden_low, dz_rows[:, far]).astype(LOW), 1
-    )
-    gate_grad = scatter_sum(
-        matmul_tn(ffn_rows[:, near], d_gate_low), matmul_tn(ffn_rows[:, far], d_gate_low).astype(LOW), 0
-    )
-    up_grad = scatter_sum(
-        matmul_tn(ffn_rows[:, near], d_up_low), matmul_tn(ffn_rows[:, far], d_up_low).astype(LOW), 0
-    )
 
     experts = jnp.arange(expert_count, dtype=jnp.int32)
     named = (all_routes[..., None] == experts).astype(FULL)
@@ -890,25 +1037,34 @@
     dy_slots = jnp.zeros((slots, half_width), FULL)
     for k in range(picks_each):
         dy_slots = dy_slots + matmul_tn(attn_picks[k], (attn_mix[:, k : k + 1] * d_attended).astype(LOW))
-    dy_rows = send_out(dy_slots.astype(LOW), 4)
+    dy_rows = send_out(after(dy_slots.astype(LOW), both_sent), 4)
     d_heads = matmul_nt(dy_rows, out_full).astype(LOW)
     dq_low, dk_low, dv_low = attend_back(
         q_low, k_low, v_low, d_heads, log_sum, query_table, key_table, groups
-    )
-    out_grad = scatter_sum(
-        matmul_tn(heads_low, dy_rows[:, near]), matmul_tn(heads_low, dy_rows[:, far]).astype(LOW), 1
-    )
-    query_grad = scatter_sum(
-        matmul_tn(rows_in[:, near], dq_low), matmul_tn(rows_in[:, far], dq_low).astype(LOW), 0
     )
     dkv_low = jnp.concatenate([dk_low, dv_low], axis=1)
     da_rows = matmul_nt(dq_low, query_full).astype(LOW).reshape(groups, capacity, features)
     da_seq = jnp.einsum("bsr,bsd->brd", expert_onehot, da_rows, preferred_element_type=FULL)
     da_seq = da_seq.reshape(groups * rows_here, features) + matmul_nt(dkv_low, kv_full)
-    da_half = send_home(da_seq.astype(LOW), 5, add_up=True)
-    kv_part = scatter_sum(
-        matmul_tn(a_seq[:, near], dkv_low), matmul_tn(a_seq[:, far], dkv_low).astype(LOW), 0
-    )
+    out_sent, out_finish = scatter_start(
+        lambda low, high: matmul_tn(heads_low, dy_rows[:, low:high]), features, 1
+    )
+    kv_sent, kv_finish = scatter_start(
+        lambda low, high: matmul_tn(a_seq[:, low:high], dkv_low), features, 0
+    )
+    query_sent, query_finish = scatter_start(
+        lambda low, high: matmul_tn(rows_in[:, low:high], dq_low), features, 0
+    )
+    ffn_back = come_home(after(ffn_out, dy_rows))
+    da_half, kv_back, out_back = send_home(
+        after(da_seq.astype(LOW), both_back, ffn_back, query_sent), 5, cargo=(kv_sent, out_sent), add_up=True
+    )
+    kv_part = kv_finish(kv_back)
+    query_grad = query_finish(last_step(after(query_sent, da_half)))
+    out_grad = out_finish(out_back)
+    down_grad = down_finish(after(down_back, da_half))
+    both_grad = both_finish(after(both_back, da_half))
+    gate_grad, up_grad = jnp.split(both_grad, 2, axis=1)
     kv_grad = block_for(kv_part, 0)
     kv_part_low = kv_part.astype(LOW)
     for distance in far_first(groups):
@@ -916,7 +1072,6 @@
             kv_grad = kv_grad + swap(block_for(kv_part_low, distance), "ctx", distance).astype(FULL)
     key_width = key_proj.shape[1]
 
-    ffn_back = send_home(ffn_out, 6)
     result = attended
     for k in range(picks_each):
         result = result + ffn_mix[:, k : k + 1] * matmul(ffn_picks[k], ffn_back)

time: 1120 us -> 899 us (0.80)
  waiting for transfers between devices: 289 us -> 142 us
  Pallas kernels: 527 us -> 459 us
    ppermute x43 -> x46, waiting for transfers between devices: 289 us -> 142 us  [swap(): return lax.ppermute(value, axis, [(i, i ^ distance) for i in range(size)])]
    pallas_call x4 -> x3, Pallas kernels: 187 us -> 156 us  [send_home(): pl.pallas_call(functools.partial(send_home_kernel, size, add_up, extra is...]
    pallas_call x1, Pallas kernels: 131 us -> 110 us  [prologue(): pl.pallas_call(functools.partial(prologue_kernel, (groups, world)), in_sp...]
    pallas_call x2, Pallas kernels: 96.7 us -> 81.7 us  [send_out(): pl.pallas_call(functools.partial(send_out_kernel, size), in_specs=[pl.Blo...]
    broadcast_in_dim x2 -> x0, other arithmetic: 11.7 us -> none  [the longest x1 6.57 us: on_device(): gate_grad[None]]
    slice x8 -> x0, local copies, waits for them, and re-layouts: 11.5 us -> none  [the longest x6 11.4 us: scatter_sum(): send = lax.slice_in_dim(total, width, 2 * width, axis=first_dim).astype(LOW)]
    dot_general x16 -> x19, matrix products: 86.8 us -> 82.4 us  [matmul_tn(): lax.dot_general(lhs, rhs, (((0,), (0,)), ((), ())), preferred_element_typ...]
    ppermute x43 -> x46, starting transfers between devices: 39.4 us -> 38 us  [swap(): return lax.ppermute(value, axis, [(i, i ^ distance) for i in range(size)])]
  transfers between devices with their start and end apart: 43 -> 46, of which waited for: 24 -> 24; matrix products, arithmetic and copies ran while one was open for 21% -> 23% of each run, Pallas kernels for 22% -> 23%
where the time goes in v3:
time: 899 us; the launch traced here: 895 us
  Pallas kernels  459 us (51%)
  matrix products  154 us (17%)
  waiting for transfers between devices  142 us (16%)
  other arithmetic  57 us (6%)
  local copies, waits for them, and re-layouts  41.1 us (5%)
  starting transfers between devices  38 us (4%)
    pallas_call x3, Pallas kernels, send_home(): pl.pallas_call(functools.partial(send_home_kernel, size, add_up, extra is...  156 us
    ppermute x46, waiting for transfers between devices, swap(): return lax.ppermute(value, axis, [(i, i ^ distance) for i in range(size)])  142 us
    pallas_call x1, Pallas kernels, prologue(): pl.pallas_call(functools.partial(prologue_kernel, (groups, world)), in_sp...  110 us
    dot_general x19, matrix products, matmul_tn(): lax.dot_general(lhs, rhs, (((0,), (0,)), ((), ())), preferred_element_typ...  82.4 us
    pallas_call x2, Pallas kernels, send_out(): pl.pallas_call(functools.partial(send_out_kernel, size), in_specs=[pl.Blo...  81.7 us
    pallas_call x1, Pallas kernels, expert_both_ways(): pl.pallas_call(functools.partial(expert_kernel, world), grid=(hidden_widt...  68.5 us
    dot_general x16, matrix products, matmul(): return jnp.dot(lhs, rhs, preferred_element_type=FULL)  39.3 us
    ppermute x46, starting transfers between devices, swap(): return lax.ppermute(value, axis, [(i, i ^ distance) for i in range(size)])  38 us
  transfers between devices with their start and end apart: 46, of which 24 were waited for; matrix products, arithmetic and copies ran while one was open for 23% of the time, Pallas kernels for 23%

profile of v3, /device:TPU:0, one launch (start us, length us, event | category | flops | bytes accessed | tf_op | source)
XLA Modules:
  0.0 894.6 jit_solution(13961362698633338937)
XLA Ops:
  6.5 109.5 %shard_map.271 = (bf16[2,1024,1024]{2,1,0:T(8,128)(2,1)}, s32[4,4,8,256]{3,2,1,0:T(8,128)}, bf16[2048,2048]{1,0:T(8,128)(2,1)}, bf16[2048,1024]{1,0:T(8,128)(2,1)}, bf16[4,1024,512]{2,1,0:T(8,128)(2,1)}) custom-call(bf16[256,1024]{1,0:T(8,128)(2,1)} %maximum_select_fusion.refs_0_, bf16[256,2048]{1,0:T(8,128)(2,1)} %pad_maximum_fusion.2.refs_1_, ...), custom_call_target="tpu_custom_call" | custom-call | bytes 100000000 | tf_op jit(solution)/shard_map/pallas_call | solution.py:577
  137.9 14.7 %fusion.146.k_lin.v_lin = f32[1024,2048]{1,0:T(8,128)} fusion(bf16[1024,2048]{1,0:T(8,128)(2,1)} %fusion.2, bf16[2048,2048]{1,0:T(8,128)(2,1)} %get-tuple-element.62), kind=kOutput, calls=%fused_computation.388 | convolution fusion | flops 8589934592 | bytes 20971520 | tf_op jit(solution)/shard_map/dot_general | solution.py:23
  163.5 19.1 %shard_map.272 = (bf16[640,1024]{1,0:T(8,128)(2,1)}, bf16[1024,1024]{1,0:T(8,128)(2,1)}, bf16[1024,1024]{1,0:T(8,128)(2,1)}, bf16[640,1024]{1,0:T(8,128)(2,1)}, f32[640,1024]{1,0:T(8,128)}) custom-call(f32[640,1024]{1,0:T(8,128)} %fusion.145.q_lin, f32[1024,2048]{1,0:T(8,128)} %fusion.146.k_lin.v_lin, f32[1024,2048]{1,0:T(8,128)} %fusion.146.k_lin.v_lin, ...), custom_call_target="tpu_custom_call" | custom-call | bytes 20971520 | tf_op jit(solution)/shard_map/pallas_call | solution.py:750
  213.6 42.4 %shard_map.273 = bf16[640,1024]{1,0:T(8,128)(2,1)} custom-call(bf16[640,2048]{1,0:T(8,128)(2,1)} %convolution_convert_fusion.4.refs_0_), custom_call_target="tpu_custom_call" | custom-call | bytes 7864320 | tf_op jit(solution)/shard_map/pallas_call | solution.py:370
  275.5 44.0 %shard_map.274.refs_0_ = bf16[640,2048]{1,0:T(8,128)(2,1)} custom-call(bf16[640,1024]{1,0:T(8,128)(2,1)} %convolution_convert_fusion.8.rows_ref), custom_call_target="tpu_custom_call" | custom-call | bytes 7864320 | tf_op jit(solution)/shard_map/pallas_call | solution.py:244
  332.8 68.5 %shard_map.275 = (bf16[640,2816]{1,0:T(8,128)(2,1)}, bf16[640,2816]{1,0:T(8,128)(2,1)}, bf16[640,2816]{1,0:T(8,128)(2,1)}, bf16[640,2048]{1,0:T(8,128)(2,1)}, bf...) custom-call(bf16[640,2048]{1,0:T(8,128)(2,1)} %shard_map.274.refs_0_, bf16[640,2048]{1,0:T(8,128)(2,1)} %copy-done.12, ...), custom_call_target="tpu_custom_call" | custom-call | flops 44291850240 | bytes 34603008 | tf_op jit(solution)/shard_map/pallas_call | solution.py:657
  401.3 9.1 %convolution_convert_fusion.1 = bf16[2816,1024]{1,0:T(8,128)(2,1)} fusion(bf16[640,2816]{1,0:T(8,128)(2,1)} %get-tuple-element.79, bf16[640,2048]{1,0:T(8,128)(2,1)S(1)} %multiply_convert_fusion.1), kind=kOutput, calls=%fused_computation.15 | convolution fusion | flops 3693871104 | bytes 10682368 | tf_op jit(solution)/shard_map/dot_general | solution.py:27
  414.4 12.2 %convolution_convert_fusion = bf16[1024,5632]{1,0:T(8,128)(2,1)} fusion(bf16[640,5632]{1,0:T(8,128)(2,1)S(1)} %constant_dynamic-update-slice_fusion, bf16[640,2048]{1,0:T(8,128)(2,1)S(1)} %copy-done.1), kind=kOutput, calls=%fused_computation.2 | convolution fusion | flops 7387742208 | bytes 20054016 | tf_op jit(solution)/shard_map/dot_general | solution.py:27
  433.1 7.3 add_convert_fusion.1
  447.8 10.6 %fusion.46 = f32[512,5632]{1,0:T(8,128)} fusion(bf16[640,5632]{1,0:T(8,128)(2,1)} %copy-done, bf16[640,2048]{1,0:T(8,128)(2,1)S(1)} %copy-done.1), kind=kOutput, calls=%fused_computation.105 | convolution fusion | flops 3690987520 | bytes 19398656 | tf_op jit(solution)/shard_map/dot_general | solution.py:27
  458.4 38.9 %shard_map.276 = (bf16[640,1024]{1,0:T(8,128)(2,1)}, f32[4,8,256]{2,1,0:T(8,128)}) custom-call(bf16[640,2048]{1,0:T(8,128)(2,1)} %get-tuple-element.80.refs_0_, f32[4,8,256]{2,1,0:T(8,128)} %pad.8.refs_1_), custom_call_target="tpu_custom_call" | custom-call | bytes 7864320 | tf_op jit(solution)/shard_map/pallas_call | solution.py:370
  518.7 8.4 add_convert_fusion
  527.8 37.7 %shard_map.277 = bf16[640,2048]{1,0:T(8,128)(2,1)} custom-call(bf16[640,1024]{1,0:T(8,128)(2,1)} %add_convert_fusion.3.rows_ref), custom_call_target="tpu_custom_call" | custom-call | bytes 7864320 | tf_op jit(solution)/shard_map/pallas_call | solution.py:244
  574.5 23.6 %shard_map.278 = (bf16[640,1024]{1,0:T(8,128)(2,1)}, bf16[1024,1024]{1,0:T(8,128)(2,1)}, bf16[1024,1024]{1,0:T(8,128)(2,1)}) custom-call(bf16[640,1024]{1,0:T(8,128)(2,1)} %get-tuple-element.89.q_low, bf16[1024,1024]{1,0:T(8,128)(2,1)} %get-tuple-element.90.k_low, bf16[1024,1024]{1,0:T(8,128)(2,1)} %get-tuple-element.91.v_low, ...), custom_call_target="tpu_custom_call" | custom-call | bytes 14680064 | tf_op jit(solution)/shard_map/pallas_call | solution.py:805
  606.9 13.0 %fusion.3.refs_0_ = bf16[1024,2048]{1,0:T(8,128)(2,1)} fusion(f32[4,256,2048]{2,1,0:T(8,128)S(1)} %fusion.59, bf16[1024,2048]{1,0:T(8,128)(2,1)S(1)} %constant_dynamic-update-slice_fusion.2, bf16[2048,2048]{1,0:T(8,128)(2,1)} %get-tuple-element.62), kind=kOutput, calls=%fused_computation.9 | convolution fusion | flops 8594128896 | bytes 25165824 | tf_op jit(solution)/shard_map/dot_general | solution.py:31
  667.1 15.3 %collective-permute-done.26 = bf16[160,1024]{1,0:T(8,128)(2,1)S(1)} collective-permute-done((bf16[160,1024]{1,0:T(8,128)(2,1)S(1)}, bf16[160,1024]{1,0:T(8,128)(2,1)S(1)}, u32[]{:S(2)}, u32[]{:S(2)}) %collective-permute-start.26) | collective-permute-done | bytes 327712 | tf_op jit(solution)/shard_map/ppermute | solution.py:40
  687.3 11.0 %collective-permute-done.29 = bf16[256,1024]{1,0:T(8,128)(2,1)S(1)} collective-permute-done((bf16[256,1024]{1,0:T(8,128)(2,1)S(1)}, bf16[256,1024]{1,0:T(8,128)(2,1)S(1)}, u32[]{:S(2)}, u32[]{:S(2)}) %collective-permute-start.29) | collective-permute-done | bytes 524320 | tf_op jit(solution)/shard_map/ppermute | solution.py:40
  707.8 75.1 %shard_map.279 = (f32[256,1024]{1,0:T(8,128)}, bf16[512,2048]{1,0:T(8,128)(2,1)}, bf16[1024,512]{1,0:T(8,128)(2,1)}) custom-call(bf16[1024,2048]{1,0:T(8,128)(2,1)} %fusion.3.refs_0_, bf16[512,2048]{1,0:T(8,128)(2,1)} %add_convert_fusion.2.refs_1_, bf16[1024,512]{1,0:T(8,128)(2,1)} %add_convert_fusion.4.refs_2_), custom_call_target="tpu_custom_call" | custom-call | bytes 12582912 | tf_op jit(solution)/shard_map/pallas_call | solution.py:370
  797.6 10.1 %convert_add_fusion = f32[512,5632]{1,0:T(8,128)} fusion(bf16[512,5632]{1,0:T(8,128)(2,1)} %collective-permute-done.30, f32[512,5632]{1,0:T(8,128)S(1)} %bitcast.148, bf16[1024,5632]{1,0:T(8,128)(2,1)} %collective-permute-done.21), kind=kLoop, calls=%fused_computation | loop fusion | flops 11534336 | bytes 34603008 | tf_op jit(solution)/shard_map/add | solution.py:684
  807.7 9.5 %slice_bitcast_fusion = (f32[1,512,2816]{2,1,0:T(8,128)}, f32[1,512,2816]{2,1,0:T(8,128)}) fusion(f32[512,5632]{1,0:T(8,128)} %convert_add_fusion), kind=kLoop, calls=%fused_computation.11 | loop fusion | bytes 23068672 | tf_op jit(solution)/shard_map/broadcast_in_dim | solution.py:1122
  819.4 8.1 add_bitcast_fusion
  827.5 17.4 %collective-permute-done.38 = f32[11,2048]{1,0:T(8,128)S(1)} collective-permute-done((f32[11,2048]{1,0:T(8,128)S(1)}, f32[11,2048]{1,0:T(8,128)S(1)}, u32[]{:S(2)}, u32[]{:S(2)}) %collective-permute-start.38) | collective-permute-done | bytes 90144 | tf_op jit(solution)/shard_map/ppermute | solution.py:40
  852.1 22.0 %collective-permute-done.40 = f32[11,2048]{1,0:T(8,128)S(1)} collective-permute-done((f32[11,2048]{1,0:T(8,128)S(1)}, f32[11,2048]{1,0:T(8,128)S(1)}, u32[]{:S(2)}, u32[]{:S(2)}) %collective-permute-start.40) | collective-permute-done | bytes 90144 | tf_op jit(solution)/shard_map/ppermute | solution.py:40
  881.8 7.7 collective-permute-done.36
  (471 shorter events, 256.7 us)
Async XLA Ops:
  117.7 71.5 %collective-permute-start = (bf16[160,1024]{1,0:T(8,128)(2,1)S(1)}, bf16[160,1024]{1,0:T(8,128)(2,1)}, u32[]{:S(2)}, u32[]{:S(2)}) collective-permute-start(bf16[160,1024]{1,0:T(8,128)(2,1)S(1)} %get-tuple-element.155), channel_id=1, source_target_pairs={{0,1},{1,0},{2,3},{3,2},{4,5},{5,4},{6,7},{7,6},{8,9},{9,8},{10,11... | collective-permute-start | bytes 983048 | tf_op jit(solution)/shard_map/ppermute | solution.py:40
  119.2 71.6 %collective-permute-start.1 = (bf16[160,1024]{1,0:T(8,128)(2,1)}, bf16[160,1024]{1,0:T(8,128)(2,1)}, u32[]{:S(2)}, u32[]{:S(2)}) collective-permute-start(bf16[160,1024]{1,0:T(8,128)(2,1)} %get-tuple-element.154), channel_id=1, source_target_pairs={{0,2},{2,0},{4,6},{6,4},{1,3},{3,1},{5,7},{7,5},{8,10},{10,8},{12,... | collective-permute-start | bytes 983048 | tf_op jit(solution)/shard_map/ppermute | solution.py:40
  119.2 73.2 %collective-permute-start.3 = (bf16[160,1024]{1,0:T(8,128)(2,1)S(1)}, bf16[160,1024]{1,0:T(8,128)(2,1)}, u32[]{:S(2)}, u32[]{:S(2)}) collective-permute-start(bf16[160,1024]{1,0:T(8,128)(2,1)S(1)} %get-tuple-element.153), channel_id=1, source_target_pairs={{0,4},{2,6},{4,0},{6,2},{1,5},{3,7},{5,1},{7,3},{8,12},{10,14},{12... | collective-permute-start | bytes 983048 | tf_op jit(solution)/shard_map/ppermute | solution.py:40
  122.1 138.5 %collective-permute-start.9 = (bf16[512,2816]{1,0:T(8,128)(2,1)}, bf16[512,2816]{1,0:T(8,128)(2,1)}, u32[]{:S(2)}, u32[]{:S(2)}) collective-permute-start(bf16[512,2816]{1,0:T(8,128)(2,1)} %bitcast.240), channel_id=1, source_target_pairs={{0,16},{8,24},{16,0},{24,8},{1,17},{9,25},{17,1},{25,9},{2,18},{10... | collective-permute-start | bytes 8650760 | tf_op jit(solution)/shard_map/ppermute | solution.py:40
  122.6 138.5 %collective-permute-start.12 = (bf16[512,2816]{1,0:T(8,128)(2,1)}, bf16[512,2816]{1,0:T(8,128)(2,1)}, u32[]{:S(2)}, u32[]{:S(2)}) collective-permute-start(bf16[512,2816]{1,0:T(8,128)(2,1)} %bitcast.243), channel_id=1, source_target_pairs={{0,16},{8,24},{16,0},{24,8},{1,17},{9,25},{17,1},{25,9},{2,18},{10... | collective-permute-start | bytes 8650760 | tf_op jit(solution)/shard_map/ppermute | solution.py:40
  199.9 66.0 %collective-permute-start.10 = (bf16[512,2816]{1,0:T(8,128)(2,1)S(1)}, bf16[512,2816]{1,0:T(8,128)(2,1)}, u32[]{:S(2)}, u32[]{:S(2)}) collective-permute-start(bf16[512,2816]{1,0:T(8,128)(2,1)S(1)} %bitcast.242), channel_id=1, source_target_pairs={{0,8},{8,0},{16,24},{24,16},{1,9},{9,1},{17,25},{25,17},{2,10},{10... | collective-permute-start | bytes 8650760 | tf_op jit(solution)/shard_map/ppermute | solution.py:40
  263.3 63.0 %collective-permute-start.15 = (bf16[2816,512]{1,0:T(8,128)(2,1)}, bf16[2816,512]{1,0:T(8,128)(2,1)}, u32[]{:S(2)}, u32[]{:S(2)}) collective-permute-start(bf16[2816,512]{1,0:T(8,128)(2,1)} %bitcast.27.refs_11_), channel_id=1, source_target_pairs={{0,16},{8,24},{16,0},{24,8},{1,17},{9,25},{17,1},{25,9},{2,18},{10... | collective-permute-start | bytes 8650760 | tf_op jit(solution)/shard_map/ppermute | solution.py:40
  410.5 22.6 %collective-permute-start.18 = (bf16[2816,1024]{1,0:T(8,128)(2,1)}, bf16[2816,1024]{1,0:T(8,128)(2,1)}, u32[]{:S(2)}, u32[]{:S(2)}) collective-permute-start(bf16[2816,1024]{1,0:T(8,128)(2,1)} %convolution_convert_fusion.1), channel_id=1, source_target_pairs={{0,8},{8,0},{16,24},{24,16},{1,9},{9,1},{17,25},{25,17},{2,10},{10... | collective-permute-start | bytes 17301512 | tf_op jit(solution)/shard_map/ppermute | solution.py:40
  426.6 92.1 %collective-permute-start.21 = (bf16[1024,5632]{1,0:T(8,128)(2,1)}, bf16[1024,5632]{1,0:T(8,128)(2,1)}, u32[]{:S(2)}, u32[]{:S(2)}) collective-permute-start(bf16[1024,5632]{1,0:T(8,128)(2,1)} %convolution_convert_fusion), channel_id=1, source_target_pairs={{0,8},{8,0},{16,24},{24,16},{1,9},{9,1},{17,25},{25,17},{2,10},{10... | collective-permute-start | bytes 34603016 | tf_op jit(solution)/shard_map/ppermute | solution.py:40
  440.4 63.7 %collective-permute-start.19 = (bf16[2816,512]{1,0:T(8,128)(2,1)}, bf16[2816,512]{1,0:T(8,128)(2,1)}, u32[]{:S(2)}, u32[]{:S(2)}) collective-permute-start(bf16[2816,512]{1,0:T(8,128)(2,1)} %add_convert_fusion.1), channel_id=1, source_target_pairs={{0,16},{8,24},{16,0},{24,8},{1,17},{9,25},{17,1},{25,9},{2,18},{10... | collective-permute-start | bytes 8650760 | tf_op jit(solution)/shard_map/ppermute | solution.py:40
  527.1 180.7 %collective-permute-start.30 = (bf16[512,5632]{1,0:T(8,128)(2,1)}, bf16[512,5632]{1,0:T(8,128)(2,1)}, u32[]{:S(2)}, u32[]{:S(2)}) collective-permute-start(bf16[512,5632]{1,0:T(8,128)(2,1)} %add_convert_fusion), channel_id=1, source_target_pairs={{0,16},{8,24},{16,0},{24,8},{1,17},{9,25},{17,1},{25,9},{2,18},{10... | collective-permute-start | bytes 17301512 | tf_op jit(solution)/shard_map/ppermute | solution.py:40
  573.4 53.7 %collective-permute-start.22 = (bf16[160,1024]{1,0:T(8,128)(2,1)}, bf16[160,1024]{1,0:T(8,128)(2,1)}, u32[]{:S(2)}, u32[]{:S(2)}) collective-permute-start(bf16[160,1024]{1,0:T(8,128)(2,1)} %broadcast_select_fusion.7), channel_id=1, source_target_pairs={{0,1},{1,0},{2,3},{3,2},{4,5},{5,4},{6,7},{7,6},{8,9},{9,8},{10,11... | collective-permute-start | bytes 983048 | tf_op jit(solution)/shard_map/ppermute | solution.py:40
  625.1 78.5 %collective-permute-start.32 = (bf16[1024,2048]{1,0:T(8,128)(2,1)S(1)}, bf16[1024,2048]{1,0:T(8,128)(2,1)S(1)}, u32[]{:S(2)}, u32[]{:S(2)}) collective-permute-start(bf16[1024,2048]{1,0:T(8,128)(2,1)S(1)} %convolution_convert_fusion.2), channel_id=1, source_target_pairs={{0,8},{8,0},{16,24},{24,16},{1,9},{9,1},{17,25},{25,17},{2,10},{10... | collective-permute-start | bytes 12582920 | tf_op jit(solution)/shard_map/ppermute | solution.py:40
  656.8 25.6 %collective-permute-start.26 = (bf16[160,1024]{1,0:T(8,128)(2,1)S(1)}, bf16[160,1024]{1,0:T(8,128)(2,1)S(1)}, u32[]{:S(2)}, u32[]{:S(2)}) collective-permute-start(bf16[160,1024]{1,0:T(8,128)(2,1)S(1)} %get-tuple-element.144), channel_id=1, source_target_pairs={{0,4},{2,6},{4,0},{6,2},{1,5},{3,7},{5,1},{7,3},{8,12},{10,14},{12... | collective-permute-start | bytes 983048 | tf_op jit(solution)/shard_map/ppermute | solution.py:40
  658.6 23.9 %collective-permute-start.28 = (bf16[160,1024]{1,0:T(8,128)(2,1)S(1)}, bf16[160,1024]{1,0:T(8,128)(2,1)S(1)}, u32[]{:S(2)}, u32[]{:S(2)}) collective-permute-start(bf16[160,1024]{1,0:T(8,128)(2,1)S(1)} %get-tuple-element.142), channel_id=1, source_target_pairs={{0,6},{2,4},{4,2},{6,0},{1,7},{3,5},{5,3},{7,1},{8,14},{10,12},{12... | collective-permute-start | bytes 983048 | tf_op jit(solution)/shard_map/ppermute | solution.py:40
  667.1 32.5 %collective-permute-start.31 = (bf16[1024,1024]{1,0:T(8,128)(2,1)S(1)}, bf16[1024,1024]{1,0:T(8,128)(2,1)S(1)}, u32[]{:S(2)}, u32[]{:S(2)}) collective-permute-start(bf16[1024,1024]{1,0:T(8,128)(2,1)S(1)} %convolution_convert_fusion.6), channel_id=1, source_target_pairs={{0,8},{8,0},{16,24},{24,16},{1,9},{9,1},{17,25},{25,17},{2,10},{10... | collective-permute-start | bytes 6291464 | tf_op jit(solution)/shard_map/ppermute | solution.py:40
  785.0 65.6 %collective-permute-start.35 = (f32[256,1]{0,1:T(1,128)S(1)}, f32[256,1]{0,1:T(1,128)S(1)}, u32[]{:S(2)}, u32[]{:S(2)}) collective-permute-start(f32[256,1]{0,1:T(1,128)S(1)} %bitcast.222), channel_id=1, source_target_pairs={{0,1},{1,0},{2,3},{3,2},{4,5},{5,4},{6,7},{7,6},{8,9},{9,8},{10,11... | collective-permute-start | bytes 3080 | tf_op jit(solution)/shard_map/ppermute | solution.py:40
  786.3 30.9 %collective-permute-start.37 = (f32[10,1024]{1,0:T(8,128)S(1)}, f32[10,1024]{1,0:T(8,128)S(1)}, u32[]{:S(2)}, u32[]{:S(2)}) collective-permute-start(f32[10,1024]{1,0:T(8,128)S(1)} %pad_maximum_fusion.8), channel_id=1, source_target_pairs={{0,1},{1,0},{2,3},{3,2},{4,5},{5,4},{6,7},{7,6},{8,9},{9,8},{10,11... | collective-permute-start | bytes 122888 | tf_op jit(solution)/shard_map/ppermute | solution.py:40
  794.1 84.6 %collective-permute-start.44 = (bf16[128,2048]{1,0:T(8,128)(2,1)}, bf16[128,2048]{1,0:T(8,128)(2,1)}, u32[]{:S(2)}, u32[]{:S(2)}) collective-permute-start(bf16[128,2048]{1,0:T(8,128)(2,1)} %get-tuple-element.150), channel_id=1, source_target_pairs={{0,2},{2,0},{4,6},{6,4},{1,3},{3,1},{5,7},{7,5},{8,10},{10,8},{12,... | collective-permute-start | bytes 1572872 | tf_op jit(solution)/shard_map/ppermute | solution.py:40
  794.7 84.1 %collective-permute-start.43 = (bf16[128,2048]{1,0:T(8,128)(2,1)}, bf16[128,2048]{1,0:T(8,128)(2,1)}, u32[]{:S(2)}, u32[]{:S(2)}) collective-permute-start(bf16[128,2048]{1,0:T(8,128)(2,1)} %get-tuple-element.151), channel_id=1, source_target_pairs={{0,6},{2,4},{4,2},{6,0},{1,7},{3,5},{5,3},{7,1},{8,14},{10,12},{12... | collective-permute-start | bytes 1572872 | tf_op jit(solution)/shard_map/ppermute | solution.py:40
  796.7 82.0 %collective-permute-start.42 = (bf16[128,2048]{1,0:T(8,128)(2,1)S(1)}, bf16[128,2048]{1,0:T(8,128)(2,1)}, u32[]{:S(2)}, u32[]{:S(2)}) collective-permute-start(bf16[128,2048]{1,0:T(8,128)(2,1)S(1)} %get-tuple-element.149), channel_id=1, source_target_pairs={{0,4},{2,6},{4,0},{6,2},{1,5},{3,7},{5,1},{7,3},{8,12},{10,14},{12... | collective-permute-start | bytes 1572872 | tf_op jit(solution)/shard_map/ppermute | solution.py:40
  817.3 27.5 %collective-permute-start.38 = (f32[11,2048]{1,0:T(8,128)S(1)}, f32[11,2048]{1,0:T(8,128)S(1)}, u32[]{:S(2)}, u32[]{:S(2)}) collective-permute-start(f32[11,2048]{1,0:T(8,128)S(1)} %pad_maximum_fusion.7), channel_id=1, source_target_pairs={{0,4},{2,6},{4,0},{6,2},{1,5},{3,7},{5,1},{7,3},{8,12},{10,14},{12... | collective-permute-start | bytes 270344 | tf_op jit(solution)/shard_map/ppermute | solution.py:40
  849.9 41.3 %collective-permute-start.45 = (bf16[512,1024]{1,0:T(8,128)(2,1)}, bf16[512,1024]{1,0:T(8,128)(2,1)S(1)}, u32[]{:S(2)}, u32[]{:S(2)}) collective-permute-start(bf16[512,1024]{1,0:T(8,128)(2,1)} %add_convert_fusion.5), channel_id=1, source_target_pairs={{0,16},{8,24},{16,0},{24,8},{1,17},{9,25},{17,1},{25,9},{2,18},{10... | collective-permute-start | bytes 3145736 | tf_op jit(solution)/shard_map/ppermute | solution.py:40
  850.6 23.4 %collective-permute-start.40 = (f32[11,2048]{1,0:T(8,128)S(1)}, f32[11,2048]{1,0:T(8,128)S(1)}, u32[]{:S(2)}, u32[]{:S(2)}) collective-permute-start(f32[11,2048]{1,0:T(8,128)S(1)} %add.300), channel_id=1, source_target_pairs={{0,16},{8,24},{16,0},{24,8},{1,17},{9,25},{17,1},{25,9},{2,18},{10... | collective-permute-start | bytes 270344 | tf_op jit(solution)/shard_map/ppermute | solution.py:40
  (124 other events, 3896.4 us)

commit v4 on v3

--- a/solution.py
+++ b/solution.py
@@ -16,7 +16,8 @@
 PRECISE = lax.Precision.HIGHEST
 LOW = jnp.bfloat16
 FULL = jnp.float32
-VMEM_BYTES = 56 * 1024 * 1024
+VMEM_BYTES = 58 * 1024 * 1024
+TILE = 256
 
 
 def matmul(lhs, rhs):
@@ -146,17 +147,6 @@
         if distance:
             block = swap(block, "ctx", distance)
         blocks[distance] = join_halves(block, swap(block, "tp", 1))
-    return place_blocks(blocks)
-
-
-def come_home(partial_rows):
-    size = lax.axis_size("ctx")
-    blocks = [None] * size
-    for distance in far_first(size):
-        block = block_for(partial_rows, distance)
-        arrived = swap(other_half(block), "tp", 1)
-        block = (my_half(block).astype(FULL) + arrived.astype(FULL)).astype(LOW)
-        blocks[distance] = swap(block, "ctx", distance) if distance else block
     return place_blocks(blocks)
 
 
@@ -254,43 +244,44 @@
     )(half_rows)
 
 
-def send_home_kernel(size, add_up, has_extra, cargoes, *refs):
-    part_ref, refs = refs[0], refs[1:]
+def send_home_kernel(size, adds, has_extra, cargoes, *refs):
+    streams = len(adds)
+    parts, refs = refs[:streams], refs[streams:]
     extra_ref, refs = (refs[0], refs[1:]) if has_extra else (None, refs)
     cargo_in, refs = refs[:cargoes], refs[cargoes:]
-    out_ref, refs = refs[0], refs[1:]
+    outs, refs = refs[:streams], refs[streams:]
     extra_out, refs = (refs[0], refs[1:]) if has_extra else (None, refs)
     cargo_out, refs = refs[:cargoes], refs[cargoes:]
-    y_land, ready, z_land, y_send, y_recv, z_send, z_recv = refs[:7]
+    lands, refs = [refs[7 * n : 7 * n + 7] for n in range(streams)], refs[7 * streams :]
     mine, first = lax.axis_index("ctx"), lax.axis_index("tp") == 0
     place = lax.axis_index("tp")
     other_tp = {"tp": 1 - place}
-    rows, width = z_land.shape[1], z_land.shape[2]
     at = [xor_index(mine, distance) for distance in range(size)]
-    columns = pl.ds(pl.multiple_of((1 - place) * width, 128), width)
     world = lax.axis_size("fsdp")
     along = [{"fsdp": xor_index(lax.axis_index("fsdp"), world // 2)}] if cargoes else []
     meet([{"ctx": at[distance]} for distance in range(1, size)] + [other_tp] + along)
     order = mixed_order(size)
     beside, across, extras = {}, {}, {}
-    cargo = [
-        remote(cargo_in[n], cargo_out[n], refs[-2:], n, along[0]) for n in range(cargoes)
-    ]
+    cargo = [remote(cargo_in[n], cargo_out[n], refs[-2:], n, along[0]) for n in range(cargoes)]
     for copy in cargo:
         copy.start()
     if has_extra:
-        ey_land, e_ready, ez_land, ey_send, ey_recv, ez_send, ez_recv = refs[7:14]
+        ey_land, e_ready, ez_land, ey_send, ey_recv, ez_send, ez_recv = refs[:7]
         extra_beside = remote(extra_ref, ey_land, (ey_send, ey_recv), 0, other_tp)
         extra_beside.start()
-    for distance in order:
-        beside[distance] = remote(
-            part_ref.at[span(at[distance], rows), columns],
-            y_land.at[distance],
-            (y_send, y_recv),
-            distance,
-            other_tp,
-        )
-        beside[distance].start()
+    for n in range(streams):
+        y_land, _, z_land, y_send, y_recv, _, _ = lands[n]
+        rows, width = z_land.shape[1], z_land.shape[2]
+        columns = pl.ds(pl.multiple_of((1 - place) * width, 128), width)
+        for distance in order:
+            beside[n, distance] = remote(
+                parts[n].at[span(at[distance], rows), columns],
+                y_land.at[distance],
+                (y_send, y_recv),
+                distance,
+                other_tp,
+            )
+            beside[n, distance].start()
     if has_extra:
         extra_beside.wait_recv()
         e_ready[...] = extra_ref[...] + ey_land[...]
@@ -304,32 +295,38 @@
                     {"ctx": at[distance]},
                 )
                 extras[distance].start()
-    for distance in order:
-        beside[distance].wait_recv()
-        whole = part_ref[span(at[distance], rows), :]
-        own = jnp.where(first, whole[:, :width], whole[:, width:])
-        total = (own.astype(FULL) + y_land[distance].astype(FULL)).astype(LOW)
-        if distance:
-            ready[distance] = total
-            across[distance] = remote(
-                ready.at[distance],
-                z_land.at[distance],
-                (z_send, z_recv),
-                distance,
-                {"ctx": at[distance]},
-            )
-            across[distance].start()
-        elif add_up:
-            out_ref[...] = total.astype(FULL)
-        else:
-            out_ref[span(mine, rows), :] = total
-    for distance in order:
-        if distance:
-            across[distance].wait_recv()
-            if add_up:
-                out_ref[...] += z_land[distance].astype(FULL)
+    for n in range(streams):
+        y_land, ready, z_land, _, _, z_send, z_recv = lands[n]
+        rows, width = z_land.shape[1], z_land.shape[2]
+        for distance in order:
+            beside[n, distance].wait_recv()
+            whole = parts[n][span(at[distance], rows), :]
+            own = jnp.where(first, whole[:, :width], whole[:, width:])
+            total = (own.astype(FULL) + y_land[distance].astype(FULL)).astype(LOW)
+            if distance:
+                ready[distance] = total
+                across[n, distance] = remote(
+                    ready.at[distance],
+                    z_land.at[distance],
+                    (z_send, z_recv),
+                    distance,
+                    {"ctx": at[distance]},
+                )
+                across[n, distance].start()
+            elif adds[n]:
+                outs[n][...] = total.astype(FULL)
             else:
-                out_ref[span(at[distance], rows), :] = z_land[distance]
+                outs[n][span(mine, rows), :] = total
+    for n in range(streams):
+        z_land = lands[n][2]
+        rows = z_land.shape[1]
+        for distance in order:
+            if distance:
+                across[n, distance].wait_recv()
+                if adds[n]:
+                    outs[n][...] += z_land[distance].astype(FULL)
+                else:
+                    outs[n][span(at[distance], rows), :] = z_land[distance]
     if has_extra:
         extra_out[mine] = e_ready[mine]
         for distance in order:
@@ -338,22 +335,29 @@
                 extra_out[at[distance]] = ez_land[distance]
                 extras[distance].wait_send()
         extra_beside.wait_send()
-    for distance in order:
-        beside[distance].wait_send()
-        if distance:
-            across[distance].wait_send()
+    for n in range(streams):
+        for distance in order:
+            beside[n, distance].wait_send()
+            if distance:
+                across[n, distance].wait_send()
     for copy in cargo:
         copy.wait()
 
 
-def send_home(partial_rows, number, extra=None, cargo=(), add_up=False):
+def send_home(partial_rows, number, extra=None, cargo=(), add_up=False, more=None):
     size = lax.axis_size("ctx")
-    total, width = partial_rows.shape[0], partial_rows.shape[1] // 2
-    rows = total // size
-    land = pltpu.VMEM((size, rows, width), LOW)
+    operands = [partial_rows] if more is None else [partial_rows, more]
+    adds = (add_up, False)[: len(operands)]
     sems = [pltpu.SemaphoreType.DMA((size,))] * 4
-    shapes = [jax.ShapeDtypeStruct((rows, width), FULL) if add_up else jax.ShapeDtypeStruct((total, width), LOW)]
-    operands, scratch = [partial_rows], [land, land, land] + sems
+    shapes, scratch, moved = [], [], 0
+    for item, added in zip(operands, adds):
+        total, width = item.shape[0], item.shape[1] // 2
+        rows = total // size
+        moved += 12 * total * width
+        shapes.append(
+            jax.ShapeDtypeStruct((rows, width), FULL) if added else jax.ShapeDtypeStruct((total, width), LOW)
+        )
+        scratch += [pltpu.VMEM((size, rows, width), LOW)] * 3 + sems
     if extra is not None:
         operands.append(extra)
         shapes.append(jax.ShapeDtypeStruct(extra.shape, FULL))
@@ -368,7 +372,7 @@
     if cargo:
         scratch += [pltpu.SemaphoreType.DMA((len(cargo),))] * 2
     results = pl.pallas_call(
-        functools.partial(send_home_kernel, size, add_up, extra is not None, len(cargo)),
+        functools.partial(send_home_kernel, size, adds, extra is not None, len(cargo)),
         in_specs=in_specs,
         out_specs=out_specs,
         out_shape=shapes,
@@ -376,7 +380,7 @@
         compiler_params=pltpu.CompilerParams(
             collective_id=number, has_side_effects=True, vmem_limit_bytes=VMEM_BYTES
         ),
-        cost_estimate=pl.CostEstimate(flops=0, bytes_accessed=12 * total * width, transcendentals=0),
+        cost_estimate=pl.CostEstimate(flops=0, bytes_accessed=moved, transcendentals=0),
     )(*operands)
     return results if len(shapes) > 1 else results[0]
 
@@ -593,19 +597,39 @@
     )(token_half, token_rows, routes, kv_rows, query_piece, out_piece)
 
 
-def expert_kernel(world, *refs):
+def expert_kernel(world, steps, *refs):
     rows_ref, cot_ref, mix_ref = refs[:3]
     gates, ups, downs = (refs[3 + n * world : 3 + (n + 1) * world] for n in range(3))
-    hidden_ref, d_gate_ref, d_up_ref, db_ref, out_ref, mix_grad_ref = refs[3 + 3 * world : 9 + 3 * world]
-    db_sum, out_sum = refs[9 + 3 * world :]
+    near_ref, landed_ref, db_ref, out_ref, mix_grad_ref = refs[3 + 3 * world : 8 + 3 * world]
+    db_sum, out_sum, rows_t_ref, cot_t_ref, far, send_sem, recv_sem = refs[8 + 3 * world :]
     step = pl.program_id(0)
-    width = rows_ref.shape[1] // world
+    slot = lax.rem(step, 2)
+    features = rows_ref.shape[1]
+    width = features // world
+    half = features // 2
+    tile = near_ref.shape[2]
+    other_core = {"fsdp": xor_index(lax.axis_index("fsdp"), 1)}
+
+    def far_copy(at, place):
+        columns = pl.ds(pl.multiple_of(at * tile, 128), tile)
+        return pltpu.make_async_remote_copy(
+            src_ref=far.at[place],
+            dst_ref=landed_ref.at[:, :, columns],
+            send_sem=send_sem.at[place],
+            recv_sem=recv_sem.at[at],
+            device_id=other_core,
+            device_id_type=pl.DeviceIdType.MESH,
+        )
 
     @pl.when(step == 0)
     def _():
+        meet([other_core])
         db_sum[...] = jnp.zeros_like(db_sum)
         out_sum[...] = jnp.zeros_like(out_sum)
         mix_grad_ref[...] = jnp.zeros_like(mix_grad_ref)
+        for at in range(0, features, tile):
+            rows_t_ref[at : at + tile, :] = rows_ref[:, at : at + tile].T
+            cot_t_ref[at : at + tile, :] = cot_ref[:, at : at + tile].T
 
     gate_lin, up_lin, d_hidden = None, None, None
     for n in range(world):
@@ -621,57 +645,115 @@
     sigmoid_gate = 1.0 / (1.0 + jnp.exp(-gate_lin))
     swish = gate_lin * sigmoid_gate
     hidden = swish * up_lin
-    mix_grad_ref[...] += jnp.broadcast_to(
-        jnp.sum(hidden * d_hidden, axis=1, keepdims=True), mix_grad_ref.shape
-    )
-    d_gated = d_hidden * mix_ref[:, :1]
+    mix_grad = hidden * d_hidden
+    for at in range(0, tile, HEAD):
+        mix_grad_ref[...] += mix_grad[:, at : at + HEAD]
+    mix = jnp.concatenate([mix_ref[...]] * (tile // HEAD), axis=1)
+    d_gated = d_hidden * mix
     hidden_low = hidden.astype(LOW)
+    mixed_low = (hidden * mix).astype(LOW)
     d_gate = (d_gated * up_lin * sigmoid_gate * (1.0 + gate_lin * (1.0 - sigmoid_gate))).astype(LOW)
     d_up = (d_gated * swish).astype(LOW)
-    hidden_ref[...] = hidden_low
-    d_gate_ref[...] = d_gate
-    d_up_ref[...] = d_up
     for n in range(world):
         columns = slice(n * width, (n + 1) * width)
         out_sum[:, columns] += matmul(hidden_low, downs[n][...])
         db_sum[:, columns] += matmul_nt(d_gate, gates[n][...]) + matmul_nt(d_up, ups[n][...])
 
-    @pl.when(step == pl.num_programs(0) - 1)
+    @pl.when(step >= 2)
+    def _():
+        far_copy(step - 2, slot).wait_send()
+
+    pairs = ((rows_t_ref, d_gate), (rows_t_ref, d_up), (cot_t_ref, mixed_low))
+    for n, (left, right) in enumerate(pairs):
+        far[slot, n] = matmul(left[half:, :], right).astype(LOW)
+    far_copy(step, slot).start()
+    for n, (left, right) in enumerate(pairs):
+        near_ref[n] = matmul(left[:half, :], right).astype(LOW)
+
+    @pl.when(step == steps - 1)
     def _():
         db_ref[...] = db_sum[...].astype(LOW)
         out_ref[...] = out_sum[...].astype(LOW)
-
-
-def expert_both_ways(rows, cot_rows, mix_rows, gate_pieces, up_pieces, down_pieces):
+        for last in range(max(steps - 2, 0), steps):
+            far_copy(last, last % 2).wait_send()
+        for last in range(steps):
+            far_copy(last, last % 2).wait_recv()
+
+
+def expert_both_ways(rows, cot_rows, mix_rows, pieces, first, steps, number):
+    gate_pieces, up_pieces, down_pieces = pieces
     world = len(gate_pieces)
     slots, features = rows.shape
-    depth, hidden_width = gate_pieces[0].shape
-    tile = 256
+    depth = gate_pieces[0].shape[0]
+    tile = TILE
     once = pl.Buffered(1)
-    whole = lambda width: pl.BlockSpec((slots, width), lambda i: (0, 0), pipeline_mode=once)
+    whole = lambda value: pl.BlockSpec(value.shape, lambda i: (0, 0), pipeline_mode=once)
     kept = lambda width: pl.BlockSpec((slots, width), lambda i: (0, 0))
-    tall = pl.BlockSpec((depth, tile), lambda i: (0, i))
-    flat = pl.BlockSpec((tile, depth), lambda i: (i, 0))
-    strip = pl.BlockSpec((slots, tile), lambda i: (0, i))
-    low = lambda width: jax.ShapeDtypeStruct((slots, width), LOW)
+    tall = pl.BlockSpec((depth, tile), lambda i: (0, i + first))
+    flat = pl.BlockSpec((tile, depth), lambda i: (i + first, 0))
+    low = lambda *shape: jax.ShapeDtypeStruct(shape, LOW)
+    grads = low(3, features // 2, steps * tile)
     return pl.pallas_call(
-        functools.partial(expert_kernel, world),
-        grid=(hidden_width // tile,),
-        in_specs=[whole(features), whole(features), whole(HEAD)]
+        functools.partial(expert_kernel, world, steps),
+        grid=(steps,),
+        in_specs=[whole(rows), whole(cot_rows), whole(mix_rows)]
         + [tall] * (2 * world)
         + [flat] * world,
-        out_specs=[strip] * 3 + [kept(features)] * 2 + [kept(HEAD)],
-        out_shape=[low(hidden_width)] * 3
-        + [low(features)] * 2
-        + [jax.ShapeDtypeStruct((slots, HEAD), FULL)],
-        scratch_shapes=[pltpu.VMEM((slots, features), FULL)] * 2,
-        compiler_params=pltpu.CompilerParams(vmem_limit_bytes=VMEM_BYTES),
+        out_specs=[
+            pl.BlockSpec((3, features // 2, tile), lambda i: (0, 0, i)),
+            pl.BlockSpec(memory_space=pl.ANY),
+            kept(features),
+            kept(features),
+            kept(HEAD),
+        ],
+        out_shape=[
+            grads,
+            grads,
+            low(slots, features),
+            low(slots, features),
+            jax.ShapeDtypeStruct((slots, HEAD), FULL),
+        ],
+        scratch_shapes=[
+            pltpu.VMEM((slots, features), FULL),
+            pltpu.VMEM((slots, features), FULL),
+            pltpu.VMEM((features, slots), LOW),
+            pltpu.VMEM((features, slots), LOW),
+            pltpu.VMEM((2, 3, features // 2, tile), LOW),
+            pltpu.SemaphoreType.DMA((2,)),
+            pltpu.SemaphoreType.DMA((steps,)),
+        ],
+        compiler_params=pltpu.CompilerParams(
+            collective_id=number, has_side_effects=True, vmem_limit_bytes=VMEM_BYTES
+        ),
         cost_estimate=pl.CostEstimate(
-            flops=12 * slots * features * hidden_width,
-            bytes_accessed=6 * features * hidden_width,
-            transcendentals=slots * hidden_width,
+            flops=0, bytes_accessed=2 * slots * features, transcendentals=0
         ),
     )(rows, cot_rows, mix_rows, *gate_pieces, *up_pieces, *down_pieces)
+
+
+def scatter_rest(near, landed):
+    pieces = lax.axis_size("fsdp")
+    arrived, high, bit = [landed], near.shape[1], 2
+
+    def part(low, high):
+        total = near[:, low:high].astype(FULL)
+        for block in arrived:
+            total = total + block[:, low:high].astype(FULL)
+        return total
+
+    while True:
+        sent = part(high // 2, high).astype(LOW)
+        high //= 2
+        if 2 * bit >= pieces:
+            break
+        arrived.append(swap(sent, "fsdp", bit))
+        bit *= 2
+
+    def finish(last):
+        arrived.append(last)
+        return part(0, high)
+
+    return sent, finish
 
 
 def scatter_start(product, features, first_dim):
@@ -984,29 +1066,27 @@
     row_mix = mix_of(matmul(ffn_rows, router2), row_onehot.astype(FULL))
     mine_too = (row_routes == mine.astype(FULL)).astype(FULL)
     mix_rows = jnp.broadcast_to(jnp.sum(row_mix * mine_too, axis=1, keepdims=True), (slots, HEAD))
-    hidden_low, d_gate_low, d_up_low, db_rows, ffn_out, mix_grad_rows = expert_both_ways(
-        ffn_rows,
-        cot_rows,
-        mix_rows,
-        gate_all,
-        up_all,
-        with_neighbours(down_pieces, ffn_rows),
-    )
+    pieces = (gate_all, up_all, with_neighbours(down_pieces, ffn_rows))
+    tiles = gate_proj.shape[2] // TILE
+    count_one = (tiles + 1) // 2
+    near_one, landed_one, db_one, out_one, mix_grad_one = expert_both_ways(
+        ffn_rows, cot_rows, mix_rows, pieces, 0, count_one, 7
+    )
+    sent_one, finish_one = scatter_rest(near_one, landed_one)
+    back_one = last_step(sent_one)
+    near_two, landed_two, db_two, out_two, mix_grad_two = expert_both_ways(
+        after(ffn_rows, sent_one), cot_rows, mix_rows, pieces, count_one, tiles - count_one, 8
+    )
+    sent_two, finish_two = scatter_rest(near_two, landed_two)
+    back_two = last_step(sent_two)
+    db_rows = (db_one.astype(FULL) + db_two.astype(FULL)).astype(LOW)
+    ffn_out = (out_one.astype(FULL) + out_two.astype(FULL)).astype(LOW)
     mix_grad_rows = jnp.pad(
-        mix_grad_rows[:, 0].reshape(groups, 1, capacity), ((0, 0), (0, 7), (0, 256 - capacity))
-    )
-    dz_rows = (cot_rows.astype(FULL) * mix_rows[:, :1]).astype(LOW)
-    down_sent, down_finish = scatter_start(
-        lambda low, high: matmul_tn(hidden_low, dz_rows[:, low:high]), features, 1
-    )
-    down_back = last_step(down_sent)
-    d_both = jnp.concatenate([d_gate_low, d_up_low], axis=1)
-    both_sent, both_finish = scatter_start(
-        lambda low, high: matmul_tn(ffn_rows[:, low:high], d_both), features, 0
-    )
-    both_back = last_step(both_sent)
-    db_back, mix_grad_back = send_home(after(db_rows, down_sent), 3, extra=mix_grad_rows)
-    db_back = after(db_back, down_back)
+        jnp.sum(mix_grad_one + mix_grad_two, axis=1).reshape(groups, 1, capacity),
+        ((0, 0), (0, 7), (0, 256 - capacity)),
+    )
+    db_back, mix_grad_back = send_home(after(db_rows, sent_two), 3, extra=mix_grad_rows)
+    db_back = after(db_back, back_one)
     mix_grad_back = mix_grad_back[:, 0, :capacity].reshape(1, slots)
 
     experts = jnp.arange(expert_count, dtype=jnp.int32)
@@ -1037,12 +1117,12 @@
     dy_slots = jnp.zeros((slots, half_width), FULL)
     for k in range(picks_each):
         dy_slots = dy_slots + matmul_tn(attn_picks[k], (attn_mix[:, k : k + 1] * d_attended).astype(LOW))
-    dy_rows = send_out(after(dy_slots.astype(LOW), both_sent), 4)
+    dy_rows = send_out(dy_slots.astype(LOW), 4)
     d_heads = matmul_nt(dy_rows, out_full).astype(LOW)
     dq_low, dk_low, dv_low = attend_back(
         q_low, k_low, v_low, d_heads, log_sum, query_table, key_table, groups
     )
-    dkv_low = jnp.concatenate([dk_low, dv_low], axis=1)
+    dkv_low = after(jnp.concatenate([dk_low, dv_low], axis=1), back_two)
     da_rows = matmul_nt(dq_low, query_full).astype(LOW).reshape(groups, capacity, features)
     da_seq = jnp.einsum("bsr,bsd->brd", expert_onehot, da_rows, preferred_element_type=FULL)
     da_seq = da_seq.reshape(groups * rows_here, features) + matmul_nt(dkv_low, kv_full)
@@ -1055,16 +1135,16 @@
     query_sent, query_finish = scatter_start(
         lambda low, high: matmul_tn(rows_in[:, low:high], dq_low), features, 0
     )
-    ffn_back = come_home(after(ffn_out, dy_rows))
-    da_half, kv_back, out_back = send_home(
-        after(da_seq.astype(LOW), both_back, ffn_back, query_sent), 5, cargo=(kv_sent, out_sent), add_up=True
+    da_half, ffn_back, kv_back, query_back, out_back = send_home(
+        da_seq.astype(LOW), 5, cargo=(kv_sent, query_sent, out_sent), add_up=True, more=ffn_out
     )
     kv_part = kv_finish(kv_back)
-    query_grad = query_finish(last_step(after(query_sent, da_half)))
+    query_grad = query_finish(query_back)
     out_grad = out_finish(out_back)
-    down_grad = down_finish(after(down_back, da_half))
-    both_grad = both_finish(after(both_back, da_half))
-    gate_grad, up_grad = jnp.split(both_grad, 2, axis=1)
+    grads = jnp.concatenate(
+        [finish_one(after(back_one, kv_part)), finish_two(after(back_two, kv_part))], axis=2
+    )
+    gate_grad, up_grad, down_grad = grads[0], grads[1], grads[2].T
     kv_grad = block_for(kv_part, 0)
     kv_part_low = kv_part.astype(LOW)
     for distance in far_first(groups):
@@ -1102,7 +1182,7 @@
     small = from_spread(join_halves(small, swap(small, "tp", 1)), 1)
     prob_sums = jnp.concatenate([jnp.sum(attn_probs, axis=0), jnp.sum(ffn_probs, axis=0)])
     small = jnp.concatenate([small, jnp.pad(prob_sums, (0, features - prob_sums.shape[0]))[None]], axis=0)
-    small = all_sum(small, ("ctx", "fsdp"))
+    small = all_sum(small, ("fsdp", "ctx"))
     prob_sums = small[-1, : 2 * expert_count].reshape(2, expert_count)
     losses = expert_count * jnp.sum(share * prob_sums / all_tokens, axis=1)
     return (

time: 899 us -> 897 us (level)
  Pallas kernels: 459 us -> 541 us
  waiting for transfers between devices: 142 us -> 86.1 us
  matrix products: 154 us -> 117 us
  other arithmetic: 57 us -> 93.1 us
  local copies, waits for them, and re-layouts: 41.1 us -> 30.3 us
  starting transfers between devices: 38 us -> 28.6 us
    pallas_call x4 -> x5, Pallas kernels: 225 us -> 303 us  [the longest x3 181 us: send_home(): pl.pallas_call(functools.partial(send_home_kernel, size, adds, extra is n...]
    ppermute x46 -> x36, waiting for transfers between devices: 142 us -> 86.1 us  [swap(): return lax.ppermute(value, axis, [(i, i ^ distance) for i in range(size)])]
    dot_general x19 -> x13, matrix products: 82.4 us -> 38.4 us  [matmul_tn(): lax.dot_general(lhs, rhs, (((0,), (0,)), ((), ())), preferred_element_typ...]
    convert_element_type x3 -> x4, other arithmetic: 1.1 us -> 21.6 us  [the longest x2 13.6 us: scatter_rest(): sent = part(high // 2, high).astype(LOW)]
    dot_general x16, matrix products: 39.3 us -> 49.6 us  [matmul(): return jnp.dot(lhs, rhs, preferred_element_type=FULL)]
    broadcast_in_dim x1 -> x0, local copies, waits for them, and re-layouts: 9.5 us -> none  [on_device(): up_grad[None]]
    ppermute x46 -> x36, starting transfers between devices: 38 us -> 28.6 us  [swap(): return lax.ppermute(value, axis, [(i, i ^ distance) for i in range(size)])]
  transfers between devices with their start and end apart: 46 -> 36, of which waited for: 24 -> 15; matrix products, arithmetic and copies ran while one was open for 23% -> 20% of each run, Pallas kernels for 23% -> 37%
where the time goes in v4:
time: 897 us; the launch traced here: 899 us
  Pallas kernels  541 us (60%)
  matrix products  117 us (13%)
  other arithmetic  93.1 us (10%)
  waiting for transfers between devices  86.1 us (10%)
  local copies, waits for them, and re-layouts  30.3 us (3%)
  starting transfers between devices  28.6 us (3%)
    pallas_call x3, Pallas kernels, send_home(): pl.pallas_call(functools.partial(send_home_kernel, size, adds, extra is n...  181 us
    pallas_call x2, Pallas kernels, expert_both_ways(): pl.pallas_call(functools.partial(expert_kernel, world, steps), grid=(step...  122 us
    pallas_call x1, Pallas kernels, prologue(): pl.pallas_call(functools.partial(prologue_kernel, (groups, world)), in_sp...  110 us
    ppermute x36, waiting for transfers between devices, swap(): return lax.ppermute(value, axis, [(i, i ^ distance) for i in range(size)])  86.1 us
    pallas_call x2, Pallas kernels, send_out(): pl.pallas_call(functools.partial(send_out_kernel, size), in_specs=[pl.Blo...  85.8 us
    dot_general x16, matrix products, matmul(): return jnp.dot(lhs, rhs, preferred_element_type=FULL)  49.6 us
    dot_general x13, matrix products, matmul_tn(): lax.dot_general(lhs, rhs, (((0,), (0,)), ((), ())), preferred_element_typ...  38.4 us
    ppermute x36, starting transfers between devices, swap(): return lax.ppermute(value, axis, [(i, i ^ distance) for i in range(size)])  28.6 us
  transfers between devices with their start and end apart: 36, of which 15 were waited for; matrix products, arithmetic and copies ran while one was open for 20% of the time, Pallas kernels for 37%

profile of v4, /device:TPU:0, one launch (start us, length us, event | category | flops | bytes accessed | tf_op | source)
XLA Modules:
  0.0 898.6 jit_solution(5976478529905819892)
XLA Ops:
  8.9 109.6 %shard_map.271 = (bf16[2,1024,1024]{2,1,0:T(8,128)(2,1)}, s32[4,4,8,256]{3,2,1,0:T(8,128)}, bf16[2048,2048]{1,0:T(8,128)(2,1)}, bf16[2048,1024]{1,0:T(8,128)(2,1)}, bf16[4,1024,512]{2,1,0:T(8,128)(2,1)}) custom-call(bf16[256,1024]{1,0:T(8,128)(2,1)} %maximum_select_fusion.refs_0_, bf16[256,2048]{1,0:T(8,128)(2,1)} %pad_maximum_fusion.4.refs_1_, ...), custom_call_target="tpu_custom_call" | custom-call | bytes 100000000 | tf_op jit(solution)/shard_map/pallas_call | solution.py:581
  144.9 14.0 %fusion.137.k_lin.v_lin = f32[1024,2048]{1,0:T(8,128)} fusion(bf16[1024,2048]{1,0:T(8,128)(2,1)S(1)} %copy-done.6, bf16[2048,2048]{1,0:T(8,128)(2,1)} %get-tuple-element.66), kind=kOutput, calls=%fused_computation.369 | convolution fusion | flops 8589934592 | bytes 20971520 | tf_op jit(solution)/shard_map/dot_general | solution.py:24
  166.9 19.1 %shard_map.272 = (bf16[640,1024]{1,0:T(8,128)(2,1)}, bf16[1024,1024]{1,0:T(8,128)(2,1)}, bf16[1024,1024]{1,0:T(8,128)(2,1)}, bf16[640,1024]{1,0:T(8,128)(2,1)}, f32[640,1024]{1,0:T(8,128)}) custom-call(f32[640,1024]{1,0:T(8,128)} %fusion.136.q_lin, f32[1024,2048]{1,0:T(8,128)} %fusion.137.k_lin.v_lin, f32[1024,2048]{1,0:T(8,128)} %fusion.137.k_lin.v_lin, ...), custom_call_target="tpu_custom_call" | custom-call | bytes 20971520 | tf_op jit(solution)/shard_map/pallas_call | solution.py:832
  186.1 18.2 %convolution_convert_fusion.2.refs_0_ = bf16[640,2048]{1,0:T(8,128)(2,1)} fusion(bf16[640,1024]{1,0:T(8,128)(2,1)} %get-tuple-element.67, bf16[1024,512]{1,0:T(8,128)(2,1)S(1)} %get-tuple-element.189, bf16[1024,512]{1,0:T(8,128)(2,1)S(1)} %get-tuple-element.190, bf16[1024,512]{1,0:T(8,128)(2,1)S(1)} %get-tuple-element.191, ...), kind=kOutput, calls=%fused_computation.36 | convolution fusion | flops 2702442496 | bytes 8126464 | tf_op jit(solution)/shard_map/dot_general | solution.py:24
  218.8 6.0 collective-permute-done.2
  229.7 36.3 %shard_map.273 = bf16[640,1024]{1,0:T(8,128)(2,1)} custom-call(bf16[640,2048]{1,0:T(8,128)(2,1)} %convolution_convert_fusion.2.refs_0_), custom_call_target="tpu_custom_call" | custom-call | bytes 7864320 | tf_op jit(solution)/shard_map/pallas_call | solution.py:374
  289.8 44.5 %shard_map.274.refs_0_ = bf16[640,2048]{1,0:T(8,128)(2,1)} custom-call(bf16[640,1024]{1,0:T(8,128)(2,1)} %convolution_convert_fusion.6.rows_ref), custom_call_target="tpu_custom_call" | custom-call | bytes 7864320 | tf_op jit(solution)/shard_map/pallas_call | solution.py:234
  348.8 65.2 %shard_map.275 = (bf16[3,1024,1536]{2,1,0:T(8,128)(2,1)}, bf16[3,1024,1536]{2,1,0:T(8,128)(2,1)}, bf16[640,2048]{1,0:T(8,128)(2,1)}, bf16[640,2048]{1,0:T(8,128)(2,1)}, f32[640,128]{1,0:T(8,128)}) custom-call(bf16[640,2048]{1,0:T(8,128)(2,1)} %shard_map.274.refs_0_, bf16[640,2048]{1,0:T(8,128)(2,1)} %copy-done, f32[640,128]{1,0:T(8,128)} %broadcast_in_dim.40.refs_2_, ...), custom_call_target="tpu_custom_call" | custom-call | bytes 2621440 | tf_op jit(solution)/shard_map/pallas_call | solution.py:696
  414.0 7.3 add_convert_fusion
  422.3 56.4 %shard_map.276 = (bf16[3,1024,1280]{2,1,0:T(8,128)(2,1)}, bf16[3,1024,1280]{2,1,0:T(8,128)(2,1)}, bf16[640,2048]{1,0:T(8,128)(2,1)}, bf16[640,2048]{1,0:T(8,128)(2,1)}, f32[640,128]{1,0:T(8,128)}) custom-call(bf16[640,2048]{1,0:T(8,128)(2,1)} %shard_map.274.refs_0_, bf16[640,2048]{1,0:T(8,128)(2,1)} %copy-done, f32[640,128]{1,0:T(8,128)} %broadcast_in_dim.40.refs_2_, ...), custom_call_target="tpu_custom_call" | custom-call | bytes 2621440 | tf_op jit(solution)/shard_map/pallas_call | solution.py:696
  480.0 6.3 add_convert_fusion.1
  490.9 45.1 %shard_map.277 = (bf16[640,1024]{1,0:T(8,128)(2,1)}, f32[4,8,256]{2,1,0:T(8,128)}) custom-call(bf16[640,2048]{1,0:T(8,128)(2,1)} %add_convert_fusion.3.refs_0_, f32[4,8,256]{2,1,0:T(8,128)} %pad.8.refs_1_), custom_call_target="tpu_custom_call" | custom-call | bytes 7864320 | tf_op jit(solution)/shard_map/pallas_call | solution.py:374
  552.3 41.3 %shard_map.278 = bf16[640,2048]{1,0:T(8,128)(2,1)} custom-call(bf16[640,1024]{1,0:T(8,128)(2,1)} %add_convert_fusion.5.rows_ref), custom_call_target="tpu_custom_call" | custom-call | bytes 7864320 | tf_op jit(solution)/shard_map/pallas_call | solution.py:234
  593.6 5.7 convolution_convert_fusion.5.d_heads
  599.4 23.5 %shard_map.279 = (bf16[640,1024]{1,0:T(8,128)(2,1)}, bf16[1024,1024]{1,0:T(8,128)(2,1)}, bf16[1024,1024]{1,0:T(8,128)(2,1)}) custom-call(bf16[640,1024]{1,0:T(8,128)(2,1)} %get-tuple-element.71.q_low, bf16[1024,1024]{1,0:T(8,128)(2,1)} %get-tuple-element.72.k_low, bf16[1024,1024]{1,0:T(8,128)(2,1)} %get-tuple-element.73.v_low, ...), custom_call_target="tpu_custom_call" | custom-call | bytes 14680064 | tf_op jit(solution)/shard_map/pallas_call | solution.py:887
  636.3 6.3 convolution_convert_fusion
  644.0 13.2 %fusion.3.refs_0_ = bf16[1024,2048]{1,0:T(8,128)(2,1)} fusion(f32[4,256,2048]{2,1,0:T(8,128)S(1)} %fusion.51, bf16[1024,2048]{1,0:T(8,128)(2,1)S(1)} %pad_maximum_fusion.3, bf16[2048,2048]{1,0:T(8,128)(2,1)} %get-tuple-element.66), kind=kOutput, calls=%fused_computation.12 | convolution fusion | flops 8594128896 | bytes 25165824 | tf_op jit(solution)/shard_map/dot_general | solution.py:32
  678.4 99.9 %shard_map.280 = (f32[256,1024]{1,0:T(8,128)}, bf16[640,1024]{1,0:T(8,128)(2,1)}, bf16[512,2048]{1,0:T(8,128)(2,1)}, bf16[512,1024]{1,0:T(8,128)(2,1)}, bf16[1024,512]{1,0:T(8,128)(2,1)}) custom-call(bf16[1024,2048]{1,0:T(8,128)(2,1)} %fusion.3.refs_0_, bf16[640,2048]{1,0:T(8,128)(2,1)} %add_convert_fusion.2.refs_1_, ...), custom_call_target="tpu_custom_call" | custom-call | bytes 20447232 | tf_op jit(solution)/shard_map/pallas_call | solution.py:374
  778.3 6.2 fusion.118
  784.5 7.3 convert_add_fusion
  791.8 7.2 convert_add_fusion.1
  799.0 8.4 fusion.6
  807.4 6.4 copy.56
  837.0 41.1 %collective-permute-done.31 = f32[11,2048]{1,0:T(8,128)S(1)} collective-permute-done((f32[11,2048]{1,0:T(8,128)S(1)}, f32[11,2048]{1,0:T(8,128)S(1)}, u32[]{:S(2)}, u32[]{:S(2)}) %collective-permute-start.31) | collective-permute-done | bytes 90144 | tf_op jit(solution)/shard_map/ppermute | solution.py:41
  (442 shorter events, 201.8 us)
Async XLA Ops:
  119.5 85.9 %collective-permute-start.3 = (bf16[160,1024]{1,0:T(8,128)(2,1)}, bf16[160,1024]{1,0:T(8,128)(2,1)}, u32[]{:S(2)}, u32[]{:S(2)}) collective-permute-start(bf16[160,1024]{1,0:T(8,128)(2,1)} %get-tuple-element.200), channel_id=1, source_target_pairs={{0,4},{2,6},{4,0},{6,2},{1,5},{3,7},{5,1},{7,3},{8,12},{10,14},{12... | collective-permute-start | bytes 983048 | tf_op jit(solution)/shard_map/ppermute | solution.py:41
  119.5 87.4 %collective-permute-start.1 = (bf16[160,1024]{1,0:T(8,128)(2,1)}, bf16[160,1024]{1,0:T(8,128)(2,1)}, u32[]{:S(2)}, u32[]{:S(2)}) collective-permute-start(bf16[160,1024]{1,0:T(8,128)(2,1)} %get-tuple-element.201), channel_id=1, source_target_pairs={{0,2},{2,0},{4,6},{6,4},{1,3},{3,1},{5,7},{7,5},{8,10},{10,8},{12,... | collective-permute-start | bytes 983048 | tf_op jit(solution)/shard_map/ppermute | solution.py:41
  122.4 85.1 %collective-permute-start = (bf16[160,1024]{1,0:T(8,128)(2,1)S(1)}, bf16[160,1024]{1,0:T(8,128)(2,1)}, u32[]{:S(2)}, u32[]{:S(2)}) collective-permute-start(bf16[160,1024]{1,0:T(8,128)(2,1)S(1)} %get-tuple-element.202), channel_id=1, source_target_pairs={{0,1},{1,0},{2,3},{3,2},{4,5},{5,4},{6,7},{7,6},{8,9},{9,8},{10,11... | collective-permute-start | bytes 983048 | tf_op jit(solution)/shard_map/ppermute | solution.py:41
  123.9 148.4 %collective-permute-start.9 = (bf16[512,2816]{1,0:T(8,128)(2,1)}, bf16[512,2816]{1,0:T(8,128)(2,1)}, u32[]{:S(2)}, u32[]{:S(2)}) collective-permute-start(bf16[512,2816]{1,0:T(8,128)(2,1)} %bitcast.25.refs_3_), channel_id=1, source_target_pairs={{0,16},{8,24},{16,0},{24,8},{1,17},{9,25},{17,1},{25,9},{2,18},{10... | collective-permute-start | bytes 8650760 | tf_op jit(solution)/shard_map/ppermute | solution.py:41
  124.4 147.9 %collective-permute-start.12 = (bf16[512,2816]{1,0:T(8,128)(2,1)}, bf16[512,2816]{1,0:T(8,128)(2,1)}, u32[]{:S(2)}, u32[]{:S(2)}) collective-permute-start(bf16[512,2816]{1,0:T(8,128)(2,1)} %bitcast.26.refs_7_), channel_id=1, source_target_pairs={{0,16},{8,24},{16,0},{24,8},{1,17},{9,25},{17,1},{25,9},{2,18},{10... | collective-permute-start | bytes 8650760 | tf_op jit(solution)/shard_map/ppermute | solution.py:41
  207.5 17.3 %collective-permute-start.2 = (bf16[160,1024]{1,0:T(8,128)(2,1)}, bf16[160,1024]{1,0:T(8,128)(2,1)S(1)}, u32[]{:S(2)}, u32[]{:S(2)}) collective-permute-start(bf16[160,1024]{1,0:T(8,128)(2,1)} %collective-permute-done.1), channel_id=1, source_target_pairs={{0,1},{1,0},{2,3},{3,2},{4,5},{5,4},{6,7},{7,6},{8,9},{9,8},{10,11... | collective-permute-start | bytes 983048 | tf_op jit(solution)/shard_map/ppermute | solution.py:41
  216.0 13.5 %collective-permute-start.6 = (bf16[160,1024]{1,0:T(8,128)(2,1)S(1)}, bf16[160,1024]{1,0:T(8,128)(2,1)S(1)}, u32[]{:S(2)}, u32[]{:S(2)}) collective-permute-start(bf16[160,1024]{1,0:T(8,128)(2,1)S(1)} %collective-permute-done.5), channel_id=1, source_target_pairs={{0,1},{1,0},{2,3},{3,2},{4,5},{5,4},{6,7},{7,6},{8,9},{9,8},{10,11... | collective-permute-start | bytes 983048 | tf_op jit(solution)/shard_map/ppermute | solution.py:41
  271.8 13.4 %collective-permute-start.10 = (bf16[512,2816]{1,0:T(8,128)(2,1)}, bf16[512,2816]{1,0:T(8,128)(2,1)}, u32[]{:S(2)}, u32[]{:S(2)}) collective-permute-start(bf16[512,2816]{1,0:T(8,128)(2,1)} %bitcast.25.refs_3_), channel_id=1, source_target_pairs={{0,8},{8,0},{16,24},{24,16},{1,9},{9,1},{17,25},{25,17},{2,10},{10... | collective-permute-start | bytes 8650760 | tf_op jit(solution)/shard_map/ppermute | solution.py:41
  272.4 17.4 %collective-permute-start.11 = (bf16[512,2816]{1,0:T(8,128)(2,1)}, bf16[512,2816]{1,0:T(8,128)(2,1)}, u32[]{:S(2)}, u32[]{:S(2)}) collective-permute-start(bf16[512,2816]{1,0:T(8,128)(2,1)} %collective-permute-done.9.refs_4_), channel_id=1, source_target_pairs={{0,8},{8,0},{16,24},{24,16},{1,9},{9,1},{17,25},{25,17},{2,10},{10... | collective-permute-start | bytes 8650760 | tf_op jit(solution)/shard_map/ppermute | solution.py:41
  274.5 63.7 %collective-permute-start.15 = (bf16[2816,512]{1,0:T(8,128)(2,1)}, bf16[2816,512]{1,0:T(8,128)(2,1)}, u32[]{:S(2)}, u32[]{:S(2)}) collective-permute-start(bf16[2816,512]{1,0:T(8,128)(2,1)} %bitcast.27.refs_11_), channel_id=1, source_target_pairs={{0,16},{8,24},{16,0},{24,8},{1,17},{9,25},{17,1},{25,9},{2,18},{10... | collective-permute-start | bytes 8650760 | tf_op jit(solution)/shard_map/ppermute | solution.py:41
  340.8 81.1 %collective-permute-start.8 = (f32[256,4]{0,1:T(4,128)S(1)}, f32[256,4]{0,1:T(4,128)S(1)}, u32[]{:S(2)}, u32[]{:S(2)}) collective-permute-start(f32[256,4]{0,1:T(4,128)S(1)} %fusion.112), channel_id=1, source_target_pairs={{0,1},{1,0},{2,3},{3,2},{4,5},{5,4},{6,7},{7,6},{8,9},{9,8},{10,11... | collective-permute-start | bytes 12296 | tf_op jit(solution)/shard_map/ppermute | solution.py:41
  421.3 121.8 %collective-permute-start.18 = (bf16[3,512,1536]{2,1,0:T(8,128)(2,1)}, bf16[3,512,1536]{2,1,0:T(8,128)(2,1)}, u32[]{:S(2)}, u32[]{:S(2)}) collective-permute-start(bf16[3,512,1536]{2,1,0:T(8,128)(2,1)} %add_convert_fusion), channel_id=1, source_target_pairs={{0,16},{8,24},{16,0},{24,8},{1,17},{9,25},{17,1},{25,9},{2,18},{10... | collective-permute-start | bytes 14155784 | tf_op jit(solution)/shard_map/ppermute | solution.py:41
  486.2 149.5 %collective-permute-start.20 = (bf16[3,512,1280]{2,1,0:T(8,128)(2,1)}, bf16[3,512,1280]{2,1,0:T(8,128)(2,1)}, u32[]{:S(2)}, u32[]{:S(2)}) collective-permute-start(bf16[3,512,1280]{2,1,0:T(8,128)(2,1)} %add_convert_fusion.1), channel_id=1, source_target_pairs={{0,16},{8,24},{16,0},{24,8},{1,17},{9,25},{17,1},{25,9},{2,18},{10... | collective-permute-start | bytes 11796488 | tf_op jit(solution)/shard_map/ppermute | solution.py:41
  549.3 116.6 %collective-permute-start.25 = (f32[256,2]{0,1:T(2,128)S(1)}, f32[256,2]{0,1:T(2,128)S(1)}, u32[]{:S(2)}, u32[]{:S(2)}) collective-permute-start(f32[256,2]{0,1:T(2,128)S(1)} %pad_maximum_fusion.15), channel_id=1, source_target_pairs={{0,1},{1,0},{2,3},{3,2},{4,5},{5,4},{6,7},{7,6},{8,9},{9,8},{10,11... | collective-permute-start | bytes 6152 | tf_op jit(solution)/shard_map/ppermute | solution.py:41
  635.7 34.1 %collective-permute-start.23 = (bf16[1024,1024]{1,0:T(8,128)(2,1)}, bf16[1024,1024]{1,0:T(8,128)(2,1)}, u32[]{:S(2)}, u32[]{:S(2)}) collective-permute-start(bf16[1024,1024]{1,0:T(8,128)(2,1)} %convolution_convert_fusion.3), channel_id=1, source_target_pairs={{0,8},{8,0},{16,24},{24,16},{1,9},{9,1},{17,25},{25,17},{2,10},{10... | collective-permute-start | bytes 6291464 | tf_op jit(solution)/shard_map/ppermute | solution.py:41
  635.8 30.8 %collective-permute-start.22 = (bf16[1024,1024]{1,0:T(8,128)(2,1)}, bf16[1024,1024]{1,0:T(8,128)(2,1)}, u32[]{:S(2)}, u32[]{:S(2)}) collective-permute-start(bf16[1024,1024]{1,0:T(8,128)(2,1)} %convolution_convert_fusion.4), channel_id=1, source_target_pairs={{0,8},{8,0},{16,24},{24,16},{1,9},{9,1},{17,25},{25,17},{2,10},{10... | collective-permute-start | bytes 6291464 | tf_op jit(solution)/shard_map/ppermute | solution.py:41
  642.6 30.5 %collective-permute-start.21 = (bf16[1024,2048]{1,0:T(8,128)(2,1)}, bf16[1024,2048]{1,0:T(8,128)(2,1)}, u32[]{:S(2)}, u32[]{:S(2)}) collective-permute-start(bf16[1024,2048]{1,0:T(8,128)(2,1)} %convolution_convert_fusion), channel_id=1, source_target_pairs={{0,8},{8,0},{16,24},{24,16},{1,9},{9,1},{17,25},{25,17},{2,10},{10... | collective-permute-start | bytes 12582920 | tf_op jit(solution)/shard_map/ppermute | solution.py:41
  814.6 21.9 %collective-permute-start.26 = (f32[256,1]{0,1:T(1,128)S(1)}, f32[256,1]{0,1:T(1,128)S(1)}, u32[]{:S(2)}, u32[]{:S(2)}) collective-permute-start(f32[256,1]{0,1:T(1,128)S(1)} %bitcast.212), channel_id=1, source_target_pairs={{0,1},{1,0},{2,3},{3,2},{4,5},{5,4},{6,7},{7,6},{8,9},{9,8},{10,11... | collective-permute-start | bytes 3080 | tf_op jit(solution)/shard_map/ppermute | solution.py:41
  815.4 13.8 %collective-permute-start.28 = (f32[10,1024]{1,0:T(8,128)S(1)}, f32[10,1024]{1,0:T(8,128)S(1)}, u32[]{:S(2)}, u32[]{:S(2)}) collective-permute-start(f32[10,1024]{1,0:T(8,128)S(1)} %pad_maximum_fusion.10), channel_id=1, source_target_pairs={{0,1},{1,0},{2,3},{3,2},{4,5},{5,4},{6,7},{7,6},{8,9},{9,8},{10,11... | collective-permute-start | bytes 122888 | tf_op jit(solution)/shard_map/ppermute | solution.py:41
  824.8 62.8 %collective-permute-start.33 = (bf16[128,2048]{1,0:T(8,128)(2,1)}, bf16[128,2048]{1,0:T(8,128)(2,1)}, u32[]{:S(2)}, u32[]{:S(2)}) collective-permute-start(bf16[128,2048]{1,0:T(8,128)(2,1)} %get-tuple-element.196), channel_id=1, source_target_pairs={{0,4},{2,6},{4,0},{6,2},{1,5},{3,7},{5,1},{7,3},{8,12},{10,14},{12... | collective-permute-start | bytes 1572872 | tf_op jit(solution)/shard_map/ppermute | solution.py:41
  825.4 62.2 %collective-permute-start.35 = (bf16[128,2048]{1,0:T(8,128)(2,1)}, bf16[128,2048]{1,0:T(8,128)(2,1)}, u32[]{:S(2)}, u32[]{:S(2)}) collective-permute-start(bf16[128,2048]{1,0:T(8,128)(2,1)} %get-tuple-element.197), channel_id=1, source_target_pairs={{0,2},{2,0},{4,6},{6,4},{1,3},{3,1},{5,7},{7,5},{8,10},{10,8},{12,... | collective-permute-start | bytes 1572872 | tf_op jit(solution)/shard_map/ppermute | solution.py:41
  826.9 60.7 %collective-permute-start.34 = (bf16[128,2048]{1,0:T(8,128)(2,1)S(1)}, bf16[128,2048]{1,0:T(8,128)(2,1)}, u32[]{:S(2)}, u32[]{:S(2)}) collective-permute-start(bf16[128,2048]{1,0:T(8,128)(2,1)S(1)} %get-tuple-element.198), channel_id=1, source_target_pairs={{0,6},{2,4},{4,2},{6,0},{1,7},{3,5},{5,3},{7,1},{8,14},{10,12},{12... | collective-permute-start | bytes 1572872 | tf_op jit(solution)/shard_map/ppermute | solution.py:41
  835.8 50.7 %collective-permute-start.24 = (bf16[256,1024]{1,0:T(8,128)(2,1)S(1)}, bf16[256,1024]{1,0:T(8,128)(2,1)}, u32[]{:S(2)}, u32[]{:S(2)}) collective-permute-start(bf16[256,1024]{1,0:T(8,128)(2,1)S(1)} %fusion.20), channel_id=1, source_target_pairs={{0,1},{1,0},{2,3},{3,2},{4,5},{5,4},{6,7},{7,6},{8,9},{9,8},{10,11... | collective-permute-start | bytes 1572872 | tf_op jit(solution)/shard_map/ppermute | solution.py:41
  836.5 41.7 %collective-permute-start.31 = (f32[11,2048]{1,0:T(8,128)S(1)}, f32[11,2048]{1,0:T(8,128)S(1)}, u32[]{:S(2)}, u32[]{:S(2)}) collective-permute-start(f32[11,2048]{1,0:T(8,128)S(1)} %add.288), channel_id=1, source_target_pairs={{0,4},{2,6},{4,0},{6,2},{1,5},{3,7},{5,1},{7,3},{8,12},{10,14},{12... | collective-permute-start | bytes 270344 | tf_op jit(solution)/shard_map/ppermute | solution.py:41
  (116 other events, 2415.7 us)

commit v5 on v4

--- a/solution.py
+++ b/solution.py
@@ -68,7 +68,9 @@
 
 
 def with_neighbours(pieces, *earlier):
-    return pieces + [swap(after(item, *earlier), "fsdp", 1) for item in pieces]
+    return pieces + [swap(pieces[0], "fsdp", 1)] + [
+        swap(after(item, *earlier), "fsdp", 1) for item in pieces[1:]
+    ]
 
 
 def flip_blocks(value, axis, index, count):
@@ -140,14 +142,8 @@
 
 
 def spread_out(half_rows):
-    size = lax.axis_size("ctx")
-    blocks = [None] * size
-    for distance in far_first(size):
-        block = block_for(half_rows, distance)
-        if distance:
-            block = swap(block, "ctx", distance)
-        blocks[distance] = join_halves(block, swap(block, "tp", 1))
-    return place_blocks(blocks)
+    blocks = [block_for(half_rows, distance) for distance in range(lax.axis_size("ctx"))]
+    return blocks[:1] + [swap(blocks[distance], "ctx", distance) for distance in range(1, len(blocks))]
 
 
 def xor_index(index, distance):
@@ -597,66 +593,157 @@
     )(token_half, token_rows, routes, kv_rows, query_piece, out_piece)
 
 
-def expert_kernel(world, steps, *refs):
-    rows_ref, cot_ref, mix_ref = refs[:3]
-    gates, ups, downs = (refs[3 + n * world : 3 + (n + 1) * world] for n in range(3))
-    near_ref, landed_ref, db_ref, out_ref, mix_grad_ref = refs[3 + 3 * world : 8 + 3 * world]
-    db_sum, out_sum, rows_t_ref, cot_t_ref, far, send_sem, recv_sem = refs[8 + 3 * world :]
+def expert_forward_kernel(world, size, *refs):
+    rows_ref = refs[0]
+    gates, ups = refs[1 : 1 + world], refs[1 + world : 1 + 2 * world]
+    refs = refs[1 + 2 * world :]
+    blocks, refs = refs[:size], refs[size:]
+    hidden_ref, by_gate_ref, by_up_ref, cot_ref, y_land, y_send, y_recv = refs
+    width = rows_ref.shape[1] // world
+    mine, place = lax.axis_index("ctx"), lax.axis_index("tp")
+    other_tp = {"tp": 1 - place}
+    beside = [
+        remote(blocks[distance], y_land.at[distance], (y_send, y_recv), distance, other_tp)
+        for distance in range(size)
+    ]
+
+    @pl.when(pl.program_id(0) == 0)
+    def _():
+        meet([other_tp])
+        for copy in beside:
+            copy.start()
+
+    gate_lin, up_lin = None, None
+    for n in range(world):
+        columns = slice(n * width, (n + 1) * width)
+        gate_term = matmul(rows_ref[:, columns], gates[n][...])
+        up_term = matmul(rows_ref[:, columns], ups[n][...])
+        gate_lin = gate_lin + gate_term if n else gate_term
+        up_lin = up_lin + up_term if n else up_term
+    sigmoid_gate = 1.0 / (1.0 + jnp.exp(-gate_lin))
+    swish = gate_lin * sigmoid_gate
+    hidden_ref[...] = (swish * up_lin).astype(LOW)
+    by_gate_ref[...] = (up_lin * sigmoid_gate * (1.0 + gate_lin * (1.0 - sigmoid_gate))).astype(LOW)
+    by_up_ref[...] = swish.astype(LOW)
+
+    @pl.when(pl.program_id(0) == pl.num_programs(0) - 1)
+    def _():
+        rows, half = y_land.shape[1], y_land.shape[2]
+        for distance, copy in enumerate(beside):
+            copy.wait_recv()
+            own, theirs = blocks[distance][...], y_land[distance]
+            here = span(xor_index(mine, distance), rows)
+            cot_ref[here, :half] = jnp.where(place == 0, own, theirs)
+            cot_ref[here, half:] = jnp.where(place == 0, theirs, own)
+        for copy in beside:
+            copy.wait_send()
+
+
+def expert_forward(rows, gate_pieces, up_pieces, cot_blocks, number):
+    world, size = len(gate_pieces), len(cot_blocks)
+    slots, features = rows.shape
+    depth, hidden_width = gate_pieces[0].shape
+    tall = pl.BlockSpec((depth, TILE), lambda i: (0, i))
+    strip = pl.BlockSpec((slots, TILE), lambda i: (0, i))
+    whole = lambda value: pl.BlockSpec(value.shape, lambda i: (0, 0), pipeline_mode=pl.Buffered(1))
+    return pl.pallas_call(
+        functools.partial(expert_forward_kernel, world, size),
+        grid=(hidden_width // TILE,),
+        in_specs=[whole(rows)] + [tall] * (2 * world) + [whole(block) for block in cot_blocks],
+        out_specs=[strip] * 3 + [pl.BlockSpec((slots, features), lambda i: (0, 0))],
+        out_shape=[jax.ShapeDtypeStruct((slots, hidden_width), LOW)] * 3
+        + [jax.ShapeDtypeStruct((slots, features), LOW)],
+        scratch_shapes=[pltpu.VMEM((size,) + cot_blocks[0].shape, LOW)]
+        + [pltpu.SemaphoreType.DMA((size,))] * 2,
+        compiler_params=pltpu.CompilerParams(
+            collective_id=number, has_side_effects=True, vmem_limit_bytes=VMEM_BYTES
+        ),
+        cost_estimate=pl.CostEstimate(flops=0, bytes_accessed=2 * slots * features, transcendentals=0),
+    )(rows, *gate_pieces, *up_pieces, *cot_blocks)
+
+
+def expert_back_kernel(world, steps, size, *refs):
+    rows_ref, cot_ref, mix_ref, hidden_ref, by_gate_ref, by_up_ref = refs[:6]
+    gates, ups, downs = (refs[6 + n * world : 6 + (n + 1) * world] for n in range(3))
+    refs = refs[6 + 3 * world :]
+    part_ref, refs = (refs[0], refs[1:]) if size else (None, refs)
+    near_ref, landed_ref, db_ref, mix_grad_ref = refs[:4]
+    home_ref, refs = (refs[4], refs[5:]) if size else (None, refs[4:])
+    db_sum, rows_t_ref, cot_t_ref, far, send_sem, recv_sem = refs[:6]
     step = pl.program_id(0)
     slot = lax.rem(step, 2)
     features = rows_ref.shape[1]
     width = features // world
     half = features // 2
-    tile = near_ref.shape[2]
+    tile = near_ref.shape[3]
     other_core = {"fsdp": xor_index(lax.axis_index("fsdp"), 1)}
-
-    def far_copy(at, place):
-        columns = pl.ds(pl.multiple_of(at * tile, 128), tile)
+    peers = [other_core]
+    if size:
+        y_land, ready, z_land, y_send, y_recv, z_send, z_recv = refs[6:]
+        mine, place = lax.axis_index("ctx"), lax.axis_index("tp")
+        other_tp = {"tp": 1 - place}
+        at = [xor_index(mine, distance) for distance in range(size)]
+        peers = peers + [other_tp] + [{"ctx": at[distance]} for distance in range(1, size)]
+        home_rows, home_width = z_land.shape[1], z_land.shape[2]
+        away = pl.ds(pl.multiple_of((1 - place) * home_width, 128), home_width)
+        order = mixed_order(size)
+
+        def beside(distance):
+            return remote(
+                part_ref.at[span(at[distance], home_rows), away],
+                y_land.at[distance],
+                (y_send, y_recv),
+                distance,
+                other_tp,
+            )
+
+        def across(distance):
+            return remote(
+                ready.at[distance],
+                z_land.at[distance],
+                (z_send, z_recv),
+                distance,
+                {"ctx": at[distance]},
+            )
+
+    def far_copy(at_step, at_slot):
         return pltpu.make_async_remote_copy(
-            src_ref=far.at[place],
-            dst_ref=landed_ref.at[:, :, columns],
-            send_sem=send_sem.at[place],
-            recv_sem=recv_sem.at[at],
+            src_ref=far.at[at_slot],
+            dst_ref=landed_ref.at[at_step],
+            send_sem=send_sem.at[at_slot],
+            recv_sem=recv_sem.at[at_step],
             device_id=other_core,
             device_id_type=pl.DeviceIdType.MESH,
         )
 
     @pl.when(step == 0)
     def _():
-        meet([other_core])
+        meet(peers)
+        if size:
+            for distance in order:
+                beside(distance).start()
         db_sum[...] = jnp.zeros_like(db_sum)
-        out_sum[...] = jnp.zeros_like(out_sum)
         mix_grad_ref[...] = jnp.zeros_like(mix_grad_ref)
-        for at in range(0, features, tile):
-            rows_t_ref[at : at + tile, :] = rows_ref[:, at : at + tile].T
-            cot_t_ref[at : at + tile, :] = cot_ref[:, at : at + tile].T
-
-    gate_lin, up_lin, d_hidden = None, None, None
+        for place_at in range(0, features, tile):
+            rows_t_ref[place_at : place_at + tile, :] = rows_ref[:, place_at : place_at + tile].T
+            cot_t_ref[place_at : place_at + tile, :] = cot_ref[:, place_at : place_at + tile].T
+
+    d_hidden = None
     for n in range(world):
         columns = slice(n * width, (n + 1) * width)
-        terms = (
-            matmul(rows_ref[:, columns], gates[n][...]),
-            matmul(rows_ref[:, columns], ups[n][...]),
-            matmul_nt(cot_ref[:, columns], downs[n][...]),
-        )
-        if n:
-            terms = (gate_lin + terms[0], up_lin + terms[1], d_hidden + terms[2])
-        gate_lin, up_lin, d_hidden = terms
-    sigmoid_gate = 1.0 / (1.0 + jnp.exp(-gate_lin))
-    swish = gate_lin * sigmoid_gate
-    hidden = swish * up_lin
+        term = matmul_nt(cot_ref[:, columns], downs[n][...])
+        d_hidden = d_hidden + term if n else term
+    hidden = hidden_ref[...].astype(FULL)
     mix_grad = hidden * d_hidden
-    for at in range(0, tile, HEAD):
-        mix_grad_ref[...] += mix_grad[:, at : at + HEAD]
+    for place_at in range(0, tile, HEAD):
+        mix_grad_ref[...] += mix_grad[:, place_at : place_at + HEAD]
     mix = jnp.concatenate([mix_ref[...]] * (tile // HEAD), axis=1)
     d_gated = d_hidden * mix
-    hidden_low = hidden.astype(LOW)
     mixed_low = (hidden * mix).astype(LOW)
-    d_gate = (d_gated * up_lin * sigmoid_gate * (1.0 + gate_lin * (1.0 - sigmoid_gate))).astype(LOW)
-    d_up = (d_gated * swish).astype(LOW)
+    d_gate = (d_gated * by_gate_ref[...].astype(FULL)).astype(LOW)
+    d_up = (d_gated * by_up_ref[...].astype(FULL)).astype(LOW)
     for n in range(world):
         columns = slice(n * width, (n + 1) * width)
-        out_sum[:, columns] += matmul(hidden_low, downs[n][...])
         db_sum[:, columns] += matmul_nt(d_gate, gates[n][...]) + matmul_nt(d_up, ups[n][...])
 
     @pl.when(step >= 2)
@@ -668,19 +755,40 @@
         far[slot, n] = matmul(left[half:, :], right).astype(LOW)
     far_copy(step, slot).start()
     for n, (left, right) in enumerate(pairs):
-        near_ref[n] = matmul(left[:half, :], right).astype(LOW)
+        near_ref[0, n] = matmul(left[:half, :], right).astype(LOW)
+
+    if size:
+        for turn, distance in enumerate(order):
+
+            @pl.when(step == min(turn + 1, steps - 1))
+            def _():
+                beside(distance).wait_recv()
+                whole = part_ref[span(at[distance], home_rows), :]
+                own = jnp.where(place == 0, whole[:, :home_width], whole[:, home_width:])
+                total = (own.astype(FULL) + y_land[distance].astype(FULL)).astype(LOW)
+                if distance:
+                    ready[distance] = total
+                    across(distance).start()
+                else:
+                    home_ref[span(mine, home_rows), :] = total
 
     @pl.when(step == steps - 1)
     def _():
         db_ref[...] = db_sum[...].astype(LOW)
-        out_ref[...] = out_sum[...].astype(LOW)
         for last in range(max(steps - 2, 0), steps):
             far_copy(last, last % 2).wait_send()
         for last in range(steps):
             far_copy(last, last % 2).wait_recv()
-
-
-def expert_both_ways(rows, cot_rows, mix_rows, pieces, first, steps, number):
+        if size:
+            for distance in order:
+                beside(distance).wait_send()
+                if distance:
+                    across(distance).wait_recv()
+                    home_ref[span(at[distance], home_rows), :] = z_land[distance]
+                    across(distance).wait_send()
+
+
+def expert_back(rows, cot_rows, mix_rows, forward, pieces, first, steps, number, going_home=None):
     gate_pieces, up_pieces, down_pieces = pieces
     world = len(gate_pieces)
     slots, features = rows.shape
@@ -691,69 +799,107 @@
     kept = lambda width: pl.BlockSpec((slots, width), lambda i: (0, 0))
     tall = pl.BlockSpec((depth, tile), lambda i: (0, i + first))
     flat = pl.BlockSpec((tile, depth), lambda i: (i + first, 0))
+    strip = pl.BlockSpec((slots, tile), lambda i: (0, i + first))
     low = lambda *shape: jax.ShapeDtypeStruct(shape, LOW)
-    grads = low(3, features // 2, steps * tile)
+    grads = low(steps, 3, features // 2, tile)
+    operands = [rows, cot_rows, mix_rows, *forward, *gate_pieces, *up_pieces, *down_pieces]
+    in_specs = [whole(rows), whole(cot_rows), whole(mix_rows)] + [strip] * 3
+    in_specs += [tall] * (2 * world) + [flat] * world
+    out_specs = [
+        pl.BlockSpec((1, 3, features // 2, tile), lambda i: (i, 0, 0, 0)),
+        pl.BlockSpec(memory_space=pl.ANY),
+        kept(features),
+        kept(HEAD),
+    ]
+    out_shape = [grads, grads, low(slots, features), jax.ShapeDtypeStruct((slots, HEAD), FULL)]
+    scratch = [
+        pltpu.VMEM((slots, features), FULL),
+        pltpu.VMEM((features, slots), LOW),
+        pltpu.VMEM((features, slots), LOW),
+        pltpu.VMEM((2, 3, features // 2, tile), LOW),
+        pltpu.SemaphoreType.DMA((2,)),
+        pltpu.SemaphoreType.DMA((steps,)),
+    ]
+    size = 0
+    if going_home is not None:
+        size = lax.axis_size("ctx")
+        operands.append(going_home)
+        in_specs.append(whole(going_home))
+        out_specs.append(kept(features // 2))
+        out_shape.append(low(slots, features // 2))
+        scratch += [pltpu.VMEM((size, slots // size, features // 2), LOW)] * 3
+        scratch += [pltpu.SemaphoreType.DMA((size,))] * 4
     return pl.pallas_call(
-        functools.partial(expert_kernel, world, steps),
+        functools.partial(expert_back_kernel, world, steps, size),
         grid=(steps,),
-        in_specs=[whole(rows), whole(cot_rows), whole(mix_rows)]
-        + [tall] * (2 * world)
-        + [flat] * world,
-        out_specs=[
-            pl.BlockSpec((3, features // 2, tile), lambda i: (0, 0, i)),
-            pl.BlockSpec(memory_space=pl.ANY),
-            kept(features),
-            kept(features),
-            kept(HEAD),
-        ],
-        out_shape=[
-            grads,
-            grads,
-            low(slots, features),
-            low(slots, features),
-            jax.ShapeDtypeStruct((slots, HEAD), FULL),
-        ],
-        scratch_shapes=[
-            pltpu.VMEM((slots, features), FULL),
-            pltpu.VMEM((slots, features), FULL),
-            pltpu.VMEM((features, slots), LOW),
-            pltpu.VMEM((features, slots), LOW),
-            pltpu.VMEM((2, 3, features // 2, tile), LOW),
-            pltpu.SemaphoreType.DMA((2,)),
-            pltpu.SemaphoreType.DMA((steps,)),
-        ],
+        in_specs=in_specs,
+        out_specs=out_specs,
+        out_shape=out_shape,
+        scratch_shapes=scratch,
         compiler_params=pltpu.CompilerParams(
             collective_id=number, has_side_effects=True, vmem_limit_bytes=VMEM_BYTES
         ),
         cost_estimate=pl.CostEstimate(
             flops=0, bytes_accessed=2 * slots * features, transcendentals=0
         ),
-    )(rows, cot_rows, mix_rows, *gate_pieces, *up_pieces, *down_pieces)
+    )(*operands)
 
 
 def scatter_rest(near, landed):
     pieces = lax.axis_size("fsdp")
-    arrived, high, bit = [landed], near.shape[1], 2
-
-    def part(low, high):
-        total = near[:, low:high].astype(FULL)
-        for block in arrived:
-            total = total + block[:, low:high].astype(FULL)
-        return total
-
+    arrived, high, bit = [near, landed], near.shape[2], 2
     while True:
-        sent = part(high // 2, high).astype(LOW)
+        total = arrived[0][:, :, high // 2 : high].astype(FULL)
+        for block in arrived[1:]:
+            total = total + block[:, :, high // 2 : high].astype(FULL)
+        sent = total.astype(LOW)
         high //= 2
         if 2 * bit >= pieces:
-            break
+            return sent, arrived
         arrived.append(swap(sent, "fsdp", bit))
         bit *= 2
 
-    def finish(last):
-        arrived.append(last)
-        return part(0, high)
-
-    return sent, finish
+
+def finish_kernel(count, steps_one, *refs):
+    ones, twos = refs[:count], refs[count : 2 * count]
+    outs = refs[2 * count :]
+
+    def add_up(parts):
+        for n, out in enumerate(outs):
+            total = parts[0][0, n].astype(FULL)
+            for part in parts[1:]:
+                total = total + part[0, n].astype(FULL)
+            out[...] = total.T if n == 2 else total
+
+    @pl.when(pl.program_id(0) < steps_one)
+    def _():
+        add_up(ones)
+
+    @pl.when(pl.program_id(0) >= steps_one)
+    def _():
+        add_up(twos)
+
+
+def finish_experts(ones, twos):
+    steps_one, steps_two = ones[0].shape[0], twos[0].shape[0]
+    depth, tile = ones[-1].shape[2:]
+    width = (steps_one + steps_two) * tile
+    block = (1, 3, depth, tile)
+    first = pl.BlockSpec(block, lambda i: (jnp.minimum(i, steps_one - 1), 0, 0, 0))
+    second = pl.BlockSpec(block, lambda i: (jnp.maximum(i - steps_one, 0), 0, 0, 0))
+    tall = pl.BlockSpec((depth, tile), lambda i: (0, i))
+    return pl.pallas_call(
+        functools.partial(finish_kernel, len(ones), steps_one),
+        grid=(steps_one + steps_two,),
+        in_specs=[first] * len(ones) + [second] * len(twos),
+        out_specs=[tall, tall, pl.BlockSpec((tile, depth), lambda i: (i, 0))],
+        out_shape=[jax.ShapeDtypeStruct((depth, width), FULL)] * 2
+        + [jax.ShapeDtypeStruct((width, depth), FULL)],
+        compiler_params=pltpu.CompilerParams(vmem_limit_bytes=VMEM_BYTES),
+        cost_estimate=pl.CostEstimate(
+            flops=0, bytes_accessed=30 * width * depth, transcendentals=0
+        ),
+    )(*ones, *twos)
 
 
 def scatter_start(product, features, first_dim):
@@ -1014,7 +1160,7 @@
     ffn_pick = ffn_picks[0]
     for pick in ffn_picks[1:]:
         ffn_pick = ffn_pick + pick
-    cot_rows = spread_out(after(matmul_tn(ffn_pick, cot_half).astype(LOW), all_routes))
+    cot_blocks = spread_out(after(matmul_tn(ffn_pick, cot_half).astype(LOW), all_routes))
 
     expert_onehot = expert_picks(seq_routes[:, :picks_each], mine, capacity)
     key_table = jnp.asarray(turn_tables(groups * rows_here))
@@ -1039,7 +1185,7 @@
     q_low, k_low, v_low, heads_low, log_sum = attend(
         query_lin, kv_lin, query_table, key_table, groups
     )
-    attn_back = send_home(after(matmul(heads_low, out_full).astype(LOW), cot_rows), 1)
+    attn_back = send_home(after(matmul(heads_low, out_full).astype(LOW), *cot_blocks), 1)
 
     input_half = my_half(tokens_spread).astype(FULL)
     attn_picked = [matmul(pick, attn_back) for pick in attn_picks]
@@ -1066,21 +1212,23 @@
     row_mix = mix_of(matmul(ffn_rows, router2), row_onehot.astype(FULL))
     mine_too = (row_routes == mine.astype(FULL)).astype(FULL)
     mix_rows = jnp.broadcast_to(jnp.sum(row_mix * mine_too, axis=1, keepdims=True), (slots, HEAD))
-    pieces = (gate_all, up_all, with_neighbours(down_pieces, ffn_rows))
+    *forward, cot_rows = expert_forward(ffn_rows, gate_all, up_all, cot_blocks, 6)
+    down_all = with_neighbours(down_pieces, forward[0])
+    ffn_out = jnp.concatenate([matmul(forward[0], piece).astype(LOW) for piece in down_all], axis=1)
+    pieces = (gate_all, up_all, down_all)
     tiles = gate_proj.shape[2] // TILE
     count_one = (tiles + 1) // 2
-    near_one, landed_one, db_one, out_one, mix_grad_one = expert_both_ways(
-        ffn_rows, cot_rows, mix_rows, pieces, 0, count_one, 7
-    )
-    sent_one, finish_one = scatter_rest(near_one, landed_one)
+    near_one, landed_one, db_one, mix_grad_one, ffn_back = expert_back(
+        ffn_rows, cot_rows, mix_rows, forward, pieces, 0, count_one, 7, going_home=ffn_out
+    )
+    sent_one, parts_one = scatter_rest(near_one, landed_one)
     back_one = last_step(sent_one)
-    near_two, landed_two, db_two, out_two, mix_grad_two = expert_both_ways(
-        after(ffn_rows, sent_one), cot_rows, mix_rows, pieces, count_one, tiles - count_one, 8
-    )
-    sent_two, finish_two = scatter_rest(near_two, landed_two)
+    near_two, landed_two, db_two, mix_grad_two = expert_back(
+        after(ffn_rows, sent_one), cot_rows, mix_rows, forward, pieces, count_one, tiles - count_one, 8
+    )
+    sent_two, parts_two = scatter_rest(near_two, landed_two)
     back_two = last_step(sent_two)
     db_rows = (db_one.astype(FULL) + db_two.astype(FULL)).astype(LOW)
-    ffn_out = (out_one.astype(FULL) + out_two.astype(FULL)).astype(LOW)
     mix_grad_rows = jnp.pad(
         jnp.sum(mix_grad_one + mix_grad_two, axis=1).reshape(groups, 1, capacity),
         ((0, 0), (0, 7), (0, 256 - capacity)),
@@ -1132,24 +1280,24 @@
     kv_sent, kv_finish = scatter_start(
         lambda low, high: matmul_tn(a_seq[:, low:high], dkv_low), features, 0
     )
+    da_half, kv_back, out_back = send_home(
+        da_seq.astype(LOW), 5, cargo=(kv_sent, out_sent), add_up=True
+    )
+    kv_part = kv_finish(kv_back)
     query_sent, query_finish = scatter_start(
-        lambda low, high: matmul_tn(rows_in[:, low:high], dq_low), features, 0
-    )
-    da_half, ffn_back, kv_back, query_back, out_back = send_home(
-        da_seq.astype(LOW), 5, cargo=(kv_sent, query_sent, out_sent), add_up=True, more=ffn_out
-    )
-    kv_part = kv_finish(kv_back)
-    query_grad = query_finish(query_back)
-    out_grad = out_finish(out_back)
-    grads = jnp.concatenate(
-        [finish_one(after(back_one, kv_part)), finish_two(after(back_two, kv_part))], axis=2
-    )
-    gate_grad, up_grad, down_grad = grads[0], grads[1], grads[2].T
+        lambda low, high: matmul_tn(rows_in[:, low:high], after(dq_low, kv_part)), features, 0
+    )
+    query_back = last_step(query_sent)
     kv_grad = block_for(kv_part, 0)
     kv_part_low = kv_part.astype(LOW)
     for distance in far_first(groups):
         if distance:
-            kv_grad = kv_grad + swap(block_for(kv_part_low, distance), "ctx", distance).astype(FULL)
+            kv_arrived = swap(block_for(kv_part_low, distance), "ctx", distance)
+            kv_grad = kv_grad + kv_arrived.astype(FULL)
+    query_grad = query_finish(query_back)
+    out_grad = out_finish(out_back)
+    back_one, back_two = lax.optimization_barrier((back_one, back_two, query_back))[:2]
+    gate_grad, up_grad, down_grad = finish_experts(parts_one + [back_one], parts_two + [back_two])
     key_width = key_proj.shape[1]
 
     result = attended
@@ -1182,7 +1330,7 @@
     small = from_spread(join_halves(small, swap(small, "tp", 1)), 1)
     prob_sums = jnp.concatenate([jnp.sum(attn_probs, axis=0), jnp.sum(ffn_probs, axis=0)])
     small = jnp.concatenate([small, jnp.pad(prob_sums, (0, features - prob_sums.shape[0]))[None]], axis=0)
-    small = all_sum(small, ("fsdp", "ctx"))
+    small = all_sum(after(all_sum(small, ("fsdp",)), query_back), ("ctx",))
     prob_sums = small[-1, : 2 * expert_count].reshape(2, expert_count)
     losses = expert_count * jnp.sum(share * prob_sums / all_tokens, axis=1)
     return (

time: 897 us -> 838 us (0.934)
  other arithmetic: 93.1 us -> 47.5 us
  waiting for transfers between devices: 86.1 us -> 53.1 us
  Pallas kernels: 541 us -> 550 us
    ppermute x36 -> x33, waiting for transfers between devices: 86.1 us -> 53.1 us  [swap(): return lax.ppermute(value, axis, [(i, i ^ distance) for i in range(size)])]
    pallas_call x2 -> x4, Pallas kernels: 122 us -> 154 us  [the longest x2 102 us: expert_back(): pl.pallas_call(functools.partial(expert_back_kernel, world, steps, size),...]
    pallas_call x3, Pallas kernels: 181 us -> 160 us  [send_home(): pl.pallas_call(functools.partial(send_home_kernel, size, adds, extra is n...]
    add x3 -> x1, other arithmetic: 16.4 us -> 0.26 us  [on_device(): kv_grad = kv_grad + kv_arrived.astype(FULL)]
    broadcast_in_dim x3 -> x0, other arithmetic: 15.3 us -> none  [the longest x1 8.38 us: on_device(): down_grad[None]]
    convert_element_type x4 -> x2, other arithmetic: 25.2 us -> 14 us  [scatter_rest(): sent = total.astype(LOW)]
    ppermute x36 -> x33, starting transfers between devices: 28.6 us -> 36.8 us  [swap(): return lax.ppermute(value, axis, [(i, i ^ distance) for i in range(size)])]
    dot_general x16 -> x20, matrix products: 49.6 us -> 52.2 us  [matmul(): return jnp.dot(lhs, rhs, preferred_element_type=FULL)]
  transfers between devices with their start and end apart: 36 -> 33, of which waited for: 15 -> 9; matrix products, arithmetic and copies ran while one was open for 20% -> 18% of each run, Pallas kernels for 37% -> 37%
where the time goes in v5:
time: 838 us; the launch traced here: 833 us
  Pallas kernels  550 us (66%)
  matrix products  121 us (14%)
  waiting for transfers between devices  53.1 us (6%)
  other arithmetic  47.5 us (6%)
  starting transfers between devices  36.8 us (4%)
  local copies, waits for them, and re-layouts  22.2 us (3%)
    pallas_call x3, Pallas kernels, send_home(): pl.pallas_call(functools.partial(send_home_kernel, size, adds, extra is n...  160 us
    pallas_call x1, Pallas kernels, prologue(): pl.pallas_call(functools.partial(prologue_kernel, (groups, world)), in_sp...  110 us
    pallas_call x2, Pallas kernels, expert_back(): pl.pallas_call(functools.partial(expert_back_kernel, world, steps, size),...  102 us
    pallas_call x2, Pallas kernels, send_out(): pl.pallas_call(functools.partial(send_out_kernel, size), in_specs=[pl.Blo...  83.5 us
    ppermute x33, waiting for transfers between devices, swap(): return lax.ppermute(value, axis, [(i, i ^ distance) for i in range(size)])  53.1 us
    dot_general x20, matrix products, matmul(): return jnp.dot(lhs, rhs, preferred_element_type=FULL)  52.2 us
    dot_general x13, matrix products, matmul_tn(): lax.dot_general(lhs, rhs, (((0,), (0,)), ((), ())), preferred_element_typ...  38.8 us
    ppermute x33, starting transfers between devices, swap(): return lax.ppermute(value, axis, [(i, i ^ distance) for i in range(size)])  36.8 us
  transfers between devices with their start and end apart: 33, of which 9 were waited for; matrix products, arithmetic and copies ran while one was open for 18% of the time, Pallas kernels for 37%

profile of v5, /device:TPU:0, one launch (start us, length us, event | category | flops | bytes accessed | tf_op | source)
XLA Modules:
  0.0 833.3 jit_solution(16966962332240049209)
XLA Ops:
  10.1 109.7 %shard_map.271 = (bf16[2,1024,1024]{2,1,0:T(8,128)(2,1)}, s32[4,4,8,256]{3,2,1,0:T(8,128)}, bf16[2048,2048]{1,0:T(8,128)(2,1)}, bf16[2048,1024]{1,0:T(8,128)(2,1)}, bf16[4,1024,512]{2,1,0:T(8,128)(2,1)}) custom-call(bf16[256,1024]{1,0:T(8,128)(2,1)} %maximum_select_fusion.refs_0_, bf16[256,2048]{1,0:T(8,128)(2,1)} %pad_maximum_fusion.4.refs_1_, ...), custom_call_target="tpu_custom_call" | custom-call | bytes 100000000 | tf_op jit(solution)/shard_map/pallas_call | solution.py:577
  146.1 14.6 %fusion.138.k_lin.v_lin = f32[1024,2048]{1,0:T(8,128)} fusion(bf16[1024,2048]{1,0:T(8,128)(2,1)} %fusion.2, bf16[2048,2048]{1,0:T(8,128)(2,1)} %get-tuple-element.69), kind=kOutput, calls=%fused_computation.351 | convolution fusion | flops 8589934592 | bytes 20971520 | tf_op jit(solution)/shard_map/dot_general | solution.py:24
  168.8 19.1 %shard_map.272 = (bf16[640,1024]{1,0:T(8,128)(2,1)}, bf16[1024,1024]{1,0:T(8,128)(2,1)}, bf16[1024,1024]{1,0:T(8,128)(2,1)}, bf16[640,1024]{1,0:T(8,128)(2,1)}, f32[640,1024]{1,0:T(8,128)}) custom-call(f32[640,1024]{1,0:T(8,128)} %fusion.137.q_lin, f32[1024,2048]{1,0:T(8,128)} %fusion.138.k_lin.v_lin, f32[1024,2048]{1,0:T(8,128)} %fusion.138.k_lin.v_lin, ...), custom_call_target="tpu_custom_call" | custom-call | bytes 20971520 | tf_op jit(solution)/shard_map/pallas_call | solution.py:978
  197.7 42.4 %shard_map.273 = bf16[640,1024]{1,0:T(8,128)(2,1)} custom-call(bf16[640,2048]{1,0:T(8,128)(2,1)} %convolution_convert_fusion.2.refs_0_), custom_call_target="tpu_custom_call" | custom-call | bytes 7864320 | tf_op jit(solution)/shard_map/pallas_call | solution.py:370
  246.0 7.8 collective-permute-done.8.refs_6_.refs_11_
  264.7 43.2 %shard_map.274.refs_0_ = bf16[640,2048]{1,0:T(8,128)(2,1)} custom-call(bf16[640,1024]{1,0:T(8,128)(2,1)} %convolution_convert_fusion.6.rows_ref), custom_call_target="tpu_custom_call" | custom-call | bytes 7864320 | tf_op jit(solution)/shard_map/pallas_call | solution.py:230
  307.9 34.4 %shard_map.275 = (bf16[640,2816]{1,0:T(8,128)(2,1)}, bf16[640,2816]{1,0:T(8,128)(2,1)}, bf16[640,2816]{1,0:T(8,128)(2,1)}, bf16[640,2048]{1,0:T(8,128)(2,1)}) custom-call(bf16[640,2048]{1,0:T(8,128)(2,1)} %shard_map.274.refs_0_, bf16[512,2816]{1,0:T(8,128)(2,1)} %bitcast.146, bf16[512,2816]{1,0:T(8,128)(2,1)} %collective-permute-done.5.refs_2_.refs_7_, ...), custom_call_target="tpu_custom_call" | custom-call | bytes 2621440 | tf_op jit(solution)/shard_map/pallas_call | solution.py:649
  363.1 55.8 %shard_map.276 = (bf16[6,3,1024,256]{3,2,1,0:T(8,128)(2,1)}, bf16[6,3,1024,256]{3,2,1,0:T(8,128)(2,1)}, bf16[640,2048]{1,0:T(8,128)(2,1)}, f32[640,128]{1,0:T(8,128)}, bf16[640,1024]{1,0:T(8,128)(2,1)}) custom-call(bf16[640,2048]{1,0:T(8,128)(2,1)} %shard_map.274.refs_0_, bf16[640,2048]{1,0:T(8,128)(2,1)} %get-tuple-element.79.refs_1_, ...), custom_call_target="tpu_custom_call" | custom-call | bytes 2621440 | tf_op jit(solution)/shard_map/pallas_call | solution.py:832
  418.9 7.5 add_convert_fusion
  427.9 46.0 %shard_map.277 = (bf16[5,3,1024,256]{3,2,1,0:T(8,128)(2,1)}, bf16[5,3,1024,256]{3,2,1,0:T(8,128)(2,1)}, bf16[640,2048]{1,0:T(8,128)(2,1)}, f32[640,128]{1,0:T(8,128)}) custom-call(bf16[640,2048]{1,0:T(8,128)(2,1)} %shard_map.274.refs_0_, bf16[640,2048]{1,0:T(8,128)(2,1)} %get-tuple-element.79.refs_1_, f32[640,128]{1,0:T(8,128)} %broadcast_in_dim.41.refs_2_, ...), custom_call_target="tpu_custom_call" | custom-call | bytes 2621440 | tf_op jit(solution)/shard_map/pallas_call | solution.py:832
  475.1 6.5 add_convert_fusion.1
  485.8 43.0 %shard_map.278 = (bf16[640,1024]{1,0:T(8,128)(2,1)}, f32[4,8,256]{2,1,0:T(8,128)}) custom-call(bf16[640,2048]{1,0:T(8,128)(2,1)} %add_convert_fusion.2.refs_0_, f32[4,8,256]{2,1,0:T(8,128)} %pad.8.refs_1_), custom_call_target="tpu_custom_call" | custom-call | bytes 7864320 | tf_op jit(solution)/shard_map/pallas_call | solution.py:370
  533.4 11.2 %collective-permute-done.14 = bf16[256,1024]{1,0:T(8,128)(2,1)S(1)} collective-permute-done((bf16[256,1024]{1,0:T(8,128)(2,1)S(1)}, bf16[256,1024]{1,0:T(8,128)(2,1)S(1)}, u32[]{:S(2)}, u32[]{:S(2)}) %collective-permute-start.14) | collective-permute-done | bytes 524320 | tf_op jit(solution)/shard_map/ppermute | solution.py:41
  555.2 40.3 %shard_map.279 = bf16[640,2048]{1,0:T(8,128)(2,1)} custom-call(bf16[640,1024]{1,0:T(8,128)(2,1)} %add_convert_fusion.4.rows_ref), custom_call_target="tpu_custom_call" | custom-call | bytes 7864320 | tf_op jit(solution)/shard_map/pallas_call | solution.py:230
  595.5 5.8 convolution_convert_fusion.5.d_heads
  601.3 23.7 %shard_map.280 = (bf16[640,1024]{1,0:T(8,128)(2,1)}, bf16[1024,1024]{1,0:T(8,128)(2,1)}, bf16[1024,1024]{1,0:T(8,128)(2,1)}) custom-call(bf16[640,1024]{1,0:T(8,128)(2,1)} %get-tuple-element.99.q_low, bf16[1024,1024]{1,0:T(8,128)(2,1)} %get-tuple-element.100.k_low, bf16[1024,1024]{1,0:T(8,128)(2,1)} %get-tuple-element.101.v_low, ...), custom_call_target="tpu_custom_call" | custom-call | bytes 14680064 | tf_op jit(solution)/shard_map/pallas_call | solution.py:1033
  632.0 6.2 convolution_convert_fusion
  643.2 12.8 %fusion.3.refs_0_ = bf16[1024,2048]{1,0:T(8,128)(2,1)} fusion(f32[4,256,2048]{2,1,0:T(8,128)S(1)} %fusion.50, bf16[1024,2048]{1,0:T(8,128)(2,1)S(1)} %pad_maximum_fusion.2, bf16[2048,2048]{1,0:T(8,128)(2,1)} %get-tuple-element.69), kind=kOutput, calls=%fused_computation.7 | convolution fusion | flops 8594128896 | bytes 25165824 | tf_op jit(solution)/shard_map/dot_general | solution.py:32
  661.3 5.6 add_convert_fusion.3.refs_1_
  667.0 74.4 %shard_map.281 = (f32[256,1024]{1,0:T(8,128)}, bf16[512,2048]{1,0:T(8,128)(2,1)}, bf16[1024,512]{1,0:T(8,128)(2,1)}) custom-call(bf16[1024,2048]{1,0:T(8,128)(2,1)} %fusion.3.refs_0_, bf16[512,2048]{1,0:T(8,128)(2,1)} %add_convert_fusion.3.refs_1_, bf16[1024,512]{1,0:T(8,128)(2,1)} %add_convert_fusion.6.refs_2_), custom_call_target="tpu_custom_call" | custom-call | bytes 12582912 | tf_op jit(solution)/shard_map/pallas_call | solution.py:370
  771.2 8.4 %collective-permute-done.30 = bf16[128,2048]{1,0:T(8,128)(2,1)S(1)} collective-permute-done((bf16[128,2048]{1,0:T(8,128)(2,1)S(1)}, bf16[128,2048]{1,0:T(8,128)(2,1)S(1)}, u32[]{:S(2)}, u32[]{:S(2)}) %collective-permute-start.30) | collective-permute-done | bytes 524320 | tf_op jit(solution)/shard_map/ppermute | solution.py:41
  779.5 10.9 %collective-permute-done.31 = bf16[128,2048]{1,0:T(8,128)(2,1)S(1)} collective-permute-done((bf16[128,2048]{1,0:T(8,128)(2,1)S(1)}, bf16[128,2048]{1,0:T(8,128)(2,1)S(1)}, u32[]{:S(2)}, u32[]{:S(2)}) %collective-permute-start.31) | collective-permute-done | bytes 524320 | tf_op jit(solution)/shard_map/ppermute | solution.py:41
  795.7 8.1 collective-permute-start.28
  812.8 18.2 %shard_map.282 = (f32[512,2816]{1,0:T(8,128)}, f32[512,2816]{1,0:T(8,128)}, f32[2816,512]{1,0:T(8,128)}) custom-call(bf16[6,3,1024,256]{3,2,1,0:T(8,128)(2,1)} %get-tuple-element.87.refs_0_, bf16[6,3,1024,256]{3,2,1,0:T(8,128)(2,1)} %get-tuple-element.88.refs_1_, bf16[6,3,512,256]{3,2,1,0:T(8,128)(2,1)} %collective-permute-done.15.refs_2_, ...), custom_call_target="tpu_custom_call" | custom-call | bytes 43253760 | tf_op jit(solution)/shard_map/pallas_call | solution.py:891
  (404 shorter events, 175.0 us)
Async XLA Ops:
  122.2 74.5 %collective-permute-start.2 = (bf16[160,1024]{1,0:T(8,128)(2,1)}, bf16[160,1024]{1,0:T(8,128)(2,1)}, u32[]{:S(2)}, u32[]{:S(2)}) collective-permute-start(bf16[160,1024]{1,0:T(8,128)(2,1)} %get-tuple-element.157), channel_id=1, source_target_pairs={{0,6},{2,4},{4,2},{6,0},{1,7},{3,5},{5,3},{7,1},{8,14},{10,12},{12... | collective-permute-start | bytes 983048 | tf_op jit(solution)/shard_map/ppermute | solution.py:41
  124.5 72.8 %collective-permute-start.1 = (bf16[160,1024]{1,0:T(8,128)(2,1)}, bf16[160,1024]{1,0:T(8,128)(2,1)}, u32[]{:S(2)}, u32[]{:S(2)}) collective-permute-start(bf16[160,1024]{1,0:T(8,128)(2,1)} %get-tuple-element.158), channel_id=1, source_target_pairs={{0,4},{2,6},{4,0},{6,2},{1,5},{3,7},{5,1},{7,3},{8,12},{10,14},{12... | collective-permute-start | bytes 983048 | tf_op jit(solution)/shard_map/ppermute | solution.py:41
  124.5 73.3 %collective-permute-start = (bf16[160,1024]{1,0:T(8,128)(2,1)}, bf16[160,1024]{1,0:T(8,128)(2,1)}, u32[]{:S(2)}, u32[]{:S(2)}) collective-permute-start(bf16[160,1024]{1,0:T(8,128)(2,1)} %get-tuple-element.159), channel_id=1, source_target_pairs={{0,2},{2,0},{4,6},{6,4},{1,3},{3,1},{5,7},{7,5},{8,10},{10,8},{12,... | collective-permute-start | bytes 983048 | tf_op jit(solution)/shard_map/ppermute | solution.py:41
  126.6 118.8 %collective-permute-start.5 = (bf16[512,2816]{1,0:T(8,128)(2,1)S(1)}, bf16[512,2816]{1,0:T(8,128)(2,1)}, u32[]{:S(2)}, u32[]{:S(2)}) collective-permute-start(bf16[512,2816]{1,0:T(8,128)(2,1)S(1)} %bitcast.149), channel_id=1, source_target_pairs={{0,16},{8,24},{16,0},{24,8},{1,17},{9,25},{17,1},{25,9},{2,18},{10... | collective-permute-start | bytes 8650760 | tf_op jit(solution)/shard_map/ppermute | solution.py:41
  127.1 126.8 %collective-permute-start.8 = (bf16[512,2816]{1,0:T(8,128)(2,1)}, bf16[512,2816]{1,0:T(8,128)(2,1)}, u32[]{:S(2)}, u32[]{:S(2)}) collective-permute-start(bf16[512,2816]{1,0:T(8,128)(2,1)} %bitcast.26.refs_5_.refs_10_), channel_id=1, source_target_pairs={{0,16},{8,24},{16,0},{24,8},{1,17},{9,25},{17,1},{25,9},{2,18},{10... | collective-permute-start | bytes 8650760 | tf_op jit(solution)/shard_map/ppermute | solution.py:41
  196.6 62.2 %collective-permute-start.6 = (bf16[512,2816]{1,0:T(8,128)(2,1)S(1)}, bf16[512,2816]{1,0:T(8,128)(2,1)}, u32[]{:S(2)}, u32[]{:S(2)}) collective-permute-start(bf16[512,2816]{1,0:T(8,128)(2,1)S(1)} %bitcast.150), channel_id=1, source_target_pairs={{0,8},{8,0},{16,24},{24,16},{1,9},{9,1},{17,25},{25,17},{2,10},{10... | collective-permute-start | bytes 8650760 | tf_op jit(solution)/shard_map/ppermute | solution.py:41
  197.2 66.0 %collective-permute-start.9 = (bf16[512,2816]{1,0:T(8,128)(2,1)}, bf16[512,2816]{1,0:T(8,128)(2,1)}, u32[]{:S(2)}, u32[]{:S(2)}) collective-permute-start(bf16[512,2816]{1,0:T(8,128)(2,1)} %bitcast.26.refs_5_.refs_10_), channel_id=1, source_target_pairs={{0,8},{8,0},{16,24},{24,16},{1,9},{9,1},{17,25},{25,17},{2,10},{10... | collective-permute-start | bytes 8650760 | tf_op jit(solution)/shard_map/ppermute | solution.py:41
  245.4 97.0 %collective-permute-start.11 = (bf16[2816,512]{1,0:T(8,128)(2,1)}, bf16[2816,512]{1,0:T(8,128)(2,1)}, u32[]{:S(2)}, u32[]{:S(2)}) collective-permute-start(bf16[2816,512]{1,0:T(8,128)(2,1)} %bitcast.151), channel_id=1, source_target_pairs={{0,16},{8,24},{16,0},{24,8},{1,17},{9,25},{17,1},{25,9},{2,18},{10... | collective-permute-start | bytes 8650760 | tf_op jit(solution)/shard_map/ppermute | solution.py:41
  258.8 94.0 %collective-permute-start.12 = (bf16[2816,512]{1,0:T(8,128)(2,1)}, bf16[2816,512]{1,0:T(8,128)(2,1)}, u32[]{:S(2)}, u32[]{:S(2)}) collective-permute-start(bf16[2816,512]{1,0:T(8,128)(2,1)} %bitcast.152), channel_id=1, source_target_pairs={{0,8},{8,0},{16,24},{24,16},{1,9},{9,1},{17,25},{25,17},{2,10},{10... | collective-permute-start | bytes 8650760 | tf_op jit(solution)/shard_map/ppermute | solution.py:41
  263.2 79.3 %collective-permute-start.4 = (f32[256,4]{0,1:T(4,128)S(1)}, f32[256,4]{0,1:T(4,128)S(1)}, u32[]{:S(2)}, u32[]{:S(2)}) collective-permute-start(f32[256,4]{0,1:T(4,128)S(1)} %fusion.111), channel_id=1, source_target_pairs={{0,1},{1,0},{2,3},{3,2},{4,5},{5,4},{6,7},{7,6},{8,9},{9,8},{10,11... | collective-permute-start | bytes 12296 | tf_op jit(solution)/shard_map/ppermute | solution.py:41
  342.4 14.3 %collective-permute-start.13 = (bf16[2816,512]{1,0:T(8,128)(2,1)}, bf16[2816,512]{1,0:T(8,128)(2,1)}, u32[]{:S(2)}, u32[]{:S(2)}) collective-permute-start(bf16[2816,512]{1,0:T(8,128)(2,1)} %collective-permute-done.11.refs_15_), channel_id=1, source_target_pairs={{0,8},{8,0},{16,24},{24,16},{1,9},{9,1},{17,25},{25,17},{2,10},{10... | collective-permute-start | bytes 8650760 | tf_op jit(solution)/shard_map/ppermute | solution.py:41
  426.4 118.4 %collective-permute-start.15 = (bf16[6,3,512,256]{3,2,1,0:T(8,128)(2,1)}, bf16[6,3,512,256]{3,2,1,0:T(8,128)(2,1)}, u32[]{:S(2)}, u32[]{:S(2)}) collective-permute-start(bf16[6,3,512,256]{3,2,1,0:T(8,128)(2,1)} %add_convert_fusion), channel_id=1, source_target_pairs={{0,16},{8,24},{16,0},{24,8},{1,17},{9,25},{17,1},{25,9},{2,18},{10... | collective-permute-start | bytes 14155784 | tf_op jit(solution)/shard_map/ppermute | solution.py:41
  481.7 150.3 %collective-permute-start.17 = (bf16[5,3,512,256]{3,2,1,0:T(8,128)(2,1)}, bf16[5,3,512,256]{3,2,1,0:T(8,128)(2,1)}, u32[]{:S(2)}, u32[]{:S(2)}) collective-permute-start(bf16[5,3,512,256]{3,2,1,0:T(8,128)(2,1)} %add_convert_fusion.1), channel_id=1, source_target_pairs={{0,16},{8,24},{16,0},{24,8},{1,17},{9,25},{17,1},{25,9},{2,18},{10... | collective-permute-start | bytes 11796488 | tf_op jit(solution)/shard_map/ppermute | solution.py:41
  551.0 105.1 %collective-permute-start.20 = (f32[256,2]{0,1:T(2,128)S(1)}, f32[256,2]{0,1:T(2,128)S(1)}, u32[]{:S(2)}, u32[]{:S(2)}) collective-permute-start(f32[256,2]{0,1:T(2,128)S(1)} %pad_maximum_fusion.15), channel_id=1, source_target_pairs={{0,1},{1,0},{2,3},{3,2},{4,5},{5,4},{6,7},{7,6},{8,9},{9,8},{10,11... | collective-permute-start | bytes 6152 | tf_op jit(solution)/shard_map/ppermute | solution.py:41
  638.2 23.2 %collective-permute-start.18 = (bf16[1024,2048]{1,0:T(8,128)(2,1)}, bf16[1024,2048]{1,0:T(8,128)(2,1)}, u32[]{:S(2)}, u32[]{:S(2)}) collective-permute-start(bf16[1024,2048]{1,0:T(8,128)(2,1)} %convolution_convert_fusion), channel_id=1, source_target_pairs={{0,8},{8,0},{16,24},{24,16},{1,9},{9,1},{17,25},{25,17},{2,10},{10... | collective-permute-start | bytes 12582920 | tf_op jit(solution)/shard_map/ppermute | solution.py:41
  641.3 16.5 %collective-permute-start.19 = (bf16[1024,1024]{1,0:T(8,128)(2,1)}, bf16[1024,1024]{1,0:T(8,128)(2,1)}, u32[]{:S(2)}, u32[]{:S(2)}) collective-permute-start(bf16[1024,1024]{1,0:T(8,128)(2,1)} %convolution_convert_fusion.4), channel_id=1, source_target_pairs={{0,8},{8,0},{16,24},{24,16},{1,9},{9,1},{17,25},{25,17},{2,10},{10... | collective-permute-start | bytes 6291464 | tf_op jit(solution)/shard_map/ppermute | solution.py:41
  752.3 17.2 %collective-permute-start.26 = (bf16[1024,1024]{1,0:T(8,128)(2,1)S(1)}, bf16[1024,1024]{1,0:T(8,128)(2,1)S(1)}, u32[]{:S(2)}, u32[]{:S(2)}) collective-permute-start(bf16[1024,1024]{1,0:T(8,128)(2,1)S(1)} %convolution_convert_fusion.3), channel_id=1, source_target_pairs={{0,8},{8,0},{16,24},{24,16},{1,9},{9,1},{17,25},{25,17},{2,10},{10... | collective-permute-start | bytes 6291464 | tf_op jit(solution)/shard_map/ppermute | solution.py:41
  752.5 27.0 %collective-permute-start.30 = (bf16[128,2048]{1,0:T(8,128)(2,1)S(1)}, bf16[128,2048]{1,0:T(8,128)(2,1)S(1)}, u32[]{:S(2)}, u32[]{:S(2)}) collective-permute-start(bf16[128,2048]{1,0:T(8,128)(2,1)S(1)} %get-tuple-element.154), channel_id=1, source_target_pairs={{0,4},{2,6},{4,0},{6,2},{1,5},{3,7},{5,1},{7,3},{8,12},{10,14},{12... | collective-permute-start | bytes 1572872 | tf_op jit(solution)/shard_map/ppermute | solution.py:41
  753.2 26.3 %collective-permute-start.32 = (bf16[128,2048]{1,0:T(8,128)(2,1)S(1)}, bf16[128,2048]{1,0:T(8,128)(2,1)S(1)}, u32[]{:S(2)}, u32[]{:S(2)}) collective-permute-start(bf16[128,2048]{1,0:T(8,128)(2,1)S(1)} %get-tuple-element.155), channel_id=1, source_target_pairs={{0,2},{2,0},{4,6},{6,4},{1,3},{3,1},{5,7},{7,5},{8,10},{10,8},{12,... | collective-permute-start | bytes 1572872 | tf_op jit(solution)/shard_map/ppermute | solution.py:41
  758.9 31.5 %collective-permute-start.31 = (bf16[128,2048]{1,0:T(8,128)(2,1)S(1)}, bf16[128,2048]{1,0:T(8,128)(2,1)S(1)}, u32[]{:S(2)}, u32[]{:S(2)}) collective-permute-start(bf16[128,2048]{1,0:T(8,128)(2,1)S(1)} %get-tuple-element.156), channel_id=1, source_target_pairs={{0,6},{2,4},{4,2},{6,0},{1,7},{3,5},{5,3},{7,1},{8,14},{10,12},{12... | collective-permute-start | bytes 1572872 | tf_op jit(solution)/shard_map/ppermute | solution.py:41
  767.4 24.4 %collective-permute-start.22 = (bf16[256,1024]{1,0:T(8,128)(2,1)S(1)}, bf16[256,1024]{1,0:T(8,128)(2,1)S(1)}, u32[]{:S(2)}, u32[]{:S(2)}) collective-permute-start(bf16[256,1024]{1,0:T(8,128)(2,1)S(1)} %fusion.23), channel_id=1, source_target_pairs={{0,1},{1,0},{2,3},{3,2},{4,5},{5,4},{6,7},{7,6},{8,9},{9,8},{10,11... | collective-permute-start | bytes 1572872 | tf_op jit(solution)/shard_map/ppermute | solution.py:41
  770.7 25.0 %collective-permute-start.27 = (bf16[512,1024]{1,0:T(8,128)(2,1)S(1)}, bf16[512,1024]{1,0:T(8,128)(2,1)S(1)}, u32[]{:S(2)}, u32[]{:S(2)}) collective-permute-start(bf16[512,1024]{1,0:T(8,128)(2,1)S(1)} %add_convert_fusion.5), channel_id=1, source_target_pairs={{0,16},{8,24},{16,0},{24,8},{1,17},{9,25},{17,1},{25,9},{2,18},{10... | collective-permute-start | bytes 3145736 | tf_op jit(solution)/shard_map/ppermute | solution.py:41
  795.7 14.6 %collective-permute-start.28 = (f32[11,2048]{1,0:T(8,128)S(1)}, f32[11,2048]{1,0:T(8,128)S(1)}, u32[]{:S(2)}, u32[]{:S(2)}) collective-permute-start(f32[11,2048]{1,0:T(8,128)S(1)} %add.267), channel_id=1, source_target_pairs={{0,4},{2,6},{4,0},{6,2},{1,5},{3,7},{5,1},{7,3},{8,12},{10,14},{12... | collective-permute-start | bytes 270344 | tf_op jit(solution)/shard_map/ppermute | solution.py:41
  810.4 20.6 %collective-permute-start.29 = (f32[11,2048]{1,0:T(8,128)S(1)}, f32[11,2048]{1,0:T(8,128)S(1)}, u32[]{:S(2)}, u32[]{:S(2)}) collective-permute-start(f32[11,2048]{1,0:T(8,128)S(1)} %add.271), channel_id=1, source_target_pairs={{0,2},{2,0},{4,6},{6,4},{1,3},{3,1},{5,7},{7,5},{8,10},{10,8},{12,... | collective-permute-start | bytes 270344 | tf_op jit(solution)/shard_map/ppermute | solution.py:41
  (102 other events, 1891.9 us)

commit v6 on v5

--- a/solution.py
+++ b/solution.py
@@ -67,10 +67,9 @@
     return pieces
 
 
-def with_neighbours(pieces, *earlier):
-    return pieces + [swap(pieces[0], "fsdp", 1)] + [
-        swap(after(item, *earlier), "fsdp", 1) for item in pieces[1:]
-    ]
+def with_neighbours(pieces, known, *earlier):
+    rest = [swap(after(item, *earlier), "fsdp", 1) for item in pieces[len(known) :]]
+    return pieces + list(known) + rest
 
 
 def flip_blocks(value, axis, index, count):
@@ -186,41 +185,63 @@
     return [distance for distance in spread_order(size) if distance] + [0]
 
 
+def cuts_of(rows):
+    for count in (4, 2):
+        if rows % (16 * count) == 0:
+            return count
+    return 1
+
+
 def send_out_kernel(size, rows_ref, out_ref, z_land, y_land, z_send, z_recv, y_send, y_recv):
     mine, first = lax.axis_index("ctx"), lax.axis_index("tp") == 0
     other_tp = {"tp": 1 - lax.axis_index("tp")}
     rows, width = z_land.shape[1], z_land.shape[2]
+    cuts = cuts_of(rows)
+    part = rows // cuts
     at = [xor_index(mine, distance) for distance in range(size)]
     meet([{"ctx": at[distance]} for distance in range(1, size)] + [other_tp])
-    order = near_first(size)
+    order = [(distance, cut) for distance in near_first(size) for cut in range(cuts)]
+    own = [(0, cut) for cut in range(cuts)]
     across, beside = {}, {}
-    for distance in order:
-        across[distance] = remote(
-            rows_ref.at[span(at[distance], rows)],
-            z_land.at[distance],
+
+    def source(distance, cut):
+        start = pl.multiple_of(at[distance] * rows + cut * part, 16)
+        return rows_ref.at[pl.ds(start, part)]
+
+    def inside(distance, cut):
+        return distance, pl.ds(cut * part, part)
+
+    for distance, cut in order:
+        across[distance, cut] = remote(
+            source(distance, cut),
+            z_land.at[inside(distance, cut)],
             (z_send, z_recv),
-            distance,
+            distance * cuts + cut,
             {"ctx": at[distance]},
         )
-        across[distance].start()
-    beside[0] = remote(rows_ref.at[span(mine, rows)], y_land.at[0], (y_send, y_recv), 0, other_tp)
-    beside[0].start()
-    for distance in order:
-        across[distance].wait_recv()
-        beside[distance] = remote(
-            z_land.at[distance], y_land.at[distance], (y_send, y_recv), distance, other_tp
+        across[distance, cut].start()
+    for distance, cut in own + order:
+        if distance:
+            across[distance, cut].wait_recv()
+        beside[distance, cut] = remote(
+            z_land.at[inside(distance, cut)] if distance else source(0, cut),
+            y_land.at[inside(distance, cut)],
+            (y_send, y_recv),
+            distance * cuts + cut,
+            other_tp,
         )
-        beside[distance].start()
-    for distance in [0] + order:
-        beside[distance].wait_recv()
-        own = z_land[distance] if distance else rows_ref[span(mine, rows), :]
-        theirs = y_land[distance]
-        out_ref[span(at[distance], rows), :width] = jnp.where(first, own, theirs)
-        out_ref[span(at[distance], rows), width:] = jnp.where(first, theirs, own)
-    for distance in order:
-        across[distance].wait_send()
-    for distance in [0] + order:
-        beside[distance].wait_send()
+        beside[distance, cut].start()
+    for distance, cut in own + order:
+        beside[distance, cut].wait_recv()
+        held = z_land[inside(distance, cut)] if distance else source(0, cut)[...]
+        theirs = y_land[inside(distance, cut)]
+        here = pl.ds(pl.multiple_of(at[distance] * rows + cut * part, 16), part)
+        out_ref[here, :width] = jnp.where(first, held, theirs)
+        out_ref[here, width:] = jnp.where(first, theirs, held)
+    for item in order:
+        across[item].wait_send()
+    for item in own + order:
+        beside[item].wait_send()
 
 
 def send_out(half_rows, number):
@@ -232,7 +253,7 @@
         in_specs=[pl.BlockSpec(memory_space=pltpu.VMEM)],
         out_specs=pl.BlockSpec(memory_space=pltpu.VMEM),
         out_shape=jax.ShapeDtypeStruct((total, 2 * width), half_rows.dtype),
-        scratch_shapes=[land, land] + [pltpu.SemaphoreType.DMA((size,))] * 4,
+        scratch_shapes=[land, land] + [pltpu.SemaphoreType.DMA((size * cuts_of(total // size),))] * 4,
         compiler_params=pltpu.CompilerParams(
             collective_id=number, has_side_effects=True, vmem_limit_bytes=VMEM_BYTES
         ),
@@ -240,7 +261,8 @@
     )(half_rows)
 
 
-def send_home_kernel(size, adds, has_extra, cargoes, *refs):
+def send_home_kernel(size, adds, has_extra, cargo_axes, *refs):
+    cargoes = len(cargo_axes)
     streams = len(adds)
     parts, refs = refs[:streams], refs[streams:]
     extra_ref, refs = (refs[0], refs[1:]) if has_extra else (None, refs)
@@ -254,30 +276,43 @@
     other_tp = {"tp": 1 - place}
     at = [xor_index(mine, distance) for distance in range(size)]
     world = lax.axis_size("fsdp")
-    along = [{"fsdp": xor_index(lax.axis_index("fsdp"), world // 2)}] if cargoes else []
-    meet([{"ctx": at[distance]} for distance in range(1, size)] + [other_tp] + along)
+    spot = lax.axis_index("fsdp")
+    along = {"tp": other_tp, "fsdp": {"fsdp": xor_index(spot, world // 2)}, "core": {"fsdp": xor_index(spot, 1)}}
+    extra_peers = [along[axis] for axis in ("fsdp", "core") if axis in cargo_axes]
+    meet([{"ctx": at[distance]} for distance in range(1, size)] + [other_tp] + extra_peers)
     order = mixed_order(size)
     beside, across, extras = {}, {}, {}
-    cargo = [remote(cargo_in[n], cargo_out[n], refs[-2:], n, along[0]) for n in range(cargoes)]
-    for copy in cargo:
-        copy.start()
+    cargo = [
+        remote(cargo_in[n], cargo_out[n], refs[-2:], n, along[axis])
+        for n, axis in enumerate(cargo_axes)
+    ]
+    for copy, axis in zip(cargo, cargo_axes):
+        if axis != "tp":
+            copy.start()
     if has_extra:
         ey_land, e_ready, ez_land, ey_send, ey_recv, ez_send, ez_recv = refs[:7]
         extra_beside = remote(extra_ref, ey_land, (ey_send, ey_recv), 0, other_tp)
         extra_beside.start()
+    turns = []
     for n in range(streams):
         y_land, _, z_land, y_send, y_recv, _, _ = lands[n]
         rows, width = z_land.shape[1], z_land.shape[2]
+        cuts = cuts_of(rows)
+        part = rows // cuts
         columns = pl.ds(pl.multiple_of((1 - place) * width, 128), width)
         for distance in order:
-            beside[n, distance] = remote(
-                parts[n].at[span(at[distance], rows), columns],
-                y_land.at[distance],
-                (y_send, y_recv),
-                distance,
-                other_tp,
-            )
-            beside[n, distance].start()
+            for cut in range(cuts):
+                inside = distance, pl.ds(cut * part, part)
+                here = pl.ds(pl.multiple_of(at[distance] * rows + cut * part, 16), part)
+                number = distance * cuts + cut
+                beside[n, number] = remote(
+                    parts[n].at[here, columns], y_land.at[inside], (y_send, y_recv), number, other_tp
+                )
+                beside[n, number].start()
+                turns.append((n, distance, cut, number, part, width, inside, here))
+    for copy, axis in zip(cargo, cargo_axes):
+        if axis == "tp":
+            copy.start()
     if has_extra:
         extra_beside.wait_recv()
         e_ready[...] = extra_ref[...] + ey_land[...]
@@ -291,38 +326,29 @@
                     {"ctx": at[distance]},
                 )
                 extras[distance].start()
-    for n in range(streams):
+    for n, distance, cut, number, part, width, inside, here in turns:
         y_land, ready, z_land, _, _, z_send, z_recv = lands[n]
-        rows, width = z_land.shape[1], z_land.shape[2]
-        for distance in order:
-            beside[n, distance].wait_recv()
-            whole = parts[n][span(at[distance], rows), :]
-            own = jnp.where(first, whole[:, :width], whole[:, width:])
-            total = (own.astype(FULL) + y_land[distance].astype(FULL)).astype(LOW)
-            if distance:
-                ready[distance] = total
-                across[n, distance] = remote(
-                    ready.at[distance],
-                    z_land.at[distance],
-                    (z_send, z_recv),
-                    distance,
-                    {"ctx": at[distance]},
-                )
-                across[n, distance].start()
-            elif adds[n]:
-                outs[n][...] = total.astype(FULL)
+        beside[n, number].wait_recv()
+        whole = parts[n][here, :]
+        own = jnp.where(first, whole[:, :width], whole[:, width:])
+        total = (own.astype(FULL) + y_land[inside].astype(FULL)).astype(LOW)
+        if distance:
+            ready[inside] = total
+            across[n, number] = remote(
+                ready.at[inside], z_land.at[inside], (z_send, z_recv), number, {"ctx": at[distance]}
+            )
+            across[n, number].start()
+        elif adds[n]:
+            outs[n][inside[1], :] = total.astype(FULL)
+        else:
+            outs[n][here, :] = total
+    for n, distance, cut, number, part, width, inside, here in turns:
+        if distance:
+            across[n, number].wait_recv()
+            if adds[n]:
+                outs[n][inside[1], :] += lands[n][2][inside].astype(FULL)
             else:
-                outs[n][span(mine, rows), :] = total
-    for n in range(streams):
-        z_land = lands[n][2]
-        rows = z_land.shape[1]
-        for distance in order:
-            if distance:
-                across[n, distance].wait_recv()
-                if adds[n]:
-                    outs[n][...] += z_land[distance].astype(FULL)
-                else:
-                    outs[n][span(at[distance], rows), :] = z_land[distance]
+                outs[n][here, :] = lands[n][2][inside]
     if has_extra:
         extra_out[mine] = e_ready[mine]
         for distance in order:
@@ -331,11 +357,8 @@
                 extra_out[at[distance]] = ez_land[distance]
                 extras[distance].wait_send()
         extra_beside.wait_send()
-    for n in range(streams):
-        for distance in order:
-            beside[n, distance].wait_send()
-            if distance:
-                across[n, distance].wait_send()
+    for copy in list(beside.values()) + list(across.values()):
+        copy.wait_send()
     for copy in cargo:
         copy.wait()
 
@@ -353,14 +376,15 @@
         shapes.append(
             jax.ShapeDtypeStruct((rows, width), FULL) if added else jax.ShapeDtypeStruct((total, width), LOW)
         )
-        scratch += [pltpu.VMEM((size, rows, width), LOW)] * 3 + sems
+        scratch += [pltpu.VMEM((size, rows, width), LOW)] * 3
+        scratch += [pltpu.SemaphoreType.DMA((size * cuts_of(rows),))] * 4
     if extra is not None:
         operands.append(extra)
         shapes.append(jax.ShapeDtypeStruct(extra.shape, FULL))
         scratch += [pltpu.VMEM(extra.shape, FULL)] * 3 + sems
     in_specs = [pl.BlockSpec(memory_space=pltpu.VMEM)] * len(operands)
     out_specs = [pl.BlockSpec(memory_space=pltpu.VMEM)] * len(shapes)
-    for item in cargo:
+    for item, _ in cargo:
         operands.append(item)
         shapes.append(jax.ShapeDtypeStruct(item.shape, item.dtype))
         in_specs.append(pl.BlockSpec(memory_space=pl.ANY))
@@ -368,7 +392,7 @@
     if cargo:
         scratch += [pltpu.SemaphoreType.DMA((len(cargo),))] * 2
     results = pl.pallas_call(
-        functools.partial(send_home_kernel, size, adds, extra is not None, len(cargo)),
+        functools.partial(send_home_kernel, size, adds, extra is not None, tuple(axis for _, axis in cargo)),
         in_specs=in_specs,
         out_specs=out_specs,
         out_shape=shapes,
@@ -597,14 +621,14 @@
     rows_ref = refs[0]
     gates, ups = refs[1 : 1 + world], refs[1 + world : 1 + 2 * world]
     refs = refs[1 + 2 * world :]
-    blocks, refs = refs[:size], refs[size:]
+    blocks, beside_ref, refs = refs[:size], refs[size], refs[size + 1 :]
     hidden_ref, by_gate_ref, by_up_ref, cot_ref, y_land, y_send, y_recv = refs
     width = rows_ref.shape[1] // world
     mine, place = lax.axis_index("ctx"), lax.axis_index("tp")
     other_tp = {"tp": 1 - place}
     beside = [
         remote(blocks[distance], y_land.at[distance], (y_send, y_recv), distance, other_tp)
-        for distance in range(size)
+        for distance in range(1, size)
     ]
 
     @pl.when(pl.program_id(0) == 0)
@@ -629,9 +653,11 @@
     @pl.when(pl.program_id(0) == pl.num_programs(0) - 1)
     def _():
         rows, half = y_land.shape[1], y_land.shape[2]
-        for distance, copy in enumerate(beside):
-            copy.wait_recv()
-            own, theirs = blocks[distance][...], y_land[distance]
+        for distance in range(size):
+            if distance:
+                beside[distance - 1].wait_recv()
+            own = blocks[distance][...]
+            theirs = y_land[distance] if distance else beside_ref[...]
             here = span(xor_index(mine, distance), rows)
             cot_ref[here, :half] = jnp.where(place == 0, own, theirs)
             cot_ref[here, half:] = jnp.where(place == 0, theirs, own)
@@ -639,7 +665,7 @@
             copy.wait_send()
 
 
-def expert_forward(rows, gate_pieces, up_pieces, cot_blocks, number):
+def expert_forward(rows, gate_pieces, up_pieces, cot_blocks, cot_beside, number):
     world, size = len(gate_pieces), len(cot_blocks)
     slots, features = rows.shape
     depth, hidden_width = gate_pieces[0].shape
@@ -649,7 +675,7 @@
     return pl.pallas_call(
         functools.partial(expert_forward_kernel, world, size),
         grid=(hidden_width // TILE,),
-        in_specs=[whole(rows)] + [tall] * (2 * world) + [whole(block) for block in cot_blocks],
+        in_specs=[whole(rows)] + [tall] * (2 * world) + [whole(block) for block in cot_blocks] + [whole(cot_beside)],
         out_specs=[strip] * 3 + [pl.BlockSpec((slots, features), lambda i: (0, 0))],
         out_shape=[jax.ShapeDtypeStruct((slots, hidden_width), LOW)] * 3
         + [jax.ShapeDtypeStruct((slots, features), LOW)],
@@ -659,7 +685,41 @@
             collective_id=number, has_side_effects=True, vmem_limit_bytes=VMEM_BYTES
         ),
         cost_estimate=pl.CostEstimate(flops=0, bytes_accessed=2 * slots * features, transcendentals=0),
-    )(rows, *gate_pieces, *up_pieces, *cot_blocks)
+    )(rows, *gate_pieces, *up_pieces, *cot_blocks, cot_beside)
+
+
+def product_kernel(world, tiles, hidden_ref, *refs):
+    downs, out_ref = refs[:world], refs[world]
+    for n in range(world):
+
+        @pl.when(pl.program_id(0) // tiles == n)
+        def _():
+            out_ref[...] = matmul(hidden_ref[...], downs[n][...]).astype(LOW)
+
+
+def expert_product(hidden, down_pieces):
+    world = len(down_pieces)
+    depth, width = down_pieces[0].shape
+    tiles = max(width // TILE, 1)
+    tile = width // tiles
+
+    def piece_spec(n):
+        return pl.BlockSpec((depth, tile), lambda i: (0, jnp.clip(i - n * tiles, 0, tiles - 1)))
+
+    return pl.pallas_call(
+        functools.partial(product_kernel, world, tiles),
+        grid=(world * tiles,),
+        in_specs=[pl.BlockSpec(hidden.shape, lambda i: (0, 0), pipeline_mode=pl.Buffered(1))]
+        + [piece_spec(n) for n in range(world)],
+        out_specs=pl.BlockSpec((hidden.shape[0], tile), lambda i: (0, i)),
+        out_shape=jax.ShapeDtypeStruct((hidden.shape[0], world * width), LOW),
+        compiler_params=pltpu.CompilerParams(vmem_limit_bytes=VMEM_BYTES),
+        cost_estimate=pl.CostEstimate(
+            flops=2 * hidden.shape[0] * depth * world * width,
+            bytes_accessed=2 * depth * world * width,
+            transcendentals=0,
+        ),
+    )(hidden, *down_pieces)
 
 
 def expert_back_kernel(world, steps, size, *refs):
@@ -742,10 +802,6 @@
     mixed_low = (hidden * mix).astype(LOW)
     d_gate = (d_gated * by_gate_ref[...].astype(FULL)).astype(LOW)
     d_up = (d_gated * by_up_ref[...].astype(FULL)).astype(LOW)
-    for n in range(world):
-        columns = slice(n * width, (n + 1) * width)
-        db_sum[:, columns] += matmul_nt(d_gate, gates[n][...]) + matmul_nt(d_up, ups[n][...])
-
     @pl.when(step >= 2)
     def _():
         far_copy(step - 2, slot).wait_send()
@@ -754,6 +810,10 @@
     for n, (left, right) in enumerate(pairs):
         far[slot, n] = matmul(left[half:, :], right).astype(LOW)
     far_copy(step, slot).start()
+    for n in range(world):
+        columns = slice(n * width, (n + 1) * width)
+        db_sum[:, columns] += matmul_nt(d_gate, gates[n][...]) + matmul_nt(d_up, ups[n][...])
+
     for n, (left, right) in enumerate(pairs):
         near_ref[0, n] = matmul(left[:half, :], right).astype(LOW)
 
@@ -1185,7 +1245,12 @@
     q_low, k_low, v_low, heads_low, log_sum = attend(
         query_lin, kv_lin, query_table, key_table, groups
     )
-    attn_back = send_home(after(matmul(heads_low, out_full).astype(LOW), *cot_blocks), 1)
+    cargo = [(item, "core") for item in gate_pieces + [up_proj[0], down_proj[0]]]
+    cargo = [(after(cot_blocks[0], *cot_blocks[1:]), "tp")] + cargo
+    attn_back, cot_beside, *known = send_home(
+        matmul(heads_low, out_full).astype(LOW), 1, cargo=cargo
+    )
+    gate_known, up_known, down_known = known[:-2], known[-2:-1], known[-1:]
 
     input_half = my_half(tokens_spread).astype(FULL)
     attn_picked = [matmul(pick, attn_back) for pick in attn_picks]
@@ -1195,10 +1260,10 @@
     square_sum = tp_sum(jnp.sum(attended * attended, axis=1, keepdims=True))
     scale_two = lax.rsqrt(square_sum / features + EPSILON)
     b_half = (attended * scale_two * gain2_half).astype(LOW)
-    gate_all = with_neighbours(gate_pieces, heads_low)
-    up_all = with_neighbours(up_pieces, attn_back)
+    gate_all = with_neighbours(gate_pieces, gate_known)
     b_slots = matmul_tn(ffn_pick, b_half).astype(LOW)
-    ffn_rows = send_out(after(b_slots, *gate_all[1:], *up_all[1:]), 2)
+    up_all = with_neighbours(up_pieces, up_known, b_slots)
+    ffn_rows = send_out(after(b_slots, up_all[-1]), 2)
     ffn_logits = tp_sum(matmul(b_half, router2_half))
     ffn_probs = jax.nn.softmax(ffn_logits, axis=1)
     ffn_mix = mix_of(ffn_logits, ffn_onehot)
@@ -1212,9 +1277,9 @@
     row_mix = mix_of(matmul(ffn_rows, router2), row_onehot.astype(FULL))
     mine_too = (row_routes == mine.astype(FULL)).astype(FULL)
     mix_rows = jnp.broadcast_to(jnp.sum(row_mix * mine_too, axis=1, keepdims=True), (slots, HEAD))
-    *forward, cot_rows = expert_forward(ffn_rows, gate_all, up_all, cot_blocks, 6)
-    down_all = with_neighbours(down_pieces, forward[0])
-    ffn_out = jnp.concatenate([matmul(forward[0], piece).astype(LOW) for piece in down_all], axis=1)
+    *forward, cot_rows = expert_forward(ffn_rows, gate_all, up_all, cot_blocks, cot_beside, 6)
+    down_all = with_neighbours(down_pieces, down_known, forward[0])
+    ffn_out = expert_product(forward[0], down_all)
     pieces = (gate_all, up_all, down_all)
     tiles = gate_proj.shape[2] // TILE
     count_one = (tiles + 1) // 2
@@ -1280,9 +1345,17 @@
     kv_sent, kv_finish = scatter_start(
         lambda low, high: matmul_tn(a_seq[:, low:high], dkv_low), features, 0
     )
-    da_half, kv_back, out_back = send_home(
-        da_seq.astype(LOW), 5, cargo=(kv_sent, out_sent), add_up=True
-    )
+    result = attended
+    for k in range(picks_each):
+        result = result + ffn_mix[:, k : k + 1] * matmul(ffn_picks[k], ffn_back)
+    result_low = result.astype(LOW)
+    da_half, kv_back, out_back, result_other = send_home(
+        da_seq.astype(LOW),
+        5,
+        cargo=((kv_sent, "fsdp"), (out_sent, "fsdp"), (result_low, "tp")),
+        add_up=True,
+    )
+    output = from_spread(join_halves(result_low, result_other), 1)
     kv_part = kv_finish(kv_back)
     query_sent, query_finish = scatter_start(
         lambda low, high: matmul_tn(rows_in[:, low:high], after(dq_low, kv_part)), features, 0
@@ -1296,15 +1369,9 @@
             kv_grad = kv_grad + kv_arrived.astype(FULL)
     query_grad = query_finish(query_back)
     out_grad = out_finish(out_back)
-    back_one, back_two = lax.optimization_barrier((back_one, back_two, query_back))[:2]
+    back_one, back_two = lax.optimization_barrier((back_one, back_two, query_sent))[:2]
     gate_grad, up_grad, down_grad = finish_experts(parts_one + [back_one], parts_two + [back_two])
     key_width = key_proj.shape[1]
-
-    result = attended
-    for k in range(picks_each):
-        result = result + ffn_mix[:, k : k + 1] * matmul(ffn_picks[k], ffn_back)
-    result_low = result.astype(LOW)
-    output = from_spread(join_halves(result_low, swap(result_low, "tp", 1)), 1)
 
     attn_mix_grad = tp_sum(
         jnp.concatenate(
@@ -1330,7 +1397,11 @@
     small = from_spread(join_halves(small, swap(small, "tp", 1)), 1)
     prob_sums = jnp.concatenate([jnp.sum(attn_probs, axis=0), jnp.sum(ffn_probs, axis=0)])
     small = jnp.concatenate([small, jnp.pad(prob_sums, (0, features - prob_sums.shape[0]))[None]], axis=0)
-    small = all_sum(after(all_sum(small, ("fsdp",)), query_back), ("ctx",))
+    small = after(all_sum(small, ("fsdp",)), query_back)
+    for bit in bits_down(groups):
+        small = small + swap(small, "ctx", bit)
+        if bit > 1:
+            small = after(small, gate_grad)
     prob_sums = small[-1, : 2 * expert_count].reshape(2, expert_count)
     losses = expert_count * jnp.sum(share * prob_sums / all_tokens, axis=1)
     return (

time: 838 us -> 801 us (0.956)
  matrix products: 121 us -> 104 us
  waiting for transfers between devices: 53.1 us -> 41.1 us
    dot_general x20 -> x16, matrix products: 52.2 us -> 36.4 us  [matmul(): return jnp.dot(lhs, rhs, preferred_element_type=FULL)]
    pallas_call x0 -> x1, Pallas kernels: none -> 14.6 us  [expert_product(): pl.pallas_call(functools.partial(product_kernel, world, tiles), grid=(wor...]
    ppermute x33 -> x28, waiting for transfers between devices: 53.1 us -> 41.1 us  [swap(): return lax.ppermute(value, axis, [(i, i ^ distance) for i in range(size)])]
    ppermute x33 -> x28, starting transfers between devices: 36.8 us -> 29.7 us  [swap(): return lax.ppermute(value, axis, [(i, i ^ distance) for i in range(size)])]
  transfers between devices with their start and end apart: 33 -> 28, of which waited for: 9 -> 12; matrix products, arithmetic and copies ran while one was open for 18% -> 18% of each run, Pallas kernels for 37% -> 36%
where the time goes in v6:
time: 801 us; the launch traced here: 796 us
  Pallas kernels  542 us (68%)
  matrix products  104 us (13%)
  other arithmetic  52.1 us (7%)
  waiting for transfers between devices  41.1 us (5%)
  starting transfers between devices  29.7 us (4%)
  local copies, waits for them, and re-layouts  24.4 us (3%)
    pallas_call x3, Pallas kernels, send_home(): pl.pallas_call(functools.partial(send_home_kernel, size, adds, extra is n...  156 us
    pallas_call x1, Pallas kernels, prologue(): pl.pallas_call(functools.partial(prologue_kernel, (groups, world)), in_sp...  110 us
    pallas_call x2, Pallas kernels, expert_back(): pl.pallas_call(functools.partial(expert_back_kernel, world, steps, size),...  96.2 us
    pallas_call x2, Pallas kernels, send_out(): pl.pallas_call(functools.partial(send_out_kernel, size), in_specs=[pl.Blo...  76.1 us
    ppermute x28, waiting for transfers between devices, swap(): return lax.ppermute(value, axis, [(i, i ^ distance) for i in range(size)])  41.1 us
    dot_general x13, matrix products, matmul_tn(): lax.dot_general(lhs, rhs, (((0,), (0,)), ((), ())), preferred_element_typ...  39 us
    dot_general x16, matrix products, matmul(): return jnp.dot(lhs, rhs, preferred_element_type=FULL)  36.4 us
    ppermute x28, starting transfers between devices, swap(): return lax.ppermute(value, axis, [(i, i ^ distance) for i in range(size)])  29.7 us
  transfers between devices with their start and end apart: 28, of which 12 were waited for; matrix products, arithmetic and copies ran while one was open for 18% of the time, Pallas kernels for 36%

profile of v6, /device:TPU:0, one launch (start us, length us, event | category | flops | bytes accessed | tf_op | source)
XLA Modules:
  0.0 795.9 jit_solution(7938174139115242825)
XLA Ops:
  10.1 109.7 %shard_map.271 = (bf16[2,1024,1024]{2,1,0:T(8,128)(2,1)}, s32[4,4,8,256]{3,2,1,0:T(8,128)}, bf16[2048,2048]{1,0:T(8,128)(2,1)}, bf16[2048,1024]{1,0:T(8,128)(2,1)}, bf16[4,1024,512]{2,1,0:T(8,128)(2,1)}) custom-call(bf16[256,1024]{1,0:T(8,128)(2,1)} %maximum_select_fusion.refs_0_, bf16[256,2048]{1,0:T(8,128)(2,1)} %pad_maximum_fusion.3.refs_1_, ...), custom_call_target="tpu_custom_call" | custom-call | bytes 100000000 | tf_op jit(solution)/shard_map/pallas_call | solution.py:601
  134.7 5.5 slice_bitcast_fusion.10
  152.8 14.7 %fusion.138.k_lin.v_lin = f32[1024,2048]{1,0:T(8,128)} fusion(bf16[1024,2048]{1,0:T(8,128)(2,1)} %fusion.2, bf16[2048,2048]{1,0:T(8,128)(2,1)} %get-tuple-element.76), kind=kOutput, calls=%fused_computation.346 | convolution fusion | flops 8589934592 | bytes 20971520 | tf_op jit(solution)/shard_map/dot_general | solution.py:24
  175.6 19.1 %shard_map.272 = (bf16[640,1024]{1,0:T(8,128)(2,1)}, bf16[1024,1024]{1,0:T(8,128)(2,1)}, bf16[1024,1024]{1,0:T(8,128)(2,1)}, bf16[640,1024]{1,0:T(8,128)(2,1)}, f32[640,1024]{1,0:T(8,128)}) custom-call(f32[640,1024]{1,0:T(8,128)} %fusion.137.q_lin, f32[1024,2048]{1,0:T(8,128)} %fusion.138.k_lin.v_lin, f32[1024,2048]{1,0:T(8,128)} %fusion.138.k_lin.v_lin, ...), custom_call_target="tpu_custom_call" | custom-call | bytes 20971520 | tf_op jit(solution)/shard_map/pallas_call | solution.py:1038
  197.6 5.3 convolution_convert_fusion.2.refs_0_
  203.0 41.9 %shard_map.273 = (bf16[640,1024]{1,0:T(8,128)(2,1)}, bf16[160,1024]{1,0:T(8,128)(2,1)}, bf16[512,2816]{1,0:T(8,128)(2,1)}, bf16[512,2816]{1,0:T(8,128)(2,1)}, bf...) custom-call(bf16[640,2048]{1,0:T(8,128)(2,1)} %convolution_convert_fusion.2.refs_0_, ...), custom_call_target="tpu_custom_call" | custom-call | bytes 7864320 | tf_op jit(solution)/shard_map/pallas_call | solution.py:394
  260.5 39.7 %shard_map.274.refs_0_ = bf16[640,2048]{1,0:T(8,128)(2,1)} custom-call(bf16[640,1024]{1,0:T(8,128)(2,1)} %convolution_convert_fusion.6.rows_ref), custom_call_target="tpu_custom_call" | custom-call | bytes 7864320 | tf_op jit(solution)/shard_map/pallas_call | solution.py:251
  300.4 28.0 %shard_map.275 = (bf16[640,2816]{1,0:T(8,128)(2,1)}, bf16[640,2816]{1,0:T(8,128)(2,1)}, bf16[640,2816]{1,0:T(8,128)(2,1)}, bf16[640,2048]{1,0:T(8,128)(2,1)}) custom-call(bf16[640,2048]{1,0:T(8,128)(2,1)} %shard_map.274.refs_0_, bf16[512,2816]{1,0:T(8,128)(2,1)} %bitcast.139, bf16[512,2816]{1,0:T(8,128)(2,1)} %collective-permute-done.3.refs_3_.refs_2_.refs_7_, ...), custom_call_target="tpu_custom_call" | custom-call | bytes 2621440 | tf_op jit(solution)/shard_map/pallas_call | solution.py:675
  334.1 14.6 %shard_map.276.refs_18_ = bf16[640,2048]{1,0:T(8,128)(2,1)} custom-call(bf16[640,2816]{1,0:T(8,128)(2,1)} %get-tuple-element.94.hidden_ref.refs_3_, bf16[2816,512]{1,0:T(8,128)(2,1)} %bitcast.21.refs_5_.refs_0_.refs_14_, bf16[2816,512]{1,0:T(8,128)(2,1)} %collective-permute-done.7.refs_1_.refs_15_, bf16[2816,512]{1,0:T(8,128)(2,1)} %get-tuple-element.98.refs_2_.refs_16_, ...), custom_call_target="tpu_custom_call" | custom-call | flops 7381975040 | bytes 11534336 | tf_op jit(solution)/shard_map/pallas_call | solution.py:709
  349.6 54.1 %shard_map.277 = (bf16[6,3,1024,256]{3,2,1,0:T(8,128)(2,1)}, bf16[6,3,1024,256]{3,2,1,0:T(8,128)(2,1)}, bf16[640,2048]{1,0:T(8,128)(2,1)}, f32[640,128]{1,0:T(8,128)}, bf16[640,1024]{1,0:T(8,128)(2,1)}) custom-call(bf16[640,2048]{1,0:T(8,128)(2,1)} %shard_map.274.refs_0_, bf16[640,2048]{1,0:T(8,128)(2,1)} %get-tuple-element.93.refs_1_, ...), custom_call_target="tpu_custom_call" | custom-call | bytes 2621440 | tf_op jit(solution)/shard_map/pallas_call | solution.py:892
  403.8 7.5 add_convert_fusion
  416.0 42.1 %shard_map.278 = (bf16[5,3,1024,256]{3,2,1,0:T(8,128)(2,1)}, bf16[5,3,1024,256]{3,2,1,0:T(8,128)(2,1)}, bf16[640,2048]{1,0:T(8,128)(2,1)}, f32[640,128]{1,0:T(8,128)}) custom-call(bf16[640,2048]{1,0:T(8,128)(2,1)} %shard_map.274.refs_0_, bf16[640,2048]{1,0:T(8,128)(2,1)} %get-tuple-element.93.refs_1_, f32[640,128]{1,0:T(8,128)} %broadcast_in_dim.41.refs_2_, ...), custom_call_target="tpu_custom_call" | custom-call | bytes 2621440 | tf_op jit(solution)/shard_map/pallas_call | solution.py:892
  459.4 6.5 add_convert_fusion.1
  470.7 39.2 %shard_map.279 = (bf16[640,1024]{1,0:T(8,128)(2,1)}, f32[4,8,256]{2,1,0:T(8,128)}) custom-call(bf16[640,2048]{1,0:T(8,128)(2,1)} %add_convert_fusion.2.refs_0_, f32[4,8,256]{2,1,0:T(8,128)} %pad.8.refs_1_), custom_call_target="tpu_custom_call" | custom-call | bytes 7864320 | tf_op jit(solution)/shard_map/pallas_call | solution.py:394
  526.6 36.3 %shard_map.280 = bf16[640,2048]{1,0:T(8,128)(2,1)} custom-call(bf16[640,1024]{1,0:T(8,128)(2,1)} %add_convert_fusion.4.rows_ref), custom_call_target="tpu_custom_call" | custom-call | bytes 7864320 | tf_op jit(solution)/shard_map/pallas_call | solution.py:251
  563.0 5.8 convolution_convert_fusion.5.d_heads
  568.8 23.6 %shard_map.281 = (bf16[640,1024]{1,0:T(8,128)(2,1)}, bf16[1024,1024]{1,0:T(8,128)(2,1)}, bf16[1024,1024]{1,0:T(8,128)(2,1)}) custom-call(bf16[640,1024]{1,0:T(8,128)(2,1)} %get-tuple-element.77.q_low, bf16[1024,1024]{1,0:T(8,128)(2,1)} %get-tuple-element.78.k_low, bf16[1024,1024]{1,0:T(8,128)(2,1)} %get-tuple-element.79.v_low, ...), custom_call_target="tpu_custom_call" | custom-call | bytes 14680064 | tf_op jit(solution)/shard_map/pallas_call | solution.py:1093
  599.4 6.2 convolution_convert_fusion
  610.7 12.8 %fusion.3.refs_0_ = bf16[1024,2048]{1,0:T(8,128)(2,1)} fusion(f32[4,256,2048]{2,1,0:T(8,128)S(1)} %fusion.52, bf16[1024,2048]{1,0:T(8,128)(2,1)S(1)} %pad_maximum_fusion.2, bf16[2048,2048]{1,0:T(8,128)(2,1)} %get-tuple-element.76), kind=kOutput, calls=%fused_computation.7 | convolution fusion | flops 8594128896 | bytes 25165824 | tf_op jit(solution)/shard_map/dot_general | solution.py:32
  628.8 5.6 add_convert_fusion.3.refs_1_
  634.4 75.1 %shard_map.282 = (f32[256,1024]{1,0:T(8,128)}, bf16[512,2048]{1,0:T(8,128)(2,1)}, bf16[1024,512]{1,0:T(8,128)(2,1)}, bf16[256,1024]{1,0:T(8,128)(2,1)}) custom-call(bf16[1024,2048]{1,0:T(8,128)(2,1)} %fusion.3.refs_0_, bf16[512,2048]{1,0:T(8,128)(2,1)} %add_convert_fusion.3.refs_1_, bf16[1024,512]{1,0:T(8,128)(2,1)} %add_convert_fusion.6.refs_2_, ...), custom_call_target="tpu_custom_call" | custom-call | bytes 12582912 | tf_op jit(solution)/shard_map/pallas_call | solution.py:394
  746.6 8.9 %collective-permute-done.26 = bf16[128,2048]{1,0:T(8,128)(2,1)S(1)} collective-permute-done((bf16[128,2048]{1,0:T(8,128)(2,1)S(1)}, bf16[128,2048]{1,0:T(8,128)(2,1)S(1)}, u32[]{:S(2)}, u32[]{:S(2)}) %collective-permute-start.26) | collective-permute-done | bytes 524320 | tf_op jit(solution)/shard_map/ppermute | solution.py:41
  757.0 8.7 %collective-permute-done.22 = bf16[512,1024]{1,0:T(8,128)(2,1)S(1)} collective-permute-done((bf16[512,1024]{1,0:T(8,128)(2,1)S(1)}, bf16[512,1024]{1,0:T(8,128)(2,1)S(1)}, u32[]{:S(2)}, u32[]{:S(2)}) %collective-permute-start.22) | collective-permute-done | bytes 1048608 | tf_op jit(solution)/shard_map/ppermute | solution.py:41
  770.2 18.3 %shard_map.283 = (f32[512,2816]{1,0:T(8,128)}, f32[512,2816]{1,0:T(8,128)}, f32[2816,512]{1,0:T(8,128)}) custom-call(bf16[6,3,1024,256]{3,2,1,0:T(8,128)(2,1)} %get-tuple-element.101.refs_0_, bf16[6,3,1024,256]{3,2,1,0:T(8,128)(2,1)} %get-tuple-element.102.refs_1_, bf16[6,3,512,256]{3,2,1,0:T(8,128)(2,1)} %collective-permute-done.9.refs_2_, ...), custom_call_target="tpu_custom_call" | custom-call | bytes 43253760 | tf_op jit(solution)/shard_map/pallas_call | solution.py:951
  (428 shorter events, 163.9 us)
Async XLA Ops:
  122.0 81.0 %collective-permute-start.2 = (bf16[160,1024]{1,0:T(8,128)(2,1)}, bf16[160,1024]{1,0:T(8,128)(2,1)}, u32[]{:S(2)}, u32[]{:S(2)}) collective-permute-start(bf16[160,1024]{1,0:T(8,128)(2,1)} %get-tuple-element.171), channel_id=1, source_target_pairs={{0,6},{2,4},{4,2},{6,0},{1,7},{3,5},{5,3},{7,1},{8,14},{10,12},{12... | collective-permute-start | bytes 983048 | tf_op jit(solution)/shard_map/ppermute | solution.py:41
  124.4 78.7 %collective-permute-start.1 = (bf16[160,1024]{1,0:T(8,128)(2,1)S(1)}, bf16[160,1024]{1,0:T(8,128)(2,1)}, u32[]{:S(2)}, u32[]{:S(2)}) collective-permute-start(bf16[160,1024]{1,0:T(8,128)(2,1)S(1)} %get-tuple-element.172), channel_id=1, source_target_pairs={{0,4},{2,6},{4,0},{6,2},{1,5},{3,7},{5,1},{7,3},{8,12},{10,14},{12... | collective-permute-start | bytes 983048 | tf_op jit(solution)/shard_map/ppermute | solution.py:41
  124.4 78.7 %collective-permute-start = (bf16[160,1024]{1,0:T(8,128)(2,1)S(1)}, bf16[160,1024]{1,0:T(8,128)(2,1)}, u32[]{:S(2)}, u32[]{:S(2)}) collective-permute-start(bf16[160,1024]{1,0:T(8,128)(2,1)S(1)} %get-tuple-element.173), channel_id=1, source_target_pairs={{0,2},{2,0},{4,6},{6,4},{1,3},{3,1},{5,7},{7,5},{8,10},{10,8},{12,... | collective-permute-start | bytes 983048 | tf_op jit(solution)/shard_map/ppermute | solution.py:41
  126.4 76.6 %collective-permute-start.3 = (bf16[512,2816]{1,0:T(8,128)(2,1)S(1)}, bf16[512,2816]{1,0:T(8,128)(2,1)}, u32[]{:S(2)}, u32[]{:S(2)}) collective-permute-start(bf16[512,2816]{1,0:T(8,128)(2,1)S(1)} %bitcast.142), channel_id=1, source_target_pairs={{0,16},{8,24},{16,0},{24,8},{1,17},{9,25},{17,1},{25,9},{2,18},{10... | collective-permute-start | bytes 8650760 | tf_op jit(solution)/shard_map/ppermute | solution.py:41
  127.0 128.0 %collective-permute-start.5 = (bf16[512,2816]{1,0:T(8,128)(2,1)}, bf16[512,2816]{1,0:T(8,128)(2,1)}, u32[]{:S(2)}, u32[]{:S(2)}) collective-permute-start(bf16[512,2816]{1,0:T(8,128)(2,1)} %bitcast.143), channel_id=1, source_target_pairs={{0,16},{8,24},{16,0},{24,8},{1,17},{9,25},{17,1},{25,9},{2,18},{10... | collective-permute-start | bytes 8650760 | tf_op jit(solution)/shard_map/ppermute | solution.py:41
  254.9 5.6 collective-permute-start.6
  255.0 73.4 %collective-permute-start.7 = (bf16[2816,512]{1,0:T(8,128)(2,1)}, bf16[2816,512]{1,0:T(8,128)(2,1)}, u32[]{:S(2)}, u32[]{:S(2)}) collective-permute-start(bf16[2816,512]{1,0:T(8,128)(2,1)} %bitcast.21.refs_5_.refs_0_.refs_14_), channel_id=1, source_target_pairs={{0,16},{8,24},{16,0},{24,8},{1,17},{9,25},{17,1},{25,9},{2,18},{10... | collective-permute-start | bytes 8650760 | tf_op jit(solution)/shard_map/ppermute | solution.py:41
  328.4 5.7 collective-permute-start.8
  411.3 105.0 %collective-permute-start.9 = (bf16[6,3,512,256]{3,2,1,0:T(8,128)(2,1)}, bf16[6,3,512,256]{3,2,1,0:T(8,128)(2,1)}, u32[]{:S(2)}, u32[]{:S(2)}) collective-permute-start(bf16[6,3,512,256]{3,2,1,0:T(8,128)(2,1)} %add_convert_fusion), channel_id=1, source_target_pairs={{0,16},{8,24},{16,0},{24,8},{1,17},{9,25},{17,1},{25,9},{2,18},{10... | collective-permute-start | bytes 14155784 | tf_op jit(solution)/shard_map/ppermute | solution.py:41
  465.9 133.5 %collective-permute-start.12 = (bf16[5,3,512,256]{3,2,1,0:T(8,128)(2,1)}, bf16[5,3,512,256]{3,2,1,0:T(8,128)(2,1)}, u32[]{:S(2)}, u32[]{:S(2)}) collective-permute-start(bf16[5,3,512,256]{3,2,1,0:T(8,128)(2,1)} %add_convert_fusion.1), channel_id=1, source_target_pairs={{0,16},{8,24},{16,0},{24,8},{1,17},{9,25},{17,1},{25,9},{2,18},{10... | collective-permute-start | bytes 11796488 | tf_op jit(solution)/shard_map/ppermute | solution.py:41
  522.5 101.0 %collective-permute-start.15 = (f32[256,2]{0,1:T(2,128)S(1)}, f32[256,2]{0,1:T(2,128)S(1)}, u32[]{:S(2)}, u32[]{:S(2)}) collective-permute-start(f32[256,2]{0,1:T(2,128)S(1)} %pad_maximum_fusion.14), channel_id=1, source_target_pairs={{0,1},{1,0},{2,3},{3,2},{4,5},{5,4},{6,7},{7,6},{8,9},{9,8},{10,11... | collective-permute-start | bytes 6152 | tf_op jit(solution)/shard_map/ppermute | solution.py:41
  605.6 23.1 %collective-permute-start.13 = (bf16[1024,2048]{1,0:T(8,128)(2,1)}, bf16[1024,2048]{1,0:T(8,128)(2,1)}, u32[]{:S(2)}, u32[]{:S(2)}) collective-permute-start(bf16[1024,2048]{1,0:T(8,128)(2,1)} %convolution_convert_fusion), channel_id=1, source_target_pairs={{0,8},{8,0},{16,24},{24,16},{1,9},{9,1},{17,25},{25,17},{2,10},{10... | collective-permute-start | bytes 12582920 | tf_op jit(solution)/shard_map/ppermute | solution.py:41
  608.8 16.5 %collective-permute-start.14 = (bf16[1024,1024]{1,0:T(8,128)(2,1)}, bf16[1024,1024]{1,0:T(8,128)(2,1)}, u32[]{:S(2)}, u32[]{:S(2)}) collective-permute-start(bf16[1024,1024]{1,0:T(8,128)(2,1)} %convolution_convert_fusion.4), channel_id=1, source_target_pairs={{0,8},{8,0},{16,24},{24,16},{1,9},{9,1},{17,25},{25,17},{2,10},{10... | collective-permute-start | bytes 6291464 | tf_op jit(solution)/shard_map/ppermute | solution.py:41
  716.9 13.8 %collective-permute-start.16 = (f32[256,1]{0,1:T(1,128)S(1)}, f32[256,1]{0,1:T(1,128)S(1)}, u32[]{:S(2)}, u32[]{:S(2)}) collective-permute-start(f32[256,1]{0,1:T(1,128)S(1)} %bitcast.219), channel_id=1, source_target_pairs={{0,1},{1,0},{2,3},{3,2},{4,5},{5,4},{6,7},{7,6},{8,9},{9,8},{10,11... | collective-permute-start | bytes 3080 | tf_op jit(solution)/shard_map/ppermute | solution.py:41
  718.5 9.9 %collective-permute-start.18 = (f32[10,1024]{1,0:T(8,128)S(1)}, f32[10,1024]{1,0:T(8,128)S(1)}, u32[]{:S(2)}, u32[]{:S(2)}) collective-permute-start(f32[10,1024]{1,0:T(8,128)S(1)} %pad_maximum_fusion.9), channel_id=1, source_target_pairs={{0,1},{1,0},{2,3},{3,2},{4,5},{5,4},{6,7},{7,6},{8,9},{9,8},{10,11... | collective-permute-start | bytes 122888 | tf_op jit(solution)/shard_map/ppermute | solution.py:41
  719.3 27.3 %collective-permute-start.25 = (bf16[128,2048]{1,0:T(8,128)(2,1)S(1)}, bf16[128,2048]{1,0:T(8,128)(2,1)S(1)}, u32[]{:S(2)}, u32[]{:S(2)}) collective-permute-start(bf16[128,2048]{1,0:T(8,128)(2,1)S(1)} %get-tuple-element.168), channel_id=1, source_target_pairs={{0,4},{2,6},{4,0},{6,2},{1,5},{3,7},{5,1},{7,3},{8,12},{10,14},{12... | collective-permute-start | bytes 1572872 | tf_op jit(solution)/shard_map/ppermute | solution.py:41
  720.9 25.7 %collective-permute-start.27 = (bf16[128,2048]{1,0:T(8,128)(2,1)S(1)}, bf16[128,2048]{1,0:T(8,128)(2,1)S(1)}, u32[]{:S(2)}, u32[]{:S(2)}) collective-permute-start(bf16[128,2048]{1,0:T(8,128)(2,1)S(1)} %get-tuple-element.169), channel_id=1, source_target_pairs={{0,2},{2,0},{4,6},{6,4},{1,3},{3,1},{5,7},{7,5},{8,10},{10,8},{12,... | collective-permute-start | bytes 1572872 | tf_op jit(solution)/shard_map/ppermute | solution.py:41
  723.4 16.3 %collective-permute-start.21 = (bf16[1024,1024]{1,0:T(8,128)(2,1)S(1)}, bf16[1024,1024]{1,0:T(8,128)(2,1)S(1)}, u32[]{:S(2)}, u32[]{:S(2)}) collective-permute-start(bf16[1024,1024]{1,0:T(8,128)(2,1)S(1)} %convolution_convert_fusion.3), channel_id=1, source_target_pairs={{0,8},{8,0},{16,24},{24,16},{1,9},{9,1},{17,25},{25,17},{2,10},{10... | collective-permute-start | bytes 6291464 | tf_op jit(solution)/shard_map/ppermute | solution.py:41
  728.4 27.0 %collective-permute-start.26 = (bf16[128,2048]{1,0:T(8,128)(2,1)S(1)}, bf16[128,2048]{1,0:T(8,128)(2,1)S(1)}, u32[]{:S(2)}, u32[]{:S(2)}) collective-permute-start(bf16[128,2048]{1,0:T(8,128)(2,1)S(1)} %get-tuple-element.170), channel_id=1, source_target_pairs={{0,6},{2,4},{4,2},{6,0},{1,7},{3,5},{5,3},{7,1},{8,14},{10,12},{12... | collective-permute-start | bytes 1572872 | tf_op jit(solution)/shard_map/ppermute | solution.py:41
  730.8 5.7 collective-permute-start.19
  737.9 18.9 %collective-permute-start.17 = (bf16[256,1024]{1,0:T(8,128)(2,1)S(1)}, bf16[256,1024]{1,0:T(8,128)(2,1)S(1)}, u32[]{:S(2)}, u32[]{:S(2)}) collective-permute-start(bf16[256,1024]{1,0:T(8,128)(2,1)S(1)} %fusion.23), channel_id=1, source_target_pairs={{0,1},{1,0},{2,3},{3,2},{4,5},{5,4},{6,7},{7,6},{8,9},{9,8},{10,11... | collective-permute-start | bytes 1572872 | tf_op jit(solution)/shard_map/ppermute | solution.py:41
  740.6 25.0 %collective-permute-start.22 = (bf16[512,1024]{1,0:T(8,128)(2,1)S(1)}, bf16[512,1024]{1,0:T(8,128)(2,1)S(1)}, u32[]{:S(2)}, u32[]{:S(2)}) collective-permute-start(bf16[512,1024]{1,0:T(8,128)(2,1)S(1)} %add_convert_fusion.5), channel_id=1, source_target_pairs={{0,16},{8,24},{16,0},{24,8},{1,17},{9,25},{17,1},{25,9},{2,18},{10... | collective-permute-start | bytes 3145736 | tf_op jit(solution)/shard_map/ppermute | solution.py:41
  765.6 22.9 %collective-permute-start.23 = (f32[11,2048]{1,0:T(8,128)S(1)}, f32[11,2048]{1,0:T(8,128)S(1)}, u32[]{:S(2)}, u32[]{:S(2)}) collective-permute-start(f32[11,2048]{1,0:T(8,128)S(1)} %add.267), channel_id=1, source_target_pairs={{0,4},{2,6},{4,0},{6,2},{1,5},{3,7},{5,1},{7,3},{8,12},{10,14},{12... | collective-permute-start | bytes 270344 | tf_op jit(solution)/shard_map/ppermute | solution.py:41
  788.6 5.0 collective-permute-start.24
  (116 other events, 1692.7 us)

commit v7 on v6

--- a/solution.py
+++ b/solution.py
@@ -138,11 +138,6 @@
     size = lax.axis_size("ctx")
     rows = value.shape[0] // size
     return lax.dynamic_slice_in_dim(value, (lax.axis_index("ctx") ^ distance) * rows, rows, 0)
-
-
-def spread_out(half_rows):
-    blocks = [block_for(half_rows, distance) for distance in range(lax.axis_size("ctx"))]
-    return blocks[:1] + [swap(blocks[distance], "ctx", distance) for distance in range(1, len(blocks))]
 
 
 def xor_index(index, distance):
@@ -407,12 +402,12 @@
 
 def prologue_kernel(sizes, *refs):
     groups, world = sizes
-    half_in, own_in, routes_in, kv_in, query_in, out_in = refs[:6]
-    seq_ref, routes_ref, kv_ref, query_ref, out_ref = refs[6:11]
-    local_sem = refs[11]
-    pairs = [(refs[12 + 2 * n], refs[13 + 2 * n]) for n in range(15)]
+    half_in, own_in, routes_in, kv_in, query_in, out_in, cot_in = refs[:7]
+    seq_ref, routes_ref, kv_ref, query_ref, out_ref, cot_ref = refs[7:13]
+    local_sem = refs[13]
+    pairs = [(refs[14 + 2 * n], refs[15 + 2 * n]) for n in range(16)]
     token_line, route_line, kv_line, token_pass, kv_pass = (pairs[2 * n : 2 * n + 2] for n in range(5))
-    kv_own, fr, fk, fq, fo = pairs[10:]
+    kv_own, fr, fk, fq, fo, cot_beside = pairs[10:]
     mine, place, spot = lax.axis_index("ctx"), lax.axis_index("tp"), lax.axis_index("fsdp")
     other_tp = {"tp": 1 - place}
     rows, width = half_in.shape
@@ -532,6 +527,7 @@
     kv_view = lambda n: kv_ref.at[pl.ds(n * piece, piece)]
     query_copies = {1: go(remote(query_in, query_view(1), fq, 1, beside[first]))}
     out_copies = {}
+    go(remote(cot_in, cot_ref, cot_beside, 0, other_tp))
     for copy in locals_:
         copy.start()
     for step in range(groups - 1):
@@ -593,28 +589,33 @@
         copy.wait_send()
 
 
-def prologue(token_half, token_rows, routes, kv_rows, query_piece, out_piece, number):
+def prologue(token_half, token_rows, routes, kv_rows, query_piece, out_piece, cot_block, number):
     groups, world = lax.axis_size("ctx"), lax.axis_size("fsdp")
     any_space = pl.BlockSpec(memory_space=pl.ANY)
     rows, features = token_rows.shape
     pair = lambda count: [pltpu.SemaphoreType.DMA((count,))] * 2
     return pl.pallas_call(
         functools.partial(prologue_kernel, (groups, world)),
-        in_specs=[pl.BlockSpec(memory_space=pltpu.VMEM)] * 6,
-        out_specs=[any_space] * 5,
+        in_specs=[pl.BlockSpec(memory_space=pltpu.VMEM)] * 7,
+        out_specs=[any_space] * 6,
         out_shape=[
             jax.ShapeDtypeStruct((2, groups * rows, features // 2), LOW),
             jax.ShapeDtypeStruct((world, groups) + routes.shape, jnp.int32),
             jax.ShapeDtypeStruct((world * groups * kv_rows.shape[0], kv_rows.shape[1]), LOW),
             jax.ShapeDtypeStruct((world * query_piece.shape[0], query_piece.shape[1]), LOW),
             jax.ShapeDtypeStruct((world,) + out_piece.shape, LOW),
+            jax.ShapeDtypeStruct(cot_block.shape, LOW),
         ],
-        scratch_shapes=[pltpu.SemaphoreType.DMA((6,))] + pair(groups) * 10 + pair(1) + pair(world) * 4,
+        scratch_shapes=[pltpu.SemaphoreType.DMA((6,))]
+        + pair(groups) * 10
+        + pair(1)
+        + pair(world) * 4
+        + pair(1),
         compiler_params=pltpu.CompilerParams(
             collective_id=number, has_side_effects=True, vmem_limit_bytes=VMEM_BYTES
         ),
         cost_estimate=pl.CostEstimate(flops=0, bytes_accessed=100000000, transcendentals=0),
-    )(token_half, token_rows, routes, kv_rows, query_piece, out_piece)
+    )(token_half, token_rows, routes, kv_rows, query_piece, out_piece, cot_block)
 
 
 def expert_forward_kernel(world, size, *refs):
@@ -1183,13 +1184,28 @@
     slots = groups * capacity
     all_tokens = rows_here * lax.axis_size("fsdp") * groups
 
+    attn_picks, attn_onehot = chosen_picks(attn_routes, expert_count, capacity)
+    ffn_picks, ffn_onehot = chosen_picks(ffn_routes, expert_count, capacity)
+    ffn_pick = ffn_picks[0]
+    for pick in ffn_picks[1:]:
+        ffn_pick = ffn_pick + pick
+    cot_half = my_half(to_spread(cotangent, 1))
+    cot_slots = matmul_tn(ffn_pick, cot_half).astype(LOW)
+
     tokens_spread = to_spread(tokens, 1)
     token_half = my_half(tokens_spread)
     routes_mine = jnp.concatenate([attn_routes.T, ffn_routes.T], axis=0)
     routes_mine = jnp.concatenate([routes_mine, jnp.zeros_like(routes_mine)], axis=0)
     kv_mine = jnp.concatenate([key_proj, value_proj], axis=1)
-    seq_low, all_routes, kv_full, query_full, out_pieces = prologue(
-        token_half, tokens_spread, routes_mine, kv_mine, query_proj[0], out_proj[0], 0
+    seq_low, all_routes, kv_full, query_full, out_pieces, cot_beside = prologue(
+        token_half,
+        tokens_spread,
+        routes_mine,
+        kv_mine,
+        query_proj[0],
+        out_proj[0],
+        block_for(cot_slots, 0),
+        0,
     )
     seq_routes = all_routes[0]
     seq_tokens = jnp.concatenate([seq_low[0], seq_low[1]], axis=1).astype(FULL)
@@ -1212,15 +1228,11 @@
     scale_one = lax.dynamic_slice_in_dim(scale_seq, mine * rows_here, rows_here, 0)
     attn_logits = matmul(a_mine, router1)
     attn_probs = jax.nn.softmax(attn_logits, axis=1)
-    attn_picks, attn_onehot = chosen_picks(attn_routes, expert_count, capacity)
-    ffn_picks, ffn_onehot = chosen_picks(ffn_routes, expert_count, capacity)
     attn_mix = mix_of(attn_logits, attn_onehot)
 
-    cot_half = my_half(to_spread(cotangent, 1))
-    ffn_pick = ffn_picks[0]
-    for pick in ffn_picks[1:]:
-        ffn_pick = ffn_pick + pick
-    cot_blocks = spread_out(after(matmul_tn(ffn_pick, cot_half).astype(LOW), all_routes))
+    later = after(cot_slots, all_routes)
+    cot_blocks = [block_for(later, distance) for distance in range(groups)]
+    cot_blocks[1:] = [swap(cot_blocks[distance], "ctx", distance) for distance in range(1, groups)]
 
     expert_onehot = expert_picks(seq_routes[:, :picks_each], mine, capacity)
     key_table = jnp.asarray(turn_tables(groups * rows_here))
@@ -1246,9 +1258,8 @@
         query_lin, kv_lin, query_table, key_table, groups
     )
     cargo = [(item, "core") for item in gate_pieces + [up_proj[0], down_proj[0]]]
-    cargo = [(after(cot_blocks[0], *cot_blocks[1:]), "tp")] + cargo
-    attn_back, cot_beside, *known = send_home(
-        matmul(heads_low, out_full).astype(LOW), 1, cargo=cargo
+    attn_back, *known = send_home(
+        after(matmul(heads_low, out_full).astype(LOW), *cot_blocks[1:]), 1, cargo=cargo
     )
     gate_known, up_known, down_known = known[:-2], known[-2:-1], known[-1:]
 
@@ -1361,16 +1372,19 @@
         lambda low, high: matmul_tn(rows_in[:, low:high], after(dq_low, kv_part)), features, 0
     )
     query_back = last_step(query_sent)
-    kv_grad = block_for(kv_part, 0)
     kv_part_low = kv_part.astype(LOW)
-    for distance in far_first(groups):
-        if distance:
-            kv_arrived = swap(block_for(kv_part_low, distance), "ctx", distance)
-            kv_grad = kv_grad + kv_arrived.astype(FULL)
+    kv_arrived = [
+        swap(block_for(kv_part_low, distance), "ctx", distance)
+        for distance in far_first(groups)
+        if distance
+    ]
     query_grad = query_finish(query_back)
     out_grad = out_finish(out_back)
     back_one, back_two = lax.optimization_barrier((back_one, back_two, query_sent))[:2]
     gate_grad, up_grad, down_grad = finish_experts(parts_one + [back_one], parts_two + [back_two])
+    kv_grad = block_for(kv_part, 0)
+    for block in lax.optimization_barrier((*kv_arrived, gate_grad))[:-1]:
+        kv_grad = kv_grad + block.astype(FULL)
     key_width = key_proj.shape[1]
 
     attn_mix_grad = tp_sum(
@@ -1397,11 +1411,8 @@
     small = from_spread(join_halves(small, swap(small, "tp", 1)), 1)
     prob_sums = jnp.concatenate([jnp.sum(attn_probs, axis=0), jnp.sum(ffn_probs, axis=0)])
     small = jnp.concatenate([small, jnp.pad(prob_sums, (0, features - prob_sums.shape[0]))[None]], axis=0)
-    small = after(all_sum(small, ("fsdp",)), query_back)
-    for bit in bits_down(groups):
-        small = small + swap(small, "ctx", bit)
-        if bit > 1:
-            small = after(small, gate_grad)
+    small = after(all_sum(small, ("fsdp",)), query_back, gate_grad)
+    small = all_sum(small, ("ctx",))
     prob_sums = small[-1, : 2 * expert_count].reshape(2, expert_count)
     losses = expert_count * jnp.sum(share * prob_sums / all_tokens, axis=1)
     return (

time: 801 us -> 792 us (0.989)
  transfers between devices with their start and end apart: 28 -> 28, of which waited for: 12 -> 13; matrix products, arithmetic and copies ran while one was open for 18% -> 18% of each run, Pallas kernels for 36% -> 36%
where the time goes in v7:
time: 792 us; the launch traced here: 787 us
  Pallas kernels  538 us (68%)
  matrix products  106 us (13%)
  other arithmetic  53.4 us (7%)
  waiting for transfers between devices  39.2 us (5%)
  local copies, waits for them, and re-layouts  25.3 us (3%)
  starting transfers between devices  21.8 us (3%)
    pallas_call x3, Pallas kernels, send_home(): pl.pallas_call(functools.partial(send_home_kernel, size, adds, extra is n...  150 us
    pallas_call x1, Pallas kernels, prologue(): pl.pallas_call(functools.partial(prologue_kernel, (groups, world)), in_sp...  110 us
    pallas_call x2, Pallas kernels, expert_back(): pl.pallas_call(functools.partial(expert_back_kernel, world, steps, size),...  94.9 us
    pallas_call x2, Pallas kernels, send_out(): pl.pallas_call(functools.partial(send_out_kernel, size), in_specs=[pl.Blo...  79.4 us
    dot_general x13, matrix products, matmul_tn(): lax.dot_general(lhs, rhs, (((0,), (0,)), ((), ())), preferred_element_typ...  40.9 us
    ppermute x28, waiting for transfers between devices, swap(): return lax.ppermute(value, axis, [(i, i ^ distance) for i in range(size)])  39.2 us
    dot_general x16, matrix products, matmul(): return jnp.dot(lhs, rhs, preferred_element_type=FULL)  36.4 us
    pallas_call x1, Pallas kernels, expert_forward(): pl.pallas_call(functools.partial(expert_forward_kernel, world, size), gri...  28.7 us
  transfers between devices with their start and end apart: 28, of which 13 were waited for; matrix products, arithmetic and copies ran while one was open for 18% of the time, Pallas kernels for 36%

profile of v7, /device:TPU:0, one launch (start us, length us, event | category | flops | bytes accessed | tf_op | source)
XLA Modules:
  0.0 786.7 jit_solution(11739567770933857686)
XLA Ops:
  9.8 109.7 %shard_map.271 = (bf16[2,1024,1024]{2,1,0:T(8,128)(2,1)}, s32[4,4,8,256]{3,2,1,0:T(8,128)}, bf16[2048,2048]{1,0:T(8,128)(2,1)}, bf16[2048,1024]{1,0:T(8,128)(2,1...) custom-call(bf16[256,1024]{1,0:T(8,128)(2,1)} %maximum_select_fusion.refs_0_, ...), custom_call_target="tpu_custom_call" | custom-call | bytes 100000000 | tf_op jit(solution)/shard_map/pallas_call | solution.py:597
  134.5 5.5 slice_bitcast_fusion.10
  152.8 14.6 %fusion.138.k_lin.v_lin = f32[1024,2048]{1,0:T(8,128)} fusion(bf16[1024,2048]{1,0:T(8,128)(2,1)} %fusion.2, bf16[2048,2048]{1,0:T(8,128)(2,1)} %get-tuple-element.78), kind=kOutput, calls=%fused_computation.347 | convolution fusion | flops 8589934592 | bytes 20971520 | tf_op jit(solution)/shard_map/dot_general | solution.py:24
  175.5 19.1 %shard_map.272 = (bf16[640,1024]{1,0:T(8,128)(2,1)}, bf16[1024,1024]{1,0:T(8,128)(2,1)}, bf16[1024,1024]{1,0:T(8,128)(2,1)}, bf16[640,1024]{1,0:T(8,128)(2,1)}, f32[640,1024]{1,0:T(8,128)}) custom-call(f32[640,1024]{1,0:T(8,128)} %fusion.137.q_lin, f32[1024,2048]{1,0:T(8,128)} %fusion.138.k_lin.v_lin, f32[1024,2048]{1,0:T(8,128)} %fusion.138.k_lin.v_lin, ...), custom_call_target="tpu_custom_call" | custom-call | bytes 20971520 | tf_op jit(solution)/shard_map/pallas_call | solution.py:1039
  202.9 35.5 %shard_map.273 = (bf16[640,1024]{1,0:T(8,128)(2,1)}, bf16[512,2816]{1,0:T(8,128)(2,1)}, bf16[512,2816]{1,0:T(8,128)(2,1)}, bf16[512,2816]{1,0:T(8,128)(2,1)}, bf16[2816,512]{1,0:T(8,128)(2,1)}) custom-call(bf16[640,2048]{1,0:T(8,128)(2,1)} %convolution_convert_fusion.2.refs_0_, bf16[512,2816]{1,0:T(8,128)(2,1)} %bitcast.138, ...), custom_call_target="tpu_custom_call" | custom-call | bytes 7864320 | tf_op jit(solution)/shard_map/pallas_call | solution.py:389
  257.6 41.8 %shard_map.274.refs_0_ = bf16[640,2048]{1,0:T(8,128)(2,1)} custom-call(bf16[640,1024]{1,0:T(8,128)(2,1)} %convolution_convert_fusion.6.rows_ref), custom_call_target="tpu_custom_call" | custom-call | bytes 7864320 | tf_op jit(solution)/shard_map/pallas_call | solution.py:246
  299.5 28.7 %shard_map.275 = (bf16[640,2816]{1,0:T(8,128)(2,1)}, bf16[640,2816]{1,0:T(8,128)(2,1)}, bf16[640,2816]{1,0:T(8,128)(2,1)}, bf16[640,2048]{1,0:T(8,128)(2,1)}) custom-call(bf16[640,2048]{1,0:T(8,128)(2,1)} %shard_map.274.refs_0_, bf16[512,2816]{1,0:T(8,128)(2,1)} %bitcast.139, bf16[512,2816]{1,0:T(8,128)(2,1)} %collective-permute-done.3.refs_2_.refs_7_, ...), custom_call_target="tpu_custom_call" | custom-call | bytes 2621440 | tf_op jit(solution)/shard_map/pallas_call | solution.py:676
  333.8 14.6 %shard_map.276.refs_18_ = bf16[640,2048]{1,0:T(8,128)(2,1)} custom-call(bf16[640,2816]{1,0:T(8,128)(2,1)} %get-tuple-element.96.hidden_ref.refs_3_, bf16[2816,512]{1,0:T(8,128)(2,1)} %bitcast.21.refs_4_.refs_0_.refs_14_, bf16[2816,512]{1,0:T(8,128)(2,1)} %collective-permute-done.7.refs_1_.refs_15_, bf16[2816,512]{1,0:T(8,128)(2,1)} %get-tuple-element.100.refs_2_.refs_16_, ...), custom_call_target="tpu_custom_call" | custom-call | flops 7381975040 | bytes 11534336 | tf_op jit(solution)/shard_map/pallas_call | solution.py:710
  349.3 52.9 %shard_map.277 = (bf16[6,3,1024,256]{3,2,1,0:T(8,128)(2,1)}, bf16[6,3,1024,256]{3,2,1,0:T(8,128)(2,1)}, bf16[640,2048]{1,0:T(8,128)(2,1)}, f32[640,128]{1,0:T(8,128)}, bf16[640,1024]{1,0:T(8,128)(2,1)}) custom-call(bf16[640,2048]{1,0:T(8,128)(2,1)} %shard_map.274.refs_0_, bf16[640,2048]{1,0:T(8,128)(2,1)} %get-tuple-element.95.refs_1_, ...), custom_call_target="tpu_custom_call" | custom-call | bytes 2621440 | tf_op jit(solution)/shard_map/pallas_call | solution.py:893
  402.3 7.5 add_convert_fusion
  414.5 42.1 %shard_map.278 = (bf16[5,3,1024,256]{3,2,1,0:T(8,128)(2,1)}, bf16[5,3,1024,256]{3,2,1,0:T(8,128)(2,1)}, bf16[640,2048]{1,0:T(8,128)(2,1)}, f32[640,128]{1,0:T(8,128)}) custom-call(bf16[640,2048]{1,0:T(8,128)(2,1)} %shard_map.274.refs_0_, bf16[640,2048]{1,0:T(8,128)(2,1)} %get-tuple-element.95.refs_1_, f32[640,128]{1,0:T(8,128)} %broadcast_in_dim.41.refs_2_, ...), custom_call_target="tpu_custom_call" | custom-call | bytes 2621440 | tf_op jit(solution)/shard_map/pallas_call | solution.py:893
  457.8 6.5 add_convert_fusion.1
  469.1 39.2 %shard_map.279 = (bf16[640,1024]{1,0:T(8,128)(2,1)}, f32[4,8,256]{2,1,0:T(8,128)}) custom-call(bf16[640,2048]{1,0:T(8,128)(2,1)} %add_convert_fusion.2.refs_0_, f32[4,8,256]{2,1,0:T(8,128)} %pad.8.refs_1_), custom_call_target="tpu_custom_call" | custom-call | bytes 7864320 | tf_op jit(solution)/shard_map/pallas_call | solution.py:389
  523.9 37.6 %shard_map.280 = bf16[640,2048]{1,0:T(8,128)(2,1)} custom-call(bf16[640,1024]{1,0:T(8,128)(2,1)} %add_convert_fusion.4.rows_ref), custom_call_target="tpu_custom_call" | custom-call | bytes 7864320 | tf_op jit(solution)/shard_map/pallas_call | solution.py:246
  561.5 5.8 convolution_convert_fusion.5.d_heads
  567.3 23.6 %shard_map.281 = (bf16[640,1024]{1,0:T(8,128)(2,1)}, bf16[1024,1024]{1,0:T(8,128)(2,1)}, bf16[1024,1024]{1,0:T(8,128)(2,1)}) custom-call(bf16[640,1024]{1,0:T(8,128)(2,1)} %get-tuple-element.79.q_low, bf16[1024,1024]{1,0:T(8,128)(2,1)} %get-tuple-element.80.k_low, bf16[1024,1024]{1,0:T(8,128)(2,1)} %get-tuple-element.81.v_low, ...), custom_call_target="tpu_custom_call" | custom-call | bytes 14680064 | tf_op jit(solution)/shard_map/pallas_call | solution.py:1094
  598.0 6.2 convolution_convert_fusion
  609.2 12.8 %fusion.3.refs_0_ = bf16[1024,2048]{1,0:T(8,128)(2,1)} fusion(f32[4,256,2048]{2,1,0:T(8,128)S(1)} %fusion.49, bf16[1024,2048]{1,0:T(8,128)(2,1)S(1)} %pad_maximum_fusion.2, bf16[2048,2048]{1,0:T(8,128)(2,1)} %get-tuple-element.78), kind=kOutput, calls=%fused_computation.7 | convolution fusion | flops 8594128896 | bytes 25165824 | tf_op jit(solution)/shard_map/dot_general | solution.py:32
  627.3 5.6 add_convert_fusion.3.refs_1_
  632.9 75.4 %shard_map.282 = (f32[256,1024]{1,0:T(8,128)}, bf16[512,2048]{1,0:T(8,128)(2,1)}, bf16[1024,512]{1,0:T(8,128)(2,1)}, bf16[256,1024]{1,0:T(8,128)(2,1)}) custom-call(bf16[1024,2048]{1,0:T(8,128)(2,1)} %fusion.3.refs_0_, bf16[512,2048]{1,0:T(8,128)(2,1)} %add_convert_fusion.3.refs_1_, bf16[1024,512]{1,0:T(8,128)(2,1)} %add_convert_fusion.6.refs_2_, ...), custom_call_target="tpu_custom_call" | custom-call | bytes 12582912 | tf_op jit(solution)/shard_map/pallas_call | solution.py:389
  710.3 6.7 fusion.117
  737.3 7.8 collective-permute-done.17
  749.6 18.2 %shard_map.283 = (f32[512,2816]{1,0:T(8,128)}, f32[512,2816]{1,0:T(8,128)}, f32[2816,512]{1,0:T(8,128)}) custom-call(bf16[6,3,1024,256]{3,2,1,0:T(8,128)(2,1)} %get-tuple-element.103.refs_0_, bf16[6,3,1024,256]{3,2,1,0:T(8,128)(2,1)} %get-tuple-element.104.refs_1_, bf16[6,3,512,256]{3,2,1,0:T(8,128)(2,1)} %collective-permute-done.9.refs_2_, ...), custom_call_target="tpu_custom_call" | custom-call | bytes 43253760 | tf_op jit(solution)/shard_map/pallas_call | solution.py:952
  773.9 5.5 collective-permute-done.23
  (435 shorter events, 161.0 us)
Async XLA Ops:
  121.8 81.0 %collective-permute-start.2 = (bf16[160,1024]{1,0:T(8,128)(2,1)}, bf16[160,1024]{1,0:T(8,128)(2,1)}, u32[]{:S(2)}, u32[]{:S(2)}) collective-permute-start(bf16[160,1024]{1,0:T(8,128)(2,1)} %get-tuple-element.176), channel_id=1, source_target_pairs={{0,6},{2,4},{4,2},{6,0},{1,7},{3,5},{5,3},{7,1},{8,14},{10,12},{12... | collective-permute-start | bytes 983048 | tf_op jit(solution)/shard_map/ppermute | solution.py:41
  124.1 78.7 %collective-permute-start.1 = (bf16[160,1024]{1,0:T(8,128)(2,1)S(1)}, bf16[160,1024]{1,0:T(8,128)(2,1)}, u32[]{:S(2)}, u32[]{:S(2)}) collective-permute-start(bf16[160,1024]{1,0:T(8,128)(2,1)S(1)} %get-tuple-element.177), channel_id=1, source_target_pairs={{0,4},{2,6},{4,0},{6,2},{1,5},{3,7},{5,1},{7,3},{8,12},{10,14},{12... | collective-permute-start | bytes 983048 | tf_op jit(solution)/shard_map/ppermute | solution.py:41
  124.1 78.7 %collective-permute-start = (bf16[160,1024]{1,0:T(8,128)(2,1)S(1)}, bf16[160,1024]{1,0:T(8,128)(2,1)}, u32[]{:S(2)}, u32[]{:S(2)}) collective-permute-start(bf16[160,1024]{1,0:T(8,128)(2,1)S(1)} %get-tuple-element.178), channel_id=1, source_target_pairs={{0,2},{2,0},{4,6},{6,4},{1,3},{3,1},{5,7},{7,5},{8,10},{10,8},{12,... | collective-permute-start | bytes 983048 | tf_op jit(solution)/shard_map/ppermute | solution.py:41
  126.2 76.7 %collective-permute-start.3 = (bf16[512,2816]{1,0:T(8,128)(2,1)S(1)}, bf16[512,2816]{1,0:T(8,128)(2,1)}, u32[]{:S(2)}, u32[]{:S(2)}) collective-permute-start(bf16[512,2816]{1,0:T(8,128)(2,1)S(1)} %bitcast.142), channel_id=1, source_target_pairs={{0,16},{8,24},{16,0},{24,8},{1,17},{9,25},{17,1},{25,9},{2,18},{10... | collective-permute-start | bytes 8650760 | tf_op jit(solution)/shard_map/ppermute | solution.py:41
  126.7 125.3 %collective-permute-start.5 = (bf16[512,2816]{1,0:T(8,128)(2,1)}, bf16[512,2816]{1,0:T(8,128)(2,1)}, u32[]{:S(2)}, u32[]{:S(2)}) collective-permute-start(bf16[512,2816]{1,0:T(8,128)(2,1)} %bitcast.143), channel_id=1, source_target_pairs={{0,16},{8,24},{16,0},{24,8},{1,17},{9,25},{17,1},{25,9},{2,18},{10... | collective-permute-start | bytes 8650760 | tf_op jit(solution)/shard_map/ppermute | solution.py:41
  252.1 5.5 collective-permute-start.6
  252.1 76.0 %collective-permute-start.7 = (bf16[2816,512]{1,0:T(8,128)(2,1)}, bf16[2816,512]{1,0:T(8,128)(2,1)}, u32[]{:S(2)}, u32[]{:S(2)}) collective-permute-start(bf16[2816,512]{1,0:T(8,128)(2,1)} %bitcast.21.refs_4_.refs_0_.refs_14_), channel_id=1, source_target_pairs={{0,16},{8,24},{16,0},{24,8},{1,17},{9,25},{17,1},{25,9},{2,18},{10... | collective-permute-start | bytes 8650760 | tf_op jit(solution)/shard_map/ppermute | solution.py:41
  328.1 5.7 collective-permute-start.8
  409.8 105.0 %collective-permute-start.9 = (bf16[6,3,512,256]{3,2,1,0:T(8,128)(2,1)}, bf16[6,3,512,256]{3,2,1,0:T(8,128)(2,1)}, u32[]{:S(2)}, u32[]{:S(2)}) collective-permute-start(bf16[6,3,512,256]{3,2,1,0:T(8,128)(2,1)} %add_convert_fusion), channel_id=1, source_target_pairs={{0,16},{8,24},{16,0},{24,8},{1,17},{9,25},{17,1},{25,9},{2,18},{10... | collective-permute-start | bytes 14155784 | tf_op jit(solution)/shard_map/ppermute | solution.py:41
  464.4 133.6 %collective-permute-start.12 = (bf16[5,3,512,256]{3,2,1,0:T(8,128)(2,1)}, bf16[5,3,512,256]{3,2,1,0:T(8,128)(2,1)}, u32[]{:S(2)}, u32[]{:S(2)}) collective-permute-start(bf16[5,3,512,256]{3,2,1,0:T(8,128)(2,1)} %add_convert_fusion.1), channel_id=1, source_target_pairs={{0,16},{8,24},{16,0},{24,8},{1,17},{9,25},{17,1},{25,9},{2,18},{10... | collective-permute-start | bytes 11796488 | tf_op jit(solution)/shard_map/ppermute | solution.py:41
  521.0 101.0 %collective-permute-start.15 = (f32[256,2]{0,1:T(2,128)S(1)}, f32[256,2]{0,1:T(2,128)S(1)}, u32[]{:S(2)}, u32[]{:S(2)}) collective-permute-start(f32[256,2]{0,1:T(2,128)S(1)} %pad_maximum_fusion.14), channel_id=1, source_target_pairs={{0,1},{1,0},{2,3},{3,2},{4,5},{5,4},{6,7},{7,6},{8,9},{9,8},{10,11... | collective-permute-start | bytes 6152 | tf_op jit(solution)/shard_map/ppermute | solution.py:41
  604.2 23.1 %collective-permute-start.13 = (bf16[1024,2048]{1,0:T(8,128)(2,1)}, bf16[1024,2048]{1,0:T(8,128)(2,1)}, u32[]{:S(2)}, u32[]{:S(2)}) collective-permute-start(bf16[1024,2048]{1,0:T(8,128)(2,1)} %convolution_convert_fusion), channel_id=1, source_target_pairs={{0,8},{8,0},{16,24},{24,16},{1,9},{9,1},{17,25},{25,17},{2,10},{10... | collective-permute-start | bytes 12582920 | tf_op jit(solution)/shard_map/ppermute | solution.py:41
  607.4 16.5 %collective-permute-start.14 = (bf16[1024,1024]{1,0:T(8,128)(2,1)}, bf16[1024,1024]{1,0:T(8,128)(2,1)}, u32[]{:S(2)}, u32[]{:S(2)}) collective-permute-start(bf16[1024,1024]{1,0:T(8,128)(2,1)} %convolution_convert_fusion.4), channel_id=1, source_target_pairs={{0,8},{8,0},{16,24},{24,16},{1,9},{9,1},{17,25},{25,17},{2,10},{10... | collective-permute-start | bytes 6291464 | tf_op jit(solution)/shard_map/ppermute | solution.py:41
  717.8 11.1 %collective-permute-start.16 = (f32[256,1]{0,1:T(1,128)S(1)}, f32[256,1]{0,1:T(1,128)S(1)}, u32[]{:S(2)}, u32[]{:S(2)}) collective-permute-start(f32[256,1]{0,1:T(1,128)S(1)} %bitcast.219), channel_id=1, source_target_pairs={{0,1},{1,0},{2,3},{3,2},{4,5},{5,4},{6,7},{7,6},{8,9},{9,8},{10,11... | collective-permute-start | bytes 3080 | tf_op jit(solution)/shard_map/ppermute | solution.py:41
  718.0 10.9 %collective-permute-start.18 = (f32[10,1024]{1,0:T(8,128)S(1)}, f32[10,1024]{1,0:T(8,128)S(1)}, u32[]{:S(2)}, u32[]{:S(2)}) collective-permute-start(f32[10,1024]{1,0:T(8,128)S(1)} %pad_maximum_fusion.9), channel_id=1, source_target_pairs={{0,1},{1,0},{2,3},{3,2},{4,5},{5,4},{6,7},{7,6},{8,9},{9,8},{10,11... | collective-permute-start | bytes 122888 | tf_op jit(solution)/shard_map/ppermute | solution.py:41
  720.2 47.6 %collective-permute-start.27 = (bf16[128,2048]{1,0:T(8,128)(2,1)S(1)}, bf16[128,2048]{1,0:T(8,128)(2,1)S(1)}, u32[]{:S(2)}, u32[]{:S(2)}) collective-permute-start(bf16[128,2048]{1,0:T(8,128)(2,1)S(1)} %get-tuple-element.172), channel_id=1, source_target_pairs={{0,2},{2,0},{4,6},{6,4},{1,3},{3,1},{5,7},{7,5},{8,10},{10,8},{12,... | collective-permute-start | bytes 1572872 | tf_op jit(solution)/shard_map/ppermute | solution.py:41
  721.4 46.3 %collective-permute-start.26 = (bf16[128,2048]{1,0:T(8,128)(2,1)S(1)}, bf16[128,2048]{1,0:T(8,128)(2,1)S(1)}, u32[]{:S(2)}, u32[]{:S(2)}) collective-permute-start(bf16[128,2048]{1,0:T(8,128)(2,1)S(1)} %get-tuple-element.173), channel_id=1, source_target_pairs={{0,6},{2,4},{4,2},{6,0},{1,7},{3,5},{5,3},{7,1},{8,14},{10,12},{12... | collective-permute-start | bytes 1572872 | tf_op jit(solution)/shard_map/ppermute | solution.py:41
  724.9 20.2 %collective-permute-start.21 = (bf16[1024,1024]{1,0:T(8,128)(2,1)S(1)}, bf16[1024,1024]{1,0:T(8,128)(2,1)S(1)}, u32[]{:S(2)}, u32[]{:S(2)}) collective-permute-start(bf16[1024,1024]{1,0:T(8,128)(2,1)S(1)} %convolution_convert_fusion.3), channel_id=1, source_target_pairs={{0,8},{8,0},{16,24},{24,16},{1,9},{9,1},{17,25},{25,17},{2,10},{10... | collective-permute-start | bytes 6291464 | tf_op jit(solution)/shard_map/ppermute | solution.py:41
  729.0 5.9 collective-permute-start.19
  731.0 14.1 %collective-permute-start.17 = (bf16[256,1024]{1,0:T(8,128)(2,1)S(1)}, bf16[256,1024]{1,0:T(8,128)(2,1)S(1)}, u32[]{:S(2)}, u32[]{:S(2)}) collective-permute-start(bf16[256,1024]{1,0:T(8,128)(2,1)S(1)} %fusion.23), channel_id=1, source_target_pairs={{0,1},{1,0},{2,3},{3,2},{4,5},{5,4},{6,7},{7,6},{8,9},{9,8},{10,11... | collective-permute-start | bytes 1572872 | tf_op jit(solution)/shard_map/ppermute | solution.py:41
  736.4 31.4 %collective-permute-start.25 = (bf16[128,2048]{1,0:T(8,128)(2,1)S(1)}, bf16[128,2048]{1,0:T(8,128)(2,1)S(1)}, u32[]{:S(2)}, u32[]{:S(2)}) collective-permute-start(bf16[128,2048]{1,0:T(8,128)(2,1)S(1)} %get-tuple-element.174), channel_id=1, source_target_pairs={{0,4},{2,6},{4,0},{6,2},{1,5},{3,7},{5,1},{7,3},{8,12},{10,14},{12... | collective-permute-start | bytes 1572872 | tf_op jit(solution)/shard_map/ppermute | solution.py:41
  747.1 24.6 %collective-permute-start.22 = (bf16[512,1024]{1,0:T(8,128)(2,1)}, bf16[512,1024]{1,0:T(8,128)(2,1)S(1)}, u32[]{:S(2)}, u32[]{:S(2)}) collective-permute-start(bf16[512,1024]{1,0:T(8,128)(2,1)} %add_convert_fusion.5), channel_id=1, source_target_pairs={{0,16},{8,24},{16,0},{24,8},{1,17},{9,25},{17,1},{25,9},{2,18},{10... | collective-permute-start | bytes 3145736 | tf_op jit(solution)/shard_map/ppermute | solution.py:41
  771.8 7.6 collective-permute-start.23
  779.4 5.0 collective-permute-start.24
  (119 other events, 1692.7 us)

commit v8 on v7

--- a/solution.py
+++ b/solution.py
@@ -1342,7 +1342,11 @@
     for k in range(picks_each):
         dy_slots = dy_slots + matmul_tn(attn_picks[k], (attn_mix[:, k : k + 1] * d_attended).astype(LOW))
     dy_rows = send_out(dy_slots.astype(LOW), 4)
-    d_heads = matmul_nt(dy_rows, out_full).astype(LOW)
+    out_sent, out_finish = scatter_start(
+        lambda low, high: matmul_tn(heads_low, dy_rows[:, low:high]), features, 1
+    )
+    out_back = last_step(out_sent)
+    d_heads = after(matmul_nt(dy_rows, out_full).astype(LOW), out_sent)
     dq_low, dk_low, dv_low = attend_back(
         q_low, k_low, v_low, d_heads, log_sum, query_table, key_table, groups
     )
@@ -1350,9 +1354,6 @@
     da_rows = matmul_nt(dq_low, query_full).astype(LOW).reshape(groups, capacity, features)
     da_seq = jnp.einsum("bsr,bsd->brd", expert_onehot, da_rows, preferred_element_type=FULL)
     da_seq = da_seq.reshape(groups * rows_here, features) + matmul_nt(dkv_low, kv_full)
-    out_sent, out_finish = scatter_start(
-        lambda low, high: matmul_tn(heads_low, dy_rows[:, low:high]), features, 1
-    )
     kv_sent, kv_finish = scatter_start(
         lambda low, high: matmul_tn(a_seq[:, low:high], dkv_low), features, 0
     )
@@ -1360,10 +1361,10 @@
     for k in range(picks_each):
         result = result + ffn_mix[:, k : k + 1] * matmul(ffn_picks[k], ffn_back)
     result_low = result.astype(LOW)
-    da_half, kv_back, out_back, result_other = send_home(
-        da_seq.astype(LOW),
+    da_half, kv_back, result_other = send_home(
+        after(da_seq.astype(LOW), out_back),
         5,
-        cargo=((kv_sent, "fsdp"), (out_sent, "fsdp"), (result_low, "tp")),
+        cargo=((kv_sent, "fsdp"), (result_low, "tp")),
         add_up=True,
     )
     output = from_spread(join_halves(result_low, result_other), 1)
@@ -1379,7 +1380,7 @@
         if distance
     ]
     query_grad = query_finish(query_back)
-    out_grad = out_finish(out_back)
+    out_grad = out_finish(after(out_back, da_half))
     back_one, back_two = lax.optimization_barrier((back_one, back_two, query_sent))[:2]
     gate_grad, up_grad, down_grad = finish_experts(parts_one + [back_one], parts_two + [back_two])
     kv_grad = block_for(kv_part, 0)
@@ -1402,7 +1403,8 @@
     inner1 = tp_sum(jnp.sum(weighted1 * input_half, axis=1, keepdims=True)) / features
     input_grad = d_attended + scale_one * weighted1 - input_half * scale_one**3 * inner1
     input_grad_low = input_grad.astype(LOW)
-    input_grad = from_spread(join_halves(input_grad_low, swap(input_grad_low, "tp", 1)), 1).astype(FULL)
+    input_grad_other = after(swap(input_grad_low, "tp", 1), gate_grad)
+    input_grad = from_spread(join_halves(input_grad_low, input_grad_other), 1).astype(FULL)
     gain1_part = jnp.sum(d_normed1 * input_half * scale_one, axis=0)
 
     small = jnp.concatenate(

time: 792 us -> 780 us (0.985)
  Pallas kernels: 538 us -> 525 us
  matrix products: 106 us -> 97.2 us
    pallas_call x3, Pallas kernels: 150 us -> 137 us  [send_home(): pl.pallas_call(functools.partial(send_home_kernel, size, adds, extra is n...]
    ppermute x28 -> x29, waiting for transfers between devices: 39.2 us -> 43.6 us  [swap(): return lax.ppermute(value, axis, [(i, i ^ distance) for i in range(size)])]
    ppermute x28 -> x29, starting transfers between devices: 21.8 us -> 20.3 us  [swap(): return lax.ppermute(value, axis, [(i, i ^ distance) for i in range(size)])]
  transfers between devices with their start and end apart: 28 -> 29, of which waited for: 13 -> 13; matrix products, arithmetic and copies ran while one was open for 18% -> 18% of each run, Pallas kernels for 36% -> 37%
where the time goes in v8:
time: 780 us; the launch traced here: 775 us
  Pallas kernels  525 us (67%)
  matrix products  97.2 us (12%)
  other arithmetic  61.3 us (8%)
  waiting for transfers between devices  43.6 us (6%)
  local copies, waits for them, and re-layouts  25 us (3%)
  starting transfers between devices  20.3 us (3%)
    pallas_call x3, Pallas kernels, send_home(): pl.pallas_call(functools.partial(send_home_kernel, size, adds, extra is n...  137 us
    pallas_call x1, Pallas kernels, prologue(): pl.pallas_call(functools.partial(prologue_kernel, (groups, world)), in_sp...  110 us
    pallas_call x2, Pallas kernels, expert_back(): pl.pallas_call(functools.partial(expert_back_kernel, world, steps, size),...  94.7 us
    pallas_call x2, Pallas kernels, send_out(): pl.pallas_call(functools.partial(send_out_kernel, size), in_specs=[pl.Blo...  79.3 us
    ppermute x29, waiting for transfers between devices, swap(): return lax.ppermute(value, axis, [(i, i ^ distance) for i in range(size)])  43.6 us
    dot_general x16, matrix products, matmul(): return jnp.dot(lhs, rhs, preferred_element_type=FULL)  36.5 us
    dot_general x13, matrix products, matmul_tn(): lax.dot_general(lhs, rhs, (((0,), (0,)), ((), ())), preferred_element_typ...  34.7 us
    pallas_call x1, Pallas kernels, expert_forward(): pl.pallas_call(functools.partial(expert_forward_kernel, world, size), gri...  28.7 us
  transfers between devices with their start and end apart: 29, of which 13 were waited for; matrix products, arithmetic and copies ran while one was open for 18% of the time, Pallas kernels for 37%

profile of v8, /device:TPU:0, one launch (start us, length us, event | category | flops | bytes accessed | tf_op | source)
XLA Modules:
  0.0 775.4 jit_solution(4904356281091690396)
XLA Ops:
  9.8 109.7 %shard_map.271 = (bf16[2,1024,1024]{2,1,0:T(8,128)(2,1)}, s32[4,4,8,256]{3,2,1,0:T(8,128)}, bf16[2048,2048]{1,0:T(8,128)(2,1)}, bf16[2048,1024]{1,0:T(8,128)(2,1...) custom-call(bf16[256,1024]{1,0:T(8,128)(2,1)} %maximum_select_fusion.refs_0_, ...), custom_call_target="tpu_custom_call" | custom-call | bytes 100000000 | tf_op jit(solution)/shard_map/pallas_call | solution.py:597
  134.5 5.5 slice_bitcast_fusion.10
  152.7 14.7 %fusion.136.k_lin.v_lin = f32[1024,2048]{1,0:T(8,128)} fusion(bf16[1024,2048]{1,0:T(8,128)(2,1)} %fusion.2, bf16[2048,2048]{1,0:T(8,128)(2,1)} %get-tuple-element.81), kind=kOutput, calls=%fused_computation.347 | convolution fusion | flops 8589934592 | bytes 20971520 | tf_op jit(solution)/shard_map/dot_general | solution.py:24
  175.4 19.1 %shard_map.272 = (bf16[640,1024]{1,0:T(8,128)(2,1)}, bf16[1024,1024]{1,0:T(8,128)(2,1)}, bf16[1024,1024]{1,0:T(8,128)(2,1)}, bf16[640,1024]{1,0:T(8,128)(2,1)}, f32[640,1024]{1,0:T(8,128)}) custom-call(f32[640,1024]{1,0:T(8,128)} %fusion.135.q_lin, f32[1024,2048]{1,0:T(8,128)} %fusion.136.k_lin.v_lin, f32[1024,2048]{1,0:T(8,128)} %fusion.136.k_lin.v_lin, ...), custom_call_target="tpu_custom_call" | custom-call | bytes 20971520 | tf_op jit(solution)/shard_map/pallas_call | solution.py:1039
  197.5 5.5 convolution_convert_fusion.2.refs_0_
  203.1 35.5 %shard_map.273 = (bf16[640,1024]{1,0:T(8,128)(2,1)}, bf16[512,2816]{1,0:T(8,128)(2,1)}, bf16[512,2816]{1,0:T(8,128)(2,1)}, bf16[512,2816]{1,0:T(8,128)(2,1)}, bf16[2816,512]{1,0:T(8,128)(2,1)}) custom-call(bf16[640,2048]{1,0:T(8,128)(2,1)} %convolution_convert_fusion.2.refs_0_, bf16[512,2816]{1,0:T(8,128)(2,1)} %bitcast.138, ...), custom_call_target="tpu_custom_call" | custom-call | bytes 7864320 | tf_op jit(solution)/shard_map/pallas_call | solution.py:389
  257.6 41.8 %shard_map.274.refs_0_ = bf16[640,2048]{1,0:T(8,128)(2,1)} custom-call(bf16[640,1024]{1,0:T(8,128)(2,1)} %convolution_convert_fusion.6.rows_ref), custom_call_target="tpu_custom_call" | custom-call | bytes 7864320 | tf_op jit(solution)/shard_map/pallas_call | solution.py:246
  299.5 28.7 %shard_map.275 = (bf16[640,2816]{1,0:T(8,128)(2,1)}, bf16[640,2816]{1,0:T(8,128)(2,1)}, bf16[640,2816]{1,0:T(8,128)(2,1)}, bf16[640,2048]{1,0:T(8,128)(2,1)}) custom-call(bf16[640,2048]{1,0:T(8,128)(2,1)} %shard_map.274.refs_0_, bf16[512,2816]{1,0:T(8,128)(2,1)} %bitcast.139, bf16[512,2816]{1,0:T(8,128)(2,1)} %collective-permute-done.3.refs_2_.refs_7_, ...), custom_call_target="tpu_custom_call" | custom-call | bytes 2621440 | tf_op jit(solution)/shard_map/pallas_call | solution.py:676
  333.9 14.6 %shard_map.276.refs_18_ = bf16[640,2048]{1,0:T(8,128)(2,1)} custom-call(bf16[640,2816]{1,0:T(8,128)(2,1)} %get-tuple-element.99.hidden_ref.refs_3_, bf16[2816,512]{1,0:T(8,128)(2,1)} %bitcast.21.refs_4_.refs_0_.refs_14_, bf16[2816,512]{1,0:T(8,128)(2,1)} %collective-permute-done.7.refs_1_.refs_15_, bf16[2816,512]{1,0:T(8,128)(2,1)} %get-tuple-element.103.refs_2_.refs_16_, ...), custom_call_target="tpu_custom_call" | custom-call | flops 7381975040 | bytes 11534336 | tf_op jit(solution)/shard_map/pallas_call | solution.py:710
  349.3 52.6 %shard_map.277 = (bf16[6,3,1024,256]{3,2,1,0:T(8,128)(2,1)}, bf16[6,3,1024,256]{3,2,1,0:T(8,128)(2,1)}, bf16[640,2048]{1,0:T(8,128)(2,1)}, f32[640,128]{1,0:T(8,128)}, bf16[640,1024]{1,0:T(8,128)(2,1)}) custom-call(bf16[640,2048]{1,0:T(8,128)(2,1)} %shard_map.274.refs_0_, bf16[640,2048]{1,0:T(8,128)(2,1)} %get-tuple-element.98.refs_1_, ...), custom_call_target="tpu_custom_call" | custom-call | bytes 2621440 | tf_op jit(solution)/shard_map/pallas_call | solution.py:893
  402.0 7.5 add_convert_fusion
  414.2 42.1 %shard_map.278 = (bf16[5,3,1024,256]{3,2,1,0:T(8,128)(2,1)}, bf16[5,3,1024,256]{3,2,1,0:T(8,128)(2,1)}, bf16[640,2048]{1,0:T(8,128)(2,1)}, f32[640,128]{1,0:T(8,128)}) custom-call(bf16[640,2048]{1,0:T(8,128)(2,1)} %shard_map.274.refs_0_, bf16[640,2048]{1,0:T(8,128)(2,1)} %get-tuple-element.98.refs_1_, f32[640,128]{1,0:T(8,128)} %broadcast_in_dim.41.refs_2_, ...), custom_call_target="tpu_custom_call" | custom-call | bytes 2621440 | tf_op jit(solution)/shard_map/pallas_call | solution.py:893
  457.6 6.5 add_convert_fusion.1
  468.9 39.1 %shard_map.279 = (bf16[640,1024]{1,0:T(8,128)(2,1)}, f32[4,8,256]{2,1,0:T(8,128)}) custom-call(bf16[640,2048]{1,0:T(8,128)(2,1)} %add_convert_fusion.2.refs_0_, f32[4,8,256]{2,1,0:T(8,128)} %pad.8.refs_1_), custom_call_target="tpu_custom_call" | custom-call | bytes 7864320 | tf_op jit(solution)/shard_map/pallas_call | solution.py:389
  523.6 37.5 %shard_map.280 = bf16[640,2048]{1,0:T(8,128)(2,1)} custom-call(bf16[640,1024]{1,0:T(8,128)(2,1)} %add_convert_fusion.4.rows_ref), custom_call_target="tpu_custom_call" | custom-call | bytes 7864320 | tf_op jit(solution)/shard_map/pallas_call | solution.py:246
  573.4 23.3 %shard_map.281 = (bf16[640,1024]{1,0:T(8,128)(2,1)}, bf16[1024,1024]{1,0:T(8,128)(2,1)}, bf16[1024,1024]{1,0:T(8,128)(2,1)}) custom-call(bf16[640,1024]{1,0:T(8,128)(2,1)} %get-tuple-element.82.q_low, bf16[1024,1024]{1,0:T(8,128)(2,1)} %get-tuple-element.83.k_low, bf16[1024,1024]{1,0:T(8,128)(2,1)} %get-tuple-element.84.v_low, ...), custom_call_target="tpu_custom_call" | custom-call | bytes 14680064 | tf_op jit(solution)/shard_map/pallas_call | solution.py:1094
  600.1 6.3 convolution_convert_fusion
  612.2 13.0 %fusion.3.refs_0_ = bf16[1024,2048]{1,0:T(8,128)(2,1)} fusion(f32[4,256,2048]{2,1,0:T(8,128)S(1)} %fusion.49, bf16[1024,2048]{1,0:T(8,128)(2,1)S(1)} %pad_maximum_fusion.2, bf16[2048,2048]{1,0:T(8,128)(2,1)} %get-tuple-element.81), kind=kOutput, calls=%fused_computation.7 | convolution fusion | flops 8594128896 | bytes 25165824 | tf_op jit(solution)/shard_map/dot_general | solution.py:32
  632.7 5.7 add_convert_fusion.3.refs_1_
  638.5 62.7 %shard_map.282 = (f32[256,1024]{1,0:T(8,128)}, bf16[512,2048]{1,0:T(8,128)(2,1)}, bf16[256,1024]{1,0:T(8,128)(2,1)}) custom-call(bf16[1024,2048]{1,0:T(8,128)(2,1)} %fusion.3.refs_0_, bf16[512,2048]{1,0:T(8,128)(2,1)} %add_convert_fusion.3.refs_1_, bf16[256,1024]{1,0:T(8,128)(2,1)} %fusion.17.refs_2_), custom_call_target="tpu_custom_call" | custom-call | bytes 12582912 | tf_op jit(solution)/shard_map/pallas_call | solution.py:389
  720.7 5.1 collective-permute-done.21
  731.1 18.2 %shard_map.283 = (f32[512,2816]{1,0:T(8,128)}, f32[512,2816]{1,0:T(8,128)}, f32[2816,512]{1,0:T(8,128)}) custom-call(bf16[6,3,1024,256]{3,2,1,0:T(8,128)(2,1)} %get-tuple-element.106.refs_0_, bf16[6,3,1024,256]{3,2,1,0:T(8,128)(2,1)} %get-tuple-element.107.refs_1_, bf16[6,3,512,256]{3,2,1,0:T(8,128)(2,1)} %collective-permute-done.9.refs_2_, ...), custom_call_target="tpu_custom_call" | custom-call | bytes 43253760 | tf_op jit(solution)/shard_map/pallas_call | solution.py:952
  749.3 8.6 %collective-permute-done.26 = bf16[128,2048]{1,0:T(8,128)(2,1)} collective-permute-done((bf16[128,2048]{1,0:T(8,128)(2,1)S(1)}, bf16[128,2048]{1,0:T(8,128)(2,1)}, u32[]{:S(2)}, u32[]{:S(2)}) %collective-permute-start.26) | collective-permute-done | bytes 524320 | tf_op jit(solution)/shard_map/ppermute | solution.py:41
  762.6 5.3 collective-permute-done.24
  (439 shorter events, 163.8 us)
Async XLA Ops:
  121.8 81.2 %collective-permute-start.2 = (bf16[160,1024]{1,0:T(8,128)(2,1)}, bf16[160,1024]{1,0:T(8,128)(2,1)}, u32[]{:S(2)}, u32[]{:S(2)}) collective-permute-start(bf16[160,1024]{1,0:T(8,128)(2,1)} %get-tuple-element.182), channel_id=1, source_target_pairs={{0,6},{2,4},{4,2},{6,0},{1,7},{3,5},{5,3},{7,1},{8,14},{10,12},{12... | collective-permute-start | bytes 983048 | tf_op jit(solution)/shard_map/ppermute | solution.py:41
  124.1 78.9 %collective-permute-start.1 = (bf16[160,1024]{1,0:T(8,128)(2,1)S(1)}, bf16[160,1024]{1,0:T(8,128)(2,1)}, u32[]{:S(2)}, u32[]{:S(2)}) collective-permute-start(bf16[160,1024]{1,0:T(8,128)(2,1)S(1)} %get-tuple-element.183), channel_id=1, source_target_pairs={{0,4},{2,6},{4,0},{6,2},{1,5},{3,7},{5,1},{7,3},{8,12},{10,14},{12... | collective-permute-start | bytes 983048 | tf_op jit(solution)/shard_map/ppermute | solution.py:41
  124.1 78.9 %collective-permute-start = (bf16[160,1024]{1,0:T(8,128)(2,1)S(1)}, bf16[160,1024]{1,0:T(8,128)(2,1)}, u32[]{:S(2)}, u32[]{:S(2)}) collective-permute-start(bf16[160,1024]{1,0:T(8,128)(2,1)S(1)} %get-tuple-element.184), channel_id=1, source_target_pairs={{0,2},{2,0},{4,6},{6,4},{1,3},{3,1},{5,7},{7,5},{8,10},{10,8},{12,... | collective-permute-start | bytes 983048 | tf_op jit(solution)/shard_map/ppermute | solution.py:41
  126.2 76.9 %collective-permute-start.3 = (bf16[512,2816]{1,0:T(8,128)(2,1)S(1)}, bf16[512,2816]{1,0:T(8,128)(2,1)}, u32[]{:S(2)}, u32[]{:S(2)}) collective-permute-start(bf16[512,2816]{1,0:T(8,128)(2,1)S(1)} %bitcast.142), channel_id=1, source_target_pairs={{0,16},{8,24},{16,0},{24,8},{1,17},{9,25},{17,1},{25,9},{2,18},{10... | collective-permute-start | bytes 8650760 | tf_op jit(solution)/shard_map/ppermute | solution.py:41
  126.7 125.3 %collective-permute-start.5 = (bf16[512,2816]{1,0:T(8,128)(2,1)}, bf16[512,2816]{1,0:T(8,128)(2,1)}, u32[]{:S(2)}, u32[]{:S(2)}) collective-permute-start(bf16[512,2816]{1,0:T(8,128)(2,1)} %bitcast.143), channel_id=1, source_target_pairs={{0,16},{8,24},{16,0},{24,8},{1,17},{9,25},{17,1},{25,9},{2,18},{10... | collective-permute-start | bytes 8650760 | tf_op jit(solution)/shard_map/ppermute | solution.py:41
  252.1 5.5 collective-permute-start.6
  252.1 76.1 %collective-permute-start.7 = (bf16[2816,512]{1,0:T(8,128)(2,1)}, bf16[2816,512]{1,0:T(8,128)(2,1)}, u32[]{:S(2)}, u32[]{:S(2)}) collective-permute-start(bf16[2816,512]{1,0:T(8,128)(2,1)} %bitcast.21.refs_4_.refs_0_.refs_14_), channel_id=1, source_target_pairs={{0,16},{8,24},{16,0},{24,8},{1,17},{9,25},{17,1},{25,9},{2,18},{10... | collective-permute-start | bytes 8650760 | tf_op jit(solution)/shard_map/ppermute | solution.py:41
  328.2 5.7 collective-permute-start.8
  409.5 105.1 %collective-permute-start.9 = (bf16[6,3,512,256]{3,2,1,0:T(8,128)(2,1)}, bf16[6,3,512,256]{3,2,1,0:T(8,128)(2,1)}, u32[]{:S(2)}, u32[]{:S(2)}) collective-permute-start(bf16[6,3,512,256]{3,2,1,0:T(8,128)(2,1)} %add_convert_fusion), channel_id=1, source_target_pairs={{0,16},{8,24},{16,0},{24,8},{1,17},{9,25},{17,1},{25,9},{2,18},{10... | collective-permute-start | bytes 14155784 | tf_op jit(solution)/shard_map/ppermute | solution.py:41
  464.2 135.3 %collective-permute-start.13 = (bf16[5,3,512,256]{3,2,1,0:T(8,128)(2,1)}, bf16[5,3,512,256]{3,2,1,0:T(8,128)(2,1)}, u32[]{:S(2)}, u32[]{:S(2)}) collective-permute-start(bf16[5,3,512,256]{3,2,1,0:T(8,128)(2,1)} %add_convert_fusion.1), channel_id=1, source_target_pairs={{0,16},{8,24},{16,0},{24,8},{1,17},{9,25},{17,1},{25,9},{2,18},{10... | collective-permute-start | bytes 11796488 | tf_op jit(solution)/shard_map/ppermute | solution.py:41
  520.8 50.5 %collective-permute-start.16 = (f32[256,2]{0,1:T(2,128)S(1)}, f32[256,2]{0,1:T(2,128)S(1)}, u32[]{:S(2)}, u32[]{:S(2)}) collective-permute-start(f32[256,2]{0,1:T(2,128)S(1)} %pad_maximum_fusion.14), channel_id=1, source_target_pairs={{0,1},{1,0},{2,3},{3,2},{4,5},{5,4},{6,7},{7,6},{8,9},{9,8},{10,11... | collective-permute-start | bytes 6152 | tf_op jit(solution)/shard_map/ppermute | solution.py:41
  564.6 6.9 collective-permute-start.12
  606.4 26.3 %collective-permute-start.15 = (bf16[1024,2048]{1,0:T(8,128)(2,1)}, bf16[1024,2048]{1,0:T(8,128)(2,1)}, u32[]{:S(2)}, u32[]{:S(2)}) collective-permute-start(bf16[1024,2048]{1,0:T(8,128)(2,1)} %convolution_convert_fusion), channel_id=1, source_target_pairs={{0,8},{8,0},{16,24},{24,16},{1,9},{9,1},{17,25},{25,17},{2,10},{10... | collective-permute-start | bytes 12582920 | tf_op jit(solution)/shard_map/ppermute | solution.py:41
  607.3 25.4 %collective-permute-start.14 = (bf16[1024,512]{1,0:T(8,128)(2,1)}, bf16[1024,512]{1,0:T(8,128)(2,1)}, u32[]{:S(2)}, u32[]{:S(2)}) collective-permute-start(bf16[1024,512]{1,0:T(8,128)(2,1)} %add_convert_fusion.6), channel_id=1, source_target_pairs={{0,16},{8,24},{16,0},{24,8},{1,17},{9,25},{17,1},{25,9},{2,18},{10... | collective-permute-start | bytes 3145736 | tf_op jit(solution)/shard_map/ppermute | solution.py:41
  708.9 11.2 %collective-permute-start.17 = (f32[256,1]{0,1:T(1,128)S(1)}, f32[256,1]{0,1:T(1,128)S(1)}, u32[]{:S(2)}, u32[]{:S(2)}) collective-permute-start(f32[256,1]{0,1:T(1,128)S(1)} %bitcast.219), channel_id=1, source_target_pairs={{0,1},{1,0},{2,3},{3,2},{4,5},{5,4},{6,7},{7,6},{8,9},{9,8},{10,11... | collective-permute-start | bytes 3080 | tf_op jit(solution)/shard_map/ppermute | solution.py:41
  710.0 8.9 %collective-permute-start.20 = (f32[10,1024]{1,0:T(8,128)S(1)}, f32[10,1024]{1,0:T(8,128)S(1)}, u32[]{:S(2)}, u32[]{:S(2)}) collective-permute-start(f32[10,1024]{1,0:T(8,128)S(1)} %pad_maximum_fusion.9), channel_id=1, source_target_pairs={{0,1},{1,0},{2,3},{3,2},{4,5},{5,4},{6,7},{7,6},{8,9},{9,8},{10,11... | collective-permute-start | bytes 122888 | tf_op jit(solution)/shard_map/ppermute | solution.py:41
  711.3 38.0 %collective-permute-start.28 = (bf16[128,2048]{1,0:T(8,128)(2,1)S(1)}, bf16[128,2048]{1,0:T(8,128)(2,1)S(1)}, u32[]{:S(2)}, u32[]{:S(2)}) collective-permute-start(bf16[128,2048]{1,0:T(8,128)(2,1)S(1)} %get-tuple-element.178), channel_id=1, source_target_pairs={{0,2},{2,0},{4,6},{6,4},{1,3},{3,1},{5,7},{7,5},{8,10},{10,8},{12,... | collective-permute-start | bytes 1572872 | tf_op jit(solution)/shard_map/ppermute | solution.py:41
  711.9 37.3 %collective-permute-start.27 = (bf16[128,2048]{1,0:T(8,128)(2,1)S(1)}, bf16[128,2048]{1,0:T(8,128)(2,1)S(1)}, u32[]{:S(2)}, u32[]{:S(2)}) collective-permute-start(bf16[128,2048]{1,0:T(8,128)(2,1)S(1)} %get-tuple-element.179), channel_id=1, source_target_pairs={{0,6},{2,4},{4,2},{6,0},{1,7},{3,5},{5,3},{7,1},{8,14},{10,12},{12... | collective-permute-start | bytes 1572872 | tf_op jit(solution)/shard_map/ppermute | solution.py:41
  715.7 13.6 %collective-permute-start.19 = (bf16[1024,1024]{1,0:T(8,128)(2,1)S(1)}, bf16[1024,1024]{1,0:T(8,128)(2,1)S(1)}, u32[]{:S(2)}, u32[]{:S(2)}) collective-permute-start(bf16[1024,1024]{1,0:T(8,128)(2,1)S(1)} %convolution_convert_fusion.3), channel_id=1, source_target_pairs={{0,8},{8,0},{16,24},{24,16},{1,9},{9,1},{17,25},{25,17},{2,10},{10... | collective-permute-start | bytes 6291464 | tf_op jit(solution)/shard_map/ppermute | solution.py:41
  719.0 38.9 %collective-permute-start.26 = (bf16[128,2048]{1,0:T(8,128)(2,1)S(1)}, bf16[128,2048]{1,0:T(8,128)(2,1)}, u32[]{:S(2)}, u32[]{:S(2)}) collective-permute-start(bf16[128,2048]{1,0:T(8,128)(2,1)S(1)} %get-tuple-element.180), channel_id=1, source_target_pairs={{0,4},{2,6},{4,0},{6,2},{1,5},{3,7},{5,1},{7,3},{8,12},{10,14},{12... | collective-permute-start | bytes 1572872 | tf_op jit(solution)/shard_map/ppermute | solution.py:41
  720.1 5.7 collective-permute-start.21
  727.2 30.7 %collective-permute-start.18 = (bf16[256,1024]{1,0:T(8,128)(2,1)S(1)}, bf16[256,1024]{1,0:T(8,128)(2,1)S(1)}, u32[]{:S(2)}, u32[]{:S(2)}) collective-permute-start(bf16[256,1024]{1,0:T(8,128)(2,1)S(1)} %fusion.23), channel_id=1, source_target_pairs={{0,1},{1,0},{2,3},{3,2},{4,5},{5,4},{6,7},{7,6},{8,9},{9,8},{10,11... | collective-permute-start | bytes 1572872 | tf_op jit(solution)/shard_map/ppermute | solution.py:41
  730.7 30.8 %collective-permute-start.23 = (bf16[512,1024]{1,0:T(8,128)(2,1)S(1)}, bf16[512,1024]{1,0:T(8,128)(2,1)S(1)}, u32[]{:S(2)}, u32[]{:S(2)}) collective-permute-start(bf16[512,1024]{1,0:T(8,128)(2,1)S(1)} %add_convert_fusion.5), channel_id=1, source_target_pairs={{0,16},{8,24},{16,0},{24,8},{1,17},{9,25},{17,1},{25,9},{2,18},{10... | collective-permute-start | bytes 3145736 | tf_op jit(solution)/shard_map/ppermute | solution.py:41
  761.5 6.4 collective-permute-start.24
  (120 other events, 1534.2 us)

commit v9 on v8

--- a/solution.py
+++ b/solution.py
@@ -181,7 +181,7 @@
 
 
 def cuts_of(rows):
-    for count in (4, 2):
+    for count in (5, 4, 2):
         if rows % (16 * count) == 0:
             return count
     return 1

time: 780 us -> 778 us (level)
  transfers between devices with their start and end apart: 29 -> 29, of which waited for: 13 -> 13; matrix products, arithmetic and copies ran while one was open for 18% -> 18% of each run, Pallas kernels for 37% -> 36%
where the time goes in v9:
time: 778 us; the launch traced here: 773 us
  Pallas kernels  521 us (67%)
  matrix products  97.3 us (13%)
  other arithmetic  61.3 us (8%)
  waiting for transfers between devices  44.5 us (6%)
  local copies, waits for them, and re-layouts  25 us (3%)
  starting transfers between devices  20.4 us (3%)
    pallas_call x3, Pallas kernels, send_home(): pl.pallas_call(functools.partial(send_home_kernel, size, adds, extra is n...  136 us
    pallas_call x1, Pallas kernels, prologue(): pl.pallas_call(functools.partial(prologue_kernel, (groups, world)), in_sp...  110 us
    pallas_call x2, Pallas kernels, expert_back(): pl.pallas_call(functools.partial(expert_back_kernel, world, steps, size),...  94.7 us
    pallas_call x2, Pallas kernels, send_out(): pl.pallas_call(functools.partial(send_out_kernel, size), in_specs=[pl.Blo...  77 us
    ppermute x29, waiting for transfers between devices, swap(): return lax.ppermute(value, axis, [(i, i ^ distance) for i in range(size)])  44.5 us
    dot_general x16, matrix products, matmul(): return jnp.dot(lhs, rhs, preferred_element_type=FULL)  36.5 us
    dot_general x13, matrix products, matmul_tn(): lax.dot_general(lhs, rhs, (((0,), (0,)), ((), ())), preferred_element_typ...  34.7 us
    pallas_call x1, Pallas kernels, expert_forward(): pl.pallas_call(functools.partial(expert_forward_kernel, world, size), gri...  28.7 us
  transfers between devices with their start and end apart: 29, of which 13 were waited for; matrix products, arithmetic and copies ran while one was open for 18% of the time, Pallas kernels for 36%

profile of v9, /device:TPU:0, one launch (start us, length us, event | category | flops | bytes accessed | tf_op | source)
XLA Modules:
  0.0 772.7 jit_solution(10717057321267449928)
XLA Ops:
  9.8 109.7 %shard_map.271 = (bf16[2,1024,1024]{2,1,0:T(8,128)(2,1)}, s32[4,4,8,256]{3,2,1,0:T(8,128)}, bf16[2048,2048]{1,0:T(8,128)(2,1)}, bf16[2048,1024]{1,0:T(8,128)(2,1...) custom-call(bf16[256,1024]{1,0:T(8,128)(2,1)} %maximum_select_fusion.refs_0_, ...), custom_call_target="tpu_custom_call" | custom-call | bytes 100000000 | tf_op jit(solution)/shard_map/pallas_call | solution.py:597
  134.5 5.5 slice_bitcast_fusion.10
  152.7 14.7 %fusion.136.k_lin.v_lin = f32[1024,2048]{1,0:T(8,128)} fusion(bf16[1024,2048]{1,0:T(8,128)(2,1)} %fusion.2, bf16[2048,2048]{1,0:T(8,128)(2,1)} %get-tuple-element.81), kind=kOutput, calls=%fused_computation.347 | convolution fusion | flops 8589934592 | bytes 20971520 | tf_op jit(solution)/shard_map/dot_general | solution.py:24
  175.4 19.1 %shard_map.272 = (bf16[640,1024]{1,0:T(8,128)(2,1)}, bf16[1024,1024]{1,0:T(8,128)(2,1)}, bf16[1024,1024]{1,0:T(8,128)(2,1)}, bf16[640,1024]{1,0:T(8,128)(2,1)}, f32[640,1024]{1,0:T(8,128)}) custom-call(f32[640,1024]{1,0:T(8,128)} %fusion.135.q_lin, f32[1024,2048]{1,0:T(8,128)} %fusion.136.k_lin.v_lin, f32[1024,2048]{1,0:T(8,128)} %fusion.136.k_lin.v_lin, ...), custom_call_target="tpu_custom_call" | custom-call | bytes 20971520 | tf_op jit(solution)/shard_map/pallas_call | solution.py:1039
  197.5 5.5 convolution_convert_fusion.2.refs_0_
  203.1 35.3 %shard_map.273 = (bf16[640,1024]{1,0:T(8,128)(2,1)}, bf16[512,2816]{1,0:T(8,128)(2,1)}, bf16[512,2816]{1,0:T(8,128)(2,1)}, bf16[512,2816]{1,0:T(8,128)(2,1)}, bf16[2816,512]{1,0:T(8,128)(2,1)}) custom-call(bf16[640,2048]{1,0:T(8,128)(2,1)} %convolution_convert_fusion.2.refs_0_, bf16[512,2816]{1,0:T(8,128)(2,1)} %bitcast.138, ...), custom_call_target="tpu_custom_call" | custom-call | bytes 7864320 | tf_op jit(solution)/shard_map/pallas_call | solution.py:389
  257.6 40.1 %shard_map.274.refs_0_ = bf16[640,2048]{1,0:T(8,128)(2,1)} custom-call(bf16[640,1024]{1,0:T(8,128)(2,1)} %convolution_convert_fusion.6.rows_ref), custom_call_target="tpu_custom_call" | custom-call | bytes 7864320 | tf_op jit(solution)/shard_map/pallas_call | solution.py:246
  297.8 28.7 %shard_map.275 = (bf16[640,2816]{1,0:T(8,128)(2,1)}, bf16[640,2816]{1,0:T(8,128)(2,1)}, bf16[640,2816]{1,0:T(8,128)(2,1)}, bf16[640,2048]{1,0:T(8,128)(2,1)}) custom-call(bf16[640,2048]{1,0:T(8,128)(2,1)} %shard_map.274.refs_0_, bf16[512,2816]{1,0:T(8,128)(2,1)} %bitcast.139, bf16[512,2816]{1,0:T(8,128)(2,1)} %collective-permute-done.3.refs_2_.refs_7_, ...), custom_call_target="tpu_custom_call" | custom-call | bytes 2621440 | tf_op jit(solution)/shard_map/pallas_call | solution.py:676
  332.2 14.6 %shard_map.276.refs_18_ = bf16[640,2048]{1,0:T(8,128)(2,1)} custom-call(bf16[640,2816]{1,0:T(8,128)(2,1)} %get-tuple-element.99.hidden_ref.refs_3_, bf16[2816,512]{1,0:T(8,128)(2,1)} %bitcast.21.refs_4_.refs_0_.refs_14_, bf16[2816,512]{1,0:T(8,128)(2,1)} %collective-permute-done.7.refs_1_.refs_15_, bf16[2816,512]{1,0:T(8,128)(2,1)} %get-tuple-element.103.refs_2_.refs_16_, ...), custom_call_target="tpu_custom_call" | custom-call | flops 7381975040 | bytes 11534336 | tf_op jit(solution)/shard_map/pallas_call | solution.py:710
  347.7 52.6 %shard_map.277 = (bf16[6,3,1024,256]{3,2,1,0:T(8,128)(2,1)}, bf16[6,3,1024,256]{3,2,1,0:T(8,128)(2,1)}, bf16[640,2048]{1,0:T(8,128)(2,1)}, f32[640,128]{1,0:T(8,128)}, bf16[640,1024]{1,0:T(8,128)(2,1)}) custom-call(bf16[640,2048]{1,0:T(8,128)(2,1)} %shard_map.274.refs_0_, bf16[640,2048]{1,0:T(8,128)(2,1)} %get-tuple-element.98.refs_1_, ...), custom_call_target="tpu_custom_call" | custom-call | bytes 2621440 | tf_op jit(solution)/shard_map/pallas_call | solution.py:893
  400.3 7.5 add_convert_fusion
  412.6 42.1 %shard_map.278 = (bf16[5,3,1024,256]{3,2,1,0:T(8,128)(2,1)}, bf16[5,3,1024,256]{3,2,1,0:T(8,128)(2,1)}, bf16[640,2048]{1,0:T(8,128)(2,1)}, f32[640,128]{1,0:T(8,128)}) custom-call(bf16[640,2048]{1,0:T(8,128)(2,1)} %shard_map.274.refs_0_, bf16[640,2048]{1,0:T(8,128)(2,1)} %get-tuple-element.98.refs_1_, f32[640,128]{1,0:T(8,128)} %broadcast_in_dim.41.refs_2_, ...), custom_call_target="tpu_custom_call" | custom-call | bytes 2621440 | tf_op jit(solution)/shard_map/pallas_call | solution.py:893
  456.0 6.5 add_convert_fusion.1
  467.3 38.0 %shard_map.279 = (bf16[640,1024]{1,0:T(8,128)(2,1)}, f32[4,8,256]{2,1,0:T(8,128)}) custom-call(bf16[640,2048]{1,0:T(8,128)(2,1)} %add_convert_fusion.2.refs_0_, f32[4,8,256]{2,1,0:T(8,128)} %pad.8.refs_1_), custom_call_target="tpu_custom_call" | custom-call | bytes 7864320 | tf_op jit(solution)/shard_map/pallas_call | solution.py:389
  522.1 36.8 %shard_map.280 = bf16[640,2048]{1,0:T(8,128)(2,1)} custom-call(bf16[640,1024]{1,0:T(8,128)(2,1)} %add_convert_fusion.4.rows_ref), custom_call_target="tpu_custom_call" | custom-call | bytes 7864320 | tf_op jit(solution)/shard_map/pallas_call | solution.py:246
  571.2 23.3 %shard_map.281 = (bf16[640,1024]{1,0:T(8,128)(2,1)}, bf16[1024,1024]{1,0:T(8,128)(2,1)}, bf16[1024,1024]{1,0:T(8,128)(2,1)}) custom-call(bf16[640,1024]{1,0:T(8,128)(2,1)} %get-tuple-element.82.q_low, bf16[1024,1024]{1,0:T(8,128)(2,1)} %get-tuple-element.83.k_low, bf16[1024,1024]{1,0:T(8,128)(2,1)} %get-tuple-element.84.v_low, ...), custom_call_target="tpu_custom_call" | custom-call | bytes 14680064 | tf_op jit(solution)/shard_map/pallas_call | solution.py:1094
  597.9 6.3 convolution_convert_fusion
  610.0 13.0 %fusion.3.refs_0_ = bf16[1024,2048]{1,0:T(8,128)(2,1)} fusion(f32[4,256,2048]{2,1,0:T(8,128)S(1)} %fusion.49, bf16[1024,2048]{1,0:T(8,128)(2,1)S(1)} %pad_maximum_fusion.2, bf16[2048,2048]{1,0:T(8,128)(2,1)} %get-tuple-element.81), kind=kOutput, calls=%fused_computation.7 | convolution fusion | flops 8594128896 | bytes 25165824 | tf_op jit(solution)/shard_map/dot_general | solution.py:32
  630.5 5.7 add_convert_fusion.3.refs_1_
  636.2 62.7 %shard_map.282 = (f32[256,1024]{1,0:T(8,128)}, bf16[512,2048]{1,0:T(8,128)(2,1)}, bf16[256,1024]{1,0:T(8,128)(2,1)}) custom-call(bf16[1024,2048]{1,0:T(8,128)(2,1)} %fusion.3.refs_0_, bf16[512,2048]{1,0:T(8,128)(2,1)} %add_convert_fusion.3.refs_1_, bf16[256,1024]{1,0:T(8,128)(2,1)} %fusion.17.refs_2_), custom_call_target="tpu_custom_call" | custom-call | bytes 12582912 | tf_op jit(solution)/shard_map/pallas_call | solution.py:389
  700.8 5.0 fusion.117
  718.5 5.0 collective-permute-done.21
  728.7 18.2 %shard_map.283 = (f32[512,2816]{1,0:T(8,128)}, f32[512,2816]{1,0:T(8,128)}, f32[2816,512]{1,0:T(8,128)}) custom-call(bf16[6,3,1024,256]{3,2,1,0:T(8,128)(2,1)} %get-tuple-element.106.refs_0_, bf16[6,3,1024,256]{3,2,1,0:T(8,128)(2,1)} %get-tuple-element.107.refs_1_, bf16[6,3,512,256]{3,2,1,0:T(8,128)(2,1)} %collective-permute-done.9.refs_2_, ...), custom_call_target="tpu_custom_call" | custom-call | bytes 43253760 | tf_op jit(solution)/shard_map/pallas_call | solution.py:952
  746.9 8.7 %collective-permute-done.26 = bf16[128,2048]{1,0:T(8,128)(2,1)} collective-permute-done((bf16[128,2048]{1,0:T(8,128)(2,1)S(1)}, bf16[128,2048]{1,0:T(8,128)(2,1)}, u32[]{:S(2)}, u32[]{:S(2)}) %collective-permute-start.26) | collective-permute-done | bytes 524320 | tf_op jit(solution)/shard_map/ppermute | solution.py:41
  (439 shorter events, 165.1 us)
Async XLA Ops:
  121.8 81.2 %collective-permute-start.2 = (bf16[160,1024]{1,0:T(8,128)(2,1)}, bf16[160,1024]{1,0:T(8,128)(2,1)}, u32[]{:S(2)}, u32[]{:S(2)}) collective-permute-start(bf16[160,1024]{1,0:T(8,128)(2,1)} %get-tuple-element.182), channel_id=1, source_target_pairs={{0,6},{2,4},{4,2},{6,0},{1,7},{3,5},{5,3},{7,1},{8,14},{10,12},{12... | collective-permute-start | bytes 983048 | tf_op jit(solution)/shard_map/ppermute | solution.py:41
  124.1 78.9 %collective-permute-start.1 = (bf16[160,1024]{1,0:T(8,128)(2,1)S(1)}, bf16[160,1024]{1,0:T(8,128)(2,1)}, u32[]{:S(2)}, u32[]{:S(2)}) collective-permute-start(bf16[160,1024]{1,0:T(8,128)(2,1)S(1)} %get-tuple-element.183), channel_id=1, source_target_pairs={{0,4},{2,6},{4,0},{6,2},{1,5},{3,7},{5,1},{7,3},{8,12},{10,14},{12... | collective-permute-start | bytes 983048 | tf_op jit(solution)/shard_map/ppermute | solution.py:41
  124.1 78.9 %collective-permute-start = (bf16[160,1024]{1,0:T(8,128)(2,1)S(1)}, bf16[160,1024]{1,0:T(8,128)(2,1)}, u32[]{:S(2)}, u32[]{:S(2)}) collective-permute-start(bf16[160,1024]{1,0:T(8,128)(2,1)S(1)} %get-tuple-element.184), channel_id=1, source_target_pairs={{0,2},{2,0},{4,6},{6,4},{1,3},{3,1},{5,7},{7,5},{8,10},{10,8},{12,... | collective-permute-start | bytes 983048 | tf_op jit(solution)/shard_map/ppermute | solution.py:41
  126.2 76.9 %collective-permute-start.3 = (bf16[512,2816]{1,0:T(8,128)(2,1)S(1)}, bf16[512,2816]{1,0:T(8,128)(2,1)}, u32[]{:S(2)}, u32[]{:S(2)}) collective-permute-start(bf16[512,2816]{1,0:T(8,128)(2,1)S(1)} %bitcast.142), channel_id=1, source_target_pairs={{0,16},{8,24},{16,0},{24,8},{1,17},{9,25},{17,1},{25,9},{2,18},{10... | collective-permute-start | bytes 8650760 | tf_op jit(solution)/shard_map/ppermute | solution.py:41
  126.7 125.3 %collective-permute-start.5 = (bf16[512,2816]{1,0:T(8,128)(2,1)}, bf16[512,2816]{1,0:T(8,128)(2,1)}, u32[]{:S(2)}, u32[]{:S(2)}) collective-permute-start(bf16[512,2816]{1,0:T(8,128)(2,1)} %bitcast.143), channel_id=1, source_target_pairs={{0,16},{8,24},{16,0},{24,8},{1,17},{9,25},{17,1},{25,9},{2,18},{10... | collective-permute-start | bytes 8650760 | tf_op jit(solution)/shard_map/ppermute | solution.py:41
  252.1 5.5 collective-permute-start.6
  252.1 74.4 %collective-permute-start.7 = (bf16[2816,512]{1,0:T(8,128)(2,1)}, bf16[2816,512]{1,0:T(8,128)(2,1)}, u32[]{:S(2)}, u32[]{:S(2)}) collective-permute-start(bf16[2816,512]{1,0:T(8,128)(2,1)} %bitcast.21.refs_4_.refs_0_.refs_14_), channel_id=1, source_target_pairs={{0,16},{8,24},{16,0},{24,8},{1,17},{9,25},{17,1},{25,9},{2,18},{10... | collective-permute-start | bytes 8650760 | tf_op jit(solution)/shard_map/ppermute | solution.py:41
  326.5 5.7 collective-permute-start.8
  407.8 105.1 %collective-permute-start.9 = (bf16[6,3,512,256]{3,2,1,0:T(8,128)(2,1)}, bf16[6,3,512,256]{3,2,1,0:T(8,128)(2,1)}, u32[]{:S(2)}, u32[]{:S(2)}) collective-permute-start(bf16[6,3,512,256]{3,2,1,0:T(8,128)(2,1)} %add_convert_fusion), channel_id=1, source_target_pairs={{0,16},{8,24},{16,0},{24,8},{1,17},{9,25},{17,1},{25,9},{2,18},{10... | collective-permute-start | bytes 14155784 | tf_op jit(solution)/shard_map/ppermute | solution.py:41
  462.5 134.7 %collective-permute-start.13 = (bf16[5,3,512,256]{3,2,1,0:T(8,128)(2,1)}, bf16[5,3,512,256]{3,2,1,0:T(8,128)(2,1)}, u32[]{:S(2)}, u32[]{:S(2)}) collective-permute-start(bf16[5,3,512,256]{3,2,1,0:T(8,128)(2,1)} %add_convert_fusion.1), channel_id=1, source_target_pairs={{0,16},{8,24},{16,0},{24,8},{1,17},{9,25},{17,1},{25,9},{2,18},{10... | collective-permute-start | bytes 11796488 | tf_op jit(solution)/shard_map/ppermute | solution.py:41
  519.1 49.9 %collective-permute-start.16 = (f32[256,2]{0,1:T(2,128)S(1)}, f32[256,2]{0,1:T(2,128)S(1)}, u32[]{:S(2)}, u32[]{:S(2)}) collective-permute-start(f32[256,2]{0,1:T(2,128)S(1)} %pad_maximum_fusion.14), channel_id=1, source_target_pairs={{0,1},{1,0},{2,3},{3,2},{4,5},{5,4},{6,7},{7,6},{8,9},{9,8},{10,11... | collective-permute-start | bytes 6152 | tf_op jit(solution)/shard_map/ppermute | solution.py:41
  562.3 6.9 collective-permute-start.12
  604.2 26.3 %collective-permute-start.15 = (bf16[1024,2048]{1,0:T(8,128)(2,1)}, bf16[1024,2048]{1,0:T(8,128)(2,1)}, u32[]{:S(2)}, u32[]{:S(2)}) collective-permute-start(bf16[1024,2048]{1,0:T(8,128)(2,1)} %convolution_convert_fusion), channel_id=1, source_target_pairs={{0,8},{8,0},{16,24},{24,16},{1,9},{9,1},{17,25},{25,17},{2,10},{10... | collective-permute-start | bytes 12582920 | tf_op jit(solution)/shard_map/ppermute | solution.py:41
  605.0 25.4 %collective-permute-start.14 = (bf16[1024,512]{1,0:T(8,128)(2,1)}, bf16[1024,512]{1,0:T(8,128)(2,1)}, u32[]{:S(2)}, u32[]{:S(2)}) collective-permute-start(bf16[1024,512]{1,0:T(8,128)(2,1)} %add_convert_fusion.6), channel_id=1, source_target_pairs={{0,16},{8,24},{16,0},{24,8},{1,17},{9,25},{17,1},{25,9},{2,18},{10... | collective-permute-start | bytes 3145736 | tf_op jit(solution)/shard_map/ppermute | solution.py:41
  706.7 11.2 %collective-permute-start.17 = (f32[256,1]{0,1:T(1,128)S(1)}, f32[256,1]{0,1:T(1,128)S(1)}, u32[]{:S(2)}, u32[]{:S(2)}) collective-permute-start(f32[256,1]{0,1:T(1,128)S(1)} %bitcast.219), channel_id=1, source_target_pairs={{0,1},{1,0},{2,3},{3,2},{4,5},{5,4},{6,7},{7,6},{8,9},{9,8},{10,11... | collective-permute-start | bytes 3080 | tf_op jit(solution)/shard_map/ppermute | solution.py:41
  707.5 8.9 %collective-permute-start.20 = (f32[10,1024]{1,0:T(8,128)S(1)}, f32[10,1024]{1,0:T(8,128)S(1)}, u32[]{:S(2)}, u32[]{:S(2)}) collective-permute-start(f32[10,1024]{1,0:T(8,128)S(1)} %pad_maximum_fusion.9), channel_id=1, source_target_pairs={{0,1},{1,0},{2,3},{3,2},{4,5},{5,4},{6,7},{7,6},{8,9},{9,8},{10,11... | collective-permute-start | bytes 122888 | tf_op jit(solution)/shard_map/ppermute | solution.py:41
  709.0 37.9 %collective-permute-start.28 = (bf16[128,2048]{1,0:T(8,128)(2,1)S(1)}, bf16[128,2048]{1,0:T(8,128)(2,1)S(1)}, u32[]{:S(2)}, u32[]{:S(2)}) collective-permute-start(bf16[128,2048]{1,0:T(8,128)(2,1)S(1)} %get-tuple-element.178), channel_id=1, source_target_pairs={{0,2},{2,0},{4,6},{6,4},{1,3},{3,1},{5,7},{7,5},{8,10},{10,8},{12,... | collective-permute-start | bytes 1572872 | tf_op jit(solution)/shard_map/ppermute | solution.py:41
  709.7 37.2 %collective-permute-start.27 = (bf16[128,2048]{1,0:T(8,128)(2,1)S(1)}, bf16[128,2048]{1,0:T(8,128)(2,1)S(1)}, u32[]{:S(2)}, u32[]{:S(2)}) collective-permute-start(bf16[128,2048]{1,0:T(8,128)(2,1)S(1)} %get-tuple-element.179), channel_id=1, source_target_pairs={{0,6},{2,4},{4,2},{6,0},{1,7},{3,5},{5,3},{7,1},{8,14},{10,12},{12... | collective-permute-start | bytes 1572872 | tf_op jit(solution)/shard_map/ppermute | solution.py:41
  713.2 13.7 %collective-permute-start.19 = (bf16[1024,1024]{1,0:T(8,128)(2,1)S(1)}, bf16[1024,1024]{1,0:T(8,128)(2,1)S(1)}, u32[]{:S(2)}, u32[]{:S(2)}) collective-permute-start(bf16[1024,1024]{1,0:T(8,128)(2,1)S(1)} %convolution_convert_fusion.3), channel_id=1, source_target_pairs={{0,8},{8,0},{16,24},{24,16},{1,9},{9,1},{17,25},{25,17},{2,10},{10... | collective-permute-start | bytes 6291464 | tf_op jit(solution)/shard_map/ppermute | solution.py:41
  716.4 39.2 %collective-permute-start.26 = (bf16[128,2048]{1,0:T(8,128)(2,1)S(1)}, bf16[128,2048]{1,0:T(8,128)(2,1)}, u32[]{:S(2)}, u32[]{:S(2)}) collective-permute-start(bf16[128,2048]{1,0:T(8,128)(2,1)S(1)} %get-tuple-element.180), channel_id=1, source_target_pairs={{0,4},{2,6},{4,0},{6,2},{1,5},{3,7},{5,1},{7,3},{8,12},{10,14},{12... | collective-permute-start | bytes 1572872 | tf_op jit(solution)/shard_map/ppermute | solution.py:41
  717.9 5.7 collective-permute-start.21
  725.0 30.7 %collective-permute-start.18 = (bf16[256,1024]{1,0:T(8,128)(2,1)S(1)}, bf16[256,1024]{1,0:T(8,128)(2,1)S(1)}, u32[]{:S(2)}, u32[]{:S(2)}) collective-permute-start(bf16[256,1024]{1,0:T(8,128)(2,1)S(1)} %fusion.23), channel_id=1, source_target_pairs={{0,1},{1,0},{2,3},{3,2},{4,5},{5,4},{6,7},{7,6},{8,9},{9,8},{10,11... | collective-permute-start | bytes 1572872 | tf_op jit(solution)/shard_map/ppermute | solution.py:41
  728.2 31.0 %collective-permute-start.23 = (bf16[512,1024]{1,0:T(8,128)(2,1)S(1)}, bf16[512,1024]{1,0:T(8,128)(2,1)S(1)}, u32[]{:S(2)}, u32[]{:S(2)}) collective-permute-start(bf16[512,1024]{1,0:T(8,128)(2,1)S(1)} %add_convert_fusion.5), channel_id=1, source_target_pairs={{0,16},{8,24},{16,0},{24,8},{1,17},{9,25},{17,1},{25,9},{2,18},{10... | collective-permute-start | bytes 3145736 | tf_op jit(solution)/shard_map/ppermute | solution.py:41
  759.2 6.1 collective-permute-start.24
  (120 other events, 1528.5 us)
